TPU v7x, 32 devices: a whole 2x2x4 slice. The times are simulated.
32 devices in a mesh: groups: 2 (over x), expert: 16 (over z, y, core).
Axes of the slice: x: 2, y: 2, z: 4, core: 2. Of those that a mesh axis runs over, the one named last changes fastest.
Arguments:
- block_values: bfloat16 [4096, 2048], P(('groups', 'expert')), parts along dimension 0, may hold values from -4 to 4
- block_exps: int32 [4096, 16], P(('groups', 'expert')), parts along dimension 0, may hold values from -3 to 1
- row_ids: int32 [4096], P(('groups', 'expert')), parts along dimension 0, may hold values from 0 to 4095, as said below
- expert_ids: int32 [4096, 4], P(('groups', 'expert')), parts along dimension 0, may hold values from 0 to 63, all different within a row; in each aligned block of 128 rows (0 to 127, 128 to 255, ...) at most 12 rows name the same one
- gate_weights: float32 [4096, 4], P(('groups', 'expert')), parts along dimension 0, may hold values from 0.05 to 0.5
- table: bfloat16 [4096, 2048], P('expert'), may hold values from -4 to 4
- w_gate: bfloat16 [64, 2048, 1408], P('expert'), may hold values from -0.125 to 0.125
- w_up: bfloat16 [64, 2048, 1408], P('expert'), may hold values from -0.125 to 0.125
- w_down: bfloat16 [64, 1408, 2048], P('expert'), may hold values from -0.15625 to 0.15625
- out_grad: bfloat16 [4096, 2048], P(('groups', 'expert')), parts along dimension 0, may hold values from -0.19921875 to 0.19921875
Outputs:
- mixed: bfloat16 [4096, 2048], P(('groups', 'expert')), parts along dimension 0
- gate_grads: float32 [4096, 4], P(('groups', 'expert')), parts along dimension 0
There are 2 independent parts, one for each index of `groups`. A program takes and returns all parts, laid end to end along the dimension named above; an argument that names none is the same for every part. Nothing has to cross between parts.
Inputs may be any that keep to these rules, and one draw needn't show every extreme that they name: `row_ids`: among the 128 tokens of one device at most 16 name rows of any one block of 256 consecutive table rows, and every device has a block named exactly 16 times. `expert_ids`: in the 128 rows of one device no expert is named by more than 12 rows, a bound that some block reaches.
All inputs are finite; a program needn't handle non-finite values.
Results may differ from a plain program's by a relative error of at most 0.0071.
Values may be sent and summed in bfloat16 or wider, within the bound.
No kernel may reach another device: no remote copies, remote signals or barrier semaphores. Data moves between devices by JAX's collectives and lax.ppermute only.
A program may use at most 192 MiB of HBM per device.

v0:
```python
import jax
import jax.numpy as jnp
from jax import lax
from jax.sharding import PartitionSpec as P

EXPERTS = 64
TOP = 4
CAP = 12


def expert_work(arrived, w_gate, w_up, w_down):
    gate_act = jnp.einsum("sjcd,jdf->sjcf", arrived, w_gate, preferred_element_type=jnp.float32)
    up_act = jnp.einsum("sjcd,jdf->sjcf", arrived, w_up, preferred_element_type=jnp.float32)
    hidden = (jax.nn.silu(gate_act) * up_act).astype(jnp.bfloat16)
    return jnp.einsum("sjcf,jfd->sjcd", hidden, w_down, preferred_element_type=jnp.float32).astype(
        jnp.bfloat16
    )


def full_path(buffer, w_gate, w_up, w_down, device_count, exp_dev, width_split, features):
    group_count = EXPERTS // exp_dev
    grouped = buffer.reshape(group_count, 1, exp_dev, CAP, features)
    outgoing = jnp.broadcast_to(
        grouped, (group_count, width_split, exp_dev, CAP, features)
    ).reshape(device_count, exp_dev, CAP, features)
    returned_out = lax.all_to_all(
        expert_work(
            lax.all_to_all(outgoing, "expert", split_axis=0, concat_axis=0, tiled=True),
            w_gate,
            w_up,
            w_down,
        ),
        "expert",
        split_axis=0,
        concat_axis=0,
        tiled=True,
    )
    pieces = returned_out.reshape(group_count, width_split, exp_dev, CAP, features).astype(
        jnp.float32
    )
    return jnp.sum(pieces, axis=1).astype(jnp.bfloat16).reshape(EXPERTS * CAP, features)


def local(
    block_values,
    block_exps,
    row_ids,
    expert_ids,
    gate_weights,
    table,
    w_gate,
    w_up,
    w_down,
    out_grad,
):
    device_count = lax.axis_size("expert")
    tok_rows = block_values.shape[0]
    features = block_values.shape[1]
    rows_held = table.shape[0]
    look_cap = max(2, 2 * tok_rows // device_count)
    exp_dev = w_gate.shape[0]
    width_split = device_count * exp_dev // EXPERTS
    owners = row_ids // rows_held
    local_row = row_ids % rows_held
    owner_hot = (owners[:, None] == jnp.arange(device_count, dtype=jnp.int32)[None, :]).astype(
        jnp.int32
    )
    owner_rank = jnp.sum((jnp.cumsum(owner_hot, axis=0) - 1) * owner_hot, axis=1)
    placed = owners * look_cap + owner_rank
    wanted = jnp.zeros((device_count * look_cap,), jnp.int32).at[placed].set(local_row)
    requested = lax.all_to_all(
        wanted.reshape(device_count, look_cap), "expert", split_axis=0, concat_axis=0, tiled=True
    )
    fetched = jnp.take(table, requested.reshape(-1), axis=0).reshape(
        device_count, look_cap, features
    )
    rows_returned = lax.all_to_all(fetched, "expert", split_axis=0, concat_axis=0, tiled=True)
    embedded = jnp.take(rows_returned.reshape(device_count * look_cap, features), placed, axis=0)
    scales = jnp.exp2(block_exps.astype(jnp.float32))
    blocks = (
        block_values.reshape(tok_rows, scales.shape[1], -1).astype(jnp.float32) * scales[:, :, None]
    )
    token_state = (blocks.reshape(tok_rows, features) + embedded.astype(jnp.float32)).astype(
        jnp.bfloat16
    )
    flat_ids = expert_ids.reshape(-1)
    expert_hot = (flat_ids[:, None] == jnp.arange(EXPERTS, dtype=jnp.int32)[None, :]).astype(
        jnp.int32
    )
    expert_rank = jnp.sum((jnp.cumsum(expert_hot, axis=0) - 1) * expert_hot, axis=1)
    slot_of = flat_ids * CAP + expert_rank
    token_index = jnp.arange(tok_rows * TOP, dtype=jnp.int32) // TOP
    source = jnp.full((EXPERTS * CAP,), tok_rows, jnp.int32).at[slot_of].set(token_index)
    padded = jnp.concatenate([token_state, jnp.zeros((1, features), jnp.bfloat16)], axis=0)
    buffer = jnp.take(padded, source, axis=0)
    expert_out = full_path(
        buffer, w_gate, w_up, w_down, device_count, exp_dev, width_split, features
    )
    chosen = jnp.take(expert_out, slot_of, axis=0).reshape(tok_rows, TOP, features)
    mixed = jnp.sum(gate_weights[:, :, None] * chosen.astype(jnp.float32), axis=1).astype(
        jnp.bfloat16
    )
    gate_grads = jnp.einsum("tkd,td->tk", chosen, out_grad, preferred_element_type=jnp.float32)
    return (mixed, gate_grads)


def solution(mesh):
    return jax.shard_map(
        local,
        mesh=mesh,
        in_specs=(
            P(("groups", "expert"), None),
            P(("groups", "expert"), None),
            P(("groups", "expert")),
            P(("groups", "expert"), None),
            P(("groups", "expert"), None),
            P("expert", None),
            P("expert", None, None),
            P("expert", None, None),
            P("expert", None, None),
            P(("groups", "expert"), None),
        ),
        out_specs=(P(("groups", "expert"), None), P(("groups", "expert"), None)),
        check_vma=False,
    )
```

profile of v0, /device:TPU:13, one launch (start us, length us, event | category | flops | bytes accessed | tf_op | source)
XLA Modules:
  0.0 282.1 jit_solution(8791168306518333516)
XLA Ops:
  0.6 0.8 and_select_fusion
  1.4 0.1 fusion.28
  1.5 0.2 reduce_window_sum.25
  1.7 0.2 select_reduce_fusion
  1.9 1.0 scatter_custom_fusion.1
  2.8 0.1 all_to_all.15
  2.9 10.2 %all_to_all.24 = s32[16,1,16]{2,1,0:T(1,128)S(1)} all-to-all(s32[16,1,16]{2,1,0:T(1,128)S(1)} %all_to_all.15), channel_id=1, replica_groups=mesh['groups'=2,'expert'=16] {'expert'}, dimensions={0} | all-to-all | bytes 2048 | tf_op jit(solution)/shard_map/all_to_all | solution.py:71
  13.1 0.5 broadcast.188
  13.6 0.7 reduce.5
  14.4 1.4 gather_fusion
  15.8 1.2 broadcast_select_fusion.3
  16.9 6.2 %all-to-all-start.1 = ((bf16[16,16,2048]{2,1,0:T(8,128)(2,1)}), bf16[16,16,2048]{2,1,0:T(8,128)(2,1)S(1)}, u32[]{:S(2)}, u32[]{:S(2)}) async-start(bf16[16,16,2048]{2,1,0:T(8,128)(2,1)} %broadcast_select_fusion.3), calls=%async_computation.1 | async-start | bytes 2097152 | tf_op jit(solution)/shard_map/all_to_all | solution.py:77
  23.1 0.1 copy.45
  23.2 0.1 eq.41
  23.3 0.1 reshape.152
  23.5 0.1 copy.51
  23.6 1.2 reduce-window.6
  24.8 0.2 slice_reduce_fusion
  25.1 0.1 copy.50
  25.2 0.1 mul.61
  25.3 0.1 fusion.26
  25.4 2.4 scatter_custom_fusion
  27.9 0.1 broadcast_in_dim.66
  28.1 19.9 %all-to-all-done.1 = bf16[16,16,2048]{2,1,0:T(8,128)(2,1)S(1)} async-done(((bf16[16,16,2048]{2,1,0:T(8,128)(2,1)}), bf16[16,16,2048]{2,1,0:T(8,128)(2,1)S(1)}, u32[]{:S(2)}, u32[]{:S(2)}) %all-to-all-start.1) | async-done | bytes 1048608 | tf_op jit(solution)/shard_map/all_to_all | solution.py:77
  48.0 0.9 gather_fusion.1
  48.9 0.3 mul.62
  49.3 0.7 fusion.22
  50.0 4.3 %gather_fusion.2 = bf16[768,2048]{1,0:T(8,128)(2,1)} fusion(bf16[129,2048]{1,0:T(8,128)(2,1)S(1)} %concatenate.3, s32[1024]{0:T(1024)S(1)} %pad_clamp_fusion.1), kind=kCustom, calls=%fused_computation.2 | custom fusion | bytes 6294528 | tf_op jit(solution)/shard_map/jit(_take)/gather | solution.py:95
  54.3 6.1 %gather.26 = bf16[16,4,12,2048]{3,2,1,0:T(8,128)(2,1)} reshape(bf16[768,2048]{1,0:T(8,128)(2,1)} %gather_fusion.2) | data formatting | bytes 6291456 | tf_op jit(solution)/shard_map/jit(_take)/gather | solution.py:95
  60.4 2.6 broadcast_select_fusion
  63.0 2.7 copy.52
  65.7 74.5 %all_to_all.25 = bf16[16,4,12,2048]{3,1,2,0:T(4,128)(2,1)S(1)} all-to-all(bf16[16,4,12,2048]{3,1,2,0:T(4,128)(2,1)S(1)} %copy.52), channel_id=1, replica_groups=mesh['groups'=2,'expert'=16] {'expert'}, dimensions={0} | all-to-all | bytes 6291456 | tf_op jit(solution)/shard_map/all_to_all | solution.py:28
  140.2 13.9 %fusion.2 = f32[4,16,12,1408]{3,1,2,0:T(8,128)} fusion(bf16[4,2048,1408]{2,1,0:T(8,128)(2,1)} %param.17, bf16[16,4,12,2048]{3,1,2,0:T(4,128)(2,1)S(1)} %all_to_all.25), kind=kOutput, calls=%fused_computation.8 | convolution fusion | flops 4429185024 | bytes 30539776 | tf_op jit(solution)/shard_map/sjcd,jdf->sjcf/dot_general | solution.py:13
  154.1 13.0 %fusion.6 = bf16[16,4,12,1408]{3,0,2,1:T(8,128)(2,1)S(1)} fusion(f32[4,16,12,1408]{3,1,2,0:T(8,128)} %fusion.2, bf16[4,2048,1408]{2,1,0:T(8,128)(2,1)} %param.16, bf16[16,4,12,2048]{3,1,2,0:T(4,128)(2,1)S(1)} %all_to_all.25), kind=kOutput, calls=%fused_computation.13 | convolution fusion | flops 4435673088 | bytes 32702464 | tf_op jit(solution)/shard_map/sjcd,jdf->sjcf/dot_general | solution.py:12
  167.1 10.3 %fusion.15 = bf16[16,4,12,2048]{3,0,2,1:T(8,128)(2,1)S(1)} fusion(bf16[16,4,12,1408]{3,0,2,1:T(8,128)(2,1)S(1)} %fusion.6, bf16[4,1408,2048]{2,1,0:T(8,128)(2,1)} %param.18), kind=kOutput, calls=%fused_computation.22 | convolution fusion | flops 4430757888 | bytes 28377088 | tf_op jit(solution)/shard_map/sjcf,jfd->sjcd/dot_general | solution.py:15
  177.5 4.1 %copy.55 = bf16[16,4,12,2048]{3,1,2,0:T(4,128)(2,1)} copy(bf16[16,4,12,2048]{3,0,2,1:T(8,128)(2,1)S(1)} %fusion.15) | data formatting | bytes 6291456 | tf_op jit(solution)/shard_map/convert_element_type | solution.py:15
  181.6 5.6 %all-to-all-start.3 = ((bf16[16,4,12,2048]{3,1,2,0:T(4,128)(2,1)}), bf16[16,4,12,2048]{3,1,2,0:T(4,128)(2,1)S(1)}, u32[]{:S(2)}, u32[]{:S(2)}) async-start(bf16[16,4,12,2048]{3,1,2,0:T(4,128)(2,1)} %copy.55), calls=%async_computation.3 | async-start | bytes 6291456 | tf_op jit(solution)/shard_map/all_to_all | solution.py:26
  187.1 0.1 reduce_sum.36
  187.3 0.1 copy.49
  187.5 0.1 copy.44
  187.6 69.4 %all-to-all-done.3 = bf16[16,4,12,2048]{3,1,2,0:T(4,128)(2,1)S(1)} async-done(((bf16[16,4,12,2048]{3,1,2,0:T(4,128)(2,1)}), bf16[16,4,12,2048]{3,1,2,0:T(4,128)(2,1)S(1)}, u32[]{:S(2)}, u32[]{:S(2)}) %all-to-all-start.3) | async-done | bytes 3145760 | tf_op jit(solution)/shard_map/all_to_all | solution.py:26
  257.0 4.2 %copy.56 = bf16[16,4,12,2048]{3,2,1,0:T(8,128)(2,1)} copy(bf16[16,4,12,2048]{3,1,2,0:T(4,128)(2,1)S(1)} %all-to-all-done.3) | data formatting | bytes 6291456 | tf_op jit(solution)/shard_map/all_to_all | solution.py:26
  261.3 4.7 %convert_element_type.52 = bf16[768,2048]{1,0:T(8,128)(2,1)S(1)} reshape(bf16[16,4,12,2048]{3,2,1,0:T(8,128)(2,1)} %copy.56) | data formatting | bytes 6291456 | tf_op jit(solution)/shard_map/convert_element_type | solution.py:41
  266.0 3.3 %gather_fusion.3 = bf16[512,2048]{1,0:T(8,128)(2,1)} fusion(bf16[768,2048]{1,0:T(8,128)(2,1)S(1)} %convert_element_type.52, s32[1024]{0:T(1024)S(1)} %pad_clamp_fusion), kind=kCustom, calls=%fused_computation.3 | custom fusion | bytes 4196352 | tf_op jit(solution)/shard_map/jit(_take)/gather | solution.py:99
  269.3 2.7 gather.28
  272.1 4.4 %fusion.20 = f32[128,1,4]{2,1,0:T(1,128)S(1)} fusion(bf16[128,4,2048]{2,1,0:T(4,128)(2,1)S(1)} %gather.28, pred[128,4]{1,0:T(8,128)(4,1)S(1)} %copy.49, bf16[128,2048,1]{1,0,2:T(8,128)(2,1)} %bitcast.80), kind=kOutput, calls=%fused_computation.26 | convolution fusion | flops 3145728 | bytes 2624000 | tf_op jit(solution)/shard_map/tkd,td->tk/dot_general | solution.py:103
  276.5 0.7 copy.61
  277.2 4.9 %multiply_reduce_fusion = bf16[128,2048]{1,0:T(8,128)(2,1)} fusion(f32[128,4]{1,0:T(8,128)S(1)} %copy.44, bf16[128,4,2048]{2,1,0:T(4,128)(2,1)S(1)} %gather.28, pred[128,4]{1,0:T(8,128)(4,1)S(1)} %copy.49), kind=kLoop, calls=%fused_computation.19 | loop fusion | flops 3932160 | bytes 2624000 | tf_op jit(solution)/shard_map/reduce_sum | solution.py:100
  (32 shorter events, 0.4 us)
Async XLA Ops:
  0.6 13.8 %copy-start = (bf16[256,2048]{1,0:T(8,128)(2,1)S(1)}, bf16[256,2048]{1,0:T(8,128)(2,1)}, u32[]{:S(2)}) copy-start(bf16[256,2048]{1,0:T(8,128)(2,1)} %param.15) | copy-start | bytes 3145732
  15.8 7.4 %copy-start.3 = (s32[128,4]{0,1:T(4,128)S(1)}, s32[128,4]{0,1:T(4,128)}, u32[]{:S(2)}) copy-start(s32[128,4]{0,1:T(4,128)} %param.13) | copy-start | bytes 6148
  15.8 7.7 %copy-start.4 = (s32[128,16]{0,1:T(8,128)S(1)}, s32[128,16]{0,1:T(8,128)}, u32[]{:S(2)}) copy-start(s32[128,16]{0,1:T(8,128)} %param.11) | copy-start | bytes 24580
  16.9 31.1 %all-to-all-start.1 = ((bf16[16,16,2048]{2,1,0:T(8,128)(2,1)}), bf16[16,16,2048]{2,1,0:T(8,128)(2,1)S(1)}, u32[]{:S(2)}, u32[]{:S(2)}) async-start(bf16[16,16,2048]{2,1,0:T(8,128)(2,1)} %broadcast_select_fusion.3), calls=%async_computation.1 | async-start | bytes 2097152 | tf_op jit(solution)/shard_map/all_to_all | solution.py:77
  24.8 24.5 %copy-start.2 = (bf16[128,2048]{1,0:T(8,128)(2,1)S(1)}, bf16[128,2048]{1,0:T(8,128)(2,1)}, u32[]{:S(2)}) copy-start(bf16[128,2048]{1,0:T(8,128)(2,1)} %param.10) | copy-start | bytes 1572868
  181.6 5.9 %copy-start.5 = (f32[128,4]{0,1:T(4,128)S(1)}, f32[128,4]{0,1:T(4,128)}, u32[]{:S(2)}) copy-start(f32[128,4]{0,1:T(4,128)} %param.14) | copy-start | bytes 6148
  181.6 75.4 %all-to-all-start.3 = ((bf16[16,4,12,2048]{3,1,2,0:T(4,128)(2,1)}), bf16[16,4,12,2048]{3,1,2,0:T(4,128)(2,1)S(1)}, u32[]{:S(2)}, u32[]{:S(2)}) async-start(bf16[16,4,12,2048]{3,1,2,0:T(4,128)(2,1)} %copy.55), calls=%async_computation.3 | async-start | bytes 6291456 | tf_op jit(solution)/shard_map/all_to_all | solution.py:26
  272.1 10.0 %copy-start.1 = (bf16[256,2048]{1,0:T(8,128)(2,1)S(1)}, bf16[256,2048]{1,0:T(8,128)(2,1)}, u32[]{:S(2)}) copy-start(bf16[256,2048]{1,0:T(8,128)(2,1)} %param.15) | copy-start | bytes 3145732
where the time goes:
time: 283 us; the launch traced here: 282 us
  waiting for transfers between devices  89.4 us (32%)
  blocking collectives  84.6 us (30%)
  matrix products  41.7 us (15%)
  local copies, waits for them, and re-layouts  41.1 us (15%)
  other arithmetic  12.7 us (4%)
  starting transfers between devices  11.7 us (4%)
    all_to_all x1, blocking collectives, full_path(): lax.all_to_all(outgoing, 'expert', split_axis=0, concat_axis=0, tiled=True)  74.5 us
    all_to_all x1, waiting for transfers between devices, full_path(): lax.all_to_all(expert_work(lax.all_to_all(outgoing, 'expert', split_axis=...  69.4 us
    all_to_all x1, waiting for transfers between devices, local(): lax.all_to_all(fetched, 'expert', split_axis=0, concat_axis=0, tiled=True)  19.9 us
    dot_general x1, matrix products, expert_work(): jnp.einsum('sjcd,jdf->sjcf', arrived, w_up, preferred_element_type=jnp.fl...  13.9 us
    dot_general x1, matrix products, expert_work(): jnp.einsum('sjcd,jdf->sjcf', arrived, w_gate, preferred_element_type=jnp....  13 us
    dot_general x1, matrix products, expert_work(): jnp.einsum('sjcf,jfd->sjcd', hidden, w_down, preferred_element_type=jnp.f...  10.3 us
    gather x2, local copies, waits for them, and re-layouts, local(): buffer = jnp.take(padded, source, axis=0)  10.3 us
    all_to_all x1, blocking collectives, local(): lax.all_to_all(wanted.reshape(device_count, look_cap), 'expert', split_ax...  10.2 us
  transfers between devices with their start and end apart: 2, of which 2 were waited for; matrix products, arithmetic and copies ran while one was open for 2% of the time, Pallas kernels for 0%

commit v1 on v0

--- a/solution.py
+++ b/solution.py
@@ -17,28 +17,47 @@
     )
 
 
-def full_path(buffer, w_gate, w_up, w_down, device_count, exp_dev, width_split, features):
+def return_path(partial, width_split):
+    device_count, exp_dev, cap, features = partial.shape
+    returned_out = lax.all_to_all(partial, "expert", split_axis=0, concat_axis=0, tiled=True)
+    group_count = device_count // width_split
+    pieces = returned_out.reshape(group_count, width_split, exp_dev, cap, features)
+    if width_split == 1:
+        return pieces.reshape(EXPERTS * CAP, features)
+    return (
+        jnp.sum(pieces.astype(jnp.float32), axis=1)
+        .astype(jnp.bfloat16)
+        .reshape(EXPERTS * CAP, features)
+    )
+
+
+def gathered_rows(token_state, expert_ids, exp_dev, width_split):
+    states = lax.all_gather(token_state, "expert", axis=0, tiled=False)
+    ids = lax.all_gather(expert_ids, "expert", axis=0, tiled=False)
+    device_count, tok_rows, features = states.shape
+    first = lax.axis_index("expert") // width_split * exp_dev
+    mine = first + jnp.arange(exp_dev, dtype=jnp.int32)
+    hit = jnp.any(ids[:, :, :, None] == mine, axis=2)
+    rank = jnp.cumsum(hit.astype(jnp.int32), axis=1) - 1
+    slot = jnp.arange(CAP, dtype=jnp.int32)
+    chosen = hit[:, :, :, None] & (rank[:, :, :, None] == slot)
+    return jnp.einsum(
+        "stjc,std->sjcd", chosen.astype(jnp.bfloat16), states, preferred_element_type=jnp.float32
+    ).astype(jnp.bfloat16)
+
+
+def sent_rows(token_state, slot_of, device_count, exp_dev, width_split):
+    tok_rows, features = token_state.shape
+    token_index = jnp.arange(tok_rows * TOP, dtype=jnp.int32) // TOP
+    source = jnp.full((EXPERTS * CAP,), tok_rows, jnp.int32).at[slot_of].set(token_index)
+    padded = jnp.concatenate([token_state, jnp.zeros((1, features), jnp.bfloat16)], axis=0)
+    buffer = jnp.take(padded, source, axis=0)
     group_count = EXPERTS // exp_dev
     grouped = buffer.reshape(group_count, 1, exp_dev, CAP, features)
     outgoing = jnp.broadcast_to(
         grouped, (group_count, width_split, exp_dev, CAP, features)
     ).reshape(device_count, exp_dev, CAP, features)
-    returned_out = lax.all_to_all(
-        expert_work(
-            lax.all_to_all(outgoing, "expert", split_axis=0, concat_axis=0, tiled=True),
-            w_gate,
-            w_up,
-            w_down,
-        ),
-        "expert",
-        split_axis=0,
-        concat_axis=0,
-        tiled=True,
-    )
-    pieces = returned_out.reshape(group_count, width_split, exp_dev, CAP, features).astype(
-        jnp.float32
-    )
-    return jnp.sum(pieces, axis=1).astype(jnp.bfloat16).reshape(EXPERTS * CAP, features)
+    return lax.all_to_all(outgoing, "expert", split_axis=0, concat_axis=0, tiled=True)
 
 
 def local(
@@ -89,13 +108,11 @@
     )
     expert_rank = jnp.sum((jnp.cumsum(expert_hot, axis=0) - 1) * expert_hot, axis=1)
     slot_of = flat_ids * CAP + expert_rank
-    token_index = jnp.arange(tok_rows * TOP, dtype=jnp.int32) // TOP
-    source = jnp.full((EXPERTS * CAP,), tok_rows, jnp.int32).at[slot_of].set(token_index)
-    padded = jnp.concatenate([token_state, jnp.zeros((1, features), jnp.bfloat16)], axis=0)
-    buffer = jnp.take(padded, source, axis=0)
-    expert_out = full_path(
-        buffer, w_gate, w_up, w_down, device_count, exp_dev, width_split, features
-    )
+    if device_count <= 32:
+        arrived = gathered_rows(token_state, expert_ids, exp_dev, width_split)
+    else:
+        arrived = sent_rows(token_state, slot_of, device_count, exp_dev, width_split)
+    expert_out = return_path(expert_work(arrived, w_gate, w_up, w_down), width_split)
     chosen = jnp.take(expert_out, slot_of, axis=0).reshape(tok_rows, TOP, features)
     mixed = jnp.sum(gate_weights[:, :, None] * chosen.astype(jnp.float32), axis=1).astype(
         jnp.bfloat16

time: 283 us -> 293 us (1.035)
  blocking collectives: 84.6 us -> 24.9 us
  waiting for transfers between devices: 89.4 us -> 126 us
  other arithmetic: 12.7 us -> 34.4 us
  local copies, waits for them, and re-layouts: 41.1 us -> 26.4 us
  between operations: 0.92 us -> 14.3 us
  matrix products: 41.7 us -> 54.3 us
    all_to_all x1 -> x0, blocking collectives: 74.5 us -> none  [full_path(): lax.all_to_all(outgoing, 'expert', split_axis=0, concat_axis=0, tiled=True)]
    all_gather x0 -> x1, waiting for transfers between devices: none -> 34.1 us  [gathered_rows(): states = lax.all_gather(token_state, 'expert', axis=0, tiled=False)]
    another operation x2 -> x3, other arithmetic: 1.24 us -> 24.8 us  [the longest x1 23.6 us: gathered_rows(): rank = jnp.cumsum(hit.astype(jnp.int32), axis=1) - 1]
    all_gather x0 -> x1, blocking collectives: none -> 14.7 us  [gathered_rows(): ids = lax.all_gather(expert_ids, 'expert', axis=0, tiled=False)]
    gather x2 -> x0, local copies, waits for them, and re-layouts: 10.3 us -> none  [local(): buffer = jnp.take(padded, source, axis=0)]
    dot_general x0 -> x1, matrix products: none -> 6.6 us  [gathered_rows(): jnp.einsum('stjc,std->sjcd', chosen.astype(jnp.bfloat16), states, preferr...]
    all_to_all x1, waiting for transfers between devices: 19.9 us -> 24.7 us  [local(): lax.all_to_all(fetched, 'expert', split_axis=0, concat_axis=0, tiled=True)]
    another operation x1 -> x2, local copies, waits for them, and re-layouts: 0.01 us -> 4.72 us  [the longest x1 4.71 us: return_path(): return pieces.reshape(EXPERTS * CAP, features)]
  transfers between devices with their start and end apart: 2 -> 3, of which waited for: 2 -> 3; matrix products, arithmetic and copies ran while one was open for 2% -> 9% of each run, Pallas kernels for 0% -> 0%
where the time goes in v1:
time: 293 us; the launch traced here: 292 us
  waiting for transfers between devices  126 us (43%)
  matrix products  54.3 us (19%)
  other arithmetic  34.4 us (12%)
  local copies, waits for them, and re-layouts  26.4 us (9%)
  blocking collectives  24.9 us (8%)
  between operations  14.3 us (5%)
  starting transfers between devices  12 us (4%)
    all_to_all x1, waiting for transfers between devices, return_path(): lax.all_to_all(partial, 'expert', split_axis=0, concat_axis=0, tiled=True)  67.2 us
    all_gather x1, waiting for transfers between devices, gathered_rows(): states = lax.all_gather(token_state, 'expert', axis=0, tiled=False)  34.1 us
    all_to_all x1, waiting for transfers between devices, local(): lax.all_to_all(fetched, 'expert', split_axis=0, concat_axis=0, tiled=True)  24.7 us
    another operation x1, other arithmetic, gathered_rows(): rank = jnp.cumsum(hit.astype(jnp.int32), axis=1) - 1  23.6 us
    dot_general x1, matrix products, expert_work(): jnp.einsum('sjcd,jdf->sjcf', arrived, w_up, preferred_element_type=jnp.fl...  16.5 us
    dot_general x1, matrix products, expert_work(): jnp.einsum('sjcd,jdf->sjcf', arrived, w_gate, preferred_element_type=jnp....  16.4 us
    all_gather x1, blocking collectives, gathered_rows(): ids = lax.all_gather(expert_ids, 'expert', axis=0, tiled=False)  14.7 us
    dot_general x1, matrix products, expert_work(): jnp.einsum('sjcf,jfd->sjcd', hidden, w_down, preferred_element_type=jnp.f...  10.4 us
  transfers between devices with their start and end apart: 3, of which 3 were waited for; matrix products, arithmetic and copies ran while one was open for 9% of the time, Pallas kernels for 0%

profile of v1, /device:TPU:13, one launch (start us, length us, event | category | flops | bytes accessed | tf_op | source)
XLA Modules:
  0.0 292.3 jit_solution(2827292117919654823)
XLA Ops:
  7.2 0.8 and_select_fusion
  7.9 0.1 fusion.31
  8.0 0.2 reduce_window_sum.37
  8.2 0.2 select_reduce_fusion
  8.4 1.0 scatter_custom_fusion
  9.4 0.1 all_to_all.12
  9.5 10.2 %all_to_all.19 = s32[16,1,16]{2,1,0:T(1,128)S(1)} all-to-all(s32[16,1,16]{2,1,0:T(1,128)S(1)} %all_to_all.12), channel_id=1, replica_groups=mesh['groups'=2,'expert'=16] {'expert'}, dimensions={0} | all-to-all | bytes 2048 | tf_op jit(solution)/shard_map/all_to_all | solution.py:90
  19.6 0.5 broadcast.182
  20.1 0.7 reduce.5
  20.9 1.4 gather_fusion
  22.3 1.2 broadcast_select_fusion.2
  23.5 6.3 %all-to-all-start.1 = ((bf16[16,16,2048]{2,1,0:T(8,128)(2,1)}), bf16[16,16,2048]{2,1,0:T(8,128)(2,1)S(1)}, u32[]{:S(2)}, u32[]{:S(2)}) async-start(bf16[16,16,2048]{2,1,0:T(8,128)(2,1)} %broadcast_select_fusion.2), calls=%async_computation.1 | async-start | bytes 2097152 | tf_op jit(solution)/shard_map/all_to_all | solution.py:96
  29.8 0.1 copy.77
  29.9 24.7 %all-to-all-done.1 = bf16[16,16,2048]{2,1,0:T(8,128)(2,1)S(1)} async-done(((bf16[16,16,2048]{2,1,0:T(8,128)(2,1)}), bf16[16,16,2048]{2,1,0:T(8,128)(2,1)S(1)}, u32[]{:S(2)}, u32[]{:S(2)}) %all-to-all-start.1) | async-done | bytes 1048608 | tf_op jit(solution)/shard_map/all_to_all | solution.py:96
  54.7 0.9 gather_fusion.1
  55.6 0.3 mul.65
  55.9 1.4 fusion.20
  57.4 14.7 %all-gather = s32[2048,4]{0,1:T(4,128)S(1)} all-gather(s32[128,4]{0,1:T(4,128)S(1)} %copy-done.3), channel_id=2, replica_groups=mesh['groups'=2,'expert'=16] {'expert'}, dimensions={0}, use_global_device_ids=true | all-gather | bytes 34816 | tf_op jit(solution)/shard_map/all_gather | solution.py:36
  72.1 0.1 compare_reduce_fusion
  72.3 0.5 copy.75
  72.8 23.6 %broadcast_add_fusion = s32[16,128,4]{2,0,1:T(8,128)S(1)} fusion(s32[16,128,4]{2,0,1:T(8,128)S(1)} %copy.75), kind=kOutput, calls=%fused_computation.30 | output fusion | flops 1048576 | bytes 65536 | tf_op jit(solution)/shard_map/jit(cumsum)/reduce_window_sum | solution.py:41
  96.4 0.4 copy.76
  96.8 34.1 %all-gather.4.cloned.1.call-done = bf16[2048,2048]{1,0:T(8,128)(2,1)} async-done(((bf16[128,2048]{1,0:T(8,128)(2,1)}), bf16[2048,2048]{1,0:T(8,128)(2,1)}) %all-gather.4.cloned.1.call-update) | async-done | bytes 8388624 | tf_op jit(solution)/shard_map/all_gather | solution.py:35
  130.9 6.6 %fusion.24 = bf16[16,4,12,2048]{3,2,1,0:T(8,128)(2,1)} fusion(bf16[16,128,2048,1]{2,1,3,0:T(8,128)(2,1)} %bitcast.85, s32[16,128,4]{1,2,0:T(4,128)S(1)} %copy.76, pred[16,128,4]{1,2,0:T(4,128)(4,1)S(1)} %copy.74), kind=kOutput, calls=%fused_computation.32 | convolution fusion | flops 402849792 | bytes 11575296 | tf_op jit(solution)/shard_map/stjc,std->sjcd/dot_general | solution.py:44
  137.5 16.5 %fusion.2 = f32[4,16,12,1408]{3,1,2,0:T(8,128)} fusion(bf16[4,2048,1408]{2,1,0:T(8,128)(2,1)} %param.17, bf16[16,4,12,2048]{3,2,1,0:T(8,128)(2,1)} %fusion.24), kind=kOutput, calls=%fused_computation.6 | convolution fusion | flops 4429185024 | bytes 30539776 | tf_op jit(solution)/shard_map/sjcd,jdf->sjcf/dot_general | solution.py:13
  154.0 16.4 %fusion.6 = bf16[16,4,12,1408]{3,0,2,1:T(8,128)(2,1)S(1)} fusion(f32[4,16,12,1408]{3,1,2,0:T(8,128)} %fusion.2, bf16[4,2048,1408]{2,1,0:T(8,128)(2,1)} %param.16, bf16[16,4,12,2048]{3,2,1,0:T(8,128)(2,1)} %fusion.24), kind=kOutput, calls=%fused_computation.12 | convolution fusion | flops 4435673088 | bytes 32702464 | tf_op jit(solution)/shard_map/sjcd,jdf->sjcf/dot_general | solution.py:12
  170.4 10.4 %fusion.15 = bf16[16,4,12,2048]{3,0,2,1:T(8,128)(2,1)S(1)} fusion(bf16[16,4,12,1408]{3,0,2,1:T(8,128)(2,1)S(1)} %fusion.6, bf16[4,1408,2048]{2,1,0:T(8,128)(2,1)} %param.18), kind=kOutput, calls=%fused_computation.20 | convolution fusion | flops 4430757888 | bytes 28377088 | tf_op jit(solution)/shard_map/sjcf,jfd->sjcd/dot_general | solution.py:15
  180.8 4.1 %copy.79 = bf16[16,4,12,2048]{3,1,2,0:T(4,128)(2,1)} copy(bf16[16,4,12,2048]{3,0,2,1:T(8,128)(2,1)S(1)} %fusion.15) | data formatting | bytes 6291456 | tf_op jit(solution)/shard_map/convert_element_type | solution.py:15
  184.9 5.6 %all-to-all-start.2 = ((bf16[16,4,12,2048]{3,1,2,0:T(4,128)(2,1)}), bf16[16,4,12,2048]{3,1,2,0:T(4,128)(2,1)S(1)}, u32[]{:S(2)}, u32[]{:S(2)}) async-start(bf16[16,4,12,2048]{3,1,2,0:T(4,128)(2,1)} %copy.79), calls=%async_computation.2 | async-start | bytes 6291456 | tf_op jit(solution)/shard_map/all_to_all | solution.py:22
  190.5 0.1 copy.69
  190.6 0.1 eq.67
  190.7 0.1 reshape.149
  190.8 1.2 reduce-window.6
  192.1 0.2 slice_reduce_fusion
  192.3 0.1 copy.81
  192.4 0.1 mul.73
  192.6 0.1 fusion.29
  192.7 0.1 reduce_sum.32
  192.9 0.1 copy.73
  193.0 0.1 copy.68
  193.2 67.2 %all-to-all-done.2 = bf16[16,4,12,2048]{3,1,2,0:T(4,128)(2,1)S(1)} async-done(((bf16[16,4,12,2048]{3,1,2,0:T(4,128)(2,1)}), bf16[16,4,12,2048]{3,1,2,0:T(4,128)(2,1)S(1)}, u32[]{:S(2)}, u32[]{:S(2)}) %all-to-all-start.2) | async-done | bytes 3145760 | tf_op jit(solution)/shard_map/all_to_all | solution.py:22
  260.4 4.2 %copy.80 = bf16[16,4,12,2048]{3,2,1,0:T(8,128)(2,1)} copy(bf16[16,4,12,2048]{3,1,2,0:T(4,128)(2,1)S(1)} %all-to-all-done.2) | data formatting | bytes 6291456 | tf_op jit(solution)/shard_map/all_to_all | solution.py:22
  264.7 4.7 %reshape_reshape.3 = bf16[768,2048]{1,0:T(8,128)(2,1)S(1)} reshape(bf16[16,4,12,2048]{3,2,1,0:T(8,128)(2,1)} %copy.80) | data formatting | bytes 6291456 | tf_op jit(solution)/shard_map/reshape;reshape | solution.py:26
  269.4 3.3 %gather_fusion.2 = bf16[512,2048]{1,0:T(8,128)(2,1)} fusion(bf16[768,2048]{1,0:T(8,128)(2,1)S(1)} %reshape_reshape.3, s32[1024]{0:T(1024)S(1)} %pad_clamp_fusion), kind=kCustom, calls=%fused_computation.2 | custom fusion | bytes 4196352 | tf_op jit(solution)/shard_map/jit(_take)/gather | solution.py:116
  272.7 2.7 gather.20
  275.5 4.4 %fusion.18 = f32[128,1,4]{2,1,0:T(1,128)S(1)} fusion(bf16[128,4,2048]{2,1,0:T(4,128)(2,1)S(1)} %gather.20, pred[128,4]{1,0:T(8,128)(4,1)S(1)} %copy.73, bf16[128,2048,1]{1,0,2:T(8,128)(2,1)} %bitcast.95), kind=kOutput, calls=%fused_computation.22 | convolution fusion | flops 3145728 | bytes 2624000 | tf_op jit(solution)/shard_map/tkd,td->tk/dot_general | solution.py:120
  279.9 0.7 copy.87
  280.6 4.9 %multiply_reduce_fusion = bf16[128,2048]{1,0:T(8,128)(2,1)} fusion(f32[128,4]{1,0:T(8,128)S(1)} %copy.68, bf16[128,4,2048]{2,1,0:T(4,128)(2,1)S(1)} %gather.20, pred[128,4]{1,0:T(8,128)(4,1)S(1)} %copy.73), kind=kLoop, calls=%fused_computation.18 | loop fusion | flops 3932160 | bytes 2624000 | tf_op jit(solution)/shard_map/reduce_sum | solution.py:117
  (33 shorter events, 0.4 us)
Async XLA Ops:
  7.2 13.8 %copy-start = (bf16[256,2048]{1,0:T(8,128)(2,1)S(1)}, bf16[256,2048]{1,0:T(8,128)(2,1)}, u32[]{:S(2)}) copy-start(bf16[256,2048]{1,0:T(8,128)(2,1)} %param.15) | copy-start | bytes 3145732
  22.3 7.5 %copy-start.4 = (s32[128,16]{0,1:T(8,128)S(1)}, s32[128,16]{0,1:T(8,128)}, u32[]{:S(2)}) copy-start(s32[128,16]{0,1:T(8,128)} %param.11) | copy-start | bytes 24580
  23.5 32.5 %copy-start.2 = (bf16[128,2048]{1,0:T(8,128)(2,1)S(1)}, bf16[128,2048]{1,0:T(8,128)(2,1)}, u32[]{:S(2)}) copy-start(bf16[128,2048]{1,0:T(8,128)(2,1)} %param.10) | copy-start | bytes 1572868
  23.5 31.2 %all-to-all-start.1 = ((bf16[16,16,2048]{2,1,0:T(8,128)(2,1)}), bf16[16,16,2048]{2,1,0:T(8,128)(2,1)S(1)}, u32[]{:S(2)}, u32[]{:S(2)}) async-start(bf16[16,16,2048]{2,1,0:T(8,128)(2,1)} %broadcast_select_fusion.2), calls=%async_computation.1 | async-start | bytes 2097152 | tf_op jit(solution)/shard_map/all_to_all | solution.py:96
  29.8 101.1 %all-gather.4.cloned.1.call-start = ((), (), s32[]{:S(2)}) async-start(), calls=%async_computation.3 | async-start | bytes 8912896 | tf_op jit(solution)/shard_map/all_gather | solution.py:35
  54.7 2.7 copy-start.3
  184.9 8.2 %copy-start.5 = (f32[128,4]{0,1:T(4,128)S(1)}, f32[128,4]{0,1:T(4,128)}, u32[]{:S(2)}) copy-start(f32[128,4]{0,1:T(4,128)} %param.14) | copy-start | bytes 6148
  184.9 75.5 %all-to-all-start.2 = ((bf16[16,4,12,2048]{3,1,2,0:T(4,128)(2,1)}), bf16[16,4,12,2048]{3,1,2,0:T(4,128)(2,1)S(1)}, u32[]{:S(2)}, u32[]{:S(2)}) async-start(bf16[16,4,12,2048]{3,1,2,0:T(4,128)(2,1)} %copy.79), calls=%async_computation.2 | async-start | bytes 6291456 | tf_op jit(solution)/shard_map/all_to_all | solution.py:22
  275.5 10.0 %copy-start.1 = (bf16[256,2048]{1,0:T(8,128)(2,1)S(1)}, bf16[256,2048]{1,0:T(8,128)(2,1)}, u32[]{:S(2)}) copy-start(bf16[256,2048]{1,0:T(8,128)(2,1)} %param.15) | copy-start | bytes 3145732
Sparse Core Ops, SparseCore 0:
  57.5 73.3 all-gather.3

commit v2 on v0

--- a/solution.py
+++ b/solution.py
@@ -1,11 +1,418 @@
+import functools
+
 import jax
 import jax.numpy as jnp
 from jax import lax
+from jax.experimental import pallas as pl
+from jax.experimental.pallas import tpu as pltpu
 from jax.sharding import PartitionSpec as P
 
 EXPERTS = 64
 TOP = 4
 CAP = 12
+BLOCK = 128
+PAIR = 2 * CAP
+VMEM = pltpu.VMEM
+F32 = jnp.float32
+BF16 = jnp.bfloat16
+
+
+def dot(a, b):
+    return jnp.dot(a, b, preferred_element_type=F32)
+
+
+def earlier(length):
+    row = lax.broadcasted_iota(jnp.int32, (length, length), 0)
+    column = lax.broadcasted_iota(jnp.int32, (length, length), 1)
+    return (row < column).astype(BF16)
+
+
+def fetch_kernel(me_ref, rows_ref, table_ref, out_ref):
+    device_count, tok_rows = rows_ref.shape
+    held = table_ref.shape[0]
+    look_cap = out_ref.shape[0] // device_count
+    start = me_ref[0] * held
+    local = rows_ref[...] - start
+    hit = (local >= 0) & (local < held)
+    rank = dot(hit.astype(F32).astype(BF16), earlier(tok_rows)).astype(jnp.int32)
+    rank = jnp.where(hit, rank, -1)
+    slot = lax.broadcasted_iota(jnp.int32, (look_cap, tok_rows), 0)
+    place = lax.broadcasted_iota(jnp.int32, (look_cap, held), 1)
+    picks = []
+    for source in range(device_count):
+        mine = jnp.where(slot == rank[source : source + 1], local[source : source + 1], 0)
+        wanted = jnp.sum(mine, axis=1, keepdims=True)
+        picks.append((place == wanted).astype(F32).astype(BF16))
+    pick = jnp.concatenate(picks, axis=0)
+    out_ref[...] = dot(pick, table_ref[...]).astype(BF16)
+
+
+def state_kernel(rows_ref, returned_ref, values_ref, scales_ref, out_ref):
+    slots = returned_ref.shape[0]
+    tok_rows, features = values_ref.shape
+    held = rows_ref.shape[0]
+    owner_of = rows_ref[...]
+    look_cap = slots // held
+    owner = lax.broadcasted_iota(jnp.int32, (held, tok_rows), 0)
+    hit = owner_of == owner
+    rank = dot(hit.astype(F32).astype(BF16), earlier(tok_rows)).astype(jnp.int32)
+    rank = jnp.where(hit, rank, -1)
+    slot = lax.broadcasted_iota(jnp.int32, (look_cap, tok_rows), 0)
+    put = jnp.concatenate(
+        [(slot == rank[o : o + 1]).astype(F32) for o in range(held)], axis=0
+    )
+    put = put.T.astype(BF16)
+    width = 512
+    for left in range(0, features, width):
+        found = dot(put, returned_ref[:, left : left + width])
+        for b in range(width // BLOCK):
+            at = left + b * BLOCK
+            scaled = values_ref[:, at : at + BLOCK].astype(F32) * scales_ref[
+                :, at // BLOCK : at // BLOCK + 1
+            ]
+            out_ref[:, at : at + BLOCK] = (
+                scaled + found[:, b * BLOCK : (b + 1) * BLOCK]
+            ).astype(BF16)
+
+
+def gather_slots(states, ids_ref, source_of, core, first, exp_dev):
+    tok_rows = ids_ref.shape[2]
+    hits = []
+    for part in range(4):
+        ids = ids_ref[source_of[part]]
+        for j in range(exp_dev):
+            hits.append(jnp.max((ids == first + j).astype(F32), axis=0, keepdims=True))
+    hits = jnp.concatenate(hits, axis=0)
+    rank = dot(hits.astype(BF16), earlier(tok_rows)).astype(jnp.int32)
+    rank = jnp.where(hits > 0, rank, -1000)
+    row = lax.broadcasted_iota(jnp.int32, (2 * PAIR, tok_rows), 0)
+    lines = []
+    for j in range(exp_dev):
+        cells = []
+        for part in range(4):
+            flip = (core + part + j) % 2
+            base = (part // 2) * PAIR + CAP * flip
+            k = part * exp_dev + j
+            cells.append((row == rank[k : k + 1] + base).astype(F32).astype(BF16))
+        lines.append(jnp.concatenate(cells, axis=1))
+    pick = jnp.concatenate(lines, axis=0)
+    return dot(pick, states)
+
+
+def expert_kernel(
+    gather,
+    first_held,
+    place_ref,
+    *refs,
+):
+    if gather:
+        ids_ref = refs[0]
+        pieces = refs[1:29]
+        wg_hbm, wu_hbm, wd_hbm, out_ref, later_ref = refs[29:34]
+        x_ref, state_ref, wg_ref, wu_ref, wd_ref, hidden_ref, result_ref, sem, state_sem = refs[34:]
+    else:
+        x_ref, wg_hbm, wu_hbm, wd_hbm, out_ref = refs[:5]
+        wg_ref, wu_ref, wd_ref, hidden_ref, result_ref, sem = refs[5:]
+    features = wg_ref.shape[1]
+    width = wg_ref.shape[2]
+    z, y, core = place_ref[0], place_ref[1], place_ref[2]
+    count = wg_ref.shape[0]
+    up_cuts = ((0, 512), (512, 512), (1024, width - 1024))
+    down_cuts = tuple((at, 512) for at in range(0, features, 512))
+
+    def weight_copies(j):
+        copies = []
+        for at, size in up_cuts:
+            for hbm, ref in ((wg_hbm, wg_ref), (wu_hbm, wu_ref)):
+                cols = pl.ds(at, size)
+                copies.append((hbm.at[first_held + j, :, cols], ref.at[j, :, cols]))
+        for at, size in down_cuts:
+            cols = pl.ds(at, size)
+            copies.append((wd_hbm.at[first_held + j, :, cols], wd_ref.at[j, :, cols]))
+        return [
+            pltpu.make_async_copy(src, dst, sem.at[j, n]) for n, (src, dst) in enumerate(copies)
+        ]
+
+    if gather:
+        options = ((0, 0), (1, 6), (2, 5), (3, 4))
+        conditions = (z >= 0, z >= 1, z <= 2, z >= 2)
+        tok_rows = ids_ref.shape[2]
+
+        def state_copy(kind, slot, part):
+            at = pl.ds((slot * 4 + part) * tok_rows, tok_rows)
+            return pltpu.make_async_copy(
+                pieces[kind * 4 + part], state_ref.at[at], state_sem.at[slot, part]
+            )
+
+        for slot in range(4):
+            yes, no = options[slot]
+            for part in range(4):
+                if yes == no:
+                    state_copy(yes, slot, part).start()
+                else:
+
+                    @pl.when(conditions[slot])
+                    def _(slot=slot, part=part, yes=yes):
+                        state_copy(yes, slot, part).start()
+
+                    @pl.when(jnp.logical_not(conditions[slot]))
+                    def _(slot=slot, part=part, no=no):
+                        state_copy(no, slot, part).start()
+
+    for j in range(count):
+        for copy in weight_copies(j):
+            copy.start()
+
+    plane = (
+        z,
+        jnp.where(z >= 1, z - 1, 3),
+        jnp.where(z <= 2, z + 1, 0),
+        jnp.where(z >= 2, z - 2, z + 2),
+    )
+    if gather:
+        exp_dev = 2 * count
+        first = place_ref[3]
+        for slot in range(4):
+            source_of = [
+                plane[slot] * 4 + ((y + part // 2) % 2) * 2 + (core + part) % 2 for part in range(4)
+            ]
+            for part in range(4):
+                state_copy(0, slot, part).wait()
+            at = slot * 4 * tok_rows
+            rows = gather_slots(
+                state_ref[at : at + 4 * tok_rows, :], ids_ref, source_of, core, first, exp_dev
+            ).astype(BF16)
+            for j in range(exp_dev):
+                block = rows[j * 2 * PAIR : (j + 1) * 2 * PAIR]
+                if j < count:
+                    x_ref[j, slot * 2 * PAIR : (slot + 1) * 2 * PAIR, :] = block
+                else:
+                    later_ref[j - count, slot * 2 * PAIR : (slot + 1) * 2 * PAIR, :] = block
+
+    @pl.loop(0, count)
+    def _(j):
+        copies = weight_copies(j)
+        n = 0
+        for at, size in up_cuts:
+            copies[n].wait()
+            copies[n + 1].wait()
+            n += 2
+            x = x_ref[j]
+            gate = dot(x, wg_ref[j, :, at : at + size])
+            up = dot(x, wu_ref[j, :, at : at + size])
+            hidden_ref[:, at : at + size] = (gate / (1.0 + jnp.exp(-gate)) * up).astype(BF16)
+        for at, size in down_cuts:
+            copies[n].wait()
+            n += 1
+            result_ref[j, :, at : at + size] = dot(hidden_ref[...], wd_ref[j, :, at : at + size])
+
+    low = lax.broadcasted_iota(jnp.int32, (PAIR, features), 0) < CAP
+    for slot in range(4):
+        for other in range(2):
+            at = (slot * 2 + other) * PAIR
+            pair = plane[slot] * 2 + (y + other) % 2
+            one = result_ref[0, at : at + PAIR, :]
+            two = result_ref[1, at : at + PAIR, :]
+            out_ref[2 * pair] = jnp.where(low, one, two).astype(BF16)
+            out_ref[2 * pair + 1] = jnp.where(low, two, one).astype(BF16)
+
+
+def expert_call(gather, first_held, place, operands, weights, device_count):
+    w_gate, w_up, w_down = weights
+    exp_dev, features, width = w_gate.shape
+    count = exp_dev // 2
+    rows = device_count * CAP
+    anywhere = pl.BlockSpec(memory_space=pl.ANY)
+    smem = pl.BlockSpec(memory_space=pltpu.SMEM)
+    vmem = pl.BlockSpec(memory_space=VMEM)
+    out_shape = [jax.ShapeDtypeStruct((device_count, PAIR, features), BF16)]
+    scratch = [
+        VMEM((count, features, width), BF16),
+        VMEM((count, features, width), BF16),
+        VMEM((count, width, features), BF16),
+        VMEM((rows, width), BF16),
+        VMEM((count, rows, features), F32),
+        pltpu.SemaphoreType.DMA((count, 10)),
+    ]
+    if gather:
+        ids, pieces = operands
+        tok_rows = ids.shape[2]
+        out_shape.append(jax.ShapeDtypeStruct((count, rows, features), BF16))
+        scratch = (
+            [VMEM((count, rows, features), BF16), VMEM((device_count * tok_rows, features), BF16)]
+            + scratch
+            + [pltpu.SemaphoreType.DMA((4, 4))]
+        )
+        inputs = [ids, *pieces]
+        in_specs = [vmem] + [anywhere] * len(pieces)
+    else:
+        inputs = [operands]
+        in_specs = [vmem]
+    return pl.pallas_call(
+        functools.partial(expert_kernel, gather, first_held),
+        out_shape=out_shape,
+        in_specs=[smem] + in_specs + [anywhere] * 3,
+        out_specs=[vmem] * len(out_shape),
+        scratch_shapes=scratch,
+        compiler_params=pltpu.CompilerParams(vmem_limit_bytes=60 * 1024 * 1024),
+        cost_estimate=pl.CostEstimate(
+            flops=6 * count * rows * features * width,
+            bytes_accessed=6 * count * features * width,
+            transcendentals=count * rows * width,
+        ),
+        name="experts_first" if gather else "experts_second",
+    )(place, *inputs, w_gate, w_up, w_down)
+
+
+def combine_kernel(slots_ref, weights_ref, first_ref, second_ref, grad_ref, mixed_ref, grads_ref):
+    tok_rows, features = grad_ref.shape
+    half = first_ref.shape[0]
+    column = lax.broadcasted_iota(jnp.int32, (tok_rows, half), 1)
+    picked = [jnp.zeros((tok_rows, 1), F32) for _ in range(TOP)]
+    spread = []
+    for part, ref in enumerate((first_ref, second_ref)):
+        inner = lax.dot_general(
+            grad_ref[...], ref[...], (((1,), (1,)), ((), ())), preferred_element_type=F32
+        )
+        total = jnp.zeros((tok_rows, half), F32)
+        for k in range(TOP):
+            here = column == slots_ref[:, k : k + 1] - part * half
+            total = total + jnp.where(here, weights_ref[:, k : k + 1], 0.0)
+            picked[k] = picked[k] + jnp.sum(jnp.where(here, inner, 0.0), axis=1, keepdims=True)
+        high = total.astype(BF16)
+        spread.append((high, (total - high.astype(F32)).astype(BF16)))
+    for k in range(TOP):
+        grads_ref[:, k : k + 1] = picked[k]
+    width = 512
+    for at in range(0, features, width):
+        value = jnp.zeros((tok_rows, width), F32)
+        for (high, low), ref in zip(spread, (first_ref, second_ref)):
+            rows = ref[:, at : at + width]
+            value = value + dot(high, rows) + dot(low, rows)
+        mixed_ref[:, at : at + width] = value.astype(BF16)
+
+
+def gather_states(state):
+    device_count = lax.axis_size("expert")
+    planes = device_count // 4
+
+    def along(array, step):
+        pairs = [
+            (i, i + 4 * step) for i in range(device_count) if 0 <= i // 4 + step < planes
+        ]
+        return lax.ppermute(array, "expert", pairs)
+
+    def across(array, bit, keep):
+        pairs = [(i, i ^ bit) for i in range(device_count) if keep(i // 4)]
+        return lax.ppermute(array, "expert", pairs)
+
+    up_1, down_1 = along(state, 1), along(state, -1)
+    up_2, down_2 = along(up_1, 1), along(down_1, -1)
+    up_3, down_3 = along(up_2, 1), along(down_2, -1)
+    kinds = (
+        (state, lambda z: True),
+        (up_1, lambda z: z >= 1),
+        (down_1, lambda z: z <= planes - 2),
+        (up_2, lambda z: z >= 2),
+        (down_2, lambda z: z <= planes - 3),
+        (up_3, lambda z: z >= 3),
+        (down_3, lambda z: z <= planes - 4),
+    )
+    pieces = []
+    for array, keep in kinds:
+        beside = across(array, 2, keep)
+        pieces += [array, across(array, 1, keep), beside, across(beside, 1, keep)]
+    return pieces
+
+
+def near_path(
+    block_values,
+    block_exps,
+    row_ids,
+    expert_ids,
+    gate_weights,
+    table,
+    w_gate,
+    w_up,
+    w_down,
+    out_grad,
+):
+    device_count = lax.axis_size("expert")
+    me = lax.axis_index("expert").astype(jnp.int32)
+    tok_rows, features = block_values.shape
+    rows_held = table.shape[0]
+    exp_dev = w_gate.shape[0]
+    look_cap = max(2, 2 * tok_rows // device_count)
+    vmem = pl.BlockSpec(memory_space=VMEM)
+    smem = pl.BlockSpec(memory_space=pltpu.SMEM)
+
+    ids = jnp.concatenate([row_ids[None, :], expert_ids.T], axis=0)
+    all_ids = lax.all_to_all(
+        jnp.broadcast_to(ids[None], (device_count, 1 + TOP, tok_rows)),
+        "expert",
+        split_axis=0,
+        concat_axis=0,
+        tiled=True,
+    )
+    fetched = pl.pallas_call(
+        fetch_kernel,
+        out_shape=jax.ShapeDtypeStruct((device_count * look_cap, features), BF16),
+        in_specs=[smem, vmem, vmem],
+        out_specs=vmem,
+        name="fetch_rows",
+    )(me[None], all_ids[:, 0, :], table)
+    returned = lax.all_to_all(
+        fetched.reshape(device_count, look_cap, features),
+        "expert",
+        split_axis=0,
+        concat_axis=0,
+        tiled=True,
+    ).reshape(device_count * look_cap, features)
+    scales = jnp.exp2(block_exps.astype(F32))
+    owners = jnp.broadcast_to((row_ids // rows_held)[None, :], (device_count, tok_rows))
+    state = pl.pallas_call(
+        state_kernel,
+        out_shape=jax.ShapeDtypeStruct((tok_rows, features), BF16),
+        in_specs=[vmem] * 4,
+        out_specs=vmem,
+        name="token_state",
+    )(owners, returned, block_values, scales)
+    pieces = gather_states(state)
+
+    core = me % 2
+    place = jnp.stack([me // 4, (me // 2) % 2, core, me * exp_dev])
+    weights = (w_gate, w_up, w_down)
+    first_out, later = expert_call(
+        True, 0, place, (all_ids[:, 1:, :], pieces), weights, device_count
+    )
+    (second_out,) = expert_call(False, exp_dev // 2, place, later, weights, device_count)
+    back = [
+        lax.all_to_all(out, "expert", split_axis=0, concat_axis=0, tiled=True).reshape(
+            device_count * PAIR, features
+        )
+        for out in (first_out, second_out)
+    ]
+
+    named = (expert_ids[:, :, None] == jnp.arange(EXPERTS, dtype=jnp.int32)).astype(F32)
+    counted = dot(earlier(tok_rows).T, jnp.sum(named, axis=1).astype(BF16))
+    rank = jnp.sum(counted[:, None, :] * named, axis=2).astype(jnp.int32)
+    inside = expert_ids % exp_dev
+    slots = (
+        (inside // 2) * (device_count * PAIR)
+        + (expert_ids // exp_dev) * PAIR
+        + ((core + inside) % 2) * CAP
+        + rank
+    )
+    return pl.pallas_call(
+        combine_kernel,
+        out_shape=(
+            jax.ShapeDtypeStruct((tok_rows, features), BF16),
+            jax.ShapeDtypeStruct((tok_rows, TOP), F32),
+        ),
+        in_specs=[vmem] * 5,
+        out_specs=(vmem, vmem),
+        name="combine",
+    )(slots, gate_weights, back[0], back[1], out_grad)
 
 
 def expert_work(arrived, w_gate, w_up, w_down):
@@ -41,7 +448,7 @@
     return jnp.sum(pieces, axis=1).astype(jnp.bfloat16).reshape(EXPERTS * CAP, features)
 
 
-def local(
+def far_path(
     block_values,
     block_exps,
     row_ids,
@@ -104,6 +511,12 @@
     return (mixed, gate_grads)
 
 
+def local(*arrays):
+    if lax.axis_size("expert") == 16 and arrays[6].shape[0] * 16 == EXPERTS:
+        return near_path(*arrays)
+    return far_path(*arrays)
+
+
 def solution(mesh):
     return jax.shard_map(
         local,

time: 283 us -> 274 us (0.968)
  the two profiles are of different devices: /device:TPU:13 before, /device:TPU:0 now
where the time goes in v2:
time: 274 us; the launch traced here: 270 us
  waiting for transfers between devices  96 us (35%)
  starting transfers between devices  68.4 us (25%)
  Pallas kernels  52.4 us (19%)
  blocking collectives  41.2 us (15%)
  local copies, waits for them, and re-layouts  8.26 us (3%)
    pallas_call x2, Pallas kernels, expert_call(): pl.pallas_call(functools.partial(expert_kernel, gather, first_held), out_...  41.7 us
    all_to_all x1, blocking collectives, near_path(): lax.all_to_all(out, 'expert', split_axis=0, concat_axis=0, tiled=True)  41.2 us
    ppermute x21, starting transfers between devices, across(): return lax.ppermute(array, 'expert', pairs)  32.8 us
    all_to_all x1, waiting for transfers between devices, near_path(): lax.all_to_all(out, 'expert', split_axis=0, concat_axis=0, tiled=True)  29.9 us
    ppermute x6, waiting for transfers between devices, along(): return lax.ppermute(array, 'expert', pairs)  27.6 us
    all_to_all x1, waiting for transfers between devices, near_path(): lax.all_to_all(fetched.reshape(device_count, look_cap, features), 'expert...  22.1 us
    ppermute x6, starting transfers between devices, along(): return lax.ppermute(array, 'expert', pairs)  19.3 us
    ppermute x21, waiting for transfers between devices, across(): return lax.ppermute(array, 'expert', pairs)  9.49 us
  transfers between devices with their start and end apart: 30, of which 11 were waited for; matrix products, arithmetic and copies ran while one was open for 1% of the time, Pallas kernels for 0%

profile of v2, /device:TPU:0, one launch (start us, length us, event | category | flops | bytes accessed | tf_op | source)
XLA Modules:
  0.0 269.7 jit_solution(9774069771029105871)
XLA Ops:
  2.0 7.4 %all-to-all-start = ((s32[16,5,128]{2,1,0:T(8,128)}), s32[16,5,128]{2,1,0:T(8,128)S(1)}, u32[]{:S(2)}, u32[]{:S(2)}) async-start(s32[16,5,128]{2,1,0:T(8,128)} %broadcast_in_dim.9), calls=%async_computation | async-start | bytes 131072 | tf_op jit(solution)/shard_map/all_to_all | solution.py:350
  9.4 6.9 %all-to-all-done = s32[16,5,128]{2,1,0:T(8,128)S(1)} async-done(((s32[16,5,128]{2,1,0:T(8,128)}), s32[16,5,128]{2,1,0:T(8,128)S(1)}, u32[]{:S(2)}, u32[]{:S(2)}) %all-to-all-start) | async-done | bytes 40992 | tf_op jit(solution)/shard_map/all_to_all | solution.py:350
  16.9 2.9 %fetch_rows.1 = bf16[256,2048]{1,0:T(8,128)(2,1)} custom-call(s32[1]{0:T(128)} %bitcast.6.me_ref, s32[16,128]{1,0:T(8,128)} %bitcast.18, bf16[256,2048]{1,0:T(8,128)(2,1)} %table_ref.1), custom_call_target="tpu_custom_call" | custom-call | tf_op jit(solution)/shard_map/fetch_rows/pallas_call | solution.py:357
  19.7 3.8 %all-to-all-start.1 = ((bf16[16,16,2048]{2,1,0:T(8,128)(2,1)}), bf16[16,16,2048]{2,1,0:T(8,128)(2,1)S(1)}, u32[]{:S(2)}, u32[]{:S(2)}) async-start(bf16[16,16,2048]{2,1,0:T(8,128)(2,1)} %bitcast.15), calls=%async_computation.1 | async-start | bytes 2097152 | tf_op jit(solution)/shard_map/all_to_all | solution.py:364
  23.6 0.7 copy.46.scales_ref
  24.3 22.1 %all-to-all-done.1 = bf16[16,16,2048]{2,1,0:T(8,128)(2,1)S(1)} async-done(((bf16[16,16,2048]{2,1,0:T(8,128)(2,1)}), bf16[16,16,2048]{2,1,0:T(8,128)(2,1)S(1)}, u32[]{:S(2)}, u32[]{:S(2)}) %all-to-all-start.1) | async-done | bytes 1048608 | tf_op jit(solution)/shard_map/all_to_all | solution.py:364
  47.4 2.7 token_state.1.refs_1_
  50.1 5.1 %collective-permute-start.3 = (bf16[128,2048]{1,0:T(8,128)(2,1)}, bf16[128,2048]{1,0:T(8,128)(2,1)S(1)}, u32[]{:S(2)}, u32[]{:S(2)}) collective-permute-start(bf16[128,2048]{1,0:T(8,128)(2,1)} %token_state.1.refs_1_), channel_id=1, source_target_pairs={{0,4},{1,5},{2,6},{3,7},{4,8},{5,9},{6,10},{7,11},{8,12},{9,13},{1... | collective-permute-start | bytes 1572872 | tf_op jit(solution)/shard_map/ppermute | solution.py:303
  55.2 1.3 collective-permute-start.7
  56.5 2.0 collective-permute-start.1
  58.6 9.1 %collective-permute-done.3.refs_5_ = bf16[128,2048]{1,0:T(8,128)(2,1)S(1)} collective-permute-done((bf16[128,2048]{1,0:T(8,128)(2,1)}, bf16[128,2048]{1,0:T(8,128)(2,1)S(1)}, u32[]{:S(2)}, u32[]{:S(2)}) %collective-permute-start.3) | collective-permute-done | bytes 524320 | tf_op jit(solution)/shard_map/ppermute | solution.py:303
  67.6 4.3 %collective-permute-start.11 = (bf16[128,2048]{1,0:T(8,128)(2,1)S(1)}, bf16[128,2048]{1,0:T(8,128)(2,1)S(1)}, u32[]{:S(2)}, u32[]{:S(2)}) collective-permute-start(bf16[128,2048]{1,0:T(8,128)(2,1)S(1)} %collective-permute-done.3.refs_5_), channel_id=1, source_target_pairs={{0,4},{1,5},{2,6},{3,7},{4,8},{5,9},{6,10},{7,11},{8,12},{9,13},{1... | collective-permute-start | bytes 1572872 | tf_op jit(solution)/shard_map/ppermute | solution.py:303
  71.9 1.3 collective-permute-start.15
  73.2 3.4 %collective-permute-start.9 = (bf16[128,2048]{1,0:T(8,128)(2,1)S(1)}, bf16[128,2048]{1,0:T(8,128)(2,1)S(1)}, u32[]{:S(2)}, u32[]{:S(2)}) collective-permute-start(bf16[128,2048]{1,0:T(8,128)(2,1)S(1)} %collective-permute-done.7.refs_9_), channel_id=1, source_target_pairs={{0,2},{1,3},{2,0},{3,1},{4,6},{5,7},{6,4},{7,5},{8,10},{9,11},{10,... | collective-permute-start | bytes 1572872 | tf_op jit(solution)/shard_map/ppermute | solution.py:307
  76.7 0.7 collective-permute-start.5
  77.4 0.7 collective-permute-start.4
  78.1 5.0 %collective-permute-done.11.refs_13_ = bf16[128,2048]{1,0:T(8,128)(2,1)S(1)} collective-permute-done((bf16[128,2048]{1,0:T(8,128)(2,1)S(1)}, bf16[128,2048]{1,0:T(8,128)(2,1)S(1)}, u32[]{:S(2)}, u32[]{:S(2)}) %collective-permute-start.11) | collective-permute-done | bytes 524320 | tf_op jit(solution)/shard_map/ppermute | solution.py:303
  83.1 1.9 collective-permute-start.8
  85.0 2.2 collective-permute-done.15.refs_17_
  87.3 1.3 collective-permute-done.9.refs_11_
  88.6 6.0 %collective-permute-start.19 = (bf16[128,2048]{1,0:T(8,128)(2,1)S(1)}, bf16[128,2048]{1,0:T(8,128)(2,1)S(1)}, u32[]{:S(2)}, u32[]{:S(2)}) collective-permute-start(bf16[128,2048]{1,0:T(8,128)(2,1)S(1)} %collective-permute-done.11.refs_13_), channel_id=1, source_target_pairs={{0,4},{1,5},{2,6},{3,7},{4,8},{5,9},{6,10},{7,11},{8,12},{9,13},{1... | collective-permute-start | bytes 1572872 | tf_op jit(solution)/shard_map/ppermute | solution.py:303
  94.6 1.3 collective-permute-start.23
  95.9 1.5 collective-permute-start.13
  97.4 3.4 %collective-permute-start.17 = (bf16[128,2048]{1,0:T(8,128)(2,1)S(1)}, bf16[128,2048]{1,0:T(8,128)(2,1)}, u32[]{:S(2)}, u32[]{:S(2)}) collective-permute-start(bf16[128,2048]{1,0:T(8,128)(2,1)S(1)} %collective-permute-done.15.refs_17_), channel_id=1, source_target_pairs={{0,2},{1,3},{2,0},{3,1},{4,6},{5,7},{6,4},{7,5},{16,18},{17,19},{1... | collective-permute-start | bytes 1572872 | tf_op jit(solution)/shard_map/ppermute | solution.py:307
  101.5 1.1 collective-permute-done.19.refs_21_
  102.6 1.9 collective-permute-start.16
  104.5 10.2 %collective-permute-done.23.refs_25_ = bf16[128,2048]{1,0:T(8,128)(2,1)} collective-permute-done((bf16[128,2048]{1,0:T(8,128)(2,1)S(1)}, bf16[128,2048]{1,0:T(8,128)(2,1)}, u32[]{:S(2)}, u32[]{:S(2)}) %collective-permute-start.23) | collective-permute-done | bytes 524320 | tf_op jit(solution)/shard_map/ppermute | solution.py:303
  114.7 1.9 collective-permute-start.10
  117.4 1.5 collective-permute-start.21
  118.8 2.5 collective-permute-start.25
  122.1 2.1 collective-permute-start.24
  124.3 1.5 collective-permute-start.14
  125.8 2.2 collective-permute-start.18
  128.0 7.4 %collective-permute-done.25.refs_27_ = bf16[128,2048]{1,0:T(8,128)(2,1)} collective-permute-done((bf16[128,2048]{1,0:T(8,128)(2,1)}, bf16[128,2048]{1,0:T(8,128)(2,1)}, u32[]{:S(2)}, u32[]{:S(2)}) %collective-permute-start.25) | collective-permute-done | bytes 524320 | tf_op jit(solution)/shard_map/ppermute | solution.py:307
  135.4 1.5 collective-permute-start.22
  136.9 0.8 copy-done.18
  137.7 2.1 collective-permute-start.26
  141.0 0.8 collective-permute-done.26.refs_28_
  141.8 26.3 %experts_first.1 = (bf16[16,24,2048]{2,1,0:T(8,128)(2,1)}, bf16[2,192,2048]{2,1,0:T(8,128)(2,1)}) custom-call(s32[4]{0:T(128)} %pad_add_fusion.1.place_ref, s32[16,4,128]{2,1,0:T(4,128)} %slice.8.refs_0_, bf16[128,2048]{1,0:T(8,128)(2,1)} %token_state.1.refs_1_, bf16[128,2048]{1,0:T(8,128)(2,1)} %copy-done.5, bf16[128,2048]{1,0:T(8,128)(2,1)} %copy-done.4, ...), custom_call_target="tpu_custom_call" | custom-call | flops 6643777536 | bytes 34603008 | tf_op jit(solution)/shard_map/experts_first/pallas_call | solution.py:251
  168.1 15.4 %experts_second.1 = bf16[16,24,2048]{2,1,0:T(8,128)(2,1)} custom-call(s32[4]{0:T(128)} %pad_add_fusion.1.place_ref, bf16[2,192,2048]{2,1,0:T(8,128)(2,1)} %get-tuple-element.5.refs_0_, bf16[4,2048,1408]{2,1,0:T(8,128)(2,1)} %refs_1_.1, bf16[4,2048,1408]{2,1,0:T(8,128)(2,1)} %refs_2_.1, bf16[4,1408,2048]{2,1,0:T(8,128)(2,1)} %refs_3_.1), custom_call_target="tpu_custom_call" | custom-call | flops 6643777536 | bytes 34603008 | tf_op jit(solution)/shard_map/experts_second/pallas_call | solution.py:251
  183.5 41.2 %all_to_all.20 = bf16[16,24,2048]{2,1,0:T(8,128)(2,1)} all-to-all(bf16[16,24,2048]{2,1,0:T(8,128)(2,1)} %experts_second.1), channel_id=1, replica_groups=mesh['groups'=2,'expert'=16] {'expert'}, dimensions={0} | all-to-all | bytes 3145728 | tf_op jit(solution)/shard_map/all_to_all | solution.py:390
  224.7 5.2 %all-to-all-start.2 = ((bf16[16,24,2048]{2,1,0:T(8,128)(2,1)}), bf16[16,24,2048]{2,1,0:T(8,128)(2,1)S(1)}, u32[]{:S(2)}, u32[]{:S(2)}) async-start(bf16[16,24,2048]{2,1,0:T(8,128)(2,1)} %get-tuple-element.4), calls=%async_computation.2 | async-start | bytes 3145728 | tf_op jit(solution)/shard_map/all_to_all | solution.py:390
  230.5 0.7 copy.47.weights_ref
  231.2 0.8 fusion.4.slots_ref
  232.0 29.9 %all-to-all-done.2 = bf16[16,24,2048]{2,1,0:T(8,128)(2,1)S(1)} async-done(((bf16[16,24,2048]{2,1,0:T(8,128)(2,1)}), bf16[16,24,2048]{2,1,0:T(8,128)(2,1)S(1)}, u32[]{:S(2)}, u32[]{:S(2)}) %all-to-all-start.2) | async-done | bytes 1572896 | tf_op jit(solution)/shard_map/all_to_all | solution.py:390
  261.9 1.2 copy-done
  263.0 5.2 %combine.1 = (bf16[128,2048]{1,0:T(8,128)(2,1)}, f32[128,4]{1,0:T(8,128)}) custom-call(s32[128,4]{1,0:T(8,128)} %fusion.4.slots_ref, f32[128,4]{1,0:T(8,128)} %copy.47.weights_ref, bf16[384,2048]{1,0:T(8,128)(2,1)} %bitcast.14, bf16[384,2048]{1,0:T(8,128)(2,1)} %bitcast.13, bf16[128,2048]{1,0:T(8,128)(2,1)} %grad_ref.1), custom_call_target="tpu_custom_call" | custom-call | tf_op jit(solution)/shard_map/combine/pallas_call | solution.py:406
  268.2 1.5 copy.48
  (84 shorter events, 6.9 us)
Async XLA Ops:
  2.0 14.3 %all-to-all-start = ((s32[16,5,128]{2,1,0:T(8,128)}), s32[16,5,128]{2,1,0:T(8,128)S(1)}, u32[]{:S(2)}, u32[]{:S(2)}) async-start(s32[16,5,128]{2,1,0:T(8,128)} %broadcast_in_dim.9), calls=%async_computation | async-start | bytes 131072 | tf_op jit(solution)/shard_map/all_to_all | solution.py:350
  19.7 26.7 %all-to-all-start.1 = ((bf16[16,16,2048]{2,1,0:T(8,128)(2,1)}), bf16[16,16,2048]{2,1,0:T(8,128)(2,1)S(1)}, u32[]{:S(2)}, u32[]{:S(2)}) async-start(bf16[16,16,2048]{2,1,0:T(8,128)(2,1)} %bitcast.15), calls=%async_computation.1 | async-start | bytes 2097152 | tf_op jit(solution)/shard_map/all_to_all | solution.py:364
  50.1 17.5 %collective-permute-start.3 = (bf16[128,2048]{1,0:T(8,128)(2,1)}, bf16[128,2048]{1,0:T(8,128)(2,1)S(1)}, u32[]{:S(2)}, u32[]{:S(2)}) collective-permute-start(bf16[128,2048]{1,0:T(8,128)(2,1)} %token_state.1.refs_1_), channel_id=1, source_target_pairs={{0,4},{1,5},{2,6},{3,7},{4,8},{5,9},{6,10},{7,11},{8,12},{9,13},{1... | collective-permute-start | bytes 1572872 | tf_op jit(solution)/shard_map/ppermute | solution.py:303
  55.2 16.7 %collective-permute-start.7 = (bf16[128,2048]{1,0:T(8,128)(2,1)}, bf16[128,2048]{1,0:T(8,128)(2,1)S(1)}, u32[]{:S(2)}, u32[]{:S(2)}) collective-permute-start(bf16[128,2048]{1,0:T(8,128)(2,1)} %token_state.1.refs_1_), channel_id=1, source_target_pairs={{4,0},{5,1},{6,2},{7,3},{8,4},{9,5},{10,6},{11,7},{12,8},{13,9},{1... | collective-permute-start | bytes 1572872 | tf_op jit(solution)/shard_map/ppermute | solution.py:303
  56.5 20.1 %collective-permute-start.1 = (bf16[128,2048]{1,0:T(8,128)(2,1)}, bf16[128,2048]{1,0:T(8,128)(2,1)S(1)}, u32[]{:S(2)}, u32[]{:S(2)}) collective-permute-start(bf16[128,2048]{1,0:T(8,128)(2,1)} %token_state.1.refs_1_), channel_id=1, source_target_pairs={{0,2},{1,3},{2,0},{3,1},{4,6},{5,7},{6,4},{7,5},{8,10},{9,11},{10,... | collective-permute-start | bytes 1572872 | tf_op jit(solution)/shard_map/ppermute | solution.py:307
  58.6 18.8 %collective-permute-start = (bf16[128,2048]{1,0:T(8,128)(2,1)}, bf16[128,2048]{1,0:T(8,128)(2,1)S(1)}, u32[]{:S(2)}, u32[]{:S(2)}) collective-permute-start(bf16[128,2048]{1,0:T(8,128)(2,1)} %token_state.1.refs_1_), channel_id=1, source_target_pairs={{0,1},{1,0},{2,3},{3,2},{4,5},{5,4},{6,7},{7,6},{8,9},{9,8},{10,11... | collective-permute-start | bytes 1572872 | tf_op jit(solution)/shard_map/ppermute | solution.py:307
  67.6 74.2 %copy-start.2 = (bf16[128,2048]{1,0:T(8,128)(2,1)}, bf16[128,2048]{1,0:T(8,128)(2,1)S(1)}, u32[]{:S(2)}) copy-start(bf16[128,2048]{1,0:T(8,128)(2,1)S(1)} %collective-permute-done.3.refs_5_) | copy-start | bytes 1572868
  67.6 15.5 %collective-permute-start.11 = (bf16[128,2048]{1,0:T(8,128)(2,1)S(1)}, bf16[128,2048]{1,0:T(8,128)(2,1)S(1)}, u32[]{:S(2)}, u32[]{:S(2)}) collective-permute-start(bf16[128,2048]{1,0:T(8,128)(2,1)S(1)} %collective-permute-done.3.refs_5_), channel_id=1, source_target_pairs={{0,4},{1,5},{2,6},{3,7},{4,8},{5,9},{6,10},{7,11},{8,12},{9,13},{1... | collective-permute-start | bytes 1572872 | tf_op jit(solution)/shard_map/ppermute | solution.py:303
  71.9 69.9 %copy-start.3 = (bf16[128,2048]{1,0:T(8,128)(2,1)}, bf16[128,2048]{1,0:T(8,128)(2,1)S(1)}, u32[]{:S(2)}) copy-start(bf16[128,2048]{1,0:T(8,128)(2,1)S(1)} %collective-permute-done.7.refs_9_) | copy-start | bytes 1572868
  71.9 15.4 %collective-permute-start.15 = (bf16[128,2048]{1,0:T(8,128)(2,1)S(1)}, bf16[128,2048]{1,0:T(8,128)(2,1)S(1)}, u32[]{:S(2)}, u32[]{:S(2)}) collective-permute-start(bf16[128,2048]{1,0:T(8,128)(2,1)S(1)} %collective-permute-done.7.refs_9_), channel_id=1, source_target_pairs={{4,0},{5,1},{6,2},{7,3},{8,4},{9,5},{10,6},{11,7},{12,8},{13,9},{1... | collective-permute-start | bytes 1572872 | tf_op jit(solution)/shard_map/ppermute | solution.py:303
  73.2 15.4 %collective-permute-start.9 = (bf16[128,2048]{1,0:T(8,128)(2,1)S(1)}, bf16[128,2048]{1,0:T(8,128)(2,1)S(1)}, u32[]{:S(2)}, u32[]{:S(2)}) collective-permute-start(bf16[128,2048]{1,0:T(8,128)(2,1)S(1)} %collective-permute-done.7.refs_9_), channel_id=1, source_target_pairs={{0,2},{1,3},{2,0},{3,1},{4,6},{5,7},{6,4},{7,5},{8,10},{9,11},{10,... | collective-permute-start | bytes 1572872 | tf_op jit(solution)/shard_map/ppermute | solution.py:307
  76.7 65.1 %copy-start.4 = (bf16[128,2048]{1,0:T(8,128)(2,1)}, bf16[128,2048]{1,0:T(8,128)(2,1)S(1)}, u32[]{:S(2)}) copy-start(bf16[128,2048]{1,0:T(8,128)(2,1)S(1)} %collective-permute-done.1.refs_3_) | copy-start | bytes 1572868
  76.7 17.9 %collective-permute-start.5 = (bf16[128,2048]{1,0:T(8,128)(2,1)S(1)}, bf16[128,2048]{1,0:T(8,128)(2,1)S(1)}, u32[]{:S(2)}, u32[]{:S(2)}) collective-permute-start(bf16[128,2048]{1,0:T(8,128)(2,1)S(1)} %collective-permute-done.3.refs_5_), channel_id=1, source_target_pairs={{4,6},{5,7},{6,4},{7,5},{8,10},{9,11},{10,8},{11,9},{12,14},{13,15... | collective-permute-start | bytes 1572872 | tf_op jit(solution)/shard_map/ppermute | solution.py:307
  77.4 64.4 %copy-start.5 = (bf16[128,2048]{1,0:T(8,128)(2,1)}, bf16[128,2048]{1,0:T(8,128)(2,1)S(1)}, u32[]{:S(2)}) copy-start(bf16[128,2048]{1,0:T(8,128)(2,1)S(1)} %collective-permute-done.refs_2_) | copy-start | bytes 1572868
  77.4 18.5 %collective-permute-start.4 = (bf16[128,2048]{1,0:T(8,128)(2,1)S(1)}, bf16[128,2048]{1,0:T(8,128)(2,1)S(1)}, u32[]{:S(2)}, u32[]{:S(2)}) collective-permute-start(bf16[128,2048]{1,0:T(8,128)(2,1)S(1)} %collective-permute-done.3.refs_5_), channel_id=1, source_target_pairs={{4,5},{5,4},{6,7},{7,6},{8,9},{9,8},{10,11},{11,10},{12,13},{13,12... | collective-permute-start | bytes 1572872 | tf_op jit(solution)/shard_map/ppermute | solution.py:307
  83.1 58.7 %copy-start.6 = (bf16[128,2048]{1,0:T(8,128)(2,1)}, bf16[128,2048]{1,0:T(8,128)(2,1)S(1)}, u32[]{:S(2)}) copy-start(bf16[128,2048]{1,0:T(8,128)(2,1)S(1)} %collective-permute-done.11.refs_13_) | copy-start | bytes 1572868
  83.1 14.2 %collective-permute-start.8 = (bf16[128,2048]{1,0:T(8,128)(2,1)S(1)}, bf16[128,2048]{1,0:T(8,128)(2,1)S(1)}, u32[]{:S(2)}, u32[]{:S(2)}) collective-permute-start(bf16[128,2048]{1,0:T(8,128)(2,1)S(1)} %collective-permute-done.7.refs_9_), channel_id=1, source_target_pairs={{0,1},{1,0},{2,3},{3,2},{4,5},{5,4},{6,7},{7,6},{8,9},{9,8},{10,11... | collective-permute-start | bytes 1572872 | tf_op jit(solution)/shard_map/ppermute | solution.py:307
  87.3 54.5 %copy-start.7 = (bf16[128,2048]{1,0:T(8,128)(2,1)}, bf16[128,2048]{1,0:T(8,128)(2,1)S(1)}, u32[]{:S(2)}) copy-start(bf16[128,2048]{1,0:T(8,128)(2,1)S(1)} %collective-permute-done.15.refs_17_) | copy-start | bytes 1572868
  87.3 13.5 %collective-permute-start.2 = (bf16[128,2048]{1,0:T(8,128)(2,1)S(1)}, bf16[128,2048]{1,0:T(8,128)(2,1)S(1)}, u32[]{:S(2)}, u32[]{:S(2)}) collective-permute-start(bf16[128,2048]{1,0:T(8,128)(2,1)S(1)} %collective-permute-done.1.refs_3_), channel_id=1, source_target_pairs={{0,1},{1,0},{2,3},{3,2},{4,5},{5,4},{6,7},{7,6},{8,9},{9,8},{10,11... | collective-permute-start | bytes 1572872 | tf_op jit(solution)/shard_map/ppermute | solution.py:307
  88.6 32.8 %copy-start.8 = (bf16[128,2048]{1,0:T(8,128)(2,1)}, bf16[128,2048]{1,0:T(8,128)(2,1)S(1)}, u32[]{:S(2)}) copy-start(bf16[128,2048]{1,0:T(8,128)(2,1)S(1)} %collective-permute-done.9.refs_11_) | copy-start | bytes 1572868
  88.6 14.0 %collective-permute-start.19 = (bf16[128,2048]{1,0:T(8,128)(2,1)S(1)}, bf16[128,2048]{1,0:T(8,128)(2,1)S(1)}, u32[]{:S(2)}, u32[]{:S(2)}) collective-permute-start(bf16[128,2048]{1,0:T(8,128)(2,1)S(1)} %collective-permute-done.11.refs_13_), channel_id=1, source_target_pairs={{0,4},{1,5},{2,6},{3,7},{4,8},{5,9},{6,10},{7,11},{8,12},{9,13},{1... | collective-permute-start | bytes 1572872 | tf_op jit(solution)/shard_map/ppermute | solution.py:303
  94.6 27.5 %copy-start.9 = (bf16[128,2048]{1,0:T(8,128)(2,1)}, bf16[128,2048]{1,0:T(8,128)(2,1)S(1)}, u32[]{:S(2)}) copy-start(bf16[128,2048]{1,0:T(8,128)(2,1)S(1)} %collective-permute-done.5.refs_7_) | copy-start | bytes 1572868
  94.6 20.1 %collective-permute-start.23 = (bf16[128,2048]{1,0:T(8,128)(2,1)S(1)}, bf16[128,2048]{1,0:T(8,128)(2,1)}, u32[]{:S(2)}, u32[]{:S(2)}) collective-permute-start(bf16[128,2048]{1,0:T(8,128)(2,1)S(1)} %collective-permute-done.15.refs_17_), channel_id=1, source_target_pairs={{4,0},{5,1},{6,2},{7,3},{8,4},{9,5},{10,6},{11,7},{12,8},{13,9},{1... | collective-permute-start | bytes 1572872 | tf_op jit(solution)/shard_map/ppermute | solution.py:303
  95.9 28.4 %copy-start.10 = (bf16[128,2048]{1,0:T(8,128)(2,1)}, bf16[128,2048]{1,0:T(8,128)(2,1)S(1)}, u32[]{:S(2)}) copy-start(bf16[128,2048]{1,0:T(8,128)(2,1)S(1)} %collective-permute-done.4.refs_6_) | copy-start | bytes 1572868
  95.9 20.7 %collective-permute-start.13 = (bf16[128,2048]{1,0:T(8,128)(2,1)S(1)}, bf16[128,2048]{1,0:T(8,128)(2,1)}, u32[]{:S(2)}, u32[]{:S(2)}) collective-permute-start(bf16[128,2048]{1,0:T(8,128)(2,1)S(1)} %collective-permute-done.11.refs_13_), channel_id=1, source_target_pairs={{8,10},{9,11},{10,8},{11,9},{12,14},{13,15},{14,12},{15,13},{24,26... | collective-permute-start | bytes 1572872 | tf_op jit(solution)/shard_map/ppermute | solution.py:307
  97.4 28.4 %copy-start.11 = (bf16[128,2048]{1,0:T(8,128)(2,1)}, bf16[128,2048]{1,0:T(8,128)(2,1)S(1)}, u32[]{:S(2)}) copy-start(bf16[128,2048]{1,0:T(8,128)(2,1)S(1)} %collective-permute-done.8.refs_10_) | copy-start | bytes 1572868
  97.4 20.0 %collective-permute-start.17 = (bf16[128,2048]{1,0:T(8,128)(2,1)S(1)}, bf16[128,2048]{1,0:T(8,128)(2,1)}, u32[]{:S(2)}, u32[]{:S(2)}) collective-permute-start(bf16[128,2048]{1,0:T(8,128)(2,1)S(1)} %collective-permute-done.15.refs_17_), channel_id=1, source_target_pairs={{0,2},{1,3},{2,0},{3,1},{4,6},{5,7},{6,4},{7,5},{16,18},{17,19},{1... | collective-permute-start | bytes 1572872 | tf_op jit(solution)/shard_map/ppermute | solution.py:307
  100.8 25.0 %copy-start.12 = (bf16[128,2048]{1,0:T(8,128)(2,1)}, bf16[128,2048]{1,0:T(8,128)(2,1)S(1)}, u32[]{:S(2)}) copy-start(bf16[128,2048]{1,0:T(8,128)(2,1)S(1)} %collective-permute-done.2.refs_4_) | copy-start | bytes 1572868
  100.8 18.0 %collective-permute-start.12 = (bf16[128,2048]{1,0:T(8,128)(2,1)S(1)}, bf16[128,2048]{1,0:T(8,128)(2,1)S(1)}, u32[]{:S(2)}, u32[]{:S(2)}) collective-permute-start(bf16[128,2048]{1,0:T(8,128)(2,1)S(1)} %collective-permute-done.11.refs_13_), channel_id=1, source_target_pairs={{8,9},{9,8},{10,11},{11,10},{12,13},{13,12},{14,15},{15,14},{24,25... | collective-permute-start | bytes 1572872 | tf_op jit(solution)/shard_map/ppermute | solution.py:307
  102.6 25.4 %copy-start.13 = (bf16[128,2048]{1,0:T(8,128)(2,1)}, bf16[128,2048]{1,0:T(8,128)(2,1)S(1)}, u32[]{:S(2)}) copy-start(bf16[128,2048]{1,0:T(8,128)(2,1)S(1)} %collective-permute-done.19.refs_21_) | copy-start | bytes 1572868
  102.6 18.8 %collective-permute-start.16 = (bf16[128,2048]{1,0:T(8,128)(2,1)S(1)}, bf16[128,2048]{1,0:T(8,128)(2,1)S(1)}, u32[]{:S(2)}, u32[]{:S(2)}) collective-permute-start(bf16[128,2048]{1,0:T(8,128)(2,1)S(1)} %collective-permute-done.15.refs_17_), channel_id=1, source_target_pairs={{0,1},{1,0},{2,3},{3,2},{4,5},{5,4},{6,7},{7,6},{16,17},{17,16},{1... | collective-permute-start | bytes 1572872 | tf_op jit(solution)/shard_map/ppermute | solution.py:307
  114.7 7.4 %collective-permute-start.10 = (bf16[128,2048]{1,0:T(8,128)(2,1)S(1)}, bf16[128,2048]{1,0:T(8,128)(2,1)S(1)}, u32[]{:S(2)}, u32[]{:S(2)}) collective-permute-start(bf16[128,2048]{1,0:T(8,128)(2,1)S(1)} %collective-permute-done.9.refs_11_), channel_id=1, source_target_pairs={{0,1},{1,0},{2,3},{3,2},{4,5},{5,4},{6,7},{7,6},{8,9},{9,8},{10,11... | collective-permute-start | bytes 1572872 | tf_op jit(solution)/shard_map/ppermute | solution.py:307
  116.6 7.6 %collective-permute-start.6 = (bf16[128,2048]{1,0:T(8,128)(2,1)S(1)}, bf16[128,2048]{1,0:T(8,128)(2,1)S(1)}, u32[]{:S(2)}, u32[]{:S(2)}) collective-permute-start(bf16[128,2048]{1,0:T(8,128)(2,1)S(1)} %collective-permute-done.5.refs_7_), channel_id=1, source_target_pairs={{4,5},{5,4},{6,7},{7,6},{8,9},{9,8},{10,11},{11,10},{12,13},{13,12... | collective-permute-start | bytes 1572872 | tf_op jit(solution)/shard_map/ppermute | solution.py:307
  117.4 8.4 %collective-permute-start.21 = (bf16[128,2048]{1,0:T(8,128)(2,1)S(1)}, bf16[128,2048]{1,0:T(8,128)(2,1)}, u32[]{:S(2)}, u32[]{:S(2)}) collective-permute-start(bf16[128,2048]{1,0:T(8,128)(2,1)S(1)} %collective-permute-done.19.refs_21_), channel_id=1, source_target_pairs={{12,14},{13,15},{14,12},{15,13},{28,30},{29,31},{30,28},{31,29}} | collective-permute-start | bytes 1572872 | tf_op jit(solution)/shard_map/ppermute | solution.py:307
  118.8 18.0 %copy-start.14 = (bf16[128,2048]{1,0:T(8,128)(2,1)}, bf16[128,2048]{1,0:T(8,128)(2,1)S(1)}, u32[]{:S(2)}) copy-start(bf16[128,2048]{1,0:T(8,128)(2,1)S(1)} %collective-permute-done.12.refs_14_) | copy-start | bytes 1572868
  118.8 16.5 %collective-permute-start.25 = (bf16[128,2048]{1,0:T(8,128)(2,1)}, bf16[128,2048]{1,0:T(8,128)(2,1)}, u32[]{:S(2)}, u32[]{:S(2)}) collective-permute-start(bf16[128,2048]{1,0:T(8,128)(2,1)} %collective-permute-done.23.refs_25_), channel_id=1, source_target_pairs={{0,2},{1,3},{2,0},{3,1},{16,18},{17,19},{18,16},{19,17}} | collective-permute-start | bytes 1572872 | tf_op jit(solution)/shard_map/ppermute | solution.py:307
  121.4 15.4 %copy-start.15 = (bf16[128,2048]{1,0:T(8,128)(2,1)}, bf16[128,2048]{1,0:T(8,128)(2,1)S(1)}, u32[]{:S(2)}) copy-start(bf16[128,2048]{1,0:T(8,128)(2,1)S(1)} %collective-permute-done.16.refs_18_) | copy-start | bytes 1572868
  121.4 15.4 %collective-permute-start.20 = (bf16[128,2048]{1,0:T(8,128)(2,1)S(1)}, bf16[128,2048]{1,0:T(8,128)(2,1)S(1)}, u32[]{:S(2)}, u32[]{:S(2)}) collective-permute-start(bf16[128,2048]{1,0:T(8,128)(2,1)S(1)} %collective-permute-done.19.refs_21_), channel_id=1, source_target_pairs={{12,13},{13,12},{14,15},{15,14},{28,29},{29,28},{30,31},{31,30}} | collective-permute-start | bytes 1572872 | tf_op jit(solution)/shard_map/ppermute | solution.py:307
  122.1 14.7 %copy-start.16 = (bf16[128,2048]{1,0:T(8,128)(2,1)}, bf16[128,2048]{1,0:T(8,128)(2,1)S(1)}, u32[]{:S(2)}) copy-start(bf16[128,2048]{1,0:T(8,128)(2,1)S(1)} %collective-permute-done.10.refs_12_) | copy-start | bytes 1572868
  122.1 18.8 %collective-permute-start.24 = (bf16[128,2048]{1,0:T(8,128)(2,1)}, bf16[128,2048]{1,0:T(8,128)(2,1)}, u32[]{:S(2)}, u32[]{:S(2)}) collective-permute-start(bf16[128,2048]{1,0:T(8,128)(2,1)} %collective-permute-done.23.refs_25_), channel_id=1, source_target_pairs={{0,1},{1,0},{2,3},{3,2},{16,17},{17,16},{18,19},{19,18}} | collective-permute-start | bytes 1572872 | tf_op jit(solution)/shard_map/ppermute | solution.py:307
  124.3 12.5 %copy-start.17 = (bf16[128,2048]{1,0:T(8,128)(2,1)}, bf16[128,2048]{1,0:T(8,128)(2,1)S(1)}, u32[]{:S(2)}) copy-start(bf16[128,2048]{1,0:T(8,128)(2,1)S(1)} %collective-permute-done.6.refs_8_) | copy-start | bytes 1572868
  124.3 16.7 %collective-permute-start.14 = (bf16[128,2048]{1,0:T(8,128)(2,1)}, bf16[128,2048]{1,0:T(8,128)(2,1)}, u32[]{:S(2)}, u32[]{:S(2)}) collective-permute-start(bf16[128,2048]{1,0:T(8,128)(2,1)} %collective-permute-done.13.refs_15_), channel_id=1, source_target_pairs={{8,9},{9,8},{10,11},{11,10},{12,13},{13,12},{14,15},{15,14},{24,25... | collective-permute-start | bytes 1572872 | tf_op jit(solution)/shard_map/ppermute | solution.py:307
  125.8 15.2 %collective-permute-start.18 = (bf16[128,2048]{1,0:T(8,128)(2,1)}, bf16[128,2048]{1,0:T(8,128)(2,1)}, u32[]{:S(2)}, u32[]{:S(2)}) collective-permute-start(bf16[128,2048]{1,0:T(8,128)(2,1)} %collective-permute-done.17.refs_19_), channel_id=1, source_target_pairs={{0,1},{1,0},{2,3},{3,2},{4,5},{5,4},{6,7},{7,6},{16,17},{17,16},{1... | collective-permute-start | bytes 1572872 | tf_op jit(solution)/shard_map/ppermute | solution.py:307
  135.4 5.6 %collective-permute-start.22 = (bf16[128,2048]{1,0:T(8,128)(2,1)}, bf16[128,2048]{1,0:T(8,128)(2,1)}, u32[]{:S(2)}, u32[]{:S(2)}) collective-permute-start(bf16[128,2048]{1,0:T(8,128)(2,1)} %collective-permute-done.21.refs_23_), channel_id=1, source_target_pairs={{12,13},{13,12},{14,15},{15,14},{28,29},{29,28},{30,31},{31,30}} | collective-permute-start | bytes 1572872 | tf_op jit(solution)/shard_map/ppermute | solution.py:307
  137.7 4.1 %collective-permute-start.26 = (bf16[128,2048]{1,0:T(8,128)(2,1)}, bf16[128,2048]{1,0:T(8,128)(2,1)}, u32[]{:S(2)}, u32[]{:S(2)}) collective-permute-start(bf16[128,2048]{1,0:T(8,128)(2,1)} %collective-permute-done.25.refs_27_), channel_id=1, source_target_pairs={{0,1},{1,0},{2,3},{3,2},{16,17},{17,16},{18,19},{19,18}} | collective-permute-start | bytes 1572872 | tf_op jit(solution)/shard_map/ppermute | solution.py:307
  224.7 5.2 %copy-start.19 = (s32[128,4]{0,1:T(4,128)S(1)}, s32[128,4]{0,1:T(4,128)}, u32[]{:S(2)}) copy-start(s32[128,4]{0,1:T(4,128)} %param.13) | copy-start | bytes 6148
  224.7 5.8 %copy-start.21 = (f32[128,4]{0,1:T(4,128)S(1)}, f32[128,4]{0,1:T(4,128)}, u32[]{:S(2)}) copy-start(f32[128,4]{0,1:T(4,128)} %param.14) | copy-start | bytes 6148
  224.7 37.1 %all-to-all-start.2 = ((bf16[16,24,2048]{2,1,0:T(8,128)(2,1)}), bf16[16,24,2048]{2,1,0:T(8,128)(2,1)S(1)}, u32[]{:S(2)}, u32[]{:S(2)}) async-start(bf16[16,24,2048]{2,1,0:T(8,128)(2,1)} %get-tuple-element.4), calls=%async_computation.2 | async-start | bytes 3145728 | tf_op jit(solution)/shard_map/all_to_all | solution.py:390
  (5 other events, 11.3 us)

commit v3 on v0

--- a/solution.py
+++ b/solution.py
@@ -1,11 +1,374 @@
+import functools
+
 import jax
 import jax.numpy as jnp
 from jax import lax
+from jax.experimental import pallas as pl
+from jax.experimental.pallas import tpu as pltpu
 from jax.sharding import PartitionSpec as P
 
 EXPERTS = 64
 TOP = 4
 CAP = 12
+BLOCK = 128
+PAIR = 2 * CAP
+VMEM = pltpu.VMEM
+F32 = jnp.float32
+BF16 = jnp.bfloat16
+
+
+def dot(a, b):
+    return jnp.dot(a, b, preferred_element_type=F32)
+
+
+def iota(shape, dimension):
+    return lax.broadcasted_iota(jnp.int32, shape, dimension)
+
+
+def flags(mask):
+    return mask.astype(F32).astype(BF16)
+
+
+def earlier(length):
+    return flags(iota((length, length), 0) < iota((length, length), 1))
+
+
+def fetch_kernel(me_ref, rows_ref, table_ref, out_ref):
+    device_count, _, tok_rows = rows_ref.shape
+    held = table_ref.shape[0]
+    look_cap = out_ref.shape[0] // device_count
+    local = rows_ref[:, 0, :] - me_ref[0] * held
+    hit = (local >= 0) & (local < held)
+    rank = dot(flags(hit), earlier(tok_rows)).astype(jnp.int32)
+    rank = jnp.where(hit, rank, -1)
+    slot = iota((look_cap, tok_rows), 0)
+    place = iota((look_cap, held), 1)
+    picks = []
+    for source in range(device_count):
+        mine = jnp.where(slot == rank[source : source + 1], local[source : source + 1], 0)
+        wanted = jnp.sum(mine, axis=1, keepdims=True)
+        picks.append(flags(place == wanted))
+    out_ref[...] = dot(jnp.concatenate(picks, axis=0), table_ref[...]).astype(BF16)
+
+
+def plan_kernel(
+    me_ref, rows_ref, across_ref, ids_ref, _, put_ref, first_ref, second_ref, slots_ref
+):
+    tok_rows = rows_ref.shape[1]
+    slots = put_ref.shape[1]
+    flip = me_ref[0] % 2
+    held = me_ref[1]
+    owners = me_ref[2]
+    device_count = first_ref.shape[0] // PAIR
+    exp_dev = EXPERTS // device_count
+    look_cap = slots // device_count
+    before = earlier(tok_rows)
+
+    row = jnp.broadcast_to(rows_ref[...], (device_count, tok_rows))
+    low = iota((device_count, tok_rows), 0) * held
+    hit = (row >= low) & (row < low + held) & (low < owners * held)
+    rank = jnp.where(hit, dot(flags(hit), before).astype(jnp.int32), -1)
+    slot = iota((look_cap, tok_rows), 0)
+    put = [(slot == rank[o : o + 1]).astype(F32) for o in range(device_count)]
+    put_ref[...] = jnp.concatenate(put, axis=0).T.astype(BF16)
+
+    expert = iota((EXPERTS, tok_rows), 0)
+    hit = functools.reduce(
+        jnp.logical_or, [across_ref[k : k + 1, :] == expert for k in range(TOP)]
+    )
+    rank = jnp.where(hit, dot(flags(hit), before).astype(jnp.int32), -1000)
+    place = iota((PAIR, tok_rows), 0)
+    for chunk, ref in enumerate((first_ref, second_ref)):
+        lines = []
+        for d in range(device_count):
+            at = d * exp_dev + 2 * chunk
+            one, two = rank[at : at + 1], rank[at + 1 : at + 2]
+            upper = jnp.where(flip == 0, one, two)
+            lower = jnp.where(flip == 0, two, one) + CAP
+            here = ((place < CAP) & (place == upper)) | ((place >= CAP) & (place == lower))
+            lines.append(here.astype(F32))
+        ref[...] = jnp.concatenate(lines, axis=0).astype(BF16)
+
+    expert = iota((tok_rows, EXPERTS), 1)
+    chosen = [ids_ref[:, k : k + 1] == expert for k in range(TOP)]
+    counted = dot(earlier(tok_rows).T, flags(functools.reduce(jnp.logical_or, chosen)))
+    shift = exp_dev.bit_length() - 1
+    for k in range(TOP):
+        ids = ids_ref[:, k : k + 1]
+        nth = jnp.sum(jnp.where(chosen[k], counted, 0.0), axis=1, keepdims=True).astype(jnp.int32)
+        inside = ids & (exp_dev - 1)
+        slots_ref[:, k : k + 1] = (
+            (inside >> 1) * (device_count * PAIR)
+            + (ids >> shift) * PAIR
+            + ((flip + inside) & 1) * CAP
+            + nth
+        )
+
+
+def state_kernel(put_ref, pick_ref, returned_ref, values_ref, scales_ref, state_ref, out_ref):
+    features = values_ref.shape[1]
+    width = 512
+    for left in range(0, features, width):
+        found = dot(put_ref[...], returned_ref[:, left : left + width])
+        for b in range(width // BLOCK):
+            at = left + b * BLOCK
+            scaled = (
+                values_ref[:, at : at + BLOCK].astype(F32)
+                * scales_ref[:, at // BLOCK : at // BLOCK + 1]
+            )
+            state_ref[:, at : at + BLOCK] = (
+                scaled + found[:, b * BLOCK : (b + 1) * BLOCK]
+            ).astype(BF16)
+        cols = slice(left, left + width)
+        out_ref[:, cols] = dot(pick_ref[...], state_ref[:, cols]).astype(BF16)
+
+
+def pick_kernel(pick_ref, state_ref, _, out_ref):
+    features = state_ref.shape[1]
+    width = 512
+    for left in range(0, features, width):
+        cols = slice(left, left + width)
+        out_ref[:, cols] = dot(pick_ref[...], state_ref[:, cols]).astype(BF16)
+
+
+def expert_kernel(
+    first_held,
+    arrived_ref,
+    wg_hbm,
+    wu_hbm,
+    wd_hbm,
+    out_ref,
+    x_ref,
+    wg_ref,
+    wu_ref,
+    wd_ref,
+    hidden_ref,
+    result_ref,
+    sem,
+):
+    count, features, width = wg_ref.shape
+    device_count = arrived_ref.shape[0]
+    up_cuts = ((0, 512), (512, 512), (1024, width - 1024))
+    down_cuts = tuple((at, 512) for at in range(0, features, 512))
+
+    def weight_copies(j):
+        copies = []
+        for at, size in up_cuts:
+            for hbm, ref in ((wg_hbm, wg_ref), (wu_hbm, wu_ref)):
+                cols = pl.ds(at, size)
+                copies.append((hbm.at[first_held + j, :, cols], ref.at[j, :, cols]))
+        for at, size in down_cuts:
+            cols = pl.ds(at, size)
+            copies.append((wd_hbm.at[first_held + j, :, cols], wd_ref.at[j, :, cols]))
+        return [
+            pltpu.make_async_copy(src, dst, sem.at[j, n]) for n, (src, dst) in enumerate(copies)
+        ]
+
+    for j in range(count):
+        for copy in weight_copies(j):
+            copy.start()
+
+    low = iota((PAIR, features), 0) < CAP
+    for quad in range(device_count // 4):
+        ones, twos = [], []
+        for pair in range(2):
+            source = 4 * quad + 2 * pair
+            even = arrived_ref[source].astype(F32)
+            odd = arrived_ref[source + 1].astype(F32)
+            ones.append(jnp.where(low, even, odd))
+            twos.append(jnp.where(low, odd, even))
+        rows = slice(quad * 2 * PAIR, (quad + 1) * 2 * PAIR)
+        x_ref[0, rows, :] = jnp.concatenate(ones, axis=0).astype(BF16)
+        x_ref[1, rows, :] = jnp.concatenate(twos, axis=0).astype(BF16)
+
+    @pl.loop(0, count)
+    def _(j):
+        copies = weight_copies(j)
+        n = 0
+        for at, size in up_cuts:
+            copies[n].wait()
+            copies[n + 1].wait()
+            n += 2
+            x = x_ref[j]
+            gate = dot(x, wg_ref[j, :, at : at + size])
+            up = dot(x, wu_ref[j, :, at : at + size])
+            hidden_ref[:, at : at + size] = (gate / (1.0 + jnp.exp(-gate)) * up).astype(BF16)
+        for at, size in down_cuts:
+            copies[n].wait()
+            n += 1
+            result_ref[j, :, at : at + size] = dot(hidden_ref[...], wd_ref[j, :, at : at + size])
+
+    for pair in range(device_count // 2):
+        one = result_ref[0, pair * PAIR : (pair + 1) * PAIR, :]
+        two = result_ref[1, pair * PAIR : (pair + 1) * PAIR, :]
+        out_ref[2 * pair] = jnp.where(low, one, two).astype(BF16)
+        out_ref[2 * pair + 1] = jnp.where(low, two, one).astype(BF16)
+
+
+def expert_call(first_held, arrived, w_gate, w_up, w_down):
+    exp_dev, features, width = w_gate.shape
+    device_count = arrived.shape[0]
+    count = 2
+    rows = device_count * CAP
+    anywhere = pl.BlockSpec(memory_space=pl.ANY)
+    vmem = pl.BlockSpec(memory_space=VMEM)
+    return pl.pallas_call(
+        functools.partial(expert_kernel, first_held),
+        out_shape=jax.ShapeDtypeStruct((device_count, PAIR, features), BF16),
+        in_specs=[vmem] + [anywhere] * 3,
+        out_specs=vmem,
+        scratch_shapes=[
+            VMEM((count, rows, features), BF16),
+            VMEM((count, features, width), BF16),
+            VMEM((count, features, width), BF16),
+            VMEM((count, width, features), BF16),
+            VMEM((rows, width), BF16),
+            VMEM((count, rows, features), F32),
+            pltpu.SemaphoreType.DMA((count, 10)),
+        ],
+        compiler_params=pltpu.CompilerParams(vmem_limit_bytes=52 * 1024 * 1024),
+        cost_estimate=pl.CostEstimate(
+            flops=6 * count * rows * features * width,
+            bytes_accessed=6 * count * features * width,
+            transcendentals=count * rows * width,
+        ),
+        name="experts_second" if first_held else "experts_first",
+    )(arrived, w_gate, w_up, w_down)
+
+
+def combine_kernel(chunk, slots_ref, weights_ref, back_ref, grad_ref, *refs):
+    sums = refs[:2] if chunk else None
+    mixed_ref, grads_ref = refs[-2:]
+    tok_rows, features = grad_ref.shape
+    half = back_ref.shape[0]
+    column = iota((tok_rows, half), 1) + chunk * half
+    inner = lax.dot_general(
+        grad_ref[...], back_ref[...], (((1,), (1,)), ((), ())), preferred_element_type=F32
+    )
+    total = jnp.zeros((tok_rows, half), F32)
+    for k in range(TOP):
+        here = column == slots_ref[:, k : k + 1]
+        total = total + jnp.where(here, weights_ref[:, k : k + 1], 0.0)
+        value = jnp.sum(jnp.where(here, inner, 0.0), axis=1, keepdims=True)
+        if chunk:
+            value = value + sums[1][:, k : k + 1]
+        grads_ref[:, k : k + 1] = value
+    high = total.astype(BF16)
+    rest = (total - high.astype(F32)).astype(BF16)
+    width = 512
+    for at in range(0, features, width):
+        rows = back_ref[:, at : at + width]
+        value = dot(high, rows) + dot(rest, rows)
+        if chunk:
+            value = value + sums[0][:, at : at + width]
+        mixed_ref[:, at : at + width] = value.astype(mixed_ref.dtype)
+
+
+def swap(array):
+    return lax.all_to_all(array, "expert", split_axis=0, concat_axis=0, tiled=True)
+
+
+def near_path(
+    block_values,
+    block_exps,
+    row_ids,
+    expert_ids,
+    gate_weights,
+    table,
+    w_gate,
+    w_up,
+    w_down,
+    out_grad,
+):
+    device_count = lax.axis_size("expert")
+    me = lax.axis_index("expert").astype(jnp.int32)
+    tok_rows, features = block_values.shape
+    rows_held = table.shape[0]
+    look_cap = max(2, 2 * tok_rows // device_count)
+    slots = device_count * PAIR
+    vmem = pl.BlockSpec(memory_space=VMEM)
+    smem = pl.BlockSpec(memory_space=pltpu.SMEM)
+    anywhere = pl.BlockSpec(memory_space=pl.ANY)
+    place = jnp.stack([me, jnp.int32(rows_held), jnp.int32(device_count)])
+
+    def shape(dims, kind):
+        return jax.ShapeDtypeStruct(dims, kind)
+
+    all_rows = swap(jnp.broadcast_to(row_ids[None, None, :], (device_count, 1, tok_rows)))
+    fetched = pl.pallas_call(
+        fetch_kernel,
+        out_shape=shape((device_count * look_cap, features), BF16),
+        in_specs=[smem, vmem, vmem],
+        out_specs=vmem,
+        name="fetch_rows",
+    )(place, all_rows, table)
+    returned = swap(fetched.reshape(device_count, look_cap, features))
+    put, first_pick, second_pick, slot_of = pl.pallas_call(
+        plan_kernel,
+        out_shape=(
+            shape((tok_rows, device_count * look_cap), BF16),
+            shape((slots, tok_rows), BF16),
+            shape((slots, tok_rows), BF16),
+            shape((tok_rows, TOP), jnp.int32),
+        ),
+        in_specs=[smem, vmem, vmem, vmem, anywhere],
+        out_specs=(vmem, vmem, vmem, vmem),
+        name="plan",
+    )(place, row_ids[None, :], expert_ids.T, expert_ids, fetched)
+    state, first_sent = pl.pallas_call(
+        state_kernel,
+        out_shape=(shape((tok_rows, features), BF16), shape((slots, features), BF16)),
+        in_specs=[vmem] * 5,
+        out_specs=(vmem, vmem),
+        name="token_state",
+    )(
+        put,
+        first_pick,
+        returned.reshape(device_count * look_cap, features),
+        block_values,
+        jnp.exp2(block_exps.astype(F32)),
+    )
+    first_rows = swap(first_sent.reshape(device_count, PAIR, features))
+    second_sent = pl.pallas_call(
+        pick_kernel,
+        out_shape=shape((slots, features), BF16),
+        in_specs=[vmem, vmem, anywhere],
+        out_specs=vmem,
+        name="second_slots",
+    )(second_pick, state, first_rows)
+    second_rows = swap(second_sent.reshape(device_count, PAIR, features))
+    first_out = expert_call(0, first_rows, w_gate, w_up, w_down)
+    first_back = swap(first_out)
+    second_out = expert_call(2, second_rows, w_gate, w_up, w_down)
+    second_back = swap(
+        pl.pallas_call(
+            lambda second_ref, first_ref, out_ref: None,
+            out_shape=shape(second_out.shape, BF16),
+            in_specs=[anywhere, anywhere],
+            out_specs=anywhere,
+            input_output_aliases={0: 0},
+            name="after_first",
+        )(second_out, first_back)
+    )
+
+    def combine(chunk, back, *sums):
+        return pl.pallas_call(
+            functools.partial(combine_kernel, chunk),
+            out_shape=(
+                shape((tok_rows, features), BF16 if chunk else F32),
+                shape((tok_rows, TOP), F32),
+            ),
+            in_specs=[vmem] * (4 + len(sums)),
+            out_specs=(vmem, vmem),
+            cost_estimate=pl.CostEstimate(
+                flops=6 * tok_rows * slots * features,
+                bytes_accessed=4 * slots * features,
+                transcendentals=0,
+            ),
+            name="combine_second" if chunk else "combine_first",
+        )(slot_of, gate_weights, back.reshape(slots, features), out_grad, *sums)
+
+    return combine(1, second_back, *combine(0, first_back))
 
 
 def expert_work(arrived, w_gate, w_up, w_down):
@@ -41,7 +404,7 @@
     return jnp.sum(pieces, axis=1).astype(jnp.bfloat16).reshape(EXPERTS * CAP, features)
 
 
-def local(
+def far_path(
     block_values,
     block_exps,
     row_ids,
@@ -104,6 +467,12 @@
     return (mixed, gate_grads)
 
 
+def local(*arrays):
+    if lax.axis_size("expert") == 16 and arrays[6].shape[0] * 16 == EXPERTS:
+        return near_path(*arrays)
+    return far_path(*arrays)
+
+
 def solution(mesh):
     return jax.shard_map(
         local,

time: 283 us -> 229 us (0.81)
  the two profiles are of different devices: /device:TPU:13 before, /device:TPU:0 now
where the time goes in v3:
time: 229 us; the launch traced here: 225 us
  waiting for transfers between devices  85.5 us (37%)
  Pallas kernels  49.2 us (21%)
  blocking collectives  43 us (19%)
  starting transfers between devices  34.5 us (15%)
  local copies, waits for them, and re-layouts  11.1 us (5%)
    all_to_all x5, waiting for transfers between devices, swap(): lax.all_to_all(array, 'expert', split_axis=0, concat_axis=0, tiled=True)  85.5 us
    all_to_all x1, blocking collectives, swap(): lax.all_to_all(array, 'expert', split_axis=0, concat_axis=0, tiled=True)  43 us
    all_to_all x5, starting transfers between devices, swap(): lax.all_to_all(array, 'expert', split_axis=0, concat_axis=0, tiled=True)  34.5 us
    pallas_call x2, Pallas kernels, expert_call(): pl.pallas_call(functools.partial(expert_kernel, first_held), out_shape=ja...  29.7 us
    pallas_call x2, Pallas kernels, combine(): pl.pallas_call(functools.partial(combine_kernel, chunk), out_shape=(shape...  7.7 us
    unnamed x20, local copies, waits for them, and re-layouts  7.67 us
  transfers between devices with their start and end apart: 5, of which 5 were waited for; matrix products, arithmetic and copies ran while one was open for 1% of the time, Pallas kernels for 16%

profile of v3, /device:TPU:0, one launch (start us, length us, event | category | flops | bytes accessed | tf_op | source)
XLA Modules:
  0.0 224.8 jit_solution(15611560309763523883)
XLA Ops:
  0.6 1.3 broadcast_in_dim.10
  1.9 7.4 %all-to-all-start = ((s32[16,1,128]{2,1,0:T(1,128)}), s32[16,1,128]{2,1,0:T(1,128)S(1)}, u32[]{:S(2)}, u32[]{:S(2)}) async-start(s32[16,1,128]{2,1,0:T(1,128)} %broadcast_in_dim.10), calls=%async_computation | async-start | bytes 16384 | tf_op jit(solution)/shard_map/all_to_all | solution.py:268
  9.3 0.7 pad_add_fusion.me_ref
  9.9 5.7 %all-to-all-done.rows_ref = s32[16,1,128]{2,1,0:T(1,128)S(1)} async-done(((s32[16,1,128]{2,1,0:T(1,128)}), s32[16,1,128]{2,1,0:T(1,128)S(1)}, u32[]{:S(2)}, u32[]{:S(2)}) %all-to-all-start) | async-done | bytes 8224 | tf_op jit(solution)/shard_map/all_to_all | solution.py:268
  15.6 0.0 copy-start.5
  15.6 0.6 copy-done.5
  16.2 2.9 %fetch_rows.1._ = bf16[256,2048]{1,0:T(8,128)(2,1)} custom-call(s32[3]{0:T(128)} %pad_add_fusion.me_ref, s32[16,1,128]{2,1,0:T(1,128)} %copy-done.5, bf16[256,2048]{1,0:T(8,128)(2,1)} %table_ref.1), custom_call_target="tpu_custom_call" | custom-call | tf_op jit(solution)/shard_map/fetch_rows/pallas_call | solution.py:298
  19.1 0.0 copy-start.6
  19.1 0.0 copy-start.7
  19.1 3.8 %all-to-all-start.1 = ((bf16[16,16,2048]{2,1,0:T(8,128)(2,1)}), bf16[16,16,2048]{2,1,0:T(8,128)(2,1)S(1)}, u32[]{:S(2)}, u32[]{:S(2)}) async-start(bf16[16,16,2048]{2,1,0:T(8,128)(2,1)} %bitcast.9), calls=%async_computation.1 | async-start | bytes 2097152 | tf_op jit(solution)/shard_map/all_to_all | solution.py:268
  22.9 0.0 copy-done.6
  22.9 0.7 copy.19.ids_ref
  23.7 0.0 copy-done.7
  23.7 0.7 copy.20.scales_ref
  24.4 2.1 plan.1
  26.5 19.3 %all-to-all-done.1 = bf16[16,16,2048]{2,1,0:T(8,128)(2,1)S(1)} async-done(((bf16[16,16,2048]{2,1,0:T(8,128)(2,1)}), bf16[16,16,2048]{2,1,0:T(8,128)(2,1)S(1)}, u32[]{:S(2)}, u32[]{:S(2)}) %all-to-all-start.1) | async-done | bytes 1048608 | tf_op jit(solution)/shard_map/all_to_all | solution.py:268
  45.8 0.0 copy-start.4
  45.8 1.0 copy-done.4
  46.8 4.0 %token_state.1 = (bf16[128,2048]{1,0:T(8,128)(2,1)}, bf16[384,2048]{1,0:T(8,128)(2,1)}) custom-call(bf16[128,256]{1,0:T(8,128)(2,1)} %get-tuple-element.12.put_ref, bf16[384,128]{1,0:T(8,128)(2,1)} %get-tuple-element.13.pick_ref, bf16[256,2048]{1,0:T(8,128)(2,1)} %bitcast.13, bf16[128,2048]{1,0:T(8,128)(2,1)} %values_ref.1, f32[128,16]{1,0:T(8,128)} %copy.20.scales_ref), custom_call_target="tpu_custom_call" | custom-call | tf_op jit(solution)/shard_map/token_state/pallas_call | solution.py:318
  50.8 43.0 %all_to_all.30._.arrived_ref = bf16[16,24,2048]{2,1,0:T(8,128)(2,1)} all-to-all(bf16[16,24,2048]{2,1,0:T(8,128)(2,1)} %bitcast.14), channel_id=1, replica_groups=mesh['groups'=2,'expert'=16] {'expert'}, dimensions={0} | all-to-all | bytes 3145728 | tf_op jit(solution)/shard_map/all_to_all | solution.py:268
  93.8 2.8 %second_slots.1 = bf16[384,2048]{1,0:T(8,128)(2,1)} custom-call(bf16[384,128]{1,0:T(8,128)(2,1)} %get-tuple-element.11.pick_ref, bf16[128,2048]{1,0:T(8,128)(2,1)} %get-tuple-element.14.state_ref, bf16[16,24,2048]{2,1,0:T(8,128)(2,1)} %all_to_all.30._.arrived_ref), custom_call_target="tpu_custom_call" | custom-call | tf_op jit(solution)/shard_map/second_slots/pallas_call | solution.py:332
  96.6 5.0 %all-to-all-start.3 = ((bf16[16,24,2048]{2,1,0:T(8,128)(2,1)}), bf16[16,24,2048]{2,1,0:T(8,128)(2,1)S(1)}, u32[]{:S(2)}, u32[]{:S(2)}) async-start(bf16[16,24,2048]{2,1,0:T(8,128)(2,1)} %bitcast.11), calls=%async_computation.3 | async-start | bytes 3145728 | tf_op jit(solution)/shard_map/all_to_all | solution.py:268
  101.6 15.4 %experts_first.1 = bf16[16,24,2048]{2,1,0:T(8,128)(2,1)} custom-call(bf16[16,24,2048]{2,1,0:T(8,128)(2,1)} %all_to_all.30._.arrived_ref, bf16[4,2048,1408]{2,1,0:T(8,128)(2,1)} %wg_hbm.3, bf16[4,2048,1408]{2,1,0:T(8,128)(2,1)} %wu_hbm.3, bf16[4,1408,2048]{2,1,0:T(8,128)(2,1)} %wd_hbm.3), custom_call_target="tpu_custom_call" | custom-call | flops 6643777536 | bytes 34603008 | tf_op jit(solution)/shard_map/experts_first/pallas_call | solution.py:215
  117.1 16.5 %all-to-all-done.3.arrived_ref = bf16[16,24,2048]{2,1,0:T(8,128)(2,1)S(1)} async-done(((bf16[16,24,2048]{2,1,0:T(8,128)(2,1)}), bf16[16,24,2048]{2,1,0:T(8,128)(2,1)S(1)}, u32[]{:S(2)}, u32[]{:S(2)}) %all-to-all-start.3) | async-done | bytes 1572896 | tf_op jit(solution)/shard_map/all_to_all | solution.py:268
  133.6 0.0 copy-start.3
  133.6 1.1 copy-done.3
  134.7 9.1 %all-to-all-start.4 = ((bf16[16,24,2048]{2,1,0:T(8,128)(2,1)}), bf16[16,24,2048]{2,1,0:T(8,128)(2,1)S(1)}, u32[]{:S(2)}, u32[]{:S(2)}) async-start(bf16[16,24,2048]{2,1,0:T(8,128)(2,1)} %experts_first.1), calls=%async_computation.4 | async-start | bytes 3145728 | tf_op jit(solution)/shard_map/all_to_all | solution.py:268
  143.9 14.3 %experts_second.1.second_ref = bf16[16,24,2048]{2,1,0:T(8,128)(2,1)S(1)} custom-call(bf16[16,24,2048]{2,1,0:T(8,128)(2,1)} %copy-done.3, bf16[4,2048,1408]{2,1,0:T(8,128)(2,1)} %wg_hbm.3, bf16[4,2048,1408]{2,1,0:T(8,128)(2,1)} %wu_hbm.3, bf16[4,1408,2048]{2,1,0:T(8,128)(2,1)} %wd_hbm.3), custom_call_target="tpu_custom_call" | custom-call | flops 6643777536 | bytes 34603008 | tf_op jit(solution)/shard_map/experts_second/pallas_call | solution.py:215
  158.1 0.0 copy-start
  158.1 1.1 copy-done
  159.3 16.6 %all-to-all-done.4.first_ref = bf16[16,24,2048]{2,1,0:T(8,128)(2,1)S(1)} async-done(((bf16[16,24,2048]{2,1,0:T(8,128)(2,1)}), bf16[16,24,2048]{2,1,0:T(8,128)(2,1)S(1)}, u32[]{:S(2)}, u32[]{:S(2)}) %all-to-all-start.4) | async-done | bytes 1572896 | tf_op jit(solution)/shard_map/all_to_all | solution.py:268
  175.8 0.0 copy-start.2
  175.8 1.2 copy-done.2
  177.0 0.0 copy-start.8
  177.0 9.2 %all-to-all-start.5 = ((bf16[16,24,2048]{2,1,0:T(8,128)(2,1)}), bf16[16,24,2048]{2,1,0:T(8,128)(2,1)S(1)}, u32[]{:S(2)}, u32[]{:S(2)}) async-start(bf16[16,24,2048]{2,1,0:T(8,128)(2,1)} %after_first.1), calls=%async_computation.5 | async-start | bytes 3145728 | tf_op jit(solution)/shard_map/all_to_all | solution.py:268
  186.2 0.0 copy-done.8
  186.3 0.7 copy.22.weights_ref
  187.0 3.8 %combine_first.1 = (f32[128,2048]{1,0:T(8,128)}, f32[128,4]{1,0:T(8,128)}) custom-call(s32[128,4]{1,0:T(8,128)} %get-tuple-element.10.slots_ref, f32[128,4]{1,0:T(8,128)} %copy.22.weights_ref, bf16[384,2048]{1,0:T(8,128)(2,1)} %bitcast.12, bf16[128,2048]{1,0:T(8,128)(2,1)} %grad_ref.3), custom_call_target="tpu_custom_call" | custom-call | flops 603979776 | bytes 3145728 | tf_op jit(solution)/shard_map/combine_first/pallas_call | solution.py:355
  190.8 27.4 %all-to-all-done.5 = bf16[16,24,2048]{2,1,0:T(8,128)(2,1)S(1)} async-done(((bf16[16,24,2048]{2,1,0:T(8,128)(2,1)}), bf16[16,24,2048]{2,1,0:T(8,128)(2,1)S(1)}, u32[]{:S(2)}, u32[]{:S(2)}) %all-to-all-start.5) | async-done | bytes 1572896 | tf_op jit(solution)/shard_map/all_to_all | solution.py:268
  218.2 0.0 copy-start.1
  218.2 1.2 copy-done.1
  219.4 3.9 %combine_second.1 = (bf16[128,2048]{1,0:T(8,128)(2,1)}, f32[128,4]{1,0:T(8,128)}) custom-call(s32[128,4]{1,0:T(8,128)} %get-tuple-element.10.slots_ref, f32[128,4]{1,0:T(8,128)} %copy.22.weights_ref, bf16[384,2048]{1,0:T(8,128)(2,1)} %bitcast.10, bf16[128,2048]{1,0:T(8,128)(2,1)} %grad_ref.3, f32[128,2048]{1,0:T(8,128)} %get-tuple-element.16.refs_0_, ...), custom_call_target="tpu_custom_call" | custom-call | flops 603979776 | bytes 3145728 | tf_op jit(solution)/shard_map/combine_second/pallas_call | solution.py:355
  223.3 1.5 copy.23
  (2 shorter events, 0.0 us)
Async XLA Ops:
  1.9 13.7 %all-to-all-start = ((s32[16,1,128]{2,1,0:T(1,128)}), s32[16,1,128]{2,1,0:T(1,128)S(1)}, u32[]{:S(2)}, u32[]{:S(2)}) async-start(s32[16,1,128]{2,1,0:T(1,128)} %broadcast_in_dim.10), calls=%async_computation | async-start | bytes 16384 | tf_op jit(solution)/shard_map/all_to_all | solution.py:268
  15.6 0.6 copy-start.5
  19.1 3.8 %copy-start.6 = (s32[128,4]{0,1:T(4,128)S(1)}, s32[128,4]{0,1:T(4,128)}, u32[]{:S(2)}) copy-start(s32[128,4]{0,1:T(4,128)} %param.13) | copy-start | bytes 6148
  19.1 4.5 %copy-start.7 = (s32[128,16]{0,1:T(8,128)S(1)}, s32[128,16]{0,1:T(8,128)}, u32[]{:S(2)}) copy-start(s32[128,16]{0,1:T(8,128)} %param.11) | copy-start | bytes 24580
  19.1 26.7 %all-to-all-start.1 = ((bf16[16,16,2048]{2,1,0:T(8,128)(2,1)}), bf16[16,16,2048]{2,1,0:T(8,128)(2,1)S(1)}, u32[]{:S(2)}, u32[]{:S(2)}) async-start(bf16[16,16,2048]{2,1,0:T(8,128)(2,1)} %bitcast.9), calls=%async_computation.1 | async-start | bytes 2097152 | tf_op jit(solution)/shard_map/all_to_all | solution.py:268
  45.8 1.0 copy-start.4
  96.6 37.0 %all-to-all-start.3 = ((bf16[16,24,2048]{2,1,0:T(8,128)(2,1)}), bf16[16,24,2048]{2,1,0:T(8,128)(2,1)S(1)}, u32[]{:S(2)}, u32[]{:S(2)}) async-start(bf16[16,24,2048]{2,1,0:T(8,128)(2,1)} %bitcast.11), calls=%async_computation.3 | async-start | bytes 3145728 | tf_op jit(solution)/shard_map/all_to_all | solution.py:268
  133.6 1.1 copy-start.3
  134.7 41.1 %all-to-all-start.4 = ((bf16[16,24,2048]{2,1,0:T(8,128)(2,1)}), bf16[16,24,2048]{2,1,0:T(8,128)(2,1)S(1)}, u32[]{:S(2)}, u32[]{:S(2)}) async-start(bf16[16,24,2048]{2,1,0:T(8,128)(2,1)} %experts_first.1), calls=%async_computation.4 | async-start | bytes 3145728 | tf_op jit(solution)/shard_map/all_to_all | solution.py:268
  158.1 1.1 copy-start
  175.8 1.2 copy-start.2
  177.0 9.2 %copy-start.8 = (f32[128,4]{0,1:T(4,128)S(1)}, f32[128,4]{0,1:T(4,128)}, u32[]{:S(2)}) copy-start(f32[128,4]{0,1:T(4,128)} %param.14) | copy-start | bytes 6148
  177.0 41.2 %all-to-all-start.5 = ((bf16[16,24,2048]{2,1,0:T(8,128)(2,1)}), bf16[16,24,2048]{2,1,0:T(8,128)(2,1)S(1)}, u32[]{:S(2)}, u32[]{:S(2)}) async-start(bf16[16,24,2048]{2,1,0:T(8,128)(2,1)} %after_first.1), calls=%async_computation.5 | async-start | bytes 3145728 | tf_op jit(solution)/shard_map/all_to_all | solution.py:268
  218.2 1.2 copy-start.1

commit v4 on v3

--- a/solution.py
+++ b/solution.py
@@ -51,61 +51,88 @@
     out_ref[...] = dot(jnp.concatenate(picks, axis=0), table_ref[...]).astype(BF16)
 
 
+def turned(rows):
+    count, length = rows.shape
+    return jnp.concatenate([rows, jnp.zeros((length - count, length), F32)], axis=0).T
+
+
 def plan_kernel(
-    me_ref, rows_ref, across_ref, ids_ref, _, put_ref, first_ref, second_ref, slots_ref
+    me_ref,
+    rows_ref,
+    small_ref,
+    other_ref,
+    scales_ref,
+    _,
+    put_ref,
+    near_ref,
+    far_first_ref,
+    far_second_ref,
+    near_slots_ref,
+    far_slots_ref,
+    columns_ref,
 ):
     tok_rows = rows_ref.shape[1]
     slots = put_ref.shape[1]
-    flip = me_ref[0] % 2
-    held = me_ref[1]
-    owners = me_ref[2]
-    device_count = first_ref.shape[0] // PAIR
+    half = near_ref.shape[0] // (2 * PAIR)
+    device_count = 2 * half
     exp_dev = EXPERTS // device_count
     look_cap = slots // device_count
+    me, held = me_ref[0], me_ref[1]
+    flip = me % 2
+    start = me // half * half * exp_dev
     before = earlier(tok_rows)
 
     row = jnp.broadcast_to(rows_ref[...], (device_count, tok_rows))
     low = iota((device_count, tok_rows), 0) * held
-    hit = (row >= low) & (row < low + held) & (low < owners * held)
+    hit = (row >= low) & (row < low + held)
     rank = jnp.where(hit, dot(flags(hit), before).astype(jnp.int32), -1)
     slot = iota((look_cap, tok_rows), 0)
     put = [(slot == rank[o : o + 1]).astype(F32) for o in range(device_count)]
     put_ref[...] = jnp.concatenate(put, axis=0).T.astype(BF16)
 
-    expert = iota((EXPERTS, tok_rows), 0)
-    hit = functools.reduce(
-        jnp.logical_or, [across_ref[k : k + 1, :] == expert for k in range(TOP)]
-    )
-    rank = jnp.where(hit, dot(flags(hit), before).astype(jnp.int32), -1000)
+    expert = iota((half * exp_dev, tok_rows), 0) + start
     place = iota((PAIR, tok_rows), 0)
-    for chunk, ref in enumerate((first_ref, second_ref)):
-        lines = []
-        for d in range(device_count):
-            at = d * exp_dev + 2 * chunk
-            one, two = rank[at : at + 1], rank[at + 1 : at + 2]
-            upper = jnp.where(flip == 0, one, two)
-            lower = jnp.where(flip == 0, two, one) + CAP
-            here = ((place < CAP) & (place == upper)) | ((place >= CAP) & (place == lower))
-            lines.append(here.astype(F32))
-        ref[...] = jnp.concatenate(lines, axis=0).astype(BF16)
-
-    expert = iota((tok_rows, EXPERTS), 1)
-    chosen = [ids_ref[:, k : k + 1] == expert for k in range(TOP)]
-    counted = dot(earlier(tok_rows).T, flags(functools.reduce(jnp.logical_or, chosen)))
-    shift = exp_dev.bit_length() - 1
-    for k in range(TOP):
-        ids = ids_ref[:, k : k + 1]
-        nth = jnp.sum(jnp.where(chosen[k], counted, 0.0), axis=1, keepdims=True).astype(jnp.int32)
-        inside = ids & (exp_dev - 1)
-        slots_ref[:, k : k + 1] = (
-            (inside >> 1) * (device_count * PAIR)
-            + (ids >> shift) * PAIR
-            + ((flip + inside) & 1) * CAP
-            + nth
+    inside = iota((half * exp_dev, tok_rows), 0)
+    flipped = ((inside + flip) & 1) * CAP
+    device = inside // exp_dev
+    chunk = (inside % exp_dev) // 2
+    for far, ref in enumerate((small_ref, other_ref)):
+        ids = [ref[k : k + 1, :].astype(jnp.int32) for k in range(TOP)]
+        chosen = [ids[k] == expert for k in range(TOP)]
+        hit = functools.reduce(jnp.logical_or, chosen)
+        rank = jnp.where(hit, dot(flags(hit), before).astype(jnp.int32), -1000)
+        lines = [[], []]
+        for d in range(half):
+            for c in range(2):
+                at = d * exp_dev + 2 * c
+                one, two = rank[at : at + 1], rank[at + 1 : at + 2]
+                upper = jnp.where(flip == 0, one, two)
+                lower = jnp.where(flip == 0, two, one) + CAP
+                here = ((place < CAP) & (place == upper)) | ((place >= CAP) & (place == lower))
+                lines[c].append(here.astype(F32))
+        if far:
+            far_first_ref[...] = jnp.concatenate(lines[0], axis=0).astype(BF16)
+            far_second_ref[...] = jnp.concatenate(lines[1], axis=0).astype(BF16)
+            slot = chunk * (half * PAIR) + device * PAIR + flipped + rank
+        else:
+            both = [line for pair in zip(*lines) for line in pair]
+            near_ref[...] = jnp.concatenate(both, axis=0).astype(BF16)
+            slot = device * (2 * PAIR) + chunk * PAIR + flipped + rank
+        found = [
+            jnp.sum(jnp.where(chosen[k], slot + 1, 0), axis=0, keepdims=True) - 1
+            for k in range(TOP)
+        ]
+        slots_out = far_slots_ref if far else near_slots_ref
+        found = turned(jnp.concatenate(found, axis=0).astype(F32))
+        slots_out[...] = found.astype(jnp.int32)
+    columns_ref[...] = turned(
+        jnp.concatenate(
+            [small_ref[TOP:, :], other_ref[TOP:, :], scales_ref[...]], axis=0
         )
-
-
-def state_kernel(put_ref, pick_ref, returned_ref, values_ref, scales_ref, state_ref, out_ref):
+    )
+
+
+def state_kernel(put_ref, pick_ref, returned_ref, values_ref, columns_ref, state_ref, out_ref):
     features = values_ref.shape[1]
     width = 512
     for left in range(0, features, width):
@@ -114,7 +141,7 @@
             at = left + b * BLOCK
             scaled = (
                 values_ref[:, at : at + BLOCK].astype(F32)
-                * scales_ref[:, at // BLOCK : at // BLOCK + 1]
+                * columns_ref[:, 2 * TOP + at // BLOCK : 2 * TOP + at // BLOCK + 1]
             )
             state_ref[:, at : at + BLOCK] = (
                 scaled + found[:, b * BLOCK : (b + 1) * BLOCK]
@@ -131,23 +158,14 @@
         out_ref[:, cols] = dot(pick_ref[...], state_ref[:, cols]).astype(BF16)
 
 
-def expert_kernel(
-    first_held,
-    arrived_ref,
-    wg_hbm,
-    wu_hbm,
-    wd_hbm,
-    out_ref,
-    x_ref,
-    wg_ref,
-    wu_ref,
-    wd_ref,
-    hidden_ref,
-    result_ref,
-    sem,
-):
+def expert_kernel(chunk, near_ref, far_ref, *refs):
+    if chunk:
+        early_ref, refs = refs[0], refs[1:]
+    wg_hbm, wu_hbm, wd_hbm, near_out_ref, far_out_ref = refs[:5]
+    x_ref, wg_ref, wu_ref, wd_ref, hidden_ref, result_ref, sem = refs[5:]
     count, features, width = wg_ref.shape
-    device_count = arrived_ref.shape[0]
+    half = far_ref.shape[0]
+    first_held = count * chunk
     up_cuts = ((0, 512), (512, 512), (1024, width - 1024))
     down_cuts = tuple((at, 512) for at in range(0, features, 512))
 
@@ -169,12 +187,17 @@
             copy.start()
 
     low = iota((PAIR, features), 0) < CAP
-    for quad in range(device_count // 4):
+    for quad in range(half // 2):
         ones, twos = [], []
         for pair in range(2):
             source = 4 * quad + 2 * pair
-            even = arrived_ref[source].astype(F32)
-            odd = arrived_ref[source + 1].astype(F32)
+            if source < half:
+                rows = slice(chunk * PAIR, (chunk + 1) * PAIR)
+                even = near_ref[source, rows, :].astype(F32)
+                odd = near_ref[source + 1, rows, :].astype(F32)
+            else:
+                even = far_ref[source - half].astype(F32)
+                odd = far_ref[source + 1 - half].astype(F32)
             ones.append(jnp.where(low, even, odd))
             twos.append(jnp.where(low, odd, even))
         rows = slice(quad * 2 * PAIR, (quad + 1) * 2 * PAIR)
@@ -198,25 +221,39 @@
             n += 1
             result_ref[j, :, at : at + size] = dot(hidden_ref[...], wd_ref[j, :, at : at + size])
 
-    for pair in range(device_count // 2):
+    for pair in range(half):
         one = result_ref[0, pair * PAIR : (pair + 1) * PAIR, :]
         two = result_ref[1, pair * PAIR : (pair + 1) * PAIR, :]
-        out_ref[2 * pair] = jnp.where(low, one, two).astype(BF16)
-        out_ref[2 * pair + 1] = jnp.where(low, two, one).astype(BF16)
-
-
-def expert_call(first_held, arrived, w_gate, w_up, w_down):
+        even = jnp.where(low, one, two)
+        odd = jnp.where(low, two, one)
+        source = 2 * pair
+        if source >= half:
+            far_out_ref[source - half] = even.astype(BF16)
+            far_out_ref[source + 1 - half] = odd.astype(BF16)
+        elif chunk:
+            for n, value in enumerate((even, odd)):
+                both = jnp.concatenate([early_ref[source + n].astype(F32), value], axis=0)
+                near_out_ref[source + n] = both.astype(BF16)
+        else:
+            near_out_ref[source] = even.astype(BF16)
+            near_out_ref[source + 1] = odd.astype(BF16)
+
+
+def expert_call(chunk, near, far, early, w_gate, w_up, w_down):
     exp_dev, features, width = w_gate.shape
-    device_count = arrived.shape[0]
+    half = far.shape[0]
     count = 2
-    rows = device_count * CAP
+    rows = 2 * half * CAP
     anywhere = pl.BlockSpec(memory_space=pl.ANY)
     vmem = pl.BlockSpec(memory_space=VMEM)
     return pl.pallas_call(
-        functools.partial(expert_kernel, first_held),
-        out_shape=jax.ShapeDtypeStruct((device_count, PAIR, features), BF16),
-        in_specs=[vmem] + [anywhere] * 3,
-        out_specs=vmem,
+        functools.partial(expert_kernel, chunk),
+        out_shape=(
+            jax.ShapeDtypeStruct((half, (1 + chunk) * PAIR, features), BF16),
+            jax.ShapeDtypeStruct((half, PAIR, features), BF16),
+        ),
+        in_specs=[vmem] * (2 + len(early)) + [anywhere] * 3,
+        out_specs=(vmem, vmem),
         scratch_shapes=[
             VMEM((count, rows, features), BF16),
             VMEM((count, features, width), BF16),
@@ -226,46 +263,69 @@
             VMEM((count, rows, features), F32),
             pltpu.SemaphoreType.DMA((count, 10)),
         ],
-        compiler_params=pltpu.CompilerParams(vmem_limit_bytes=52 * 1024 * 1024),
+        compiler_params=pltpu.CompilerParams(vmem_limit_bytes=54 * 1024 * 1024),
         cost_estimate=pl.CostEstimate(
             flops=6 * count * rows * features * width,
             bytes_accessed=6 * count * features * width,
             transcendentals=count * rows * width,
         ),
-        name="experts_second" if first_held else "experts_first",
-    )(arrived, w_gate, w_up, w_down)
-
-
-def combine_kernel(chunk, slots_ref, weights_ref, back_ref, grad_ref, *refs):
-    sums = refs[:2] if chunk else None
-    mixed_ref, grads_ref = refs[-2:]
+        name="experts_second" if chunk else "experts_first",
+    )(near, far, *early, w_gate, w_up, w_down)
+
+
+def mix(slots_ref, columns_ref, first_column, parts, grad_ref, mixed_ref, far_ref):
     tok_rows, features = grad_ref.shape
-    half = back_ref.shape[0]
-    column = iota((tok_rows, half), 1) + chunk * half
-    inner = lax.dot_general(
-        grad_ref[...], back_ref[...], (((1,), (1,)), ((), ())), preferred_element_type=F32
-    )
-    total = jnp.zeros((tok_rows, half), F32)
-    for k in range(TOP):
-        here = column == slots_ref[:, k : k + 1]
-        total = total + jnp.where(here, weights_ref[:, k : k + 1], 0.0)
-        value = jnp.sum(jnp.where(here, inner, 0.0), axis=1, keepdims=True)
-        if chunk:
-            value = value + sums[1][:, k : k + 1]
-        grads_ref[:, k : k + 1] = value
-    high = total.astype(BF16)
-    rest = (total - high.astype(F32)).astype(BF16)
+    picked = [jnp.zeros((tok_rows, 1), F32) for _ in range(TOP)]
+    spread = []
+    start = 0
+    for ref in parts:
+        count = ref.shape[0]
+        column = iota((tok_rows, count), 1) + start
+        start += count
+        inner = lax.dot_general(
+            grad_ref[...], ref[...], (((1,), (1,)), ((), ())), preferred_element_type=F32
+        )
+        total = jnp.zeros((tok_rows, count), F32)
+        for k in range(TOP):
+            here = column == slots_ref[:, k : k + 1]
+            weight = columns_ref[:, first_column + k : first_column + k + 1]
+            total = total + jnp.where(here, weight, 0.0)
+            picked[k] = picked[k] + jnp.sum(jnp.where(here, inner, 0.0), axis=1, keepdims=True)
+        high = total.astype(BF16)
+        spread.append((high, (total - high.astype(F32)).astype(BF16)))
     width = 512
     for at in range(0, features, width):
-        rows = back_ref[:, at : at + width]
-        value = dot(high, rows) + dot(rest, rows)
-        if chunk:
-            value = value + sums[0][:, at : at + width]
-        mixed_ref[:, at : at + width] = value.astype(mixed_ref.dtype)
-
-
-def swap(array):
-    return lax.all_to_all(array, "expert", split_axis=0, concat_axis=0, tiled=True)
+        cols = slice(at, at + width)
+        value = 0.0 if far_ref is None else far_ref[:, cols].astype(F32)
+        for (high, rest), ref in zip(spread, parts):
+            rows = ref[:, cols]
+            value = value + dot(high, rows) + dot(rest, rows)
+        mixed_ref[:, cols] = value.astype(BF16)
+    column = iota((tok_rows, tok_rows), 1)
+    wide = jnp.zeros((tok_rows, tok_rows), F32)
+    for k in range(TOP):
+        wide = wide + jnp.where(column == k, picked[k], 0.0)
+    return wide.T
+
+
+def far_kernel(slots_ref, columns_ref, first_ref, second_ref, grad_ref, mixed_ref, grads_ref):
+    turned_grads = mix(
+        slots_ref, columns_ref, TOP, (first_ref, second_ref), grad_ref, mixed_ref, None
+    )
+    grads_ref[...] = turned_grads[: grads_ref.shape[0], :]
+
+
+def near_kernel(
+    slots_ref, columns_ref, back_ref, grad_ref, far_ref, far_grads_ref, mixed_ref, grads_ref
+):
+    turned_grads = mix(slots_ref, columns_ref, 0, (back_ref,), grad_ref, mixed_ref, far_ref)
+    grads_ref[...] = turned_grads[:TOP, :] + far_grads_ref[:TOP, :]
+
+
+def swap(array, groups=None):
+    return lax.all_to_all(
+        array, "expert", split_axis=0, concat_axis=0, tiled=True, axis_index_groups=groups
+    )
 
 
 def near_path(
@@ -281,19 +341,47 @@
     out_grad,
 ):
     device_count = lax.axis_size("expert")
+    half = device_count // 2
+    halves = [list(range(half)), list(range(half, device_count))]
     me = lax.axis_index("expert").astype(jnp.int32)
     tok_rows, features = block_values.shape
     rows_held = table.shape[0]
     look_cap = max(2, 2 * tok_rows // device_count)
-    slots = device_count * PAIR
+    near_slots, far_slots = half * 2 * PAIR, half * PAIR
     vmem = pl.BlockSpec(memory_space=VMEM)
     smem = pl.BlockSpec(memory_space=pltpu.SMEM)
     anywhere = pl.BlockSpec(memory_space=pl.ANY)
-    place = jnp.stack([me, jnp.int32(rows_held), jnp.int32(device_count)])
+    place = jnp.stack([me, jnp.int32(rows_held)])
 
     def shape(dims, kind):
         return jax.ShapeDtypeStruct(dims, kind)
 
+    def mirrored(array):
+        pairs = [(i, (i + half) % device_count) for i in range(device_count)]
+        return lax.ppermute(array, "expert", pairs)
+
+    def ordered(array, earlier_array):
+        return pl.pallas_call(
+            lambda array_ref, earlier_ref, out_ref: None,
+            out_shape=shape(array.shape, array.dtype),
+            in_specs=[anywhere, anywhere],
+            out_specs=anywhere,
+            input_output_aliases={0: 0},
+            name="ordered",
+        )(array, earlier_array)
+
+    def picked(pick, states, earlier_array, name):
+        return pl.pallas_call(
+            pick_kernel,
+            out_shape=shape((pick.shape[0], features), BF16),
+            in_specs=[vmem, vmem, anywhere],
+            out_specs=vmem,
+            name=name,
+        )(pick, states, earlier_array)
+
+    small = jnp.concatenate([expert_ids.T.astype(F32), gate_weights.T], axis=0)
+    other = mirrored(small)
+    other_grad = mirrored(out_grad)
     all_rows = swap(jnp.broadcast_to(row_ids[None, None, :], (device_count, 1, tok_rows)))
     fetched = pl.pallas_call(
         fetch_kernel,
@@ -303,72 +391,70 @@
         name="fetch_rows",
     )(place, all_rows, table)
     returned = swap(fetched.reshape(device_count, look_cap, features))
-    put, first_pick, second_pick, slot_of = pl.pallas_call(
+    put, near_pick, far_first_pick, far_second_pick, near_of, far_of, columns = pl.pallas_call(
         plan_kernel,
         out_shape=(
             shape((tok_rows, device_count * look_cap), BF16),
-            shape((slots, tok_rows), BF16),
-            shape((slots, tok_rows), BF16),
-            shape((tok_rows, TOP), jnp.int32),
+            shape((near_slots, tok_rows), BF16),
+            shape((far_slots, tok_rows), BF16),
+            shape((far_slots, tok_rows), BF16),
+            shape((tok_rows, tok_rows), jnp.int32),
+            shape((tok_rows, tok_rows), jnp.int32),
+            shape((tok_rows, tok_rows), F32),
         ),
-        in_specs=[smem, vmem, vmem, vmem, anywhere],
-        out_specs=(vmem, vmem, vmem, vmem),
+        in_specs=[smem, vmem, vmem, vmem, vmem, anywhere],
+        out_specs=(vmem,) * 7,
         name="plan",
-    )(place, row_ids[None, :], expert_ids.T, expert_ids, fetched)
-    state, first_sent = pl.pallas_call(
+    )(place, row_ids[None, :], small, other, jnp.exp2(block_exps.T.astype(F32)), fetched)
+    state, near_sent = pl.pallas_call(
         state_kernel,
-        out_shape=(shape((tok_rows, features), BF16), shape((slots, features), BF16)),
+        out_shape=(shape((tok_rows, features), BF16), shape((near_slots, features), BF16)),
         in_specs=[vmem] * 5,
         out_specs=(vmem, vmem),
         name="token_state",
+    )(put, near_pick, returned.reshape(device_count * look_cap, features), block_values, columns)
+    other_state = mirrored(state)
+    near_rows = swap(near_sent.reshape(half, 2 * PAIR, features), halves)
+    far_sent = picked(far_first_pick, other_state, near_rows, "far_first")
+    far_rows = swap(far_sent.reshape(half, PAIR, features), halves)
+    far_later_sent = picked(far_second_pick, other_state, far_rows, "far_second")
+    far_later_rows = swap(far_later_sent.reshape(half, PAIR, features), halves)
+
+    weights = (w_gate, w_up, w_down)
+    near_out, far_out = expert_call(0, near_rows, far_rows, (), *weights)
+    far_back = swap(far_out, halves)
+    near_out, far_later_out = expert_call(1, near_rows, far_later_rows, (near_out,), *weights)
+    far_later_back = swap(ordered(far_later_out, far_back), halves)
+    near_back = swap(ordered(near_out, far_later_back), halves)
+
+    far_mixed, far_grads = pl.pallas_call(
+        far_kernel,
+        out_shape=(shape((tok_rows, features), BF16), shape((2 * TOP, tok_rows), F32)),
+        in_specs=[vmem] * 5,
+        out_specs=(vmem, vmem),
+        name="mix_far",
     )(
-        put,
-        first_pick,
-        returned.reshape(device_count * look_cap, features),
-        block_values,
-        jnp.exp2(block_exps.astype(F32)),
-    )
-    first_rows = swap(first_sent.reshape(device_count, PAIR, features))
-    second_sent = pl.pallas_call(
-        pick_kernel,
-        out_shape=shape((slots, features), BF16),
-        in_specs=[vmem, vmem, anywhere],
-        out_specs=vmem,
-        name="second_slots",
-    )(second_pick, state, first_rows)
-    second_rows = swap(second_sent.reshape(device_count, PAIR, features))
-    first_out = expert_call(0, first_rows, w_gate, w_up, w_down)
-    first_back = swap(first_out)
-    second_out = expert_call(2, second_rows, w_gate, w_up, w_down)
-    second_back = swap(
-        pl.pallas_call(
-            lambda second_ref, first_ref, out_ref: None,
-            out_shape=shape(second_out.shape, BF16),
-            in_specs=[anywhere, anywhere],
-            out_specs=anywhere,
-            input_output_aliases={0: 0},
-            name="after_first",
-        )(second_out, first_back)
-    )
-
-    def combine(chunk, back, *sums):
-        return pl.pallas_call(
-            functools.partial(combine_kernel, chunk),
-            out_shape=(
-                shape((tok_rows, features), BF16 if chunk else F32),
-                shape((tok_rows, TOP), F32),
-            ),
-            in_specs=[vmem] * (4 + len(sums)),
-            out_specs=(vmem, vmem),
-            cost_estimate=pl.CostEstimate(
-                flops=6 * tok_rows * slots * features,
-                bytes_accessed=4 * slots * features,
-                transcendentals=0,
-            ),
-            name="combine_second" if chunk else "combine_first",
-        )(slot_of, gate_weights, back.reshape(slots, features), out_grad, *sums)
-
-    return combine(1, second_back, *combine(0, first_back))
+        far_of,
+        columns,
+        far_back.reshape(far_slots, features),
+        far_later_back.reshape(far_slots, features),
+        other_grad,
+    )
+    mixed, grads = pl.pallas_call(
+        near_kernel,
+        out_shape=(shape((tok_rows, features), BF16), shape((TOP, tok_rows), F32)),
+        in_specs=[vmem] * 6,
+        out_specs=(vmem, vmem),
+        name="mix_near",
+    )(
+        near_of,
+        columns,
+        near_back.reshape(near_slots, features),
+        out_grad,
+        mirrored(far_mixed),
+        mirrored(far_grads),
+    )
+    return mixed, grads.T
 
 
 def expert_work(arrived, w_gate, w_up, w_down):

time: 229 us -> 240 us (1.048); the launches traced: 225 us -> 239 us
  waiting for transfers between devices: 85.5 us -> 110 us
  blocking collectives: 43 us -> 32 us
  local copies, waits for them, and re-layouts: 11.1 us -> 7.65 us
  Pallas kernels: 49.2 us -> 52.4 us
    ppermute x0 -> x5, waiting for transfers between devices: none -> 102 us  [mirrored(): return lax.ppermute(array, 'expert', pairs)]
    all_to_all x5 -> x6, waiting for transfers between devices: 85.5 us -> 7.84 us  [swap(): lax.all_to_all(array, 'expert', split_axis=0, concat_axis=0, tiled=True,...]
    all_to_all x1 -> x2, blocking collectives: 43 us -> 32 us  [swap(): lax.all_to_all(array, 'expert', split_axis=0, concat_axis=0, tiled=True,...]
    ppermute x0 -> x5, starting transfers between devices: none -> 8.42 us  [mirrored(): return lax.ppermute(array, 'expert', pairs)]
    all_to_all x5 -> x6, starting transfers between devices: 34.5 us -> 26.5 us  [swap(): lax.all_to_all(array, 'expert', split_axis=0, concat_axis=0, tiled=True,...]
    pallas_call x6 -> x8, Pallas kernels: 40.2 us -> 43.7 us  [the longest x2 31.6 us: expert_call(): pl.pallas_call(functools.partial(expert_kernel, chunk), out_shape=(jax.Sh...]
    unnamed x20 -> x34, local copies, waits for them, and re-layouts: 7.67 us -> 6.39 us
  transfers between devices with their start and end apart: 5 -> 11, of which waited for: 5 -> 6; matrix products, arithmetic and copies ran while one was open for 1% -> 1% of each run, Pallas kernels for 16% -> 16%
where the time goes in v4:
time: 240 us; the launch traced here: 239 us
  waiting for transfers between devices  110 us (46%)
  Pallas kernels  52.4 us (22%)
  starting transfers between devices  34.9 us (15%)
  blocking collectives  32 us (13%)
  local copies, waits for them, and re-layouts  7.65 us (3%)
    ppermute x5, waiting for transfers between devices, mirrored(): return lax.ppermute(array, 'expert', pairs)  102 us
    all_to_all x2, blocking collectives, swap(): lax.all_to_all(array, 'expert', split_axis=0, concat_axis=0, tiled=True,...  32 us
    pallas_call x2, Pallas kernels, expert_call(): pl.pallas_call(functools.partial(expert_kernel, chunk), out_shape=(jax.Sh...  31.6 us
    all_to_all x6, starting transfers between devices, swap(): lax.all_to_all(array, 'expert', split_axis=0, concat_axis=0, tiled=True,...  26.5 us
    ppermute x5, starting transfers between devices, mirrored(): return lax.ppermute(array, 'expert', pairs)  8.42 us
    all_to_all x6, waiting for transfers between devices, swap(): lax.all_to_all(array, 'expert', split_axis=0, concat_axis=0, tiled=True,...  7.84 us
    unnamed x34, local copies, waits for them, and re-layouts  6.39 us
  transfers between devices with their start and end apart: 11, of which 6 were waited for; matrix products, arithmetic and copies ran while one was open for 1% of the time, Pallas kernels for 16%

profile of v4, /device:TPU:0, one launch (start us, length us, event | category | flops | bytes accessed | tf_op | source)
XLA Modules:
  0.0 239.2 jit_solution(2063662244246715528)
XLA Ops:
  0.6 1.3 broadcast_in_dim.10
  1.9 7.4 %all-to-all-start = ((s32[16,1,128]{2,1,0:T(1,128)}), s32[16,1,128]{2,1,0:T(1,128)S(1)}, u32[]{:S(2)}, u32[]{:S(2)}) async-start(s32[16,1,128]{2,1,0:T(1,128)} %broadcast_in_dim.10), calls=%async_computation | async-start | bytes 16384 | tf_op jit(solution)/shard_map/all_to_all | solution.py:326
  9.3 0.6 pad_add_fusion.me_ref
  9.9 5.7 %all-to-all-done.rows_ref = s32[16,1,128]{2,1,0:T(1,128)S(1)} async-done(((s32[16,1,128]{2,1,0:T(1,128)}), s32[16,1,128]{2,1,0:T(1,128)S(1)}, u32[]{:S(2)}, u32[]{:S(2)}) %all-to-all-start) | async-done | bytes 8224 | tf_op jit(solution)/shard_map/all_to_all | solution.py:326
  15.6 0.6 copy-done.9
  16.2 2.9 %fetch_rows.1._ = bf16[256,2048]{1,0:T(8,128)(2,1)} custom-call(s32[2]{0:T(128)} %pad_add_fusion.me_ref, s32[16,1,128]{2,1,0:T(1,128)} %copy-done.9, bf16[256,2048]{1,0:T(8,128)(2,1)} %table_ref.1), custom_call_target="tpu_custom_call" | custom-call | tf_op jit(solution)/shard_map/fetch_rows/pallas_call | solution.py:386
  19.1 3.8 %all-to-all-start.1 = ((bf16[16,16,2048]{2,1,0:T(8,128)(2,1)}), bf16[16,16,2048]{2,1,0:T(8,128)(2,1)S(1)}, u32[]{:S(2)}, u32[]{:S(2)}) async-start(bf16[16,16,2048]{2,1,0:T(8,128)(2,1)} %bitcast.16), calls=%async_computation.1 | async-start | bytes 2097152 | tf_op jit(solution)/shard_map/all_to_all | solution.py:326
  23.0 2.8 %collective-permute-start = (f32[8,128]{1,0:T(8,128)S(1)}, f32[8,128]{1,0:T(8,128)S(1)}, u32[]{:S(2)}, u32[]{:S(2)}) collective-permute-start(f32[8,128]{1,0:T(8,128)S(1)} %pad_maximum_fusion.small_ref), channel_id=1, source_target_pairs={{0,8},{1,9},{2,10},{3,11},{4,12},{5,13},{6,14},{7,15},{8,0},{9,1},... | collective-permute-start | bytes 12296 | tf_op jit(solution)/shard_map/ppermute | solution.py:361
  25.8 0.0 copy-done.11
  25.8 0.6 exponential_bitcast_fusion.scales_ref
  26.4 23.2 %collective-permute-done.other_ref = f32[8,128]{1,0:T(8,128)S(1)} collective-permute-done((f32[8,128]{1,0:T(8,128)S(1)}, f32[8,128]{1,0:T(8,128)S(1)}, u32[]{:S(2)}, u32[]{:S(2)}) %collective-permute-start) | collective-permute-done | bytes 4128 | tf_op jit(solution)/shard_map/ppermute | solution.py:361
  49.6 0.0 copy-done.10
  49.6 0.6 copy-done.13
  50.1 1.8 plan.1
  51.9 0.0 all-to-all-done.1
  52.0 1.0 copy-done.3
  52.9 4.0 %token_state.1 = (bf16[128,2048]{1,0:T(8,128)(2,1)}, bf16[384,2048]{1,0:T(8,128)(2,1)}) custom-call(bf16[128,256]{1,0:T(8,128)(2,1)} %get-tuple-element.21.put_ref, bf16[384,128]{1,0:T(8,128)(2,1)} %get-tuple-element.22.pick_ref, bf16[256,2048]{1,0:T(8,128)(2,1)} %bitcast.20, bf16[128,2048]{1,0:T(8,128)(2,1)} %values_ref.1, ...), custom_call_target="tpu_custom_call" | custom-call | tf_op jit(solution)/shard_map/token_state/pallas_call | solution.py:409
  56.9 3.7 %all-to-all-start.2 = ((bf16[8,48,2048]{2,1,0:T(8,128)(2,1)}), bf16[8,48,2048]{2,1,0:T(8,128)(2,1)S(1)}, u32[]{:S(2)}, u32[]{:S(2)}) async-start(bf16[8,48,2048]{2,1,0:T(8,128)(2,1)} %bitcast.23), calls=%async_computation.2 | async-start | bytes 3145728 | tf_op jit(solution)/shard_map/all_to_all | solution.py:326
  60.7 0.0 copy-done.16
  60.7 0.7 collective-permute-start.1
  61.3 28.5 %collective-permute-done.1.state_ref = bf16[128,2048]{1,0:T(8,128)(2,1)S(1)} collective-permute-done((bf16[128,2048]{1,0:T(8,128)(2,1)S(1)}, bf16[128,2048]{1,0:T(8,128)(2,1)S(1)}, u32[]{:S(2)}, u32[]{:S(2)}) %collective-permute-start.1) | collective-permute-done | bytes 524320 | tf_op jit(solution)/shard_map/ppermute | solution.py:361
  89.8 2.1 all-to-all-done.2._.near_ref
  91.9 1.2 copy-done
  93.1 2.3 far_first.1
  95.4 15.9 %all_to_all.40._.far_ref = bf16[8,24,2048]{2,1,0:T(8,128)(2,1)} all-to-all(bf16[8,24,2048]{2,1,0:T(8,128)(2,1)} %bitcast.22), channel_id=1, replica_groups={{0,1,2,3,4,5,6,7},{8,9,10,11,12,13,14,15},{16,17,18,19,20,21,22,23},{24..., dimensions={0} | all-to-all | bytes 1572864 | tf_op jit(solution)/shard_map/all_to_all | solution.py:326
  111.3 2.3 far_second.1
  113.6 3.5 %all-to-all-start.4 = ((bf16[8,24,2048]{2,1,0:T(8,128)(2,1)}), bf16[8,24,2048]{2,1,0:T(8,128)(2,1)S(1)}, u32[]{:S(2)}, u32[]{:S(2)}) async-start(bf16[8,24,2048]{2,1,0:T(8,128)(2,1)} %bitcast.21), calls=%async_computation.4 | async-start | bytes 1572864 | tf_op jit(solution)/shard_map/all_to_all | solution.py:326
  117.2 15.5 %experts_first.1 = (bf16[8,24,2048]{2,1,0:T(8,128)(2,1)}, bf16[8,24,2048]{2,1,0:T(8,128)(2,1)}) custom-call(bf16[8,48,2048]{2,1,0:T(8,128)(2,1)} %copy-done, bf16[8,24,2048]{2,1,0:T(8,128)(2,1)} %all_to_all.40._.far_ref, bf16[4,2048,1408]{2,1,0:T(8,128)(2,1)} %refs_1_.3, bf16[4,2048,1408]{2,1,0:T(8,128)(2,1)} %refs_2_.3, bf16[4,1408,2048]{2,1,0:T(8,128)(2,1)} %refs_3_.1), custom_call_target="tpu_custom_call" | custom-call | flops 6643777536 | bytes 34603008 | tf_op jit(solution)/shard_map/experts_first/pallas_call | solution.py:249
  132.7 0.0 all-to-all-done.4.far_ref
  132.8 4.1 %all-to-all-start.5 = ((bf16[8,24,2048]{2,1,0:T(8,128)(2,1)}), bf16[8,24,2048]{2,1,0:T(8,128)(2,1)S(1)}, u32[]{:S(2)}, u32[]{:S(2)}) async-start(bf16[8,24,2048]{2,1,0:T(8,128)(2,1)} %get-tuple-element.30), calls=%async_computation.5 | async-start | bytes 1572864 | tf_op jit(solution)/shard_map/all_to_all | solution.py:326
  136.9 16.1 %experts_second.1 = (bf16[8,48,2048]{2,1,0:T(8,128)(2,1)}, bf16[8,24,2048]{2,1,0:T(8,128)(2,1)}) custom-call(bf16[8,48,2048]{2,1,0:T(8,128)(2,1)} %copy-done, bf16[8,24,2048]{2,1,0:T(8,128)(2,1)} %copy-done.4, bf16[8,24,2048]{2,1,0:T(8,128)(2,1)} %get-tuple-element.27.refs_0_, bf16[4,2048,1408]{2,1,0:T(8,128)(2,1)} %refs_1_.3, ...), custom_call_target="tpu_custom_call" | custom-call | flops 6643777536 | bytes 34603008 | tf_op jit(solution)/shard_map/experts_second/pallas_call | solution.py:249
  153.0 0.0 all-to-all-done.5.earlier_ref
  153.0 0.9 copy-done.1
  153.9 16.0 %all_to_all.41.earlier_ref = bf16[8,24,2048]{2,1,0:T(8,128)(2,1)} all-to-all(bf16[8,24,2048]{2,1,0:T(8,128)(2,1)} %ordered.2), channel_id=1, replica_groups={{0,1,2,3,4,5,6,7},{8,9,10,11,12,13,14,15},{16,17,18,19,20,21,22,23},{24..., dimensions={0} | all-to-all | bytes 1572864 | tf_op jit(solution)/shard_map/all_to_all | solution.py:326
  169.9 3.9 %all-to-all-start.7 = ((bf16[8,48,2048]{2,1,0:T(8,128)(2,1)}), bf16[8,48,2048]{2,1,0:T(8,128)(2,1)S(1)}, u32[]{:S(2)}, u32[]{:S(2)}) async-start(bf16[8,48,2048]{2,1,0:T(8,128)(2,1)} %ordered.3), calls=%async_computation.7 | async-start | bytes 3145728 | tf_op jit(solution)/shard_map/all_to_all | solution.py:326
  173.9 1.5 collective-permute-start.2
  175.4 27.4 %collective-permute-done.2.grad_ref = bf16[128,2048]{1,0:T(8,128)(2,1)S(1)} collective-permute-done((bf16[128,2048]{1,0:T(8,128)(2,1)S(1)}, bf16[128,2048]{1,0:T(8,128)(2,1)S(1)}, u32[]{:S(2)}, u32[]{:S(2)}) %collective-permute-start.2) | collective-permute-done | bytes 524320 | tf_op jit(solution)/shard_map/ppermute | solution.py:361
  202.8 0.8 copy-done.6
  203.6 3.7 %mix_far.1 = (bf16[128,2048]{1,0:T(8,128)(2,1)}, f32[8,128]{1,0:T(8,128)}) custom-call(s32[128,128]{1,0:T(8,128)} %get-tuple-element.31.slots_ref, f32[128,128]{1,0:T(8,128)} %get-tuple-element.20.columns_ref, bf16[192,2048]{1,0:T(8,128)(2,1)} %bitcast.17, bf16[192,2048]{1,0:T(8,128)(2,1)} %bitcast.18, bf16[128,2048]{1,0:T(8,128)(2,1)} %copy-done.6), custom_call_target="tpu_custom_call" | custom-call | tf_op jit(solution)/shard_map/mix_far/pallas_call | solution.py:430
  207.2 3.4 %collective-permute-start.3 = (bf16[128,2048]{1,0:T(8,128)(2,1)}, bf16[128,2048]{1,0:T(8,128)(2,1)S(1)}, u32[]{:S(2)}, u32[]{:S(2)}) collective-permute-start(bf16[128,2048]{1,0:T(8,128)(2,1)} %get-tuple-element.32), channel_id=1, source_target_pairs={{0,8},{1,9},{2,10},{3,11},{4,12},{5,13},{6,14},{7,15},{8,0},{9,1},... | collective-permute-start | bytes 1572872 | tf_op jit(solution)/shard_map/ppermute | solution.py:361
  210.6 0.0 collective-permute-start.4
  210.7 23.4 %collective-permute-done.4.far_grads_ref = f32[8,128]{1,0:T(8,128)S(1)} collective-permute-done((f32[8,128]{1,0:T(8,128)}, f32[8,128]{1,0:T(8,128)S(1)}, u32[]{:S(2)}, u32[]{:S(2)}) %collective-permute-start.4) | collective-permute-done | bytes 4128 | tf_op jit(solution)/shard_map/ppermute | solution.py:361
  234.1 0.0 collective-permute-done.3.far_ref
  234.1 0.0 all-to-all-done.7
  234.1 0.6 copy-done.12
  234.7 0.2 copy-done.8
  234.9 0.6 copy-done.2
  235.5 3.8 %mix_near.1 = (bf16[128,2048]{1,0:T(8,128)(2,1)}, f32[4,128]{1,0:T(4,128)}) custom-call(s32[128,128]{1,0:T(8,128)} %get-tuple-element.19.slots_ref, f32[128,128]{1,0:T(8,128)} %get-tuple-element.20.columns_ref, bf16[384,2048]{1,0:T(8,128)(2,1)} %bitcast.19, bf16[128,2048]{1,0:T(8,128)(2,1)} %grad_ref.1, bf16[128,2048]{1,0:T(8,128)(2,1)} %copy-done.8, ...), custom_call_target="tpu_custom_call" | custom-call | tf_op jit(solution)/shard_map/mix_near/pallas_call | solution.py:443
  (26 shorter events, 0.1 us)
Async XLA Ops:
  1.9 13.7 %all-to-all-start = ((s32[16,1,128]{2,1,0:T(1,128)}), s32[16,1,128]{2,1,0:T(1,128)S(1)}, u32[]{:S(2)}, u32[]{:S(2)}) async-start(s32[16,1,128]{2,1,0:T(1,128)} %broadcast_in_dim.10), calls=%async_computation | async-start | bytes 16384 | tf_op jit(solution)/shard_map/all_to_all | solution.py:326
  15.6 0.6 copy-start.9
  19.1 3.8 %copy-start.14 = (s32[128,4]{0,1:T(4,128)S(1)}, s32[128,4]{0,1:T(4,128)}, u32[]{:S(2)}) copy-start(s32[128,4]{0,1:T(4,128)} %param.13) | copy-start | bytes 6148
  19.1 3.8 %copy-start.15 = (f32[128,4]{0,1:T(4,128)S(1)}, f32[128,4]{0,1:T(4,128)}, u32[]{:S(2)}) copy-start(f32[128,4]{0,1:T(4,128)} %param.14) | copy-start | bytes 6148
  19.1 6.7 %copy-start.11 = (s32[128,16]{0,1:T(8,128)S(1)}, s32[128,16]{0,1:T(8,128)}, u32[]{:S(2)}) copy-start(s32[128,16]{0,1:T(8,128)} %param.11) | copy-start | bytes 24580
  19.1 32.8 %all-to-all-start.1 = ((bf16[16,16,2048]{2,1,0:T(8,128)(2,1)}), bf16[16,16,2048]{2,1,0:T(8,128)(2,1)S(1)}, u32[]{:S(2)}, u32[]{:S(2)}) async-start(bf16[16,16,2048]{2,1,0:T(8,128)(2,1)} %bitcast.16), calls=%async_computation.1 | async-start | bytes 2097152 | tf_op jit(solution)/shard_map/all_to_all | solution.py:326
  23.0 26.6 %copy-start.10 = (f32[8,128]{1,0:T(8,128)}, f32[8,128]{1,0:T(8,128)S(1)}, u32[]{:S(2)}) copy-start(f32[8,128]{1,0:T(8,128)S(1)} %pad_maximum_fusion.small_ref) | copy-start | bytes 12292
  23.0 26.6 %collective-permute-start = (f32[8,128]{1,0:T(8,128)S(1)}, f32[8,128]{1,0:T(8,128)S(1)}, u32[]{:S(2)}, u32[]{:S(2)}) collective-permute-start(f32[8,128]{1,0:T(8,128)S(1)} %pad_maximum_fusion.small_ref), channel_id=1, source_target_pairs={{0,8},{1,9},{2,10},{3,11},{4,12},{5,13},{6,14},{7,15},{8,0},{9,1},... | collective-permute-start | bytes 12296 | tf_op jit(solution)/shard_map/ppermute | solution.py:361
  49.6 0.6 copy-start.13
  51.9 1.0 copy-start.3
  56.9 3.7 %copy-start.16 = (bf16[128,2048]{1,0:T(8,128)(2,1)S(1)}, bf16[128,2048]{1,0:T(8,128)(2,1)}, u32[]{:S(2)}) copy-start(bf16[128,2048]{1,0:T(8,128)(2,1)} %get-tuple-element.25) | copy-start | bytes 1572868
  56.9 35.0 %all-to-all-start.2 = ((bf16[8,48,2048]{2,1,0:T(8,128)(2,1)}), bf16[8,48,2048]{2,1,0:T(8,128)(2,1)S(1)}, u32[]{:S(2)}, u32[]{:S(2)}) async-start(bf16[8,48,2048]{2,1,0:T(8,128)(2,1)} %bitcast.23), calls=%async_computation.2 | async-start | bytes 3145728 | tf_op jit(solution)/shard_map/all_to_all | solution.py:326
  60.7 29.1 %collective-permute-start.1 = (bf16[128,2048]{1,0:T(8,128)(2,1)S(1)}, bf16[128,2048]{1,0:T(8,128)(2,1)S(1)}, u32[]{:S(2)}, u32[]{:S(2)}) collective-permute-start(bf16[128,2048]{1,0:T(8,128)(2,1)S(1)} %copy-done.16), channel_id=1, source_target_pairs={{0,8},{1,9},{2,10},{3,11},{4,12},{5,13},{6,14},{7,15},{8,0},{9,1},... | collective-permute-start | bytes 1572872 | tf_op jit(solution)/shard_map/ppermute | solution.py:361
  89.8 2.1 copy-start.5
  91.9 1.2 copy-start
  113.6 19.1 %all-to-all-start.4 = ((bf16[8,24,2048]{2,1,0:T(8,128)(2,1)}), bf16[8,24,2048]{2,1,0:T(8,128)(2,1)S(1)}, u32[]{:S(2)}, u32[]{:S(2)}) async-start(bf16[8,24,2048]{2,1,0:T(8,128)(2,1)} %bitcast.21), calls=%async_computation.4 | async-start | bytes 1572864 | tf_op jit(solution)/shard_map/all_to_all | solution.py:326
  132.7 4.2 %copy-start.4 = (bf16[8,24,2048]{2,1,0:T(8,128)(2,1)}, bf16[8,24,2048]{2,1,0:T(8,128)(2,1)S(1)}, u32[]{:S(2)}) copy-start(bf16[8,24,2048]{2,1,0:T(8,128)(2,1)S(1)} %all-to-all-done.4.far_ref) | copy-start | bytes 2359300
  132.8 20.3 %all-to-all-start.5 = ((bf16[8,24,2048]{2,1,0:T(8,128)(2,1)}), bf16[8,24,2048]{2,1,0:T(8,128)(2,1)S(1)}, u32[]{:S(2)}, u32[]{:S(2)}) async-start(bf16[8,24,2048]{2,1,0:T(8,128)(2,1)} %get-tuple-element.30), calls=%async_computation.5 | async-start | bytes 1572864 | tf_op jit(solution)/shard_map/all_to_all | solution.py:326
  153.0 0.9 copy-start.1
  169.9 3.9 %copy-start.7 = (bf16[128,2048]{1,0:T(8,128)(2,1)S(1)}, bf16[128,2048]{1,0:T(8,128)(2,1)}, u32[]{:S(2)}) copy-start(bf16[128,2048]{1,0:T(8,128)(2,1)} %grad_ref.1) | copy-start | bytes 1572868
  169.9 64.2 %all-to-all-start.7 = ((bf16[8,48,2048]{2,1,0:T(8,128)(2,1)}), bf16[8,48,2048]{2,1,0:T(8,128)(2,1)S(1)}, u32[]{:S(2)}, u32[]{:S(2)}) async-start(bf16[8,48,2048]{2,1,0:T(8,128)(2,1)} %ordered.3), calls=%async_computation.7 | async-start | bytes 3145728 | tf_op jit(solution)/shard_map/all_to_all | solution.py:326
  173.9 28.9 %collective-permute-start.2 = (bf16[128,2048]{1,0:T(8,128)(2,1)S(1)}, bf16[128,2048]{1,0:T(8,128)(2,1)S(1)}, u32[]{:S(2)}, u32[]{:S(2)}) collective-permute-start(bf16[128,2048]{1,0:T(8,128)(2,1)S(1)} %copy-done.7), channel_id=1, source_target_pairs={{0,8},{1,9},{2,10},{3,11},{4,12},{5,13},{6,14},{7,15},{8,0},{9,1},... | collective-permute-start | bytes 1572872 | tf_op jit(solution)/shard_map/ppermute | solution.py:361
  202.8 0.8 copy-start.6
  207.2 26.9 %collective-permute-start.3 = (bf16[128,2048]{1,0:T(8,128)(2,1)}, bf16[128,2048]{1,0:T(8,128)(2,1)S(1)}, u32[]{:S(2)}, u32[]{:S(2)}) collective-permute-start(bf16[128,2048]{1,0:T(8,128)(2,1)} %get-tuple-element.32), channel_id=1, source_target_pairs={{0,8},{1,9},{2,10},{3,11},{4,12},{5,13},{6,14},{7,15},{8,0},{9,1},... | collective-permute-start | bytes 1572872 | tf_op jit(solution)/shard_map/ppermute | solution.py:361
  210.6 23.5 %collective-permute-start.4 = (f32[8,128]{1,0:T(8,128)}, f32[8,128]{1,0:T(8,128)S(1)}, u32[]{:S(2)}, u32[]{:S(2)}) collective-permute-start(f32[8,128]{1,0:T(8,128)} %get-tuple-element.33), channel_id=1, source_target_pairs={{0,8},{1,9},{2,10},{3,11},{4,12},{5,13},{6,14},{7,15},{8,0},{9,1},... | collective-permute-start | bytes 12296 | tf_op jit(solution)/shard_map/ppermute | solution.py:361
  234.1 0.6 copy-start.12
  234.1 0.8 copy-start.8
  234.1 1.3 copy-start.2

commit v5 on v4

--- a/solution.py
+++ b/solution.py
@@ -33,7 +33,7 @@
     return flags(iota((length, length), 0) < iota((length, length), 1))
 
 
-def fetch_kernel(me_ref, rows_ref, table_ref, out_ref):
+def fetch_kernel(me_ref, rows_ref, table_ref, _, out_ref):
     device_count, _, tok_rows = rows_ref.shape
     held = table_ref.shape[0]
     look_cap = out_ref.shape[0] // device_count
@@ -65,8 +65,7 @@
     _,
     put_ref,
     near_ref,
-    far_first_ref,
-    far_second_ref,
+    far_ref,
     near_slots_ref,
     far_slots_ref,
     columns_ref,
@@ -110,13 +109,12 @@
                 lower = jnp.where(flip == 0, two, one) + CAP
                 here = ((place < CAP) & (place == upper)) | ((place >= CAP) & (place == lower))
                 lines[c].append(here.astype(F32))
+        both = [line for pair in zip(*lines) for line in pair]
+        pick_ref = far_ref if far else near_ref
+        pick_ref[...] = jnp.concatenate(both, axis=0).astype(BF16)
         if far:
-            far_first_ref[...] = jnp.concatenate(lines[0], axis=0).astype(BF16)
-            far_second_ref[...] = jnp.concatenate(lines[1], axis=0).astype(BF16)
             slot = chunk * (half * PAIR) + device * PAIR + flipped + rank
         else:
-            both = [line for pair in zip(*lines) for line in pair]
-            near_ref[...] = jnp.concatenate(both, axis=0).astype(BF16)
             slot = device * (2 * PAIR) + chunk * PAIR + flipped + rank
         found = [
             jnp.sum(jnp.where(chosen[k], slot + 1, 0), axis=0, keepdims=True) - 1
@@ -132,7 +130,7 @@
     )
 
 
-def state_kernel(put_ref, pick_ref, returned_ref, values_ref, columns_ref, state_ref, out_ref):
+def state_kernel(put_ref, returned_ref, values_ref, columns_ref, state_ref):
     features = values_ref.shape[1]
     width = 512
     for left in range(0, features, width):
@@ -146,11 +144,10 @@
             state_ref[:, at : at + BLOCK] = (
                 scaled + found[:, b * BLOCK : (b + 1) * BLOCK]
             ).astype(BF16)
-        cols = slice(left, left + width)
-        out_ref[:, cols] = dot(pick_ref[...], state_ref[:, cols]).astype(BF16)
-
-
-def pick_kernel(pick_ref, state_ref, _, out_ref):
+
+
+def pick_kernel(pick_ref, state_ref, *refs):
+    out_ref = refs[-1]
     features = state_ref.shape[1]
     width = 512
     for left in range(0, features, width):
@@ -158,13 +155,13 @@
         out_ref[:, cols] = dot(pick_ref[...], state_ref[:, cols]).astype(BF16)
 
 
-def expert_kernel(chunk, near_ref, far_ref, *refs):
-    if chunk:
+def expert_kernel(chunk, join, after, rows_ref, *refs):
+    if join:
         early_ref, refs = refs[0], refs[1:]
-    wg_hbm, wu_hbm, wd_hbm, near_out_ref, far_out_ref = refs[:5]
-    x_ref, wg_ref, wu_ref, wd_ref, hidden_ref, result_ref, sem = refs[5:]
+    wg_hbm, wu_hbm, wd_hbm, out_ref = refs[after : after + 4]
+    x_ref, wg_ref, wu_ref, wd_ref, hidden_ref, result_ref, sem = refs[after + 4 :]
     count, features, width = wg_ref.shape
-    half = far_ref.shape[0]
+    half = rows_ref.shape[0]
     first_held = count * chunk
     up_cuts = ((0, 512), (512, 512), (1024, width - 1024))
     down_cuts = tuple((at, 512) for at in range(0, features, 512))
@@ -187,17 +184,13 @@
             copy.start()
 
     low = iota((PAIR, features), 0) < CAP
-    for quad in range(half // 2):
+    here = slice(chunk * PAIR, (chunk + 1) * PAIR)
+    for quad in range(half // 4):
         ones, twos = [], []
         for pair in range(2):
             source = 4 * quad + 2 * pair
-            if source < half:
-                rows = slice(chunk * PAIR, (chunk + 1) * PAIR)
-                even = near_ref[source, rows, :].astype(F32)
-                odd = near_ref[source + 1, rows, :].astype(F32)
-            else:
-                even = far_ref[source - half].astype(F32)
-                odd = far_ref[source + 1 - half].astype(F32)
+            even = rows_ref[source, here, :].astype(F32)
+            odd = rows_ref[source + 1, here, :].astype(F32)
             ones.append(jnp.where(low, even, odd))
             twos.append(jnp.where(low, odd, even))
         rows = slice(quad * 2 * PAIR, (quad + 1) * 2 * PAIR)
@@ -221,39 +214,31 @@
             n += 1
             result_ref[j, :, at : at + size] = dot(hidden_ref[...], wd_ref[j, :, at : at + size])
 
-    for pair in range(half):
+    for pair in range(half // 2):
         one = result_ref[0, pair * PAIR : (pair + 1) * PAIR, :]
         two = result_ref[1, pair * PAIR : (pair + 1) * PAIR, :]
-        even = jnp.where(low, one, two)
-        odd = jnp.where(low, two, one)
-        source = 2 * pair
-        if source >= half:
-            far_out_ref[source - half] = even.astype(BF16)
-            far_out_ref[source + 1 - half] = odd.astype(BF16)
-        elif chunk:
-            for n, value in enumerate((even, odd)):
-                both = jnp.concatenate([early_ref[source + n].astype(F32), value], axis=0)
-                near_out_ref[source + n] = both.astype(BF16)
-        else:
-            near_out_ref[source] = even.astype(BF16)
-            near_out_ref[source + 1] = odd.astype(BF16)
-
-
-def expert_call(chunk, near, far, early, w_gate, w_up, w_down):
+        for source, value in (
+            (2 * pair, jnp.where(low, one, two)),
+            (2 * pair + 1, jnp.where(low, two, one)),
+        ):
+            if join:
+                value = jnp.concatenate([early_ref[source].astype(F32), value], axis=0)
+            out_ref[source] = value.astype(BF16)
+
+
+def expert_call(name, chunk, rows_in, weights, early=(), after=()):
+    w_gate, w_up, w_down = weights
     exp_dev, features, width = w_gate.shape
-    half = far.shape[0]
+    half = rows_in.shape[0]
     count = 2
-    rows = 2 * half * CAP
+    rows = half * CAP
     anywhere = pl.BlockSpec(memory_space=pl.ANY)
     vmem = pl.BlockSpec(memory_space=VMEM)
     return pl.pallas_call(
-        functools.partial(expert_kernel, chunk),
-        out_shape=(
-            jax.ShapeDtypeStruct((half, (1 + chunk) * PAIR, features), BF16),
-            jax.ShapeDtypeStruct((half, PAIR, features), BF16),
-        ),
-        in_specs=[vmem] * (2 + len(early)) + [anywhere] * 3,
-        out_specs=(vmem, vmem),
+        functools.partial(expert_kernel, chunk, bool(early), len(after)),
+        out_shape=jax.ShapeDtypeStruct((half, (1 + len(early)) * PAIR, features), BF16),
+        in_specs=[vmem] * (1 + len(early)) + [anywhere] * (3 + len(after)),
+        out_specs=vmem,
         scratch_shapes=[
             VMEM((count, rows, features), BF16),
             VMEM((count, features, width), BF16),
@@ -263,14 +248,14 @@
             VMEM((count, rows, features), F32),
             pltpu.SemaphoreType.DMA((count, 10)),
         ],
-        compiler_params=pltpu.CompilerParams(vmem_limit_bytes=54 * 1024 * 1024),
+        compiler_params=pltpu.CompilerParams(vmem_limit_bytes=48 * 1024 * 1024),
         cost_estimate=pl.CostEstimate(
-            flops=6 * count * rows * features * width,
+            flops=12 * count * rows * features * width,
             bytes_accessed=6 * count * features * width,
             transcendentals=count * rows * width,
         ),
-        name="experts_second" if chunk else "experts_first",
-    )(near, far, *early, w_gate, w_up, w_down)
+        name=name,
+    )(rows_in, *early, *after, w_gate, w_up, w_down)
 
 
 def mix(slots_ref, columns_ref, first_column, parts, grad_ref, mixed_ref, far_ref):
@@ -370,14 +355,14 @@
             name="ordered",
         )(array, earlier_array)
 
-    def picked(pick, states, earlier_array, name):
+    def picked(name, pick, states, *after):
         return pl.pallas_call(
             pick_kernel,
             out_shape=shape((pick.shape[0], features), BF16),
-            in_specs=[vmem, vmem, anywhere],
+            in_specs=[vmem, vmem] + [anywhere] * len(after),
             out_specs=vmem,
             name=name,
-        )(pick, states, earlier_array)
+        )(pick, states, *after).reshape(half, 2 * PAIR, features)
 
     small = jnp.concatenate([expert_ids.T.astype(F32), gate_weights.T], axis=0)
     other = mirrored(small)
@@ -386,46 +371,44 @@
     fetched = pl.pallas_call(
         fetch_kernel,
         out_shape=shape((device_count * look_cap, features), BF16),
-        in_specs=[smem, vmem, vmem],
+        in_specs=[smem, vmem, vmem, anywhere],
         out_specs=vmem,
         name="fetch_rows",
-    )(place, all_rows, table)
+    )(place, all_rows, table, other)
     returned = swap(fetched.reshape(device_count, look_cap, features))
-    put, near_pick, far_first_pick, far_second_pick, near_of, far_of, columns = pl.pallas_call(
+    put, near_pick, far_pick, near_of, far_of, columns = pl.pallas_call(
         plan_kernel,
         out_shape=(
             shape((tok_rows, device_count * look_cap), BF16),
             shape((near_slots, tok_rows), BF16),
-            shape((far_slots, tok_rows), BF16),
-            shape((far_slots, tok_rows), BF16),
+            shape((near_slots, tok_rows), BF16),
             shape((tok_rows, tok_rows), jnp.int32),
             shape((tok_rows, tok_rows), jnp.int32),
             shape((tok_rows, tok_rows), F32),
         ),
         in_specs=[smem, vmem, vmem, vmem, vmem, anywhere],
-        out_specs=(vmem,) * 7,
+        out_specs=(vmem,) * 6,
         name="plan",
     )(place, row_ids[None, :], small, other, jnp.exp2(block_exps.T.astype(F32)), fetched)
-    state, near_sent = pl.pallas_call(
+    state = pl.pallas_call(
         state_kernel,
-        out_shape=(shape((tok_rows, features), BF16), shape((near_slots, features), BF16)),
-        in_specs=[vmem] * 5,
-        out_specs=(vmem, vmem),
+        out_shape=shape((tok_rows, features), BF16),
+        in_specs=[vmem] * 4,
+        out_specs=vmem,
         name="token_state",
-    )(put, near_pick, returned.reshape(device_count * look_cap, features), block_values, columns)
+    )(put, returned.reshape(device_count * look_cap, features), block_values, columns)
     other_state = mirrored(state)
-    near_rows = swap(near_sent.reshape(half, 2 * PAIR, features), halves)
-    far_sent = picked(far_first_pick, other_state, near_rows, "far_first")
-    far_rows = swap(far_sent.reshape(half, PAIR, features), halves)
-    far_later_sent = picked(far_second_pick, other_state, far_rows, "far_second")
-    far_later_rows = swap(far_later_sent.reshape(half, PAIR, features), halves)
+    near_rows = swap(picked("near_slots", near_pick, state), halves)
+    far_sent = picked("far_slots", far_pick, other_state, near_rows)
+    far_rows = swap(far_sent, halves)
 
     weights = (w_gate, w_up, w_down)
-    near_out, far_out = expert_call(0, near_rows, far_rows, (), *weights)
+    near_out = expert_call("near_first", 0, near_rows, weights, after=(far_sent,))
+    near_out = expert_call("near_second", 1, near_rows, weights, early=(near_out,))
+    far_out = expert_call("far_first", 0, far_rows, weights, after=(near_out, other_grad))
     far_back = swap(far_out, halves)
-    near_out, far_later_out = expert_call(1, near_rows, far_later_rows, (near_out,), *weights)
+    far_later_out = expert_call("far_second", 1, far_rows, weights, after=(far_out,))
     far_later_back = swap(ordered(far_later_out, far_back), halves)
-    near_back = swap(ordered(near_out, far_later_back), halves)
 
     far_mixed, far_grads = pl.pallas_call(
         far_kernel,
@@ -440,6 +423,7 @@
         far_later_back.reshape(far_slots, features),
         other_grad,
     )
+    near_back = swap(ordered(near_out, far_mixed), halves)
     mixed, grads = pl.pallas_call(
         near_kernel,
         out_shape=(shape((tok_rows, features), BF16), shape((TOP, tok_rows), F32)),

time: 240 us -> 227 us (0.946)
  waiting for transfers between devices: 110 us -> 88.8 us
  Pallas kernels: 52.4 us -> 71.8 us
  blocking collectives: 32 us -> 15.9 us
    ppermute x5, waiting for transfers between devices: 102 us -> 57.2 us  [mirrored(): return lax.ppermute(array, 'expert', pairs)]
    all_to_all x6, waiting for transfers between devices: 7.84 us -> 31.6 us  [swap(): lax.all_to_all(array, 'expert', split_axis=0, concat_axis=0, tiled=True,...]
    pallas_call x3 -> x5, Pallas kernels: 35.6 us -> 54 us  [the longest x4 51.4 us: expert_call(): pl.pallas_call(functools.partial(expert_kernel, chunk, bool(early), len(a...]
    all_to_all x2 -> x1, blocking collectives: 32 us -> 15.9 us  [swap(): lax.all_to_all(array, 'expert', split_axis=0, concat_axis=0, tiled=True,...]
    unnamed x34 -> x40, local copies, waits for them, and re-layouts: 6.39 us -> 7.58 us
  transfers between devices with their start and end apart: 11 -> 11, of which waited for: 6 -> 8; matrix products, arithmetic and copies ran while one was open for 1% -> 1% of each run, Pallas kernels for 16% -> 17%
where the time goes in v5:
time: 227 us; the launch traced here: 226 us
  waiting for transfers between devices  88.8 us (39%)
  Pallas kernels  71.8 us (32%)
  starting transfers between devices  37.1 us (16%)
  blocking collectives  15.9 us (7%)
  local copies, waits for them, and re-layouts  8.84 us (4%)
  other arithmetic  2.65 us (1%)
    ppermute x5, waiting for transfers between devices, mirrored(): return lax.ppermute(array, 'expert', pairs)  57.2 us
    pallas_call x4, Pallas kernels, expert_call(): pl.pallas_call(functools.partial(expert_kernel, chunk, bool(early), len(a...  51.4 us
    all_to_all x6, waiting for transfers between devices, swap(): lax.all_to_all(array, 'expert', split_axis=0, concat_axis=0, tiled=True,...  31.6 us
    all_to_all x6, starting transfers between devices, swap(): lax.all_to_all(array, 'expert', split_axis=0, concat_axis=0, tiled=True,...  26.4 us
    all_to_all x1, blocking collectives, swap(): lax.all_to_all(array, 'expert', split_axis=0, concat_axis=0, tiled=True,...  15.9 us
    ppermute x5, starting transfers between devices, mirrored(): return lax.ppermute(array, 'expert', pairs)  10.7 us
    unnamed x40, local copies, waits for them, and re-layouts  7.58 us
    pallas_call x2, Pallas kernels, picked(): pl.pallas_call(pick_kernel, out_shape=shape((pick.shape[0], features), BF...  5.64 us
  transfers between devices with their start and end apart: 11, of which 8 were waited for; matrix products, arithmetic and copies ran while one was open for 1% of the time, Pallas kernels for 17%

profile of v5, /device:TPU:0, one launch (start us, length us, event | category | flops | bytes accessed | tf_op | source)
XLA Modules:
  0.0 225.9 jit_solution(3201850910652899904)
XLA Ops:
  0.6 0.7 convert_bitcast_fusion
  1.3 0.7 pad_maximum_fusion.small_ref
  2.0 4.0 %collective-permute-start = (f32[8,128]{1,0:T(8,128)S(1)}, f32[8,128]{1,0:T(8,128)S(1)}, u32[]{:S(2)}, u32[]{:S(2)}) collective-permute-start(f32[8,128]{1,0:T(8,128)S(1)} %pad_maximum_fusion.small_ref), channel_id=1, source_target_pairs={{0,8},{1,9},{2,10},{3,11},{4,12},{5,13},{6,14},{7,15},{8,0},{9,1},... | collective-permute-start | bytes 12296 | tf_op jit(solution)/shard_map/ppermute | solution.py:346
  6.0 1.3 broadcast_in_dim.10
  7.3 3.9 %all-to-all-start = ((s32[16,1,128]{2,1,0:T(1,128)}), s32[16,1,128]{2,1,0:T(1,128)S(1)}, u32[]{:S(2)}, u32[]{:S(2)}) async-start(s32[16,1,128]{2,1,0:T(1,128)} %broadcast_in_dim.10), calls=%async_computation | async-start | bytes 16384 | tf_op jit(solution)/shard_map/all_to_all | solution.py:311
  11.2 0.7 pad_add_fusion.me_ref
  11.9 0.0 collective-permute-done._.other_ref
  11.9 5.7 %all-to-all-done.rows_ref = s32[16,1,128]{2,1,0:T(1,128)S(1)} async-done(((s32[16,1,128]{2,1,0:T(1,128)}), s32[16,1,128]{2,1,0:T(1,128)S(1)}, u32[]{:S(2)}, u32[]{:S(2)}) %all-to-all-start) | async-done | bytes 8224 | tf_op jit(solution)/shard_map/all_to_all | solution.py:311
  17.6 0.6 copy-done.14
  18.2 2.9 %fetch_rows.1._ = bf16[256,2048]{1,0:T(8,128)(2,1)} custom-call(s32[2]{0:T(128)} %pad_add_fusion.me_ref, s32[16,1,128]{2,1,0:T(1,128)} %copy-done.14, bf16[256,2048]{1,0:T(8,128)(2,1)} %table_ref.1, f32[8,128]{1,0:T(8,128)} %copy-done.15), custom_call_target="tpu_custom_call" | custom-call | tf_op jit(solution)/shard_map/fetch_rows/pallas_call | solution.py:371
  21.0 3.8 %all-to-all-start.1 = ((bf16[16,16,2048]{2,1,0:T(8,128)(2,1)}), bf16[16,16,2048]{2,1,0:T(8,128)(2,1)S(1)}, u32[]{:S(2)}, u32[]{:S(2)}) async-start(bf16[16,16,2048]{2,1,0:T(8,128)(2,1)} %bitcast.17), calls=%async_computation.1 | async-start | bytes 2097152 | tf_op jit(solution)/shard_map/all_to_all | solution.py:311
  24.9 0.6 exponential_bitcast_fusion.scales_ref
  25.5 1.8 plan.1
  27.3 20.5 %all-to-all-done.1 = bf16[16,16,2048]{2,1,0:T(8,128)(2,1)S(1)} async-done(((bf16[16,16,2048]{2,1,0:T(8,128)(2,1)}), bf16[16,16,2048]{2,1,0:T(8,128)(2,1)S(1)}, u32[]{:S(2)}, u32[]{:S(2)}) %all-to-all-start.1) | async-done | bytes 1048608 | tf_op jit(solution)/shard_map/all_to_all | solution.py:311
  47.7 1.0 copy-done.9
  48.7 2.6 %token_state.1.state_ref = bf16[128,2048]{1,0:T(8,128)(2,1)} custom-call(bf16[128,256]{1,0:T(8,128)(2,1)} %get-tuple-element.15.put_ref, bf16[256,2048]{1,0:T(8,128)(2,1)} %bitcast.21, bf16[128,2048]{1,0:T(8,128)(2,1)} %values_ref.1, f32[128,128]{1,0:T(8,128)} %get-tuple-element.13.columns_ref), custom_call_target="tpu_custom_call" | custom-call | tf_op jit(solution)/shard_map/token_state/pallas_call | solution.py:393
  51.3 2.8 %near_slots.1 = bf16[384,2048]{1,0:T(8,128)(2,1)} custom-call(bf16[384,128]{1,0:T(8,128)(2,1)} %get-tuple-element.14.pick_ref, bf16[128,2048]{1,0:T(8,128)(2,1)} %token_state.1.state_ref), custom_call_target="tpu_custom_call" | custom-call | tf_op jit(solution)/shard_map/near_slots/pallas_call | solution.py:359
  54.1 6.0 %all-to-all-start.2 = ((bf16[8,48,2048]{2,1,0:T(8,128)(2,1)}), bf16[8,48,2048]{2,1,0:T(8,128)(2,1)S(1)}, u32[]{:S(2)}, u32[]{:S(2)}) async-start(bf16[8,48,2048]{2,1,0:T(8,128)(2,1)} %bitcast.19), calls=%async_computation.2 | async-start | bytes 3145728 | tf_op jit(solution)/shard_map/all_to_all | solution.py:311
  60.1 0.0 copy-done.10
  60.1 2.8 %collective-permute-start.1 = (bf16[128,2048]{1,0:T(8,128)(2,1)S(1)}, bf16[128,2048]{1,0:T(8,128)(2,1)S(1)}, u32[]{:S(2)}, u32[]{:S(2)}) collective-permute-start(bf16[128,2048]{1,0:T(8,128)(2,1)S(1)} %copy-done.10), channel_id=1, source_target_pairs={{0,8},{1,9},{2,10},{3,11},{4,12},{5,13},{6,14},{7,15},{8,0},{9,1},... | collective-permute-start | bytes 1572872 | tf_op jit(solution)/shard_map/ppermute | solution.py:346
  63.0 26.4 %collective-permute-done.1.state_ref = bf16[128,2048]{1,0:T(8,128)(2,1)S(1)} collective-permute-done((bf16[128,2048]{1,0:T(8,128)(2,1)S(1)}, bf16[128,2048]{1,0:T(8,128)(2,1)S(1)}, u32[]{:S(2)}, u32[]{:S(2)}) %collective-permute-start.1) | collective-permute-done | bytes 524320 | tf_op jit(solution)/shard_map/ppermute | solution.py:346
  89.4 2.1 all-to-all-done.2.refs_0_.rows_ref
  91.5 1.2 copy-done.1
  92.6 2.8 %far_slots.1 = bf16[384,2048]{1,0:T(8,128)(2,1)} custom-call(bf16[384,128]{1,0:T(8,128)(2,1)} %get-tuple-element.16.pick_ref, bf16[128,2048]{1,0:T(8,128)(2,1)} %copy-done.12, bf16[8,48,2048]{2,1,0:T(8,128)(2,1)} %copy-done.1), custom_call_target="tpu_custom_call" | custom-call | tf_op jit(solution)/shard_map/far_slots/pallas_call | solution.py:359
  95.4 5.3 %all-to-all-start.3 = ((bf16[8,48,2048]{2,1,0:T(8,128)(2,1)}), bf16[8,48,2048]{2,1,0:T(8,128)(2,1)}, u32[]{:S(2)}, u32[]{:S(2)}) async-start(bf16[8,48,2048]{2,1,0:T(8,128)(2,1)} %bitcast.15), calls=%async_computation.3 | async-start | bytes 3145728 | tf_op jit(solution)/shard_map/all_to_all | solution.py:311
  100.7 0.8 collective-permute-start.2
  101.6 11.9 %near_first.1.refs_0_ = bf16[8,24,2048]{2,1,0:T(8,128)(2,1)S(1)} custom-call(bf16[8,48,2048]{2,1,0:T(8,128)(2,1)S(1)} %copy-done.2, bf16[8,48,2048]{2,1,0:T(8,128)(2,1)S(1)} %bitcast.16, bf16[4,2048,1408]{2,1,0:T(8,128)(2,1)} %refs_1_.5, bf16[4,2048,1408]{2,1,0:T(8,128)(2,1)} %refs_2_.7, bf16[4,1408,2048]{2,1,0:T(8,128)(2,1)} %refs_3_.7), custom_call_target="tpu_custom_call" | custom-call | flops 6643777536 | bytes 34603008 | tf_op jit(solution)/shard_map/near_first/pallas_call | solution.py:237
  113.5 12.0 %near_second.1.refs_0_.array_ref = bf16[8,48,2048]{2,1,0:T(8,128)(2,1)S(1)} custom-call(bf16[8,48,2048]{2,1,0:T(8,128)(2,1)S(1)} %copy-done.2, bf16[8,24,2048]{2,1,0:T(8,128)(2,1)S(1)} %near_first.1.refs_0_, bf16[4,2048,1408]{2,1,0:T(8,128)(2,1)} %refs_1_.5, bf16[4,2048,1408]{2,1,0:T(8,128)(2,1)} %refs_2_.7, bf16[4,1408,2048]{2,1,0:T(8,128)(2,1)} %refs_3_.7), custom_call_target="tpu_custom_call" | custom-call | flops 6643777536 | bytes 34603008 | tf_op jit(solution)/shard_map/near_second/pallas_call | solution.py:237
  125.5 4.6 %collective-permute-done.2.refs_1_.grad_ref = bf16[128,2048]{1,0:T(8,128)(2,1)S(1)} collective-permute-done((bf16[128,2048]{1,0:T(8,128)(2,1)}, bf16[128,2048]{1,0:T(8,128)(2,1)S(1)}, u32[]{:S(2)}, u32[]{:S(2)}) %collective-permute-start.2) | collective-permute-done | bytes 524320 | tf_op jit(solution)/shard_map/ppermute | solution.py:346
  130.1 0.8 copy-done.5
  130.9 1.3 all-to-all-done.3.rows_ref
  132.2 1.0 copy-done.6
  133.2 14.2 %far_first.1.refs_0_ = bf16[8,24,2048]{2,1,0:T(8,128)(2,1)} custom-call(bf16[8,48,2048]{2,1,0:T(8,128)(2,1)} %all-to-all-done.3.rows_ref, bf16[8,48,2048]{2,1,0:T(8,128)(2,1)S(1)} %near_second.1.refs_0_.array_ref, bf16[128,2048]{1,0:T(8,128)(2,1)S(1)} %copy-done.6, bf16[4,2048,1408]{2,1,0:T(8,128)(2,1)} %refs_1_.5, bf16[4,2048,1408]{2,1,0:T(8,128)(2,1)} %refs_2_.7, ...), custom_call_target="tpu_custom_call" | custom-call | flops 6643777536 | bytes 34603008 | tf_op jit(solution)/shard_map/far_first/pallas_call | solution.py:237
  147.4 3.7 %all-to-all-start.4 = ((bf16[8,24,2048]{2,1,0:T(8,128)(2,1)}), bf16[8,24,2048]{2,1,0:T(8,128)(2,1)S(1)}, u32[]{:S(2)}, u32[]{:S(2)}) async-start(bf16[8,24,2048]{2,1,0:T(8,128)(2,1)} %far_first.1.refs_0_), calls=%async_computation.4 | async-start | bytes 1572864 | tf_op jit(solution)/shard_map/all_to_all | solution.py:311
  151.2 13.3 %far_second.1.array_ref = bf16[8,24,2048]{2,1,0:T(8,128)(2,1)S(1)} custom-call(bf16[8,48,2048]{2,1,0:T(8,128)(2,1)} %all-to-all-done.3.rows_ref, bf16[8,24,2048]{2,1,0:T(8,128)(2,1)} %far_first.1.refs_0_, bf16[4,2048,1408]{2,1,0:T(8,128)(2,1)} %refs_1_.5, bf16[4,2048,1408]{2,1,0:T(8,128)(2,1)} %refs_2_.7, bf16[4,1408,2048]{2,1,0:T(8,128)(2,1)} %refs_3_.7), custom_call_target="tpu_custom_call" | custom-call | flops 6643777536 | bytes 34603008 | tf_op jit(solution)/shard_map/far_second/pallas_call | solution.py:237
  164.5 0.9 copy-done.4
  165.4 0.0 all-to-all-done.4.earlier_ref
  165.4 0.9 copy-done.7
  166.2 15.9 %all_to_all.35 = bf16[8,24,2048]{2,1,0:T(8,128)(2,1)} all-to-all(bf16[8,24,2048]{2,1,0:T(8,128)(2,1)} %ordered.2), channel_id=1, replica_groups={{0,1,2,3,4,5,6,7},{8,9,10,11,12,13,14,15},{16,17,18,19,20,21,22,23},{24..., dimensions={0} | all-to-all | bytes 1572864 | tf_op jit(solution)/shard_map/all_to_all | solution.py:311
  182.2 3.7 %mix_far.1 = (bf16[128,2048]{1,0:T(8,128)(2,1)}, f32[8,128]{1,0:T(8,128)}) custom-call(s32[128,128]{1,0:T(8,128)} %get-tuple-element.17.slots_ref, f32[128,128]{1,0:T(8,128)} %get-tuple-element.13.columns_ref, bf16[192,2048]{1,0:T(8,128)(2,1)} %bitcast.18, bf16[192,2048]{1,0:T(8,128)(2,1)} %bitcast.22, bf16[128,2048]{1,0:T(8,128)(2,1)} %copy-done.5), custom_call_target="tpu_custom_call" | custom-call | tf_op jit(solution)/shard_map/mix_far/pallas_call | solution.py:413
  185.9 3.7 %all-to-all-start.6 = ((bf16[8,48,2048]{2,1,0:T(8,128)(2,1)}), bf16[8,48,2048]{2,1,0:T(8,128)(2,1)S(1)}, u32[]{:S(2)}, u32[]{:S(2)}) async-start(bf16[8,48,2048]{2,1,0:T(8,128)(2,1)} %ordered.3), calls=%async_computation.6 | async-start | bytes 3145728 | tf_op jit(solution)/shard_map/all_to_all | solution.py:311
  189.6 2.1 collective-permute-start.3
  191.7 0.9 collective-permute-start.4
  192.6 26.2 %collective-permute-done.4.far_grads_ref = f32[8,128]{1,0:T(8,128)S(1)} collective-permute-done((f32[8,128]{1,0:T(8,128)S(1)}, f32[8,128]{1,0:T(8,128)S(1)}, u32[]{:S(2)}, u32[]{:S(2)}) %collective-permute-start.4) | collective-permute-done | bytes 4128 | tf_op jit(solution)/shard_map/ppermute | solution.py:346
  218.8 0.0 collective-permute-done.3.far_ref
  218.8 2.1 all-to-all-done.6
  220.9 1.2 copy-done.8
  222.1 3.8 %mix_near.1 = (bf16[128,2048]{1,0:T(8,128)(2,1)}, f32[4,128]{1,0:T(4,128)}) custom-call(s32[128,128]{1,0:T(8,128)} %get-tuple-element.12.slots_ref, f32[128,128]{1,0:T(8,128)} %get-tuple-element.13.columns_ref, bf16[384,2048]{1,0:T(8,128)(2,1)} %bitcast.20, bf16[128,2048]{1,0:T(8,128)(2,1)} %grad_ref.1, bf16[128,2048]{1,0:T(8,128)(2,1)} %copy-done.13, ...), custom_call_target="tpu_custom_call" | custom-call | tf_op jit(solution)/shard_map/mix_near/pallas_call | solution.py:427
  (33 shorter events, 0.1 us)
Async XLA Ops:
  2.0 19.0 %copy-start.16 = (f32[8,128]{1,0:T(8,128)}, f32[8,128]{1,0:T(8,128)S(1)}, u32[]{:S(2)}) copy-start(f32[8,128]{1,0:T(8,128)S(1)} %pad_maximum_fusion.small_ref) | copy-start | bytes 12292
  2.0 9.9 %collective-permute-start = (f32[8,128]{1,0:T(8,128)S(1)}, f32[8,128]{1,0:T(8,128)S(1)}, u32[]{:S(2)}, u32[]{:S(2)}) collective-permute-start(f32[8,128]{1,0:T(8,128)S(1)} %pad_maximum_fusion.small_ref), channel_id=1, source_target_pairs={{0,8},{1,9},{2,10},{3,11},{4,12},{5,13},{6,14},{7,15},{8,0},{9,1},... | collective-permute-start | bytes 12296 | tf_op jit(solution)/shard_map/ppermute | solution.py:346
  7.3 10.3 %all-to-all-start = ((s32[16,1,128]{2,1,0:T(1,128)}), s32[16,1,128]{2,1,0:T(1,128)S(1)}, u32[]{:S(2)}, u32[]{:S(2)}) async-start(s32[16,1,128]{2,1,0:T(1,128)} %broadcast_in_dim.10), calls=%async_computation | async-start | bytes 16384 | tf_op jit(solution)/shard_map/all_to_all | solution.py:311
  11.9 5.7 %copy-start.15 = (f32[8,128]{1,0:T(8,128)}, f32[8,128]{1,0:T(8,128)S(1)}, u32[]{:S(2)}) copy-start(f32[8,128]{1,0:T(8,128)S(1)} %collective-permute-done._.other_ref) | copy-start | bytes 12292
  17.6 0.6 copy-start.14
  21.0 3.8 %copy-start.17 = (s32[128,16]{0,1:T(8,128)S(1)}, s32[128,16]{0,1:T(8,128)}, u32[]{:S(2)}) copy-start(s32[128,16]{0,1:T(8,128)} %param.11) | copy-start | bytes 24580
  21.0 26.7 %all-to-all-start.1 = ((bf16[16,16,2048]{2,1,0:T(8,128)(2,1)}), bf16[16,16,2048]{2,1,0:T(8,128)(2,1)S(1)}, u32[]{:S(2)}, u32[]{:S(2)}) async-start(bf16[16,16,2048]{2,1,0:T(8,128)(2,1)} %bitcast.17), calls=%async_computation.1 | async-start | bytes 2097152 | tf_op jit(solution)/shard_map/all_to_all | solution.py:311
  47.7 1.0 copy-start.9
  54.1 6.0 %copy-start.10 = (bf16[128,2048]{1,0:T(8,128)(2,1)S(1)}, bf16[128,2048]{1,0:T(8,128)(2,1)}, u32[]{:S(2)}) copy-start(bf16[128,2048]{1,0:T(8,128)(2,1)} %token_state.1.state_ref) | copy-start | bytes 1572868
  54.1 37.3 %all-to-all-start.2 = ((bf16[8,48,2048]{2,1,0:T(8,128)(2,1)}), bf16[8,48,2048]{2,1,0:T(8,128)(2,1)S(1)}, u32[]{:S(2)}, u32[]{:S(2)}) async-start(bf16[8,48,2048]{2,1,0:T(8,128)(2,1)} %bitcast.19), calls=%async_computation.2 | async-start | bytes 3145728 | tf_op jit(solution)/shard_map/all_to_all | solution.py:311
  60.1 29.2 %collective-permute-start.1 = (bf16[128,2048]{1,0:T(8,128)(2,1)S(1)}, bf16[128,2048]{1,0:T(8,128)(2,1)S(1)}, u32[]{:S(2)}, u32[]{:S(2)}) collective-permute-start(bf16[128,2048]{1,0:T(8,128)(2,1)S(1)} %copy-done.10), channel_id=1, source_target_pairs={{0,8},{1,9},{2,10},{3,11},{4,12},{5,13},{6,14},{7,15},{8,0},{9,1},... | collective-permute-start | bytes 1572872 | tf_op jit(solution)/shard_map/ppermute | solution.py:346
  89.4 2.1 copy-start.12
  91.5 1.2 copy-start.1
  95.4 6.1 %copy-start.2 = (bf16[8,48,2048]{2,1,0:T(8,128)(2,1)S(1)}, bf16[8,48,2048]{2,1,0:T(8,128)(2,1)}, u32[]{:S(2)}) copy-start(bf16[8,48,2048]{2,1,0:T(8,128)(2,1)} %copy-done.1) | copy-start | bytes 4718596
  95.4 6.1 %copy-start.3 = (bf16[384,2048]{1,0:T(8,128)(2,1)S(1)}, bf16[384,2048]{1,0:T(8,128)(2,1)}, u32[]{:S(2)}) copy-start(bf16[384,2048]{1,0:T(8,128)(2,1)} %far_slots.1) | copy-start | bytes 4718596
  95.4 36.7 %all-to-all-start.3 = ((bf16[8,48,2048]{2,1,0:T(8,128)(2,1)}), bf16[8,48,2048]{2,1,0:T(8,128)(2,1)}, u32[]{:S(2)}, u32[]{:S(2)}) async-start(bf16[8,48,2048]{2,1,0:T(8,128)(2,1)} %bitcast.15), calls=%async_computation.3 | async-start | bytes 3145728 | tf_op jit(solution)/shard_map/all_to_all | solution.py:311
  100.7 29.3 %collective-permute-start.2 = (bf16[128,2048]{1,0:T(8,128)(2,1)}, bf16[128,2048]{1,0:T(8,128)(2,1)S(1)}, u32[]{:S(2)}, u32[]{:S(2)}) collective-permute-start(bf16[128,2048]{1,0:T(8,128)(2,1)} %grad_ref.1), channel_id=1, source_target_pairs={{0,8},{1,9},{2,10},{3,11},{4,12},{5,13},{6,14},{7,15},{8,0},{9,1},... | collective-permute-start | bytes 1572872 | tf_op jit(solution)/shard_map/ppermute | solution.py:346
  125.5 21.9 %copy-start = (bf16[8,48,2048]{2,1,0:T(8,128)(2,1)}, bf16[8,48,2048]{2,1,0:T(8,128)(2,1)S(1)}, u32[]{:S(2)}) copy-start(bf16[8,48,2048]{2,1,0:T(8,128)(2,1)S(1)} %near_second.1.refs_0_.array_ref) | copy-start | bytes 4718596
  130.1 0.8 copy-start.5
  132.2 1.0 copy-start.6
  147.4 18.0 %all-to-all-start.4 = ((bf16[8,24,2048]{2,1,0:T(8,128)(2,1)}), bf16[8,24,2048]{2,1,0:T(8,128)(2,1)S(1)}, u32[]{:S(2)}, u32[]{:S(2)}) async-start(bf16[8,24,2048]{2,1,0:T(8,128)(2,1)} %far_first.1.refs_0_), calls=%async_computation.4 | async-start | bytes 1572864 | tf_op jit(solution)/shard_map/all_to_all | solution.py:311
  164.5 0.9 copy-start.4
  165.4 0.9 copy-start.7
  185.9 3.7 %copy-start.11 = (bf16[128,2048]{1,0:T(8,128)(2,1)S(1)}, bf16[128,2048]{1,0:T(8,128)(2,1)}, u32[]{:S(2)}) copy-start(bf16[128,2048]{1,0:T(8,128)(2,1)} %get-tuple-element.18.earlier_ref) | copy-start | bytes 1572868
  185.9 5.8 %copy-start.19 = (f32[8,128]{1,0:T(8,128)S(1)}, f32[8,128]{1,0:T(8,128)}, u32[]{:S(2)}) copy-start(f32[8,128]{1,0:T(8,128)} %get-tuple-element.19) | copy-start | bytes 12292
  185.9 35.1 %all-to-all-start.6 = ((bf16[8,48,2048]{2,1,0:T(8,128)(2,1)}), bf16[8,48,2048]{2,1,0:T(8,128)(2,1)S(1)}, u32[]{:S(2)}, u32[]{:S(2)}) async-start(bf16[8,48,2048]{2,1,0:T(8,128)(2,1)} %ordered.3), calls=%async_computation.6 | async-start | bytes 3145728 | tf_op jit(solution)/shard_map/all_to_all | solution.py:311
  189.6 29.2 %collective-permute-start.3 = (bf16[128,2048]{1,0:T(8,128)(2,1)S(1)}, bf16[128,2048]{1,0:T(8,128)(2,1)S(1)}, u32[]{:S(2)}, u32[]{:S(2)}) collective-permute-start(bf16[128,2048]{1,0:T(8,128)(2,1)S(1)} %copy-done.11), channel_id=1, source_target_pairs={{0,8},{1,9},{2,10},{3,11},{4,12},{5,13},{6,14},{7,15},{8,0},{9,1},... | collective-permute-start | bytes 1572872 | tf_op jit(solution)/shard_map/ppermute | solution.py:346
  191.7 27.1 %collective-permute-start.4 = (f32[8,128]{1,0:T(8,128)S(1)}, f32[8,128]{1,0:T(8,128)S(1)}, u32[]{:S(2)}, u32[]{:S(2)}) collective-permute-start(f32[8,128]{1,0:T(8,128)S(1)} %copy-done.19), channel_id=1, source_target_pairs={{0,8},{1,9},{2,10},{3,11},{4,12},{5,13},{6,14},{7,15},{8,0},{9,1},... | collective-permute-start | bytes 12296 | tf_op jit(solution)/shard_map/ppermute | solution.py:346
  218.8 2.1 copy-start.18
  218.8 2.1 copy-start.13
  220.9 1.2 copy-start.8

commit v6 on v5

--- a/solution.py
+++ b/solution.py
@@ -33,11 +33,26 @@
     return flags(iota((length, length), 0) < iota((length, length), 1))
 
 
-def fetch_kernel(me_ref, rows_ref, table_ref, _, out_ref):
-    device_count, _, tok_rows = rows_ref.shape
+def pack_kernel(rows_ref, ids_ref, weights_ref, out_ref):
+    count, lines, tok_rows = out_ref.shape
+    packed = jnp.concatenate(
+        [
+            rows_ref[...].astype(F32),
+            ids_ref[...].astype(F32),
+            weights_ref[...],
+            jnp.zeros((lines - 1 - 2 * TOP, tok_rows), F32),
+        ],
+        axis=0,
+    )
+    for n in range(count):
+        out_ref[n] = packed
+
+
+def fetch_kernel(me_ref, packed_ref, table_ref, out_ref):
+    device_count, _, tok_rows = packed_ref.shape
     held = table_ref.shape[0]
     look_cap = out_ref.shape[0] // device_count
-    local = rows_ref[:, 0, :] - me_ref[0] * held
+    local = packed_ref[:, 0, :].astype(jnp.int32) - me_ref[0] * held
     hit = (local >= 0) & (local < held)
     rank = dot(flags(hit), earlier(tok_rows)).astype(jnp.int32)
     rank = jnp.where(hit, rank, -1)
@@ -59,10 +74,10 @@
 def plan_kernel(
     me_ref,
     rows_ref,
-    small_ref,
-    other_ref,
+    packed_ref,
     scales_ref,
-    _,
+    fetched_ref,
+    grad_ref,
     put_ref,
     near_ref,
     far_ref,
@@ -95,8 +110,10 @@
     flipped = ((inside + flip) & 1) * CAP
     device = inside // exp_dev
     chunk = (inside % exp_dev) // 2
-    for far, ref in enumerate((small_ref, other_ref)):
-        ids = [ref[k : k + 1, :].astype(jnp.int32) for k in range(TOP)]
+    mine = packed_ref[me]
+    other = packed_ref[(me + half) % device_count]
+    for far, packed in enumerate((mine, other)):
+        ids = [packed[1 + k : 2 + k].astype(jnp.int32) for k in range(TOP)]
         chosen = [ids[k] == expert for k in range(TOP)]
         hit = functools.reduce(jnp.logical_or, chosen)
         rank = jnp.where(hit, dot(flags(hit), before).astype(jnp.int32), -1000)
@@ -112,10 +129,7 @@
         both = [line for pair in zip(*lines) for line in pair]
         pick_ref = far_ref if far else near_ref
         pick_ref[...] = jnp.concatenate(both, axis=0).astype(BF16)
-        if far:
-            slot = chunk * (half * PAIR) + device * PAIR + flipped + rank
-        else:
-            slot = device * (2 * PAIR) + chunk * PAIR + flipped + rank
+        slot = device * (2 * PAIR) + chunk * PAIR + flipped + rank
         found = [
             jnp.sum(jnp.where(chosen[k], slot + 1, 0), axis=0, keepdims=True) - 1
             for k in range(TOP)
@@ -125,12 +139,12 @@
         slots_out[...] = found.astype(jnp.int32)
     columns_ref[...] = turned(
         jnp.concatenate(
-            [small_ref[TOP:, :], other_ref[TOP:, :], scales_ref[...]], axis=0
+            [mine[1 + TOP : 1 + 2 * TOP], other[1 + TOP : 1 + 2 * TOP], scales_ref[...]], axis=0
         )
     )
 
 
-def state_kernel(put_ref, returned_ref, values_ref, columns_ref, state_ref):
+def state_kernel(put_ref, pick_ref, returned_ref, values_ref, columns_ref, state_ref, out_ref):
     features = values_ref.shape[1]
     width = 512
     for left in range(0, features, width):
@@ -144,6 +158,8 @@
             state_ref[:, at : at + BLOCK] = (
                 scaled + found[:, b * BLOCK : (b + 1) * BLOCK]
             ).astype(BF16)
+        cols = slice(left, left + width)
+        out_ref[:, cols] = dot(pick_ref[...], state_ref[:, cols]).astype(BF16)
 
 
 def pick_kernel(pick_ref, state_ref, *refs):
@@ -155,156 +171,148 @@
         out_ref[:, cols] = dot(pick_ref[...], state_ref[:, cols]).astype(BF16)
 
 
-def expert_kernel(chunk, join, after, rows_ref, *refs):
-    if join:
-        early_ref, refs = refs[0], refs[1:]
+def expert_kernel(after, rows_ref, *refs):
     wg_hbm, wu_hbm, wd_hbm, out_ref = refs[after : after + 4]
     x_ref, wg_ref, wu_ref, wd_ref, hidden_ref, result_ref, sem = refs[after + 4 :]
-    count, features, width = wg_ref.shape
+    exp_dev = wg_hbm.shape[0]
+    held, features, width = wg_ref.shape
     half = rows_ref.shape[0]
-    first_held = count * chunk
     up_cuts = ((0, 512), (512, 512), (1024, width - 1024))
     down_cuts = tuple((at, 512) for at in range(0, features, 512))
 
-    def weight_copies(j):
+    def weight_copies(j, place):
         copies = []
         for at, size in up_cuts:
             for hbm, ref in ((wg_hbm, wg_ref), (wu_hbm, wu_ref)):
                 cols = pl.ds(at, size)
-                copies.append((hbm.at[first_held + j, :, cols], ref.at[j, :, cols]))
+                copies.append((hbm.at[j, :, cols], ref.at[place, :, cols]))
         for at, size in down_cuts:
             cols = pl.ds(at, size)
-            copies.append((wd_hbm.at[first_held + j, :, cols], wd_ref.at[j, :, cols]))
+            copies.append((wd_hbm.at[j, :, cols], wd_ref.at[place, :, cols]))
         return [
-            pltpu.make_async_copy(src, dst, sem.at[j, n]) for n, (src, dst) in enumerate(copies)
+            pltpu.make_async_copy(src, dst, sem.at[place, n])
+            for n, (src, dst) in enumerate(copies)
         ]
 
-    for j in range(count):
-        for copy in weight_copies(j):
+    for j in range(held):
+        for copy in weight_copies(j, j):
             copy.start()
 
     low = iota((PAIR, features), 0) < CAP
-    here = slice(chunk * PAIR, (chunk + 1) * PAIR)
-    for quad in range(half // 4):
-        ones, twos = [], []
-        for pair in range(2):
-            source = 4 * quad + 2 * pair
-            even = rows_ref[source, here, :].astype(F32)
-            odd = rows_ref[source + 1, here, :].astype(F32)
-            ones.append(jnp.where(low, even, odd))
-            twos.append(jnp.where(low, odd, even))
-        rows = slice(quad * 2 * PAIR, (quad + 1) * 2 * PAIR)
-        x_ref[0, rows, :] = jnp.concatenate(ones, axis=0).astype(BF16)
-        x_ref[1, rows, :] = jnp.concatenate(twos, axis=0).astype(BF16)
-
-    @pl.loop(0, count)
+    for chunk in range(exp_dev // 2):
+        here = slice(chunk * PAIR, (chunk + 1) * PAIR)
+        for quad in range(half // 4):
+            ones, twos = [], []
+            for pair in range(2):
+                source = 4 * quad + 2 * pair
+                even = rows_ref[source, here, :].astype(F32)
+                odd = rows_ref[source + 1, here, :].astype(F32)
+                ones.append(jnp.where(low, even, odd))
+                twos.append(jnp.where(low, odd, even))
+            rows = slice(quad * 2 * PAIR, (quad + 1) * 2 * PAIR)
+            x_ref[2 * chunk, rows, :] = jnp.concatenate(ones, axis=0).astype(BF16)
+            x_ref[2 * chunk + 1, rows, :] = jnp.concatenate(twos, axis=0).astype(BF16)
+
+    @pl.loop(0, exp_dev)
     def _(j):
-        copies = weight_copies(j)
+        place = j % held
+        copies = weight_copies(j, place)
+        later = weight_copies(jnp.minimum(j + held, exp_dev - 1), place)
+
+        def refill(first, count):
+            @pl.when(j + held < exp_dev)
+            def _():
+                for n in range(first, first + count):
+                    later[n].start()
+
         n = 0
         for at, size in up_cuts:
             copies[n].wait()
             copies[n + 1].wait()
+            x = x_ref[j]
+            gate = dot(x, wg_ref[place, :, at : at + size])
+            up = dot(x, wu_ref[place, :, at : at + size])
+            hidden_ref[:, at : at + size] = (gate / (1.0 + jnp.exp(-gate)) * up).astype(BF16)
+            refill(n, 2)
             n += 2
-            x = x_ref[j]
-            gate = dot(x, wg_ref[j, :, at : at + size])
-            up = dot(x, wu_ref[j, :, at : at + size])
-            hidden_ref[:, at : at + size] = (gate / (1.0 + jnp.exp(-gate)) * up).astype(BF16)
         for at, size in down_cuts:
             copies[n].wait()
+            result_ref[j, :, at : at + size] = dot(
+                hidden_ref[...], wd_ref[place, :, at : at + size]
+            )
+            refill(n, 1)
             n += 1
-            result_ref[j, :, at : at + size] = dot(hidden_ref[...], wd_ref[j, :, at : at + size])
 
     for pair in range(half // 2):
-        one = result_ref[0, pair * PAIR : (pair + 1) * PAIR, :]
-        two = result_ref[1, pair * PAIR : (pair + 1) * PAIR, :]
-        for source, value in (
-            (2 * pair, jnp.where(low, one, two)),
-            (2 * pair + 1, jnp.where(low, two, one)),
-        ):
-            if join:
-                value = jnp.concatenate([early_ref[source].astype(F32), value], axis=0)
-            out_ref[source] = value.astype(BF16)
-
-
-def expert_call(name, chunk, rows_in, weights, early=(), after=()):
+        rows = slice(pair * PAIR, (pair + 1) * PAIR)
+        values = [result_ref[j, rows, :] for j in range(exp_dev)]
+        for odd in range(2):
+            parts = [
+                jnp.where(low, values[j + odd], values[j + 1 - odd]) for j in range(0, exp_dev, 2)
+            ]
+            out_ref[2 * pair + odd] = jnp.concatenate(parts, axis=0).astype(BF16)
+
+
+def expert_call(name, rows_in, weights, after=()):
     w_gate, w_up, w_down = weights
     exp_dev, features, width = w_gate.shape
     half = rows_in.shape[0]
-    count = 2
+    held = 2
     rows = half * CAP
     anywhere = pl.BlockSpec(memory_space=pl.ANY)
     vmem = pl.BlockSpec(memory_space=VMEM)
     return pl.pallas_call(
-        functools.partial(expert_kernel, chunk, bool(early), len(after)),
-        out_shape=jax.ShapeDtypeStruct((half, (1 + len(early)) * PAIR, features), BF16),
-        in_specs=[vmem] * (1 + len(early)) + [anywhere] * (3 + len(after)),
+        functools.partial(expert_kernel, len(after)),
+        out_shape=jax.ShapeDtypeStruct((half, exp_dev * CAP, features), BF16),
+        in_specs=[vmem] + [anywhere] * (3 + len(after)),
         out_specs=vmem,
         scratch_shapes=[
-            VMEM((count, rows, features), BF16),
-            VMEM((count, features, width), BF16),
-            VMEM((count, features, width), BF16),
-            VMEM((count, width, features), BF16),
+            VMEM((exp_dev, rows, features), BF16),
+            VMEM((held, features, width), BF16),
+            VMEM((held, features, width), BF16),
+            VMEM((held, width, features), BF16),
             VMEM((rows, width), BF16),
-            VMEM((count, rows, features), F32),
-            pltpu.SemaphoreType.DMA((count, 10)),
+            VMEM((exp_dev, rows, features), F32),
+            pltpu.SemaphoreType.DMA((held, 10)),
         ],
-        compiler_params=pltpu.CompilerParams(vmem_limit_bytes=48 * 1024 * 1024),
+        compiler_params=pltpu.CompilerParams(vmem_limit_bytes=50 * 1024 * 1024),
         cost_estimate=pl.CostEstimate(
-            flops=12 * count * rows * features * width,
-            bytes_accessed=6 * count * features * width,
-            transcendentals=count * rows * width,
+            flops=12 * exp_dev * rows * features * width,
+            bytes_accessed=6 * exp_dev * features * width,
+            transcendentals=exp_dev * rows * width,
         ),
         name=name,
-    )(rows_in, *early, *after, w_gate, w_up, w_down)
-
-
-def mix(slots_ref, columns_ref, first_column, parts, grad_ref, mixed_ref, far_ref):
+    )(rows_in, *after, w_gate, w_up, w_down)
+
+
+def mix_kernel(first_column, slots_ref, columns_ref, back_ref, grad_ref, mixed_ref, grads_ref):
     tok_rows, features = grad_ref.shape
-    picked = [jnp.zeros((tok_rows, 1), F32) for _ in range(TOP)]
-    spread = []
-    start = 0
-    for ref in parts:
-        count = ref.shape[0]
-        column = iota((tok_rows, count), 1) + start
-        start += count
-        inner = lax.dot_general(
-            grad_ref[...], ref[...], (((1,), (1,)), ((), ())), preferred_element_type=F32
-        )
-        total = jnp.zeros((tok_rows, count), F32)
-        for k in range(TOP):
-            here = column == slots_ref[:, k : k + 1]
-            weight = columns_ref[:, first_column + k : first_column + k + 1]
-            total = total + jnp.where(here, weight, 0.0)
-            picked[k] = picked[k] + jnp.sum(jnp.where(here, inner, 0.0), axis=1, keepdims=True)
-        high = total.astype(BF16)
-        spread.append((high, (total - high.astype(F32)).astype(BF16)))
+    count = back_ref.shape[0]
+    column = iota((tok_rows, count), 1)
+    inner = lax.dot_general(
+        grad_ref[...], back_ref[...], (((1,), (1,)), ((), ())), preferred_element_type=F32
+    )
+    total = jnp.zeros((tok_rows, count), F32)
+    place = iota((tok_rows, tok_rows), 1)
+    wide = jnp.zeros((tok_rows, tok_rows), F32)
+    for k in range(TOP):
+        here = column == slots_ref[:, k : k + 1]
+        weight = columns_ref[:, first_column + k : first_column + k + 1]
+        total = total + jnp.where(here, weight, 0.0)
+        value = jnp.sum(jnp.where(here, inner, 0.0), axis=1, keepdims=True)
+        wide = wide + jnp.where(place == k, value, 0.0)
+    high = total.astype(BF16)
+    rest = (total - high.astype(F32)).astype(BF16)
     width = 512
     for at in range(0, features, width):
-        cols = slice(at, at + width)
-        value = 0.0 if far_ref is None else far_ref[:, cols].astype(F32)
-        for (high, rest), ref in zip(spread, parts):
-            rows = ref[:, cols]
-            value = value + dot(high, rows) + dot(rest, rows)
-        mixed_ref[:, cols] = value.astype(BF16)
-    column = iota((tok_rows, tok_rows), 1)
-    wide = jnp.zeros((tok_rows, tok_rows), F32)
-    for k in range(TOP):
-        wide = wide + jnp.where(column == k, picked[k], 0.0)
-    return wide.T
-
-
-def far_kernel(slots_ref, columns_ref, first_ref, second_ref, grad_ref, mixed_ref, grads_ref):
-    turned_grads = mix(
-        slots_ref, columns_ref, TOP, (first_ref, second_ref), grad_ref, mixed_ref, None
-    )
-    grads_ref[...] = turned_grads[: grads_ref.shape[0], :]
-
-
-def near_kernel(
-    slots_ref, columns_ref, back_ref, grad_ref, far_ref, far_grads_ref, mixed_ref, grads_ref
-):
-    turned_grads = mix(slots_ref, columns_ref, 0, (back_ref,), grad_ref, mixed_ref, far_ref)
-    grads_ref[...] = turned_grads[:TOP, :] + far_grads_ref[:TOP, :]
+        rows = back_ref[:, at : at + width]
+        mixed_ref[:, at : at + width] = (dot(high, rows) + dot(rest, rows)).astype(mixed_ref.dtype)
+    grads_ref[...] = wide.T[: grads_ref.shape[0], :]
+
+
+def sum_kernel(near_ref, near_grads_ref, far_ref, far_grads_ref, mixed_ref, grads_ref):
+    mixed_ref[...] = (near_ref[...] + far_ref[...].astype(F32)).astype(BF16)
+    grads_ref[...] = near_grads_ref[:TOP, :] + far_grads_ref[:TOP, :]
 
 
 def swap(array, groups=None):
@@ -332,7 +340,7 @@
     tok_rows, features = block_values.shape
     rows_held = table.shape[0]
     look_cap = max(2, 2 * tok_rows // device_count)
-    near_slots, far_slots = half * 2 * PAIR, half * PAIR
+    slots = half * 2 * PAIR
     vmem = pl.BlockSpec(memory_space=VMEM)
     smem = pl.BlockSpec(memory_space=pltpu.SMEM)
     anywhere = pl.BlockSpec(memory_space=pl.ANY)
@@ -364,80 +372,73 @@
             name=name,
         )(pick, states, *after).reshape(half, 2 * PAIR, features)
 
-    small = jnp.concatenate([expert_ids.T.astype(F32), gate_weights.T], axis=0)
-    other = mirrored(small)
     other_grad = mirrored(out_grad)
-    all_rows = swap(jnp.broadcast_to(row_ids[None, None, :], (device_count, 1, tok_rows)))
+    packed = pl.pallas_call(
+        pack_kernel,
+        out_shape=shape((device_count, 16, tok_rows), F32),
+        in_specs=[vmem] * 3,
+        out_specs=vmem,
+        name="pack",
+    )(row_ids[None, :], expert_ids.T, gate_weights.T)
+    packed = swap(packed)
     fetched = pl.pallas_call(
         fetch_kernel,
         out_shape=shape((device_count * look_cap, features), BF16),
-        in_specs=[smem, vmem, vmem, anywhere],
+        in_specs=[smem, vmem, vmem],
         out_specs=vmem,
         name="fetch_rows",
-    )(place, all_rows, table, other)
+    )(place, packed, table)
     returned = swap(fetched.reshape(device_count, look_cap, features))
     put, near_pick, far_pick, near_of, far_of, columns = pl.pallas_call(
         plan_kernel,
         out_shape=(
             shape((tok_rows, device_count * look_cap), BF16),
-            shape((near_slots, tok_rows), BF16),
-            shape((near_slots, tok_rows), BF16),
+            shape((slots, tok_rows), BF16),
+            shape((slots, tok_rows), BF16),
             shape((tok_rows, tok_rows), jnp.int32),
             shape((tok_rows, tok_rows), jnp.int32),
             shape((tok_rows, tok_rows), F32),
         ),
-        in_specs=[smem, vmem, vmem, vmem, vmem, anywhere],
+        in_specs=[smem, vmem, vmem, vmem, anywhere, anywhere],
         out_specs=(vmem,) * 6,
         name="plan",
-    )(place, row_ids[None, :], small, other, jnp.exp2(block_exps.T.astype(F32)), fetched)
-    state = pl.pallas_call(
+    )(place, row_ids[None, :], packed, jnp.exp2(block_exps.T.astype(F32)), fetched, other_grad)
+    state, near_sent = pl.pallas_call(
         state_kernel,
-        out_shape=shape((tok_rows, features), BF16),
-        in_specs=[vmem] * 4,
-        out_specs=vmem,
+        out_shape=(shape((tok_rows, features), BF16), shape((slots, features), BF16)),
+        in_specs=[vmem] * 5,
+        out_specs=(vmem, vmem),
         name="token_state",
-    )(put, returned.reshape(device_count * look_cap, features), block_values, columns)
+    )(put, near_pick, returned.reshape(device_count * look_cap, features), block_values, columns)
     other_state = mirrored(state)
-    near_rows = swap(picked("near_slots", near_pick, state), halves)
+    near_rows = swap(near_sent.reshape(half, 2 * PAIR, features), halves)
     far_sent = picked("far_slots", far_pick, other_state, near_rows)
     far_rows = swap(far_sent, halves)
 
     weights = (w_gate, w_up, w_down)
-    near_out = expert_call("near_first", 0, near_rows, weights, after=(far_sent,))
-    near_out = expert_call("near_second", 1, near_rows, weights, early=(near_out,))
-    far_out = expert_call("far_first", 0, far_rows, weights, after=(near_out, other_grad))
-    far_back = swap(far_out, halves)
-    far_later_out = expert_call("far_second", 1, far_rows, weights, after=(far_out,))
-    far_later_back = swap(ordered(far_later_out, far_back), halves)
-
-    far_mixed, far_grads = pl.pallas_call(
-        far_kernel,
-        out_shape=(shape((tok_rows, features), BF16), shape((2 * TOP, tok_rows), F32)),
-        in_specs=[vmem] * 5,
+    near_out = expert_call("near_experts", near_rows, weights, after=(far_sent,))
+    far_out = expert_call("far_experts", far_rows, weights, after=(near_out,))
+    near_back = swap(near_out, halves)
+    far_back = swap(ordered(far_out, near_back), halves)
+
+    def mixed_rows(name, first_column, slot_of, back, grad, kind):
+        return pl.pallas_call(
+            functools.partial(mix_kernel, first_column),
+            out_shape=(shape((tok_rows, features), kind), shape((2 * TOP, tok_rows), F32)),
+            in_specs=[vmem] * 4,
+            out_specs=(vmem, vmem),
+            name=name,
+        )(slot_of, columns, back.reshape(slots, features), grad)
+
+    near_mixed, near_grads = mixed_rows("mix_near", 0, near_of, near_back, out_grad, F32)
+    far_mixed, far_grads = mixed_rows("mix_far", TOP, far_of, far_back, other_grad, BF16)
+    mixed, grads = pl.pallas_call(
+        sum_kernel,
+        out_shape=(shape((tok_rows, features), BF16), shape((TOP, tok_rows), F32)),
+        in_specs=[vmem] * 4,
         out_specs=(vmem, vmem),
-        name="mix_far",
-    )(
-        far_of,
-        columns,
-        far_back.reshape(far_slots, features),
-        far_later_back.reshape(far_slots, features),
-        other_grad,
-    )
-    near_back = swap(ordered(near_out, far_mixed), halves)
-    mixed, grads = pl.pallas_call(
-        near_kernel,
-        out_shape=(shape((tok_rows, features), BF16), shape((TOP, tok_rows), F32)),
-        in_specs=[vmem] * 6,
-        out_specs=(vmem, vmem),
-        name="mix_near",
-    )(
-        near_of,
-        columns,
-        near_back.reshape(near_slots, features),
-        out_grad,
-        mirrored(far_mixed),
-        mirrored(far_grads),
-    )
+        name="sum_mixes",
+    )(near_mixed, near_grads, mirrored(far_mixed), mirrored(far_grads))
     return mixed, grads.T
 
 

time: 227 us -> 235 us (1.035)
  waiting for transfers between devices: 88.8 us -> 103 us
  blocking collectives: 15.9 us -> 24.8 us
  starting transfers between devices: 37.1 us -> 29.1 us
  Pallas kernels: 71.8 us -> 68.6 us
    ppermute x5 -> x4, waiting for transfers between devices: 57.2 us -> 93.4 us  [mirrored(): return lax.ppermute(array, 'expert', pairs)]
    all_to_all x6 -> x5, waiting for transfers between devices: 31.6 us -> 9.44 us  [swap(): lax.all_to_all(array, 'expert', split_axis=0, concat_axis=0, tiled=True,...]
    all_to_all x1, blocking collectives: 15.9 us -> 24.8 us  [swap(): lax.all_to_all(array, 'expert', split_axis=0, concat_axis=0, tiled=True,...]
    ppermute x5 -> x4, starting transfers between devices: 10.7 us -> 6.4 us  [mirrored(): return lax.ppermute(array, 'expert', pairs)]
    all_to_all x6 -> x5, starting transfers between devices: 26.4 us -> 22.7 us  [swap(): lax.all_to_all(array, 'expert', split_axis=0, concat_axis=0, tiled=True,...]
    pallas_call x2 -> x1, Pallas kernels: 5.64 us -> 2.85 us  [picked(): pl.pallas_call(pick_kernel, out_shape=shape((pick.shape[0], features), BF...]
    unnamed x40 -> x26, local copies, waits for them, and re-layouts: 7.58 us -> 6.76 us
  transfers between devices with their start and end apart: 11 -> 9, of which waited for: 8 -> 5; matrix products, arithmetic and copies ran while one was open for 1% -> 1% of each run, Pallas kernels for 17% -> 22%
where the time goes in v6:
time: 235 us; the launch traced here: 234 us
  waiting for transfers between devices  103 us (44%)
  Pallas kernels  68.6 us (29%)
  starting transfers between devices  29.1 us (12%)
  blocking collectives  24.8 us (11%)
  local copies, waits for them, and re-layouts  6.76 us (3%)
    ppermute x4, waiting for transfers between devices, mirrored(): return lax.ppermute(array, 'expert', pairs)  93.4 us
    pallas_call x2, Pallas kernels, expert_call(): pl.pallas_call(functools.partial(expert_kernel, len(after)), out_shape=ja...  45.9 us
    all_to_all x1, blocking collectives, swap(): lax.all_to_all(array, 'expert', split_axis=0, concat_axis=0, tiled=True,...  24.8 us
    all_to_all x5, starting transfers between devices, swap(): lax.all_to_all(array, 'expert', split_axis=0, concat_axis=0, tiled=True,...  22.7 us
    all_to_all x5, waiting for transfers between devices, swap(): lax.all_to_all(array, 'expert', split_axis=0, concat_axis=0, tiled=True,...  9.44 us
    pallas_call x2, Pallas kernels, mixed_rows(): pl.pallas_call(functools.partial(mix_kernel, first_column), out_shape=(sh...  7.42 us
    unnamed x26, local copies, waits for them, and re-layouts  6.76 us
    ppermute x4, starting transfers between devices, mirrored(): return lax.ppermute(array, 'expert', pairs)  6.4 us
  transfers between devices with their start and end apart: 9, of which 5 were waited for; matrix products, arithmetic and copies ran while one was open for 1% of the time, Pallas kernels for 22%

profile of v6, /device:TPU:0, one launch (start us, length us, event | category | flops | bytes accessed | tf_op | source)
XLA Modules:
  0.0 234.1 jit_solution(13247913458181037043)
XLA Ops:
  0.6 1.4 pack.1
  2.0 7.4 %all-to-all-start = ((f32[16,16,128]{2,1,0:T(8,128)}), f32[16,16,128]{2,1,0:T(8,128)S(1)}, u32[]{:S(2)}, u32[]{:S(2)}) async-start(f32[16,16,128]{2,1,0:T(8,128)} %pack.1), calls=%async_computation | async-start | bytes 262144 | tf_op jit(solution)/shard_map/all_to_all | solution.py:319
  9.4 0.6 pad_add_fusion.me_ref
  10.0 7.3 %all-to-all-done.packed_ref = f32[16,16,128]{2,1,0:T(8,128)S(1)} async-done(((f32[16,16,128]{2,1,0:T(8,128)}), f32[16,16,128]{2,1,0:T(8,128)S(1)}, u32[]{:S(2)}, u32[]{:S(2)}) %all-to-all-start) | async-done | bytes 131104 | tf_op jit(solution)/shard_map/all_to_all | solution.py:319
  17.3 0.0 copy-start.6
  17.3 0.6 copy-done.6
  18.0 3.0 %fetch_rows.1.fetched_ref = bf16[256,2048]{1,0:T(8,128)(2,1)} custom-call(s32[2]{0:T(128)} %pad_add_fusion.me_ref, f32[16,16,128]{2,1,0:T(8,128)} %copy-done.6, bf16[256,2048]{1,0:T(8,128)(2,1)} %table_ref.1), custom_call_target="tpu_custom_call" | custom-call | tf_op jit(solution)/shard_map/fetch_rows/pallas_call | solution.py:384
  20.9 0.0 copy-start.7
  20.9 0.0 copy-start.10
  20.9 3.8 %all-to-all-start.1 = ((bf16[16,16,2048]{2,1,0:T(8,128)(2,1)}), bf16[16,16,2048]{2,1,0:T(8,128)(2,1)S(1)}, u32[]{:S(2)}, u32[]{:S(2)}) async-start(bf16[16,16,2048]{2,1,0:T(8,128)(2,1)} %bitcast.16), calls=%async_computation.1 | async-start | bytes 2097152 | tf_op jit(solution)/shard_map/all_to_all | solution.py:319
  24.7 0.0 copy-done.7
  24.7 2.8 %collective-permute-start = (bf16[128,2048]{1,0:T(8,128)(2,1)S(1)}, bf16[128,2048]{1,0:T(8,128)(2,1)S(1)}, u32[]{:S(2)}, u32[]{:S(2)}) collective-permute-start(bf16[128,2048]{1,0:T(8,128)(2,1)S(1)} %copy-done.7), channel_id=1, source_target_pairs={{0,8},{1,9},{2,10},{3,11},{4,12},{5,13},{6,14},{7,15},{8,0},{9,1},... | collective-permute-start | bytes 1572872 | tf_op jit(solution)/shard_map/ppermute | solution.py:354
  27.6 0.0 copy-done.10
  27.6 0.6 exponential_bitcast_fusion.scales_ref
  28.2 45.5 %collective-permute-done.grad_ref = bf16[128,2048]{1,0:T(8,128)(2,1)S(1)} collective-permute-done((bf16[128,2048]{1,0:T(8,128)(2,1)S(1)}, bf16[128,2048]{1,0:T(8,128)(2,1)S(1)}, u32[]{:S(2)}, u32[]{:S(2)}) %collective-permute-start) | collective-permute-done | bytes 524320 | tf_op jit(solution)/shard_map/ppermute | solution.py:354
  73.7 0.8 copy-done.5
  74.5 1.9 plan.1
  76.4 0.0 all-to-all-done.1
  76.4 1.0 copy-done.4
  77.4 4.0 %token_state.1 = (bf16[128,2048]{1,0:T(8,128)(2,1)}, bf16[384,2048]{1,0:T(8,128)(2,1)}) custom-call(bf16[128,256]{1,0:T(8,128)(2,1)} %get-tuple-element.18.put_ref, bf16[384,128]{1,0:T(8,128)(2,1)} %get-tuple-element.19.pick_ref, bf16[256,2048]{1,0:T(8,128)(2,1)} %bitcast.18, bf16[128,2048]{1,0:T(8,128)(2,1)} %values_ref.1, ...), custom_call_target="tpu_custom_call" | custom-call | tf_op jit(solution)/shard_map/token_state/pallas_call | solution.py:406
  81.4 3.7 %all-to-all-start.2 = ((bf16[8,48,2048]{2,1,0:T(8,128)(2,1)}), bf16[8,48,2048]{2,1,0:T(8,128)(2,1)S(1)}, u32[]{:S(2)}, u32[]{:S(2)}) async-start(bf16[8,48,2048]{2,1,0:T(8,128)(2,1)} %bitcast.19), calls=%async_computation.2 | async-start | bytes 3145728 | tf_op jit(solution)/shard_map/all_to_all | solution.py:319
  85.1 0.0 copy-done.12
  85.1 0.7 collective-permute-start.1
  85.8 28.5 %collective-permute-done.1.state_ref = bf16[128,2048]{1,0:T(8,128)(2,1)S(1)} collective-permute-done((bf16[128,2048]{1,0:T(8,128)(2,1)S(1)}, bf16[128,2048]{1,0:T(8,128)(2,1)S(1)}, u32[]{:S(2)}, u32[]{:S(2)}) %collective-permute-start.1) | collective-permute-done | bytes 524320 | tf_op jit(solution)/shard_map/ppermute | solution.py:354
  114.2 2.1 all-to-all-done.2.refs_0_.rows_ref
  116.3 0.0 copy-done.9
  116.3 1.1 copy-done
  117.5 2.8 %far_slots.1 = bf16[384,2048]{1,0:T(8,128)(2,1)} custom-call(bf16[384,128]{1,0:T(8,128)(2,1)} %get-tuple-element.21.pick_ref, bf16[128,2048]{1,0:T(8,128)(2,1)} %copy-done.9, bf16[8,48,2048]{2,1,0:T(8,128)(2,1)} %copy-done), custom_call_target="tpu_custom_call" | custom-call | tf_op jit(solution)/shard_map/far_slots/pallas_call | solution.py:367
  120.3 3.7 %all-to-all-start.4 = ((bf16[8,48,2048]{2,1,0:T(8,128)(2,1)}), bf16[8,48,2048]{2,1,0:T(8,128)(2,1)S(1)}, u32[]{:S(2)}, u32[]{:S(2)}) async-start(bf16[8,48,2048]{2,1,0:T(8,128)(2,1)} %bitcast.14), calls=%async_computation.4 | async-start | bytes 3145728 | tf_op jit(solution)/shard_map/all_to_all | solution.py:319
  124.1 0.0 copy-done.1
  124.1 23.5 %near_experts.1.refs_0_ = bf16[8,48,2048]{2,1,0:T(8,128)(2,1)} custom-call(bf16[8,48,2048]{2,1,0:T(8,128)(2,1)S(1)} %copy-done.1, bf16[8,48,2048]{2,1,0:T(8,128)(2,1)} %bitcast.15, bf16[4,2048,1408]{2,1,0:T(8,128)(2,1)} %refs_1_.3, bf16[4,2048,1408]{2,1,0:T(8,128)(2,1)} %refs_2_.3, bf16[4,1408,2048]{2,1,0:T(8,128)(2,1)} %refs_3_.3), custom_call_target="tpu_custom_call" | custom-call | flops 13287555072 | bytes 69206016 | tf_op jit(solution)/shard_map/near_experts/pallas_call | solution.py:264
  147.6 0.0 all-to-all-done.4.rows_ref
  147.6 4.1 %all-to-all-start.3 = ((bf16[8,48,2048]{2,1,0:T(8,128)(2,1)}), bf16[8,48,2048]{2,1,0:T(8,128)(2,1)S(1)}, u32[]{:S(2)}, u32[]{:S(2)}) async-start(bf16[8,48,2048]{2,1,0:T(8,128)(2,1)} %near_experts.1.refs_0_), calls=%async_computation.3 | async-start | bytes 3145728 | tf_op jit(solution)/shard_map/all_to_all | solution.py:319
  151.7 22.4 %far_experts.1.array_ref = bf16[8,48,2048]{2,1,0:T(8,128)(2,1)S(1)} custom-call(bf16[8,48,2048]{2,1,0:T(8,128)(2,1)S(1)} %all-to-all-done.4.rows_ref, bf16[8,48,2048]{2,1,0:T(8,128)(2,1)} %near_experts.1.refs_0_, bf16[4,2048,1408]{2,1,0:T(8,128)(2,1)} %refs_1_.3, bf16[4,2048,1408]{2,1,0:T(8,128)(2,1)} %refs_2_.3, bf16[4,1408,2048]{2,1,0:T(8,128)(2,1)} %refs_3_.3), custom_call_target="tpu_custom_call" | custom-call | flops 13287555072 | bytes 69206016 | tf_op jit(solution)/shard_map/far_experts/pallas_call | solution.py:264
  174.1 0.0 copy-start.2
  174.1 1.2 copy-done.2
  175.3 0.0 all-to-all-done.3.earlier_ref
  175.3 1.2 copy-done.3
  176.5 24.8 %all_to_all.30 = bf16[8,48,2048]{2,1,0:T(8,128)(2,1)} all-to-all(bf16[8,48,2048]{2,1,0:T(8,128)(2,1)} %ordered.1), channel_id=1, replica_groups={{0,1,2,3,4,5,6,7},{8,9,10,11,12,13,14,15},{16,17,18,19,20,21,22,23},{24..., dimensions={0} | all-to-all | bytes 3145728 | tf_op jit(solution)/shard_map/all_to_all | solution.py:319
  201.2 3.6 %mix_far.1 = (bf16[128,2048]{1,0:T(8,128)(2,1)}, f32[8,128]{1,0:T(8,128)}) custom-call(s32[128,128]{1,0:T(8,128)} %get-tuple-element.25.slots_ref, f32[128,128]{1,0:T(8,128)} %get-tuple-element.17.columns_ref, bf16[384,2048]{1,0:T(8,128)(2,1)} %bitcast.17, bf16[128,2048]{1,0:T(8,128)(2,1)} %copy-done.5), custom_call_target="tpu_custom_call" | custom-call | tf_op jit(solution)/shard_map/mix_far/pallas_call | solution.py:425
  204.9 1.4 collective-permute-start.2
  206.3 1.5 collective-permute-start.3
  207.8 3.8 %mix_near.1 = (f32[128,2048]{1,0:T(8,128)}, f32[8,128]{1,0:T(8,128)}) custom-call(s32[128,128]{1,0:T(8,128)} %get-tuple-element.16.slots_ref, f32[128,128]{1,0:T(8,128)} %get-tuple-element.17.columns_ref, bf16[384,2048]{1,0:T(8,128)(2,1)} %bitcast.13, bf16[128,2048]{1,0:T(8,128)(2,1)} %grad_ref.1), custom_call_target="tpu_custom_call" | custom-call | tf_op jit(solution)/shard_map/mix_near/pallas_call | solution.py:425
  211.6 19.4 %collective-permute-done.3.far_grads_ref = f32[8,128]{1,0:T(8,128)S(1)} collective-permute-done((f32[8,128]{1,0:T(8,128)}, f32[8,128]{1,0:T(8,128)S(1)}, u32[]{:S(2)}, u32[]{:S(2)}) %collective-permute-start.3) | collective-permute-done | bytes 4128 | tf_op jit(solution)/shard_map/ppermute | solution.py:354
  231.0 0.0 collective-permute-done.2.far_ref
  231.0 0.6 copy-done.11
  231.6 0.2 copy-done.8
  231.8 2.2 sum_mixes.1
  (10 shorter events, 0.0 us)
Async XLA Ops:
  2.0 15.3 %all-to-all-start = ((f32[16,16,128]{2,1,0:T(8,128)}), f32[16,16,128]{2,1,0:T(8,128)S(1)}, u32[]{:S(2)}, u32[]{:S(2)}) async-start(f32[16,16,128]{2,1,0:T(8,128)} %pack.1), calls=%async_computation | async-start | bytes 262144 | tf_op jit(solution)/shard_map/all_to_all | solution.py:319
  17.3 0.6 copy-start.6
  20.9 3.8 %copy-start.7 = (bf16[128,2048]{1,0:T(8,128)(2,1)S(1)}, bf16[128,2048]{1,0:T(8,128)(2,1)}, u32[]{:S(2)}) copy-start(bf16[128,2048]{1,0:T(8,128)(2,1)} %grad_ref.1) | copy-start | bytes 1572868
  20.9 6.6 %copy-start.10 = (s32[128,16]{0,1:T(8,128)S(1)}, s32[128,16]{0,1:T(8,128)}, u32[]{:S(2)}) copy-start(s32[128,16]{0,1:T(8,128)} %param.11) | copy-start | bytes 24580
  20.9 55.4 %all-to-all-start.1 = ((bf16[16,16,2048]{2,1,0:T(8,128)(2,1)}), bf16[16,16,2048]{2,1,0:T(8,128)(2,1)S(1)}, u32[]{:S(2)}, u32[]{:S(2)}) async-start(bf16[16,16,2048]{2,1,0:T(8,128)(2,1)} %bitcast.16), calls=%async_computation.1 | async-start | bytes 2097152 | tf_op jit(solution)/shard_map/all_to_all | solution.py:319
  24.7 48.9 %collective-permute-start = (bf16[128,2048]{1,0:T(8,128)(2,1)S(1)}, bf16[128,2048]{1,0:T(8,128)(2,1)S(1)}, u32[]{:S(2)}, u32[]{:S(2)}) collective-permute-start(bf16[128,2048]{1,0:T(8,128)(2,1)S(1)} %copy-done.7), channel_id=1, source_target_pairs={{0,8},{1,9},{2,10},{3,11},{4,12},{5,13},{6,14},{7,15},{8,0},{9,1},... | collective-permute-start | bytes 1572872 | tf_op jit(solution)/shard_map/ppermute | solution.py:354
  73.7 0.8 copy-start.5
  76.4 1.0 copy-start.4
  81.4 3.7 %copy-start.12 = (bf16[128,2048]{1,0:T(8,128)(2,1)S(1)}, bf16[128,2048]{1,0:T(8,128)(2,1)}, u32[]{:S(2)}) copy-start(bf16[128,2048]{1,0:T(8,128)(2,1)} %get-tuple-element.22) | copy-start | bytes 1572868
  81.4 35.0 %all-to-all-start.2 = ((bf16[8,48,2048]{2,1,0:T(8,128)(2,1)}), bf16[8,48,2048]{2,1,0:T(8,128)(2,1)S(1)}, u32[]{:S(2)}, u32[]{:S(2)}) async-start(bf16[8,48,2048]{2,1,0:T(8,128)(2,1)} %bitcast.19), calls=%async_computation.2 | async-start | bytes 3145728 | tf_op jit(solution)/shard_map/all_to_all | solution.py:319
  85.1 29.1 %collective-permute-start.1 = (bf16[128,2048]{1,0:T(8,128)(2,1)S(1)}, bf16[128,2048]{1,0:T(8,128)(2,1)S(1)}, u32[]{:S(2)}, u32[]{:S(2)}) collective-permute-start(bf16[128,2048]{1,0:T(8,128)(2,1)S(1)} %copy-done.12), channel_id=1, source_target_pairs={{0,8},{1,9},{2,10},{3,11},{4,12},{5,13},{6,14},{7,15},{8,0},{9,1},... | collective-permute-start | bytes 1572872 | tf_op jit(solution)/shard_map/ppermute | solution.py:354
  114.2 2.1 copy-start.9
  116.3 1.1 copy-start
  120.3 3.7 %copy-start.1 = (bf16[8,48,2048]{2,1,0:T(8,128)(2,1)S(1)}, bf16[8,48,2048]{2,1,0:T(8,128)(2,1)}, u32[]{:S(2)}) copy-start(bf16[8,48,2048]{2,1,0:T(8,128)(2,1)} %copy-done) | copy-start | bytes 4718596
  120.3 27.3 %all-to-all-start.4 = ((bf16[8,48,2048]{2,1,0:T(8,128)(2,1)}), bf16[8,48,2048]{2,1,0:T(8,128)(2,1)S(1)}, u32[]{:S(2)}, u32[]{:S(2)}) async-start(bf16[8,48,2048]{2,1,0:T(8,128)(2,1)} %bitcast.14), calls=%async_computation.4 | async-start | bytes 3145728 | tf_op jit(solution)/shard_map/all_to_all | solution.py:319
  147.6 27.7 %all-to-all-start.3 = ((bf16[8,48,2048]{2,1,0:T(8,128)(2,1)}), bf16[8,48,2048]{2,1,0:T(8,128)(2,1)S(1)}, u32[]{:S(2)}, u32[]{:S(2)}) async-start(bf16[8,48,2048]{2,1,0:T(8,128)(2,1)} %near_experts.1.refs_0_), calls=%async_computation.3 | async-start | bytes 3145728 | tf_op jit(solution)/shard_map/all_to_all | solution.py:319
  174.1 1.2 copy-start.2
  175.3 1.2 copy-start.3
  204.9 26.1 %collective-permute-start.2 = (bf16[128,2048]{1,0:T(8,128)(2,1)}, bf16[128,2048]{1,0:T(8,128)(2,1)S(1)}, u32[]{:S(2)}, u32[]{:S(2)}) collective-permute-start(bf16[128,2048]{1,0:T(8,128)(2,1)} %get-tuple-element.26), channel_id=1, source_target_pairs={{0,8},{1,9},{2,10},{3,11},{4,12},{5,13},{6,14},{7,15},{8,0},{9,1},... | collective-permute-start | bytes 1572872 | tf_op jit(solution)/shard_map/ppermute | solution.py:354
  206.3 24.7 %collective-permute-start.3 = (f32[8,128]{1,0:T(8,128)}, f32[8,128]{1,0:T(8,128)S(1)}, u32[]{:S(2)}, u32[]{:S(2)}) collective-permute-start(f32[8,128]{1,0:T(8,128)} %get-tuple-element.27), channel_id=1, source_target_pairs={{0,8},{1,9},{2,10},{3,11},{4,12},{5,13},{6,14},{7,15},{8,0},{9,1},... | collective-permute-start | bytes 12296 | tf_op jit(solution)/shard_map/ppermute | solution.py:354
  231.0 0.6 copy-start.11
  231.0 0.8 copy-start.8

commit v7 on v6

--- a/solution.py
+++ b/solution.py
@@ -15,6 +15,7 @@
 VMEM = pltpu.VMEM
 F32 = jnp.float32
 BF16 = jnp.bfloat16
+SMALL = pltpu.CompilerParams(vmem_limit_bytes=16 * 1024 * 1024)
 
 
 def dot(a, b):
@@ -77,7 +78,6 @@
     packed_ref,
     scales_ref,
     fetched_ref,
-    grad_ref,
     put_ref,
     near_ref,
     far_ref,
@@ -285,12 +285,14 @@
     )(rows_in, *after, w_gate, w_up, w_down)
 
 
-def mix_kernel(first_column, slots_ref, columns_ref, back_ref, grad_ref, mixed_ref, grads_ref):
-    tok_rows, features = grad_ref.shape
-    count = back_ref.shape[0]
+def mix_kernel(first_column, slots_ref, columns_ref, back_ref, *refs):
+    mixed_ref, grads_ref = refs[-2:]
+    tok_rows = slots_ref.shape[0]
+    count, features = back_ref.shape
+    grad = jnp.concatenate([ref[...] for ref in refs[:-2]], axis=0)
     column = iota((tok_rows, count), 1)
     inner = lax.dot_general(
-        grad_ref[...], back_ref[...], (((1,), (1,)), ((), ())), preferred_element_type=F32
+        grad, back_ref[...], (((1,), (1,)), ((), ())), preferred_element_type=F32
     )
     total = jnp.zeros((tok_rows, count), F32)
     place = iota((tok_rows, tok_rows), 1)
@@ -308,11 +310,6 @@
         rows = back_ref[:, at : at + width]
         mixed_ref[:, at : at + width] = (dot(high, rows) + dot(rest, rows)).astype(mixed_ref.dtype)
     grads_ref[...] = wide.T[: grads_ref.shape[0], :]
-
-
-def sum_kernel(near_ref, near_grads_ref, far_ref, far_grads_ref, mixed_ref, grads_ref):
-    mixed_ref[...] = (near_ref[...] + far_ref[...].astype(F32)).astype(BF16)
-    grads_ref[...] = near_grads_ref[:TOP, :] + far_grads_ref[:TOP, :]
 
 
 def swap(array, groups=None):
@@ -353,15 +350,16 @@
         pairs = [(i, (i + half) % device_count) for i in range(device_count)]
         return lax.ppermute(array, "expert", pairs)
 
-    def ordered(array, earlier_array):
+    def ordered(array, *earlier_arrays):
         return pl.pallas_call(
-            lambda array_ref, earlier_ref, out_ref: None,
+            lambda *refs: None,
             out_shape=shape(array.shape, array.dtype),
-            in_specs=[anywhere, anywhere],
+            in_specs=[anywhere] * (1 + len(earlier_arrays)),
             out_specs=anywhere,
             input_output_aliases={0: 0},
+            compiler_params=SMALL,
             name="ordered",
-        )(array, earlier_array)
+        )(array, *earlier_arrays)
 
     def picked(name, pick, states, *after):
         return pl.pallas_call(
@@ -369,15 +367,18 @@
             out_shape=shape((pick.shape[0], features), BF16),
             in_specs=[vmem, vmem] + [anywhere] * len(after),
             out_specs=vmem,
+            compiler_params=SMALL,
             name=name,
         )(pick, states, *after).reshape(half, 2 * PAIR, features)
 
-    other_grad = mirrored(out_grad)
+    split = tok_rows // 2
+    other_grads = (mirrored(out_grad[:split]), mirrored(out_grad[split:]))
     packed = pl.pallas_call(
         pack_kernel,
         out_shape=shape((device_count, 16, tok_rows), F32),
         in_specs=[vmem] * 3,
         out_specs=vmem,
+        compiler_params=SMALL,
         name="pack",
     )(row_ids[None, :], expert_ids.T, gate_weights.T)
     packed = swap(packed)
@@ -386,6 +387,7 @@
         out_shape=shape((device_count * look_cap, features), BF16),
         in_specs=[smem, vmem, vmem],
         out_specs=vmem,
+        compiler_params=SMALL,
         name="fetch_rows",
     )(place, packed, table)
     returned = swap(fetched.reshape(device_count, look_cap, features))
@@ -399,46 +401,44 @@
             shape((tok_rows, tok_rows), jnp.int32),
             shape((tok_rows, tok_rows), F32),
         ),
-        in_specs=[smem, vmem, vmem, vmem, anywhere, anywhere],
+        in_specs=[smem, vmem, vmem, vmem, anywhere],
         out_specs=(vmem,) * 6,
+        compiler_params=SMALL,
         name="plan",
-    )(place, row_ids[None, :], packed, jnp.exp2(block_exps.T.astype(F32)), fetched, other_grad)
+    )(place, row_ids[None, :], packed, jnp.exp2(block_exps.T.astype(F32)), fetched)
     state, near_sent = pl.pallas_call(
         state_kernel,
         out_shape=(shape((tok_rows, features), BF16), shape((slots, features), BF16)),
         in_specs=[vmem] * 5,
         out_specs=(vmem, vmem),
+        compiler_params=SMALL,
         name="token_state",
     )(put, near_pick, returned.reshape(device_count * look_cap, features), block_values, columns)
     other_state = mirrored(state)
     near_rows = swap(near_sent.reshape(half, 2 * PAIR, features), halves)
-    far_sent = picked("far_slots", far_pick, other_state, near_rows)
+    far_sent = picked("far_slots", far_pick, other_state)
     far_rows = swap(far_sent, halves)
 
     weights = (w_gate, w_up, w_down)
     near_out = expert_call("near_experts", near_rows, weights, after=(far_sent,))
-    far_out = expert_call("far_experts", far_rows, weights, after=(near_out,))
+    far_out = expert_call("far_experts", far_rows, weights, after=(near_out, other_grads[0]))
     near_back = swap(near_out, halves)
-    far_back = swap(ordered(far_out, near_back), halves)
-
-    def mixed_rows(name, first_column, slot_of, back, grad, kind):
+    far_back = swap(ordered(far_out, near_back, other_grads[1]), halves)
+
+    def mixed_rows(name, first_column, slot_of, back, grads, kind):
         return pl.pallas_call(
             functools.partial(mix_kernel, first_column),
             out_shape=(shape((tok_rows, features), kind), shape((2 * TOP, tok_rows), F32)),
-            in_specs=[vmem] * 4,
+            in_specs=[vmem] * (3 + len(grads)),
             out_specs=(vmem, vmem),
+            compiler_params=SMALL,
             name=name,
-        )(slot_of, columns, back.reshape(slots, features), grad)
-
-    near_mixed, near_grads = mixed_rows("mix_near", 0, near_of, near_back, out_grad, F32)
-    far_mixed, far_grads = mixed_rows("mix_far", TOP, far_of, far_back, other_grad, BF16)
-    mixed, grads = pl.pallas_call(
-        sum_kernel,
-        out_shape=(shape((tok_rows, features), BF16), shape((TOP, tok_rows), F32)),
-        in_specs=[vmem] * 4,
-        out_specs=(vmem, vmem),
-        name="sum_mixes",
-    )(near_mixed, near_grads, mirrored(far_mixed), mirrored(far_grads))
+        )(slot_of, columns, back.reshape(slots, features), *grads)
+
+    near_mixed, near_grads = mixed_rows("mix_near", 0, near_of, near_back, (out_grad,), F32)
+    far_mixed, far_grads = mixed_rows("mix_far", TOP, far_of, far_back, other_grads, BF16)
+    mixed = (near_mixed + mirrored(far_mixed).astype(F32)).astype(BF16)
+    grads = (near_grads + mirrored(far_grads))[:TOP]
     return mixed, grads.T
 
 

time: 235 us -> 228 us (0.970)
  Pallas kernels: 68.6 us -> 55.1 us
  starting transfers between devices: 29.1 us -> 36.7 us
  waiting for transfers between devices: 103 us -> 98.5 us
  local copies, waits for them, and re-layouts: 6.76 us -> 10.7 us
    ppermute x4 -> x5, waiting for transfers between devices: 93.4 us -> 68.9 us  [mirrored(): return lax.ppermute(array, 'expert', pairs)]
    all_to_all x5, waiting for transfers between devices: 9.44 us -> 29.6 us  [swap(): lax.all_to_all(array, 'expert', split_axis=0, concat_axis=0, tiled=True,...]
    all_to_all x5, starting transfers between devices: 22.7 us -> 27.9 us  [swap(): lax.all_to_all(array, 'expert', split_axis=0, concat_axis=0, tiled=True,...]
    pallas_call x2, Pallas kernels: 7.42 us -> 2.45 us  [mixed_rows(): pl.pallas_call(functools.partial(mix_kernel, first_column), out_shape=(sh...]
    unnamed x26 -> x38, local copies, waits for them, and re-layouts: 6.76 us -> 10.1 us
    pallas_call x1, Pallas kernels: 4.01 us -> 1.34 us  [near_path(): pl.pallas_call(state_kernel, out_shape=(shape((tok_rows, features), BF16)...]
    ppermute x4 -> x5, starting transfers between devices: 6.4 us -> 8.79 us  [mirrored(): return lax.ppermute(array, 'expert', pairs)]
  transfers between devices with their start and end apart: 9 -> 10, of which waited for: 5 -> 6; matrix products, arithmetic and copies ran while one was open for 1% -> 0% of each run, Pallas kernels for 22% -> 22%
where the time goes in v7:
time: 228 us
  waiting for transfers between devices  98.5 us (43%)
  Pallas kernels  55.1 us (24%)
  starting transfers between devices  36.7 us (16%)
  blocking collectives  24.7 us (11%)
  local copies, waits for them, and re-layouts  10.7 us (5%)
    ppermute x5, waiting for transfers between devices, mirrored(): return lax.ppermute(array, 'expert', pairs)  68.9 us
    pallas_call x2, Pallas kernels, expert_call(): pl.pallas_call(functools.partial(expert_kernel, len(after)), out_shape=ja...  45.9 us
    all_to_all x5, waiting for transfers between devices, swap(): lax.all_to_all(array, 'expert', split_axis=0, concat_axis=0, tiled=True,...  29.6 us
    all_to_all x5, starting transfers between devices, swap(): lax.all_to_all(array, 'expert', split_axis=0, concat_axis=0, tiled=True,...  27.9 us
    all_to_all x1, blocking collectives, swap(): lax.all_to_all(array, 'expert', split_axis=0, concat_axis=0, tiled=True,...  24.7 us
    unnamed x38, local copies, waits for them, and re-layouts  10.1 us
    ppermute x5, starting transfers between devices, mirrored(): return lax.ppermute(array, 'expert', pairs)  8.79 us
  transfers between devices with their start and end apart: 10, of which 6 were waited for; matrix products, arithmetic and copies ran while one was open for 0% of the time, Pallas kernels for 22%

profile of v7, /device:TPU:0, one launch (start us, length us, event | category | flops | bytes accessed | tf_op | source)
XLA Modules:
  0.0 227.6 jit_solution(13209499757888859387)
XLA Ops:
  0.6 0.0 copy-start.12
  0.6 0.7 copy-done.12
  1.3 0.7 copy-done.13
  2.0 0.7 copy-done.14
  2.7 0.7 pack.1
  3.3 7.4 %all-to-all-start = ((f32[16,16,128]{2,1,0:T(8,128)}), f32[16,16,128]{2,1,0:T(8,128)S(1)}, u32[]{:S(2)}, u32[]{:S(2)}) async-start(f32[16,16,128]{2,1,0:T(8,128)} %pack.1), calls=%async_computation | async-start | bytes 262144 | tf_op jit(solution)/shard_map/all_to_all | solution.py:316
  10.7 0.1 pad_add_fusion.me_ref
  10.8 7.9 %all-to-all-done.packed_ref = f32[16,16,128]{2,1,0:T(8,128)S(1)} async-done(((f32[16,16,128]{2,1,0:T(8,128)}), f32[16,16,128]{2,1,0:T(8,128)S(1)}, u32[]{:S(2)}, u32[]{:S(2)}) %all-to-all-start) | async-done | bytes 131104 | tf_op jit(solution)/shard_map/all_to_all | solution.py:316
  18.6 1.2 copy-done.8
  19.9 2.2 fetch_rows.1.fetched_ref
  22.0 3.8 %all-to-all-start.1 = ((bf16[16,16,2048]{2,1,0:T(8,128)(2,1)}), bf16[16,16,2048]{2,1,0:T(8,128)(2,1)S(1)}, u32[]{:S(2)}, u32[]{:S(2)}) async-start(bf16[16,16,2048]{2,1,0:T(8,128)(2,1)} %bitcast.5), calls=%async_computation.1 | async-start | bytes 2097152 | tf_op jit(solution)/shard_map/all_to_all | solution.py:316
  25.9 0.9 plan.1
  26.8 0.6 copy-done.10
  27.4 21.3 %all-to-all-done.1 = bf16[16,16,2048]{2,1,0:T(8,128)(2,1)S(1)} async-done(((bf16[16,16,2048]{2,1,0:T(8,128)(2,1)}), bf16[16,16,2048]{2,1,0:T(8,128)(2,1)S(1)}, u32[]{:S(2)}, u32[]{:S(2)}) %all-to-all-start.1) | async-done | bytes 1048608 | tf_op jit(solution)/shard_map/all_to_all | solution.py:316
  48.7 1.3 token_state.1
  50.1 0.0 copy-start.16
  50.1 0.8 copy-done.16
  50.9 1.2 copy-done.4
  52.1 6.0 %all-to-all-start.2 = ((bf16[8,48,2048]{2,1,0:T(8,128)(2,1)}), bf16[8,48,2048]{2,1,0:T(8,128)(2,1)S(1)}, u32[]{:S(2)}, u32[]{:S(2)}) async-start(bf16[8,48,2048]{2,1,0:T(8,128)(2,1)} %bitcast.17), calls=%async_computation.2 | async-start | bytes 3145728 | tf_op jit(solution)/shard_map/all_to_all | solution.py:316
  58.1 2.8 %collective-permute-start = (bf16[128,2048]{1,0:T(8,128)(2,1)S(1)}, bf16[128,2048]{1,0:T(8,128)(2,1)S(1)}, u32[]{:S(2)}, u32[]{:S(2)}) collective-permute-start(bf16[128,2048]{1,0:T(8,128)(2,1)S(1)} %copy-done.17), channel_id=1, source_target_pairs={{0,8},{1,9},{2,10},{3,11},{4,12},{5,13},{6,14},{7,15},{8,0},{9,1},... | collective-permute-start | bytes 1572872 | tf_op jit(solution)/shard_map/ppermute | solution.py:351
  60.9 26.4 %collective-permute-done.state_ref = bf16[128,2048]{1,0:T(8,128)(2,1)S(1)} collective-permute-done((bf16[128,2048]{1,0:T(8,128)(2,1)S(1)}, bf16[128,2048]{1,0:T(8,128)(2,1)S(1)}, u32[]{:S(2)}, u32[]{:S(2)}) %collective-permute-start) | collective-permute-done | bytes 524320 | tf_op jit(solution)/shard_map/ppermute | solution.py:351
  87.3 1.7 far_slots.1
  89.0 0.4 all-to-all-done.2.rows_ref
  89.4 6.6 %all-to-all-start.4 = ((bf16[8,48,2048]{2,1,0:T(8,128)(2,1)}), bf16[8,48,2048]{2,1,0:T(8,128)(2,1)S(1)}, u32[]{:S(2)}, u32[]{:S(2)}) async-start(bf16[8,48,2048]{2,1,0:T(8,128)(2,1)} %bitcast.8.refs_0_), calls=%async_computation.4 | async-start | bytes 3145728 | tf_op jit(solution)/shard_map/all_to_all | solution.py:316
  96.0 23.5 %near_experts.1.refs_0_ = bf16[8,48,2048]{2,1,0:T(8,128)(2,1)} custom-call(bf16[8,48,2048]{2,1,0:T(8,128)(2,1)S(1)} %all-to-all-done.2.rows_ref, bf16[8,48,2048]{2,1,0:T(8,128)(2,1)} %bitcast.8.refs_0_, bf16[4,2048,1408]{2,1,0:T(8,128)(2,1)} %refs_2_.3, bf16[4,2048,1408]{2,1,0:T(8,128)(2,1)} %refs_3_.3, bf16[4,1408,2048]{2,1,0:T(8,128)(2,1)} %refs_4_.1), custom_call_target="tpu_custom_call" | custom-call | flops 13287555072 | bytes 69206016 | tf_op jit(solution)/shard_map/near_experts/pallas_call | solution.py:264
  119.5 0.0 copy-start.2
  119.5 0.0 all-to-all-done.4.rows_ref
  119.6 1.1 copy-done
  120.7 4.2 %all-to-all-start.3 = ((bf16[8,48,2048]{2,1,0:T(8,128)(2,1)}), bf16[8,48,2048]{2,1,0:T(8,128)(2,1)S(1)}, u32[]{:S(2)}, u32[]{:S(2)}) async-start(bf16[8,48,2048]{2,1,0:T(8,128)(2,1)} %near_experts.1.refs_0_), calls=%async_computation.3 | async-start | bytes 3145728 | tf_op jit(solution)/shard_map/all_to_all | solution.py:316
  125.0 0.1 collective-permute-start.1
  125.0 2.9 %collective-permute-start.2 = (bf16[64,2048]{1,0:T(8,128)(2,1)S(1)}, bf16[64,2048]{1,0:T(8,128)(2,1)S(1)}, u32[]{:S(2)}, u32[]{:S(2)}) collective-permute-start(bf16[64,2048]{1,0:T(8,128)(2,1)S(1)} %get-tuple-element.26), channel_id=1, source_target_pairs={{0,8},{1,9},{2,10},{3,11},{4,12},{5,13},{6,14},{7,15},{8,0},{9,1},... | collective-permute-start | bytes 786440 | tf_op jit(solution)/shard_map/ppermute | solution.py:351
  128.0 20.8 %collective-permute-done.1.refs_1_.refs_0_ = bf16[64,2048]{1,0:T(8,128)(2,1)S(1)} collective-permute-done((bf16[64,2048]{1,0:T(8,128)(2,1)S(1)}, bf16[64,2048]{1,0:T(8,128)(2,1)S(1)}, u32[]{:S(2)}, u32[]{:S(2)}) %collective-permute-start.1) | collective-permute-done | bytes 262176 | tf_op jit(solution)/shard_map/ppermute | solution.py:351
  148.7 1.4 copy-done.1
  150.1 22.4 %far_experts.1.refs_0_ = bf16[8,48,2048]{2,1,0:T(8,128)(2,1)S(1)} custom-call(bf16[8,48,2048]{2,1,0:T(8,128)(2,1)S(1)} %copy-done.1, bf16[8,48,2048]{2,1,0:T(8,128)(2,1)} %near_experts.1.refs_0_, bf16[64,2048]{1,0:T(8,128)(2,1)S(1)} %collective-permute-done.1.refs_1_.refs_0_, bf16[4,2048,1408]{2,1,0:T(8,128)(2,1)} %refs_2_.3, ...), custom_call_target="tpu_custom_call" | custom-call | flops 13287555072 | bytes 69206016 | tf_op jit(solution)/shard_map/far_experts/pallas_call | solution.py:264
  172.5 0.0 collective-permute-done.2.refs_2_.refs_1_
  172.5 0.0 copy-start.5
  172.5 0.7 copy-done.5
  173.2 0.0 all-to-all-done.3.refs_1_
  173.2 0.9 copy-done.6
  174.2 24.7 %all_to_all.30 = bf16[8,48,2048]{2,1,0:T(8,128)(2,1)S(1)} all-to-all(bf16[8,48,2048]{2,1,0:T(8,128)(2,1)S(1)} %ordered.1), channel_id=1, replica_groups={{0,1,2,3,4,5,6,7},{8,9,10,11,12,13,14,15},{16,17,18,19,20,21,22,23},{24..., dimensions={0} | all-to-all | bytes 3145728 | tf_op jit(solution)/shard_map/all_to_all | solution.py:316
  198.9 1.2 mix_far.1
  200.1 2.1 collective-permute-start.3
  202.2 0.9 collective-permute-start.4
  203.1 1.2 mix_near.1
  204.3 21.7 %collective-permute-done.4 = f32[8,128]{1,0:T(8,128)S(1)} collective-permute-done((f32[8,128]{1,0:T(8,128)S(1)}, f32[8,128]{1,0:T(8,128)S(1)}, u32[]{:S(2)}, u32[]{:S(2)}) %collective-permute-start.4) | collective-permute-done | bytes 4128 | tf_op jit(solution)/shard_map/ppermute | solution.py:351
  226.1 0.6 slice_bitcast_fusion
  226.7 0.0 collective-permute-done.3
  226.7 0.9 add_convert_fusion
  (27 shorter events, 0.1 us)
Async XLA Ops:
  0.6 0.7 copy-start.12
  1.3 0.7 copy-start.13
  2.0 0.7 copy-start.14
  3.3 15.3 %all-to-all-start = ((f32[16,16,128]{2,1,0:T(8,128)}), f32[16,16,128]{2,1,0:T(8,128)S(1)}, u32[]{:S(2)}, u32[]{:S(2)}) async-start(f32[16,16,128]{2,1,0:T(8,128)} %pack.1), calls=%async_computation | async-start | bytes 262144 | tf_op jit(solution)/shard_map/all_to_all | solution.py:316
  18.6 1.2 copy-start.8
  22.0 3.8 %copy-start.18 = (s32[128,16]{0,1:T(8,128)S(1)}, s32[128,16]{0,1:T(8,128)}, u32[]{:S(2)}) copy-start(s32[128,16]{0,1:T(8,128)} %param.11) | copy-start | bytes 24580
  22.0 3.8 %copy-start.15 = (s32[128]{0:T(128)S(1)}, s32[128]{0:T(128)}, u32[]{:S(2)}) copy-start(s32[128]{0:T(128)} %param.12) | copy-start | bytes 1540
  22.0 26.7 %copy-start.9 = (bf16[128,2048]{1,0:T(8,128)(2,1)S(1)}, bf16[128,2048]{1,0:T(8,128)(2,1)}, u32[]{:S(2)}) copy-start(bf16[128,2048]{1,0:T(8,128)(2,1)} %values_ref.1) | copy-start | bytes 1572868
  22.0 26.7 %all-to-all-start.1 = ((bf16[16,16,2048]{2,1,0:T(8,128)(2,1)}), bf16[16,16,2048]{2,1,0:T(8,128)(2,1)S(1)}, u32[]{:S(2)}, u32[]{:S(2)}) async-start(bf16[16,16,2048]{2,1,0:T(8,128)(2,1)} %bitcast.5), calls=%async_computation.1 | async-start | bytes 2097152 | tf_op jit(solution)/shard_map/all_to_all | solution.py:316
  26.8 0.6 copy-start.10
  50.1 0.8 copy-start.16
  50.9 1.2 copy-start.4
  52.1 6.0 %copy-start.17 = (bf16[128,2048]{1,0:T(8,128)(2,1)S(1)}, bf16[128,2048]{1,0:T(8,128)(2,1)}, u32[]{:S(2)}) copy-start(bf16[128,2048]{1,0:T(8,128)(2,1)} %copy-done.16) | copy-start | bytes 1572868
  52.1 37.3 %all-to-all-start.2 = ((bf16[8,48,2048]{2,1,0:T(8,128)(2,1)}), bf16[8,48,2048]{2,1,0:T(8,128)(2,1)S(1)}, u32[]{:S(2)}, u32[]{:S(2)}) async-start(bf16[8,48,2048]{2,1,0:T(8,128)(2,1)} %bitcast.17), calls=%async_computation.2 | async-start | bytes 3145728 | tf_op jit(solution)/shard_map/all_to_all | solution.py:316
  58.1 29.2 %collective-permute-start = (bf16[128,2048]{1,0:T(8,128)(2,1)S(1)}, bf16[128,2048]{1,0:T(8,128)(2,1)S(1)}, u32[]{:S(2)}, u32[]{:S(2)}) collective-permute-start(bf16[128,2048]{1,0:T(8,128)(2,1)S(1)} %copy-done.17), channel_id=1, source_target_pairs={{0,8},{1,9},{2,10},{3,11},{4,12},{5,13},{6,14},{7,15},{8,0},{9,1},... | collective-permute-start | bytes 1572872 | tf_op jit(solution)/shard_map/ppermute | solution.py:351
  89.4 30.1 %all-to-all-start.4 = ((bf16[8,48,2048]{2,1,0:T(8,128)(2,1)}), bf16[8,48,2048]{2,1,0:T(8,128)(2,1)S(1)}, u32[]{:S(2)}, u32[]{:S(2)}) async-start(bf16[8,48,2048]{2,1,0:T(8,128)(2,1)} %bitcast.8.refs_0_), calls=%async_computation.4 | async-start | bytes 3145728 | tf_op jit(solution)/shard_map/all_to_all | solution.py:316
  119.5 5.4 %copy-start.2 = (bf16[128,2048]{1,0:T(8,128)(2,1)S(1)}, bf16[128,2048]{1,0:T(8,128)(2,1)}, u32[]{:S(2)}) copy-start(bf16[128,2048]{1,0:T(8,128)(2,1)} %refs_0_.1) | copy-start | bytes 1572868
  119.5 1.2 copy-start
  120.7 52.5 %all-to-all-start.3 = ((bf16[8,48,2048]{2,1,0:T(8,128)(2,1)}), bf16[8,48,2048]{2,1,0:T(8,128)(2,1)S(1)}, u32[]{:S(2)}, u32[]{:S(2)}) async-start(bf16[8,48,2048]{2,1,0:T(8,128)(2,1)} %near_experts.1.refs_0_), calls=%async_computation.3 | async-start | bytes 3145728 | tf_op jit(solution)/shard_map/all_to_all | solution.py:316
  125.0 23.8 %collective-permute-start.1 = (bf16[64,2048]{1,0:T(8,128)(2,1)S(1)}, bf16[64,2048]{1,0:T(8,128)(2,1)S(1)}, u32[]{:S(2)}, u32[]{:S(2)}) collective-permute-start(bf16[64,2048]{1,0:T(8,128)(2,1)S(1)} %get-tuple-element.27), channel_id=1, source_target_pairs={{0,8},{1,9},{2,10},{3,11},{4,12},{5,13},{6,14},{7,15},{8,0},{9,1},... | collective-permute-start | bytes 786440 | tf_op jit(solution)/shard_map/ppermute | solution.py:351
  125.0 47.4 %collective-permute-start.2 = (bf16[64,2048]{1,0:T(8,128)(2,1)S(1)}, bf16[64,2048]{1,0:T(8,128)(2,1)S(1)}, u32[]{:S(2)}, u32[]{:S(2)}) collective-permute-start(bf16[64,2048]{1,0:T(8,128)(2,1)S(1)} %get-tuple-element.26), channel_id=1, source_target_pairs={{0,8},{1,9},{2,10},{3,11},{4,12},{5,13},{6,14},{7,15},{8,0},{9,1},... | collective-permute-start | bytes 786440 | tf_op jit(solution)/shard_map/ppermute | solution.py:351
  148.7 1.4 copy-start.1
  172.5 0.7 copy-start.5
  173.2 1.0 copy-start.6
  174.2 24.7 %copy-start.7 = (bf16[64,2048]{1,0:T(8,128)(2,1)S(1)}, bf16[64,2048]{1,0:T(8,128)(2,1)}, u32[]{:S(2)}) copy-start(bf16[64,2048]{1,0:T(8,128)(2,1)} %copy-done.5) | copy-start | bytes 786436
  174.2 24.7 %copy-start.11 = (s32[128,128]{1,0:T(8,128)S(1)}, s32[128,128]{1,0:T(8,128)}, u32[]{:S(2)}) copy-start(s32[128,128]{1,0:T(8,128)} %copy-done.10) | copy-start | bytes 196612
  198.9 4.2 %copy-start.3 = (bf16[128,2048]{1,0:T(8,128)(2,1)S(1)}, bf16[128,2048]{1,0:T(8,128)(2,1)}, u32[]{:S(2)}) copy-start(bf16[128,2048]{1,0:T(8,128)(2,1)} %refs_0_.1) | copy-start | bytes 1572868
  200.1 26.6 %collective-permute-start.3 = (bf16[128,2048]{1,0:T(8,128)(2,1)S(1)}, bf16[128,2048]{1,0:T(8,128)(2,1)S(1)}, u32[]{:S(2)}, u32[]{:S(2)}) collective-permute-start(bf16[128,2048]{1,0:T(8,128)(2,1)S(1)} %get-tuple-element.23), channel_id=1, source_target_pairs={{0,8},{1,9},{2,10},{3,11},{4,12},{5,13},{6,14},{7,15},{8,0},{9,1},... | collective-permute-start | bytes 1572872 | tf_op jit(solution)/shard_map/ppermute | solution.py:351
  202.2 23.8 %collective-permute-start.4 = (f32[8,128]{1,0:T(8,128)S(1)}, f32[8,128]{1,0:T(8,128)S(1)}, u32[]{:S(2)}, u32[]{:S(2)}) collective-permute-start(f32[8,128]{1,0:T(8,128)S(1)} %get-tuple-element.25), channel_id=1, source_target_pairs={{0,8},{1,9},{2,10},{3,11},{4,12},{5,13},{6,14},{7,15},{8,0},{9,1},... | collective-permute-start | bytes 12296 | tf_op jit(solution)/shard_map/ppermute | solution.py:351

commit v8 on v7

--- a/solution.py
+++ b/solution.py
@@ -144,9 +144,22 @@
     )
 
 
-def state_kernel(put_ref, pick_ref, returned_ref, values_ref, columns_ref, state_ref, out_ref):
+def pick_slots(pick_ref, state_ref, out_hbm, sent_ref, sem, left, width):
+    cols = pl.ds(left, width)
+    sent_ref[:, cols] = dot(pick_ref[...], state_ref[:, cols]).astype(BF16)
+    copy = pltpu.make_async_copy(
+        sent_ref.at[:, cols], out_hbm.at[:, cols], sem.at[left // width]
+    )
+    copy.start()
+    return copy
+
+
+def state_kernel(
+    put_ref, pick_ref, returned_ref, values_ref, columns_ref, state_ref, out_hbm, sent_ref, sem
+):
     features = values_ref.shape[1]
-    width = 512
+    width = features // sem.shape[0]
+    copies = []
     for left in range(0, features, width):
         found = dot(put_ref[...], returned_ref[:, left : left + width])
         for b in range(width // BLOCK):
@@ -158,17 +171,20 @@
             state_ref[:, at : at + BLOCK] = (
                 scaled + found[:, b * BLOCK : (b + 1) * BLOCK]
             ).astype(BF16)
-        cols = slice(left, left + width)
-        out_ref[:, cols] = dot(pick_ref[...], state_ref[:, cols]).astype(BF16)
-
-
-def pick_kernel(pick_ref, state_ref, *refs):
-    out_ref = refs[-1]
+        copies.append(pick_slots(pick_ref, state_ref, out_hbm, sent_ref, sem, left, width))
+    for copy in copies:
+        copy.wait()
+
+
+def pick_kernel(pick_ref, state_ref, out_hbm, sent_ref, sem):
     features = state_ref.shape[1]
-    width = 512
-    for left in range(0, features, width):
-        cols = slice(left, left + width)
-        out_ref[:, cols] = dot(pick_ref[...], state_ref[:, cols]).astype(BF16)
+    width = features // sem.shape[0]
+    copies = [
+        pick_slots(pick_ref, state_ref, out_hbm, sent_ref, sem, left, width)
+        for left in range(0, features, width)
+    ]
+    for copy in copies:
+        copy.wait()
 
 
 def expert_kernel(after, rows_ref, *refs):
@@ -275,7 +291,7 @@
             VMEM((exp_dev, rows, features), F32),
             pltpu.SemaphoreType.DMA((held, 10)),
         ],
-        compiler_params=pltpu.CompilerParams(vmem_limit_bytes=50 * 1024 * 1024),
+        compiler_params=pltpu.CompilerParams(vmem_limit_bytes=43 * 1024 * 1024),
         cost_estimate=pl.CostEstimate(
             flops=12 * exp_dev * rows * features * width,
             bytes_accessed=6 * exp_dev * features * width,
@@ -361,16 +377,6 @@
             name="ordered",
         )(array, *earlier_arrays)
 
-    def picked(name, pick, states, *after):
-        return pl.pallas_call(
-            pick_kernel,
-            out_shape=shape((pick.shape[0], features), BF16),
-            in_specs=[vmem, vmem] + [anywhere] * len(after),
-            out_specs=vmem,
-            compiler_params=SMALL,
-            name=name,
-        )(pick, states, *after).reshape(half, 2 * PAIR, features)
-
     split = tok_rows // 2
     other_grads = (mirrored(out_grad[:split]), mirrored(out_grad[split:]))
     packed = pl.pallas_call(
@@ -378,7 +384,6 @@
         out_shape=shape((device_count, 16, tok_rows), F32),
         in_specs=[vmem] * 3,
         out_specs=vmem,
-        compiler_params=SMALL,
         name="pack",
     )(row_ids[None, :], expert_ids.T, gate_weights.T)
     packed = swap(packed)
@@ -406,23 +411,37 @@
         compiler_params=SMALL,
         name="plan",
     )(place, row_ids[None, :], packed, jnp.exp2(block_exps.T.astype(F32)), fetched)
+    sent_shape = pltpu.HBM((slots, features), BF16)
+    sent_scratch = [VMEM((slots, features), BF16), pltpu.SemaphoreType.DMA((4,))]
     state, near_sent = pl.pallas_call(
         state_kernel,
-        out_shape=(shape((tok_rows, features), BF16), shape((slots, features), BF16)),
+        out_shape=(shape((tok_rows, features), BF16), sent_shape),
         in_specs=[vmem] * 5,
-        out_specs=(vmem, vmem),
+        out_specs=(vmem, anywhere),
+        scratch_shapes=sent_scratch,
         compiler_params=SMALL,
         name="token_state",
     )(put, near_pick, returned.reshape(device_count * look_cap, features), block_values, columns)
     other_state = mirrored(state)
     near_rows = swap(near_sent.reshape(half, 2 * PAIR, features), halves)
-    far_sent = picked("far_slots", far_pick, other_state)
+    far_sent = pl.pallas_call(
+        pick_kernel,
+        out_shape=sent_shape,
+        in_specs=[vmem, vmem],
+        out_specs=anywhere,
+        scratch_shapes=sent_scratch,
+        compiler_params=SMALL,
+        cost_estimate=pl.CostEstimate(
+            flops=20_000_000_000, bytes_accessed=4 * slots * features, transcendentals=0
+        ),
+        name="far_slots",
+    )(far_pick, other_state).reshape(half, 2 * PAIR, features)
     far_rows = swap(far_sent, halves)
 
     weights = (w_gate, w_up, w_down)
     near_out = expert_call("near_experts", near_rows, weights, after=(far_sent,))
-    far_out = expert_call("far_experts", far_rows, weights, after=(near_out, other_grads[0]))
-    near_back = swap(near_out, halves)
+    far_out = expert_call("far_experts", far_rows, weights, after=(near_out,))
+    near_back = swap(ordered(near_out, other_grads[0]), halves)
     far_back = swap(ordered(far_out, near_back, other_grads[1]), halves)
 
     def mixed_rows(name, first_column, slot_of, back, grads, kind):

time: 228 us -> 208 us (0.912)
  waiting for transfers between devices: 98.5 us -> 78 us
    ppermute x5, waiting for transfers between devices: 68.9 us -> 48.2 us  [mirrored(): return lax.ppermute(array, 'expert', pairs)]
    unnamed x38 -> x29, local copies, waits for them, and re-layouts: 10.1 us -> 9.64 us
  transfers between devices with their start and end apart: 10 -> 10, of which waited for: 6 -> 5; matrix products, arithmetic and copies ran while one was open for 0% -> 2% of each run, Pallas kernels for 22% -> 23%
where the time goes in v8:
time: 208 us
  waiting for transfers between devices  78 us (38%)
  Pallas kernels  55.2 us (27%)
  starting transfers between devices  36.3 us (17%)
  blocking collectives  24.4 us (12%)
  local copies, waits for them, and re-layouts  12 us (6%)
    ppermute x5, waiting for transfers between devices, mirrored(): return lax.ppermute(array, 'expert', pairs)  48.2 us
    pallas_call x2, Pallas kernels, expert_call(): pl.pallas_call(functools.partial(expert_kernel, len(after)), out_shape=ja...  44.7 us
    all_to_all x5, waiting for transfers between devices, swap(): lax.all_to_all(array, 'expert', split_axis=0, concat_axis=0, tiled=True,...  29.8 us
    all_to_all x5, starting transfers between devices, swap(): lax.all_to_all(array, 'expert', split_axis=0, concat_axis=0, tiled=True,...  27.5 us
    all_to_all x1, blocking collectives, swap(): lax.all_to_all(array, 'expert', split_axis=0, concat_axis=0, tiled=True,...  24.4 us
    unnamed x29, local copies, waits for them, and re-layouts  9.64 us
    ppermute x5, starting transfers between devices, mirrored(): return lax.ppermute(array, 'expert', pairs)  8.76 us
  transfers between devices with their start and end apart: 10, of which 5 were waited for; matrix products, arithmetic and copies ran while one was open for 2% of the time, Pallas kernels for 23%

profile of v8, /device:TPU:0, one launch (start us, length us, event | category | flops | bytes accessed | tf_op | source)
XLA Modules:
  0.0 207.8 jit_solution(18040559215614853409)
XLA Ops:
  0.6 1.4 pack.1
  2.0 7.4 %all-to-all-start = ((f32[16,16,128]{2,1,0:T(8,128)}), f32[16,16,128]{2,1,0:T(8,128)S(1)}, u32[]{:S(2)}, u32[]{:S(2)}) async-start(f32[16,16,128]{2,1,0:T(8,128)} %pack.1), calls=%async_computation | async-start | bytes 262144 | tf_op jit(solution)/shard_map/all_to_all | solution.py:332
  9.4 0.1 pad_add_fusion.me_ref
  9.5 7.9 %all-to-all-done.packed_ref = f32[16,16,128]{2,1,0:T(8,128)S(1)} async-done(((f32[16,16,128]{2,1,0:T(8,128)}), f32[16,16,128]{2,1,0:T(8,128)S(1)}, u32[]{:S(2)}, u32[]{:S(2)}) %all-to-all-start) | async-done | bytes 131104 | tf_op jit(solution)/shard_map/all_to_all | solution.py:332
  17.3 1.2 copy-done.6
  18.6 2.2 %fetch_rows.1.fetched_ref = bf16[256,2048]{1,0:T(8,128)(2,1)} custom-call(s32[2]{0:T(128)S(1)} %pad_add_fusion.me_ref, f32[16,16,128]{2,1,0:T(8,128)S(1)} %all-to-all-done.packed_ref, bf16[256,2048]{1,0:T(8,128)(2,1)S(1)} %copy-done.6), custom_call_target="tpu_custom_call" | custom-call | tf_op jit(solution)/shard_map/fetch_rows/pallas_call | solution.py:390
  20.7 3.8 %all-to-all-start.1 = ((bf16[16,16,2048]{2,1,0:T(8,128)(2,1)}), bf16[16,16,2048]{2,1,0:T(8,128)(2,1)S(1)}, u32[]{:S(2)}, u32[]{:S(2)}) async-start(bf16[16,16,2048]{2,1,0:T(8,128)(2,1)} %bitcast.5), calls=%async_computation.1 | async-start | bytes 2097152 | tf_op jit(solution)/shard_map/all_to_all | solution.py:332
  24.5 0.0 copy-done.13
  24.6 0.0 copy-done.12
  24.6 0.9 plan.1
  25.5 0.6 copy-done.10
  26.1 21.3 %all-to-all-done.1 = bf16[16,16,2048]{2,1,0:T(8,128)(2,1)S(1)} async-done(((bf16[16,16,2048]{2,1,0:T(8,128)(2,1)}), bf16[16,16,2048]{2,1,0:T(8,128)(2,1)S(1)}, u32[]{:S(2)}, u32[]{:S(2)}) %all-to-all-start.1) | async-done | bytes 1048608 | tf_op jit(solution)/shard_map/all_to_all | solution.py:332
  47.4 2.2 %token_state.1 = (bf16[128,2048]{1,0:T(8,128)(2,1)S(1)}, bf16[384,2048]{1,0:T(8,128)(2,1)}) custom-call(bf16[128,256]{1,0:T(8,128)(2,1)S(1)} %get-tuple-element.16.put_ref, bf16[384,128]{1,0:T(8,128)(2,1)S(1)} %get-tuple-element.17.pick_ref, bf16[256,2048]{1,0:T(8,128)(2,1)S(1)} %bitcast.18, bf16[128,2048]{1,0:T(8,128)(2,1)S(1)} %copy-done.9, ...), custom_call_target="tpu_custom_call" | custom-call | tf_op jit(solution)/shard_map/token_state/pallas_call | solution.py:416
  49.6 5.9 %all-to-all-start.2 = ((bf16[8,48,2048]{2,1,0:T(8,128)(2,1)}), bf16[8,48,2048]{2,1,0:T(8,128)(2,1)S(1)}, u32[]{:S(2)}, u32[]{:S(2)}) async-start(bf16[8,48,2048]{2,1,0:T(8,128)(2,1)} %bitcast.21), calls=%async_computation.2 | async-start | bytes 3145728 | tf_op jit(solution)/shard_map/all_to_all | solution.py:332
  55.5 2.8 %collective-permute-start = (bf16[128,2048]{1,0:T(8,128)(2,1)S(1)}, bf16[128,2048]{1,0:T(8,128)(2,1)S(1)}, u32[]{:S(2)}, u32[]{:S(2)}) collective-permute-start(bf16[128,2048]{1,0:T(8,128)(2,1)S(1)} %get-tuple-element.20), channel_id=1, source_target_pairs={{0,8},{1,9},{2,10},{3,11},{4,12},{5,13},{6,14},{7,15},{8,0},{9,1},... | collective-permute-start | bytes 1572872 | tf_op jit(solution)/shard_map/ppermute | solution.py:367
  58.3 26.4 %collective-permute-done.state_ref = bf16[128,2048]{1,0:T(8,128)(2,1)S(1)} collective-permute-done((bf16[128,2048]{1,0:T(8,128)(2,1)S(1)}, bf16[128,2048]{1,0:T(8,128)(2,1)S(1)}, u32[]{:S(2)}, u32[]{:S(2)}) %collective-permute-start) | collective-permute-done | bytes 524320 | tf_op jit(solution)/shard_map/ppermute | solution.py:367
  84.7 1.4 far_slots.1
  86.2 0.6 all-to-all-done.2.rows_ref
  86.8 6.3 %all-to-all-start.4 = ((bf16[8,48,2048]{2,1,0:T(8,128)(2,1)}), bf16[8,48,2048]{2,1,0:T(8,128)(2,1)S(1)}, u32[]{:S(2)}, u32[]{:S(2)}) async-start(bf16[8,48,2048]{2,1,0:T(8,128)(2,1)} %bitcast.16), calls=%async_computation.4 | async-start | bytes 3145728 | tf_op jit(solution)/shard_map/all_to_all | solution.py:332
  93.2 1.8 fusion
  94.9 0.0 collective-permute-start.1
  95.0 1.4 copy-done.4
  96.4 22.4 %near_experts.1.refs_0_ = bf16[8,48,2048]{2,1,0:T(8,128)(2,1)S(1)} custom-call(bf16[8,48,2048]{2,1,0:T(8,128)(2,1)S(1)} %all-to-all-done.2.rows_ref, bf16[8,48,2048]{2,1,0:T(8,128)(2,1)S(1)} %bitcast.17, bf16[4,2048,1408]{2,1,0:T(8,128)(2,1)} %refs_1_.3, bf16[4,2048,1408]{2,1,0:T(8,128)(2,1)} %refs_2_.3, bf16[4,1408,2048]{2,1,0:T(8,128)(2,1)} %refs_3_.3), custom_call_target="tpu_custom_call" | custom-call | flops 13287555072 | bytes 69206016 | tf_op jit(solution)/shard_map/near_experts/pallas_call | solution.py:280
  118.8 1.2 copy.14.refs_0_
  119.9 0.5 copy-done
  120.4 0.0 collective-permute-done.1.refs_1_.refs_0_
  120.4 0.7 copy-done.7
  121.1 0.0 all-to-all-done.4.rows_ref
  121.1 1.2 copy-done.2
  122.3 4.2 %all-to-all-start.3 = ((bf16[8,48,2048]{2,1,0:T(8,128)(2,1)}), bf16[8,48,2048]{2,1,0:T(8,128)(2,1)S(1)}, u32[]{:S(2)}, u32[]{:S(2)}) async-start(bf16[8,48,2048]{2,1,0:T(8,128)(2,1)} %ordered.2), calls=%async_computation.3 | async-start | bytes 3145728 | tf_op jit(solution)/shard_map/all_to_all | solution.py:332
  126.5 2.9 %collective-permute-start.2 = (bf16[64,2048]{1,0:T(8,128)(2,1)}, bf16[64,2048]{1,0:T(8,128)(2,1)S(1)}, u32[]{:S(2)}, u32[]{:S(2)}) collective-permute-start(bf16[64,2048]{1,0:T(8,128)(2,1)} %get-tuple-element.26), channel_id=1, source_target_pairs={{0,8},{1,9},{2,10},{3,11},{4,12},{5,13},{6,14},{7,15},{8,0},{9,1},... | collective-permute-start | bytes 786440 | tf_op jit(solution)/shard_map/ppermute | solution.py:367
  129.4 1.4 copy-done.1
  130.8 1.4 copy-done.3
  132.2 22.4 %far_experts.1.refs_0_ = bf16[8,48,2048]{2,1,0:T(8,128)(2,1)S(1)} custom-call(bf16[8,48,2048]{2,1,0:T(8,128)(2,1)S(1)} %copy-done.3, bf16[8,48,2048]{2,1,0:T(8,128)(2,1)S(1)} %copy-done.1, bf16[4,2048,1408]{2,1,0:T(8,128)(2,1)} %refs_1_.3, bf16[4,2048,1408]{2,1,0:T(8,128)(2,1)} %refs_2_.3, bf16[4,1408,2048]{2,1,0:T(8,128)(2,1)} %refs_3_.3), custom_call_target="tpu_custom_call" | custom-call | flops 13287555072 | bytes 69206016 | tf_op jit(solution)/shard_map/far_experts/pallas_call | solution.py:280
  154.6 0.0 collective-permute-done.2.refs_2_.refs_1_
  154.6 0.0 all-to-all-done.3.refs_1_
  154.6 0.0 copy-start.8
  154.6 0.0 copy-start.11
  154.6 24.4 %all_to_all.30 = bf16[8,48,2048]{2,1,0:T(8,128)(2,1)S(1)} all-to-all(bf16[8,48,2048]{2,1,0:T(8,128)(2,1)S(1)} %ordered.3), channel_id=1, replica_groups={{0,1,2,3,4,5,6,7},{8,9,10,11,12,13,14,15},{16,17,18,19,20,21,22,23},{24..., dimensions={0} | all-to-all | bytes 3145728 | tf_op jit(solution)/shard_map/all_to_all | solution.py:332
  179.0 0.0 copy-done.11
  179.0 1.2 mix_far.1
  180.3 0.1 collective-permute-start.3
  180.4 2.9 %collective-permute-start.4 = (f32[8,128]{1,0:T(8,128)S(1)}, f32[8,128]{1,0:T(8,128)S(1)}, u32[]{:S(2)}, u32[]{:S(2)}) collective-permute-start(f32[8,128]{1,0:T(8,128)S(1)} %get-tuple-element.25), channel_id=1, source_target_pairs={{0,8},{1,9},{2,10},{3,11},{4,12},{5,13},{6,14},{7,15},{8,0},{9,1},... | collective-permute-start | bytes 12296 | tf_op jit(solution)/shard_map/ppermute | solution.py:367
  183.3 1.2 mix_near.1
  184.5 21.8 %collective-permute-done.4 = f32[8,128]{1,0:T(8,128)S(1)} collective-permute-done((f32[8,128]{1,0:T(8,128)S(1)}, f32[8,128]{1,0:T(8,128)S(1)}, u32[]{:S(2)}, u32[]{:S(2)}) %collective-permute-start.4) | collective-permute-done | bytes 4128 | tf_op jit(solution)/shard_map/ppermute | solution.py:367
  206.3 0.6 slice_bitcast_fusion
  206.8 0.0 collective-permute-done.3
  206.9 0.9 add_convert_fusion
  (19 shorter events, 0.0 us)
Async XLA Ops:
  2.0 15.3 %all-to-all-start = ((f32[16,16,128]{2,1,0:T(8,128)}), f32[16,16,128]{2,1,0:T(8,128)S(1)}, u32[]{:S(2)}, u32[]{:S(2)}) async-start(f32[16,16,128]{2,1,0:T(8,128)} %pack.1), calls=%async_computation | async-start | bytes 262144 | tf_op jit(solution)/shard_map/all_to_all | solution.py:332
  17.3 1.2 copy-start.6
  20.7 3.8 %copy-start.13 = (s32[128,16]{0,1:T(8,128)S(1)}, s32[128,16]{0,1:T(8,128)}, u32[]{:S(2)}) copy-start(s32[128,16]{0,1:T(8,128)} %param.11) | copy-start | bytes 24580
  20.7 3.8 %copy-start.12 = (s32[128]{0:T(128)S(1)}, s32[128]{0:T(128)}, u32[]{:S(2)}) copy-start(s32[128]{0:T(128)} %param.12) | copy-start | bytes 1540
  20.7 26.7 %copy-start.9 = (bf16[128,2048]{1,0:T(8,128)(2,1)S(1)}, bf16[128,2048]{1,0:T(8,128)(2,1)}, u32[]{:S(2)}) copy-start(bf16[128,2048]{1,0:T(8,128)(2,1)} %values_ref.1) | copy-start | bytes 1572868
  20.7 26.7 %all-to-all-start.1 = ((bf16[16,16,2048]{2,1,0:T(8,128)(2,1)}), bf16[16,16,2048]{2,1,0:T(8,128)(2,1)S(1)}, u32[]{:S(2)}, u32[]{:S(2)}) async-start(bf16[16,16,2048]{2,1,0:T(8,128)(2,1)} %bitcast.5), calls=%async_computation.1 | async-start | bytes 2097152 | tf_op jit(solution)/shard_map/all_to_all | solution.py:332
  25.5 0.6 copy-start.10
  49.6 37.2 %all-to-all-start.2 = ((bf16[8,48,2048]{2,1,0:T(8,128)(2,1)}), bf16[8,48,2048]{2,1,0:T(8,128)(2,1)S(1)}, u32[]{:S(2)}, u32[]{:S(2)}) async-start(bf16[8,48,2048]{2,1,0:T(8,128)(2,1)} %bitcast.21), calls=%async_computation.2 | async-start | bytes 3145728 | tf_op jit(solution)/shard_map/all_to_all | solution.py:332
  55.5 29.2 %collective-permute-start = (bf16[128,2048]{1,0:T(8,128)(2,1)S(1)}, bf16[128,2048]{1,0:T(8,128)(2,1)S(1)}, u32[]{:S(2)}, u32[]{:S(2)}) collective-permute-start(bf16[128,2048]{1,0:T(8,128)(2,1)S(1)} %get-tuple-element.20), channel_id=1, source_target_pairs={{0,8},{1,9},{2,10},{3,11},{4,12},{5,13},{6,14},{7,15},{8,0},{9,1},... | collective-permute-start | bytes 1572872 | tf_op jit(solution)/shard_map/ppermute | solution.py:367
  86.8 34.3 %all-to-all-start.4 = ((bf16[8,48,2048]{2,1,0:T(8,128)(2,1)}), bf16[8,48,2048]{2,1,0:T(8,128)(2,1)S(1)}, u32[]{:S(2)}, u32[]{:S(2)}) async-start(bf16[8,48,2048]{2,1,0:T(8,128)(2,1)} %bitcast.16), calls=%async_computation.4 | async-start | bytes 3145728 | tf_op jit(solution)/shard_map/all_to_all | solution.py:332
  94.9 25.5 %collective-permute-start.1 = (bf16[64,2048]{1,0:T(8,128)(2,1)S(1)}, bf16[64,2048]{1,0:T(8,128)(2,1)S(1)}, u32[]{:S(2)}, u32[]{:S(2)}) collective-permute-start(bf16[64,2048]{1,0:T(8,128)(2,1)S(1)} %get-tuple-element.27), channel_id=1, source_target_pairs={{0,8},{1,9},{2,10},{3,11},{4,12},{5,13},{6,14},{7,15},{8,0},{9,1},... | collective-permute-start | bytes 786440 | tf_op jit(solution)/shard_map/ppermute | solution.py:367
  95.0 1.4 copy-start.4
  118.7 1.7 copy-start
  120.4 0.7 copy-start.7
  121.1 1.2 copy-start.2
  122.3 32.3 %all-to-all-start.3 = ((bf16[8,48,2048]{2,1,0:T(8,128)(2,1)}), bf16[8,48,2048]{2,1,0:T(8,128)(2,1)S(1)}, u32[]{:S(2)}, u32[]{:S(2)}) async-start(bf16[8,48,2048]{2,1,0:T(8,128)(2,1)} %ordered.2), calls=%async_computation.3 | async-start | bytes 3145728 | tf_op jit(solution)/shard_map/all_to_all | solution.py:332
  126.5 28.1 %collective-permute-start.2 = (bf16[64,2048]{1,0:T(8,128)(2,1)}, bf16[64,2048]{1,0:T(8,128)(2,1)S(1)}, u32[]{:S(2)}, u32[]{:S(2)}) collective-permute-start(bf16[64,2048]{1,0:T(8,128)(2,1)} %get-tuple-element.26), channel_id=1, source_target_pairs={{0,8},{1,9},{2,10},{3,11},{4,12},{5,13},{6,14},{7,15},{8,0},{9,1},... | collective-permute-start | bytes 786440 | tf_op jit(solution)/shard_map/ppermute | solution.py:367
  129.4 1.4 copy-start.1
  130.8 1.4 copy-start.3
  154.6 24.4 %copy-start.8 = (bf16[64,2048]{1,0:T(8,128)(2,1)S(1)}, bf16[64,2048]{1,0:T(8,128)(2,1)}, u32[]{:S(2)}) copy-start(bf16[64,2048]{1,0:T(8,128)(2,1)} %copy-done.7) | copy-start | bytes 786436
  154.6 24.4 %copy-start.11 = (s32[128,128]{1,0:T(8,128)S(1)}, s32[128,128]{1,0:T(8,128)}, u32[]{:S(2)}) copy-start(s32[128,128]{1,0:T(8,128)} %copy-done.10) | copy-start | bytes 196612
  179.0 4.3 %copy-start.5 = (bf16[128,2048]{1,0:T(8,128)(2,1)S(1)}, bf16[128,2048]{1,0:T(8,128)(2,1)}, u32[]{:S(2)}) copy-start(bf16[128,2048]{1,0:T(8,128)(2,1)} %refs_0_.1) | copy-start | bytes 1572868
  180.3 26.6 %collective-permute-start.3 = (bf16[128,2048]{1,0:T(8,128)(2,1)S(1)}, bf16[128,2048]{1,0:T(8,128)(2,1)S(1)}, u32[]{:S(2)}, u32[]{:S(2)}) collective-permute-start(bf16[128,2048]{1,0:T(8,128)(2,1)S(1)} %get-tuple-element.23), channel_id=1, source_target_pairs={{0,8},{1,9},{2,10},{3,11},{4,12},{5,13},{6,14},{7,15},{8,0},{9,1},... | collective-permute-start | bytes 1572872 | tf_op jit(solution)/shard_map/ppermute | solution.py:367
  180.4 25.9 %collective-permute-start.4 = (f32[8,128]{1,0:T(8,128)S(1)}, f32[8,128]{1,0:T(8,128)S(1)}, u32[]{:S(2)}, u32[]{:S(2)}) collective-permute-start(f32[8,128]{1,0:T(8,128)S(1)} %get-tuple-element.25), channel_id=1, source_target_pairs={{0,8},{1,9},{2,10},{3,11},{4,12},{5,13},{6,14},{7,15},{8,0},{9,1},... | collective-permute-start | bytes 12296 | tf_op jit(solution)/shard_map/ppermute | solution.py:367

commit v9 on v8

--- a/solution.py
+++ b/solution.py
@@ -49,7 +49,15 @@
         out_ref[n] = packed
 
 
-def fetch_kernel(me_ref, packed_ref, table_ref, out_ref):
+def fetch_kernel(me_ref, packed_ref, table_hbm, out_ref, table_ref, sem):
+    width = table_ref.shape[1] // sem.shape[0]
+    copies = []
+    for n in range(sem.shape[0]):
+        cols = pl.ds(n * width, width)
+        copies.append(
+            pltpu.make_async_copy(table_hbm.at[:, cols], table_ref.at[:, cols], sem.at[n])
+        )
+        copies[-1].start()
     device_count, _, tok_rows = packed_ref.shape
     held = table_ref.shape[0]
     look_cap = out_ref.shape[0] // device_count
@@ -64,7 +72,11 @@
         mine = jnp.where(slot == rank[source : source + 1], local[source : source + 1], 0)
         wanted = jnp.sum(mine, axis=1, keepdims=True)
         picks.append(flags(place == wanted))
-    out_ref[...] = dot(jnp.concatenate(picks, axis=0), table_ref[...]).astype(BF16)
+    pick = jnp.concatenate(picks, axis=0)
+    for n, copy in enumerate(copies):
+        copy.wait()
+        cols = slice(n * width, (n + 1) * width)
+        out_ref[:, cols] = dot(pick, table_ref[:, cols]).astype(BF16)
 
 
 def turned(rows):
@@ -176,13 +188,17 @@
         copy.wait()
 
 
-def pick_kernel(pick_ref, state_ref, out_hbm, sent_ref, sem):
-    features = state_ref.shape[1]
+def pick_kernel(
+    pick_ref, state_ref, grad_ref, out_hbm, upper_grad_ref, lower_grad_ref, sent_ref, sem
+):
+    tok_rows, features = state_ref.shape
     width = features // sem.shape[0]
     copies = [
         pick_slots(pick_ref, state_ref, out_hbm, sent_ref, sem, left, width)
         for left in range(0, features, width)
     ]
+    upper_grad_ref[...] = grad_ref[: tok_rows // 2, :]
+    lower_grad_ref[...] = grad_ref[tok_rows // 2 :, :]
     for copy in copies:
         copy.wait()
 
@@ -273,7 +289,7 @@
     w_gate, w_up, w_down = weights
     exp_dev, features, width = w_gate.shape
     half = rows_in.shape[0]
-    held = 2
+    held = 1
     rows = half * CAP
     anywhere = pl.BlockSpec(memory_space=pl.ANY)
     vmem = pl.BlockSpec(memory_space=VMEM)
@@ -291,7 +307,7 @@
             VMEM((exp_dev, rows, features), F32),
             pltpu.SemaphoreType.DMA((held, 10)),
         ],
-        compiler_params=pltpu.CompilerParams(vmem_limit_bytes=43 * 1024 * 1024),
+        compiler_params=pltpu.CompilerParams(vmem_limit_bytes=27 * 1024 * 1024),
         cost_estimate=pl.CostEstimate(
             flops=12 * exp_dev * rows * features * width,
             bytes_accessed=6 * exp_dev * features * width,
@@ -377,8 +393,7 @@
             name="ordered",
         )(array, *earlier_arrays)
 
-    split = tok_rows // 2
-    other_grads = (mirrored(out_grad[:split]), mirrored(out_grad[split:]))
+    split = shape((tok_rows // 2, features), BF16)
     packed = pl.pallas_call(
         pack_kernel,
         out_shape=shape((device_count, 16, tok_rows), F32),
@@ -390,8 +405,9 @@
     fetched = pl.pallas_call(
         fetch_kernel,
         out_shape=shape((device_count * look_cap, features), BF16),
-        in_specs=[smem, vmem, vmem],
+        in_specs=[smem, vmem, pl.BlockSpec(memory_space=pltpu.HBM)],
         out_specs=vmem,
+        scratch_shapes=[VMEM(table.shape, BF16), pltpu.SemaphoreType.DMA((4,))],
         compiler_params=SMALL,
         name="fetch_rows",
     )(place, packed, table)
@@ -424,24 +440,27 @@
     )(put, near_pick, returned.reshape(device_count * look_cap, features), block_values, columns)
     other_state = mirrored(state)
     near_rows = swap(near_sent.reshape(half, 2 * PAIR, features), halves)
-    far_sent = pl.pallas_call(
+    far_sent, *grad_halves = pl.pallas_call(
         pick_kernel,
-        out_shape=sent_shape,
-        in_specs=[vmem, vmem],
-        out_specs=anywhere,
+        out_shape=(sent_shape, split, split),
+        in_specs=[vmem, vmem, vmem],
+        out_specs=(anywhere, vmem, vmem),
         scratch_shapes=sent_scratch,
         compiler_params=SMALL,
         cost_estimate=pl.CostEstimate(
-            flops=20_000_000_000, bytes_accessed=4 * slots * features, transcendentals=0
+            flops=400_000_000_000, bytes_accessed=4 * slots * features, transcendentals=0
         ),
         name="far_slots",
-    )(far_pick, other_state).reshape(half, 2 * PAIR, features)
+    )(far_pick, other_state, out_grad)
+    other_grads = [mirrored(array) for array in grad_halves]
+    far_sent = far_sent.reshape(half, 2 * PAIR, features)
     far_rows = swap(far_sent, halves)
 
     weights = (w_gate, w_up, w_down)
     near_out = expert_call("near_experts", near_rows, weights, after=(far_sent,))
+    near_out = ordered(near_out, other_grads[0])
     far_out = expert_call("far_experts", far_rows, weights, after=(near_out,))
-    near_back = swap(ordered(near_out, other_grads[0]), halves)
+    near_back = swap(near_out, halves)
     far_back = swap(ordered(far_out, near_back, other_grads[1]), halves)
 
     def mixed_rows(name, first_column, slot_of, back, grads, kind):

time: 208 us -> 212 us (1.019)
  local copies, waits for them, and re-layouts: 12 us -> 20.3 us
  Pallas kernels: 55.2 us -> 51.5 us
    unnamed x29 -> x30, local copies, waits for them, and re-layouts: 9.64 us -> 19.7 us
    all_to_all x5, waiting for transfers between devices: 29.8 us -> 38.9 us  [swap(): lax.all_to_all(array, 'expert', split_axis=0, concat_axis=0, tiled=True,...]
    ppermute x5, waiting for transfers between devices: 48.2 us -> 40.4 us  [mirrored(): return lax.ppermute(array, 'expert', pairs)]
    pallas_call x2, Pallas kernels: 44.7 us -> 39.5 us  [expert_call(): pl.pallas_call(functools.partial(expert_kernel, len(after)), out_shape=ja...]
    all_to_all x5, starting transfers between devices: 27.5 us -> 23.5 us  [swap(): lax.all_to_all(array, 'expert', split_axis=0, concat_axis=0, tiled=True,...]
    ppermute x5, starting transfers between devices: 8.76 us -> 10.9 us  [mirrored(): return lax.ppermute(array, 'expert', pairs)]
  transfers between devices with their start and end apart: 10 -> 10, of which waited for: 5 -> 5; matrix products, arithmetic and copies ran while one was open for 2% -> 0% of each run, Pallas kernels for 23% -> 21%
where the time goes in v9:
time: 212 us
  waiting for transfers between devices  79.3 us (37%)
  Pallas kernels  51.5 us (24%)
  starting transfers between devices  34.5 us (16%)
  blocking collectives  24.4 us (12%)
  local copies, waits for them, and re-layouts  20.3 us (10%)
    ppermute x5, waiting for transfers between devices, mirrored(): return lax.ppermute(array, 'expert', pairs)  40.4 us
    pallas_call x2, Pallas kernels, expert_call(): pl.pallas_call(functools.partial(expert_kernel, len(after)), out_shape=ja...  39.5 us
    all_to_all x5, waiting for transfers between devices, swap(): lax.all_to_all(array, 'expert', split_axis=0, concat_axis=0, tiled=True,...  38.9 us
    all_to_all x1, blocking collectives, swap(): lax.all_to_all(array, 'expert', split_axis=0, concat_axis=0, tiled=True,...  24.4 us
    all_to_all x5, starting transfers between devices, swap(): lax.all_to_all(array, 'expert', split_axis=0, concat_axis=0, tiled=True,...  23.5 us
    unnamed x30, local copies, waits for them, and re-layouts  19.7 us
    ppermute x5, starting transfers between devices, mirrored(): return lax.ppermute(array, 'expert', pairs)  10.9 us
  transfers between devices with their start and end apart: 10, of which 5 were waited for; matrix products, arithmetic and copies ran while one was open for 0% of the time, Pallas kernels for 21%

profile of v9, /device:TPU:0, one launch (start us, length us, event | category | flops | bytes accessed | tf_op | source)
XLA Modules:
  0.0 211.7 jit_solution(4393237810600187259)
XLA Ops:
  0.6 1.4 pack.1
  2.0 7.4 %all-to-all-start = ((f32[16,16,128]{2,1,0:T(8,128)}), f32[16,16,128]{2,1,0:T(8,128)S(1)}, u32[]{:S(2)}, u32[]{:S(2)}) async-start(f32[16,16,128]{2,1,0:T(8,128)} %pack.1), calls=%async_computation | async-start | bytes 262144 | tf_op jit(solution)/shard_map/all_to_all | solution.py:348
  9.4 0.1 pad_add_fusion.me_ref
  9.5 7.9 %all-to-all-done.packed_ref = f32[16,16,128]{2,1,0:T(8,128)S(1)} async-done(((f32[16,16,128]{2,1,0:T(8,128)}), f32[16,16,128]{2,1,0:T(8,128)S(1)}, u32[]{:S(2)}, u32[]{:S(2)}) %all-to-all-start) | async-done | bytes 131104 | tf_op jit(solution)/shard_map/all_to_all | solution.py:348
  17.3 1.2 copy-done.5
  18.6 2.9 %fetch_rows.1.fetched_ref = bf16[256,2048]{1,0:T(8,128)(2,1)} custom-call(s32[2]{0:T(128)S(1)} %pad_add_fusion.me_ref, f32[16,16,128]{2,1,0:T(8,128)S(1)} %all-to-all-done.packed_ref, bf16[256,2048]{1,0:T(8,128)(2,1)S(1)} %copy-done.5), custom_call_target="tpu_custom_call" | custom-call | tf_op jit(solution)/shard_map/fetch_rows/pallas_call | solution.py:405
  21.5 0.0 copy-start.14
  21.5 0.0 copy-start.13
  21.5 0.0 copy-start.10
  21.5 3.8 %all-to-all-start.1 = ((bf16[16,16,2048]{2,1,0:T(8,128)(2,1)}), bf16[16,16,2048]{2,1,0:T(8,128)(2,1)S(1)}, u32[]{:S(2)}, u32[]{:S(2)}) async-start(bf16[16,16,2048]{2,1,0:T(8,128)(2,1)} %bitcast.5), calls=%async_computation.1 | async-start | bytes 2097152 | tf_op jit(solution)/shard_map/all_to_all | solution.py:348
  25.3 0.0 copy-done.14
  25.4 0.0 copy-done.13
  25.4 0.9 plan.1
  26.2 0.0 copy-start.8
  26.3 22.0 %all-to-all-done.1 = bf16[16,16,2048]{2,1,0:T(8,128)(2,1)S(1)} async-done(((bf16[16,16,2048]{2,1,0:T(8,128)(2,1)}), bf16[16,16,2048]{2,1,0:T(8,128)(2,1)S(1)}, u32[]{:S(2)}, u32[]{:S(2)}) %all-to-all-start.1) | async-done | bytes 1048608 | tf_op jit(solution)/shard_map/all_to_all | solution.py:348
  48.2 0.0 copy-done.10
  48.2 2.2 %token_state.1 = (bf16[128,2048]{1,0:T(8,128)(2,1)S(1)}, bf16[384,2048]{1,0:T(8,128)(2,1)}) custom-call(bf16[128,256]{1,0:T(8,128)(2,1)S(1)} %get-tuple-element.19.put_ref, bf16[384,128]{1,0:T(8,128)(2,1)S(1)} %get-tuple-element.20.pick_ref, bf16[256,2048]{1,0:T(8,128)(2,1)S(1)} %bitcast.18, bf16[128,2048]{1,0:T(8,128)(2,1)S(1)} %copy-done.10, ...), custom_call_target="tpu_custom_call" | custom-call | tf_op jit(solution)/shard_map/token_state/pallas_call | solution.py:432
  50.4 5.1 %collective-permute-start = (bf16[128,2048]{1,0:T(8,128)(2,1)S(1)}, bf16[128,2048]{1,0:T(8,128)(2,1)S(1)}, u32[]{:S(2)}, u32[]{:S(2)}) collective-permute-start(bf16[128,2048]{1,0:T(8,128)(2,1)S(1)} %get-tuple-element.23), channel_id=1, source_target_pairs={{0,8},{1,9},{2,10},{3,11},{4,12},{5,13},{6,14},{7,15},{8,0},{9,1},... | collective-permute-start | bytes 1572872 | tf_op jit(solution)/shard_map/ppermute | solution.py:383
  55.5 4.4 %all-to-all-start.2 = ((bf16[8,48,2048]{2,1,0:T(8,128)(2,1)}), bf16[8,48,2048]{2,1,0:T(8,128)(2,1)}, u32[]{:S(2)}, u32[]{:S(2)}) async-start(bf16[8,48,2048]{2,1,0:T(8,128)(2,1)} %bitcast.21), calls=%async_computation.2 | async-start | bytes 3145728 | tf_op jit(solution)/shard_map/all_to_all | solution.py:348
  60.0 18.6 %collective-permute-done.state_ref = bf16[128,2048]{1,0:T(8,128)(2,1)S(1)} collective-permute-done((bf16[128,2048]{1,0:T(8,128)(2,1)S(1)}, bf16[128,2048]{1,0:T(8,128)(2,1)S(1)}, u32[]{:S(2)}, u32[]{:S(2)}) %collective-permute-start) | collective-permute-done | bytes 524320 | tf_op jit(solution)/shard_map/ppermute | solution.py:383
  78.6 2.2 %far_slots.1 = (bf16[384,2048]{1,0:T(8,128)(2,1)}, bf16[64,2048]{1,0:T(8,128)(2,1)S(1)}, bf16[64,2048]{1,0:T(8,128)(2,1)}) custom-call(bf16[384,128]{1,0:T(8,128)(2,1)S(1)} %get-tuple-element.22.pick_ref, bf16[128,2048]{1,0:T(8,128)(2,1)S(1)} %collective-permute-done.state_ref, bf16[128,2048]{1,0:T(8,128)(2,1)S(1)} %copy-done.11), custom_call_target="tpu_custom_call" | custom-call | flops 399999991808 | bytes 3145728 | tf_op jit(solution)/shard_map/far_slots/pallas_call | solution.py:443
  80.7 9.1 %all-to-all-done.2.rows_ref = bf16[8,48,2048]{2,1,0:T(8,128)(2,1)} async-done(((bf16[8,48,2048]{2,1,0:T(8,128)(2,1)}), bf16[8,48,2048]{2,1,0:T(8,128)(2,1)}, u32[]{:S(2)}, u32[]{:S(2)}) %all-to-all-start.2) | async-done | bytes 1572896 | tf_op jit(solution)/shard_map/all_to_all | solution.py:348
  89.8 3.7 %all-to-all-start.4 = ((bf16[8,48,2048]{2,1,0:T(8,128)(2,1)}), bf16[8,48,2048]{2,1,0:T(8,128)(2,1)S(1)}, u32[]{:S(2)}, u32[]{:S(2)}) async-start(bf16[8,48,2048]{2,1,0:T(8,128)(2,1)} %bitcast.16), calls=%async_computation.4 | async-start | bytes 3145728 | tf_op jit(solution)/shard_map/all_to_all | solution.py:348
  93.5 0.6 collective-permute-start.1
  94.1 7.6 %copy-done = bf16[4,2048,1408]{2,1,0:T(8,128)(2,1)S(1)} copy-done((bf16[4,2048,1408]{2,1,0:T(8,128)(2,1)S(1)}, bf16[4,2048,1408]{2,1,0:T(8,128)(2,1)}, u32[]{:S(2)}) %copy-start) | copy-done | bytes 23068696
  101.6 21.1 %near_experts.1.refs_0_ = bf16[8,48,2048]{2,1,0:T(8,128)(2,1)} custom-call(bf16[8,48,2048]{2,1,0:T(8,128)(2,1)} %all-to-all-done.2.rows_ref, bf16[8,48,2048]{2,1,0:T(8,128)(2,1)S(1)} %bitcast.17, bf16[4,2048,1408]{2,1,0:T(8,128)(2,1)S(1)} %copy-done, bf16[4,2048,1408]{2,1,0:T(8,128)(2,1)} %refs_2_.3, bf16[4,1408,2048]{2,1,0:T(8,128)(2,1)} %refs_3_.3), custom_call_target="tpu_custom_call" | custom-call | flops 13287555072 | bytes 69206016 | tf_op jit(solution)/shard_map/near_experts/pallas_call | solution.py:296
  122.7 0.0 collective-permute-done.1.refs_1_.refs_0_
  122.7 0.7 copy-done.6
  123.4 0.0 all-to-all-done.4.rows_ref
  123.4 1.2 copy-done.2
  124.6 4.2 %all-to-all-start.3 = ((bf16[8,48,2048]{2,1,0:T(8,128)(2,1)}), bf16[8,48,2048]{2,1,0:T(8,128)(2,1)S(1)}, u32[]{:S(2)}, u32[]{:S(2)}) async-start(bf16[8,48,2048]{2,1,0:T(8,128)(2,1)} %ordered.2.refs_0_), calls=%async_computation.3 | async-start | bytes 3145728 | tf_op jit(solution)/shard_map/all_to_all | solution.py:348
  128.8 2.3 %collective-permute-start.2 = (bf16[64,2048]{1,0:T(8,128)(2,1)}, bf16[64,2048]{1,0:T(8,128)(2,1)S(1)}, u32[]{:S(2)}, u32[]{:S(2)}) collective-permute-start(bf16[64,2048]{1,0:T(8,128)(2,1)} %get-tuple-element.28), channel_id=1, source_target_pairs={{0,8},{1,9},{2,10},{3,11},{4,12},{5,13},{6,14},{7,15},{8,0},{9,1},... | collective-permute-start | bytes 786440 | tf_op jit(solution)/shard_map/ppermute | solution.py:383
  131.1 7.6 %copy-done.1 = bf16[4,2048,1408]{2,1,0:T(8,128)(2,1)S(1)} copy-done((bf16[4,2048,1408]{2,1,0:T(8,128)(2,1)S(1)}, bf16[4,2048,1408]{2,1,0:T(8,128)(2,1)}, u32[]{:S(2)}) %copy-start.1) | copy-done | bytes 23068696
  138.7 1.4 copy-done.3
  140.1 18.5 %far_experts.1.refs_0_ = bf16[8,48,2048]{2,1,0:T(8,128)(2,1)S(1)} custom-call(bf16[8,48,2048]{2,1,0:T(8,128)(2,1)S(1)} %copy-done.3, bf16[8,48,2048]{2,1,0:T(8,128)(2,1)} %ordered.2.refs_0_, bf16[4,2048,1408]{2,1,0:T(8,128)(2,1)S(1)} %copy-done.1, bf16[4,2048,1408]{2,1,0:T(8,128)(2,1)} %refs_2_.3, bf16[4,1408,2048]{2,1,0:T(8,128)(2,1)} %refs_3_.3), custom_call_target="tpu_custom_call" | custom-call | flops 13287555072 | bytes 69206016 | tf_op jit(solution)/shard_map/far_experts/pallas_call | solution.py:296
  158.6 0.0 collective-permute-done.2.refs_2_.refs_1_
  158.6 0.0 all-to-all-done.3.refs_1_
  158.6 0.0 copy-start.7
  158.6 0.0 copy-start.9
  158.6 24.4 %all_to_all.30 = bf16[8,48,2048]{2,1,0:T(8,128)(2,1)S(1)} all-to-all(bf16[8,48,2048]{2,1,0:T(8,128)(2,1)S(1)} %ordered.3), channel_id=1, replica_groups={{0,1,2,3,4,5,6,7},{8,9,10,11,12,13,14,15},{16,17,18,19,20,21,22,23},{24..., dimensions={0} | all-to-all | bytes 3145728 | tf_op jit(solution)/shard_map/all_to_all | solution.py:348
  183.1 1.2 mix_far.1
  184.3 0.7 collective-permute-start.3
  185.0 2.3 %collective-permute-start.4 = (f32[8,128]{1,0:T(8,128)S(1)}, f32[8,128]{1,0:T(8,128)S(1)}, u32[]{:S(2)}, u32[]{:S(2)}) collective-permute-start(f32[8,128]{1,0:T(8,128)S(1)} %get-tuple-element.31), channel_id=1, source_target_pairs={{0,8},{1,9},{2,10},{3,11},{4,12},{5,13},{6,14},{7,15},{8,0},{9,1},... | collective-permute-start | bytes 12296 | tf_op jit(solution)/shard_map/ppermute | solution.py:383
  187.3 1.2 mix_near.1
  188.5 21.8 %collective-permute-done.4 = f32[8,128]{1,0:T(8,128)S(1)} collective-permute-done((f32[8,128]{1,0:T(8,128)S(1)}, f32[8,128]{1,0:T(8,128)S(1)}, u32[]{:S(2)}, u32[]{:S(2)}) %collective-permute-start.4) | collective-permute-done | bytes 4128 | tf_op jit(solution)/shard_map/ppermute | solution.py:383
  210.3 0.6 slice_bitcast_fusion
  210.8 0.0 collective-permute-done.3
  210.8 0.9 add_convert_fusion
  (19 shorter events, 0.0 us)
Async XLA Ops:
  2.0 15.3 %all-to-all-start = ((f32[16,16,128]{2,1,0:T(8,128)}), f32[16,16,128]{2,1,0:T(8,128)S(1)}, u32[]{:S(2)}, u32[]{:S(2)}) async-start(f32[16,16,128]{2,1,0:T(8,128)} %pack.1), calls=%async_computation | async-start | bytes 262144 | tf_op jit(solution)/shard_map/all_to_all | solution.py:348
  17.3 1.2 copy-start.5
  21.5 3.8 %copy-start.14 = (s32[128,16]{0,1:T(8,128)S(1)}, s32[128,16]{0,1:T(8,128)}, u32[]{:S(2)}) copy-start(s32[128,16]{0,1:T(8,128)} %param.11) | copy-start | bytes 24580
  21.5 3.9 %copy-start.13 = (s32[128]{0:T(128)S(1)}, s32[128]{0:T(128)}, u32[]{:S(2)}) copy-start(s32[128]{0:T(128)} %param.12) | copy-start | bytes 1540
  21.5 26.7 %copy-start.10 = (bf16[128,2048]{1,0:T(8,128)(2,1)S(1)}, bf16[128,2048]{1,0:T(8,128)(2,1)}, u32[]{:S(2)}) copy-start(bf16[128,2048]{1,0:T(8,128)(2,1)} %values_ref.1) | copy-start | bytes 1572868
  21.5 26.7 %all-to-all-start.1 = ((bf16[16,16,2048]{2,1,0:T(8,128)(2,1)}), bf16[16,16,2048]{2,1,0:T(8,128)(2,1)S(1)}, u32[]{:S(2)}, u32[]{:S(2)}) async-start(bf16[16,16,2048]{2,1,0:T(8,128)(2,1)} %bitcast.5), calls=%async_computation.1 | async-start | bytes 2097152 | tf_op jit(solution)/shard_map/all_to_all | solution.py:348
  26.2 29.3 %copy-start.8 = (f32[128,128]{1,0:T(8,128)}, f32[128,128]{1,0:T(8,128)S(1)}, u32[]{:S(2)}) copy-start(f32[128,128]{1,0:T(8,128)S(1)} %get-tuple-element.18.columns_ref) | copy-start | bytes 196612
  50.4 28.1 %collective-permute-start = (bf16[128,2048]{1,0:T(8,128)(2,1)S(1)}, bf16[128,2048]{1,0:T(8,128)(2,1)S(1)}, u32[]{:S(2)}, u32[]{:S(2)}) collective-permute-start(bf16[128,2048]{1,0:T(8,128)(2,1)S(1)} %get-tuple-element.23), channel_id=1, source_target_pairs={{0,8},{1,9},{2,10},{3,11},{4,12},{5,13},{6,14},{7,15},{8,0},{9,1},... | collective-permute-start | bytes 1572872 | tf_op jit(solution)/shard_map/ppermute | solution.py:383
  55.5 23.1 %copy-start.11 = (bf16[128,2048]{1,0:T(8,128)(2,1)S(1)}, bf16[128,2048]{1,0:T(8,128)(2,1)}, u32[]{:S(2)}) copy-start(bf16[128,2048]{1,0:T(8,128)(2,1)} %refs_0_.1) | copy-start | bytes 1572868
  55.5 34.3 %all-to-all-start.2 = ((bf16[8,48,2048]{2,1,0:T(8,128)(2,1)}), bf16[8,48,2048]{2,1,0:T(8,128)(2,1)}, u32[]{:S(2)}, u32[]{:S(2)}) async-start(bf16[8,48,2048]{2,1,0:T(8,128)(2,1)} %bitcast.21), calls=%async_computation.2 | async-start | bytes 3145728 | tf_op jit(solution)/shard_map/all_to_all | solution.py:348
  89.8 4.3 %copy-start.4 = (bf16[384,2048]{1,0:T(8,128)(2,1)S(1)}, bf16[384,2048]{1,0:T(8,128)(2,1)}, u32[]{:S(2)}) copy-start(bf16[384,2048]{1,0:T(8,128)(2,1)} %get-tuple-element.24) | copy-start | bytes 4718596
  89.8 33.6 %all-to-all-start.4 = ((bf16[8,48,2048]{2,1,0:T(8,128)(2,1)}), bf16[8,48,2048]{2,1,0:T(8,128)(2,1)S(1)}, u32[]{:S(2)}, u32[]{:S(2)}) async-start(bf16[8,48,2048]{2,1,0:T(8,128)(2,1)} %bitcast.16), calls=%async_computation.4 | async-start | bytes 3145728 | tf_op jit(solution)/shard_map/all_to_all | solution.py:348
  93.5 29.2 %collective-permute-start.1 = (bf16[64,2048]{1,0:T(8,128)(2,1)S(1)}, bf16[64,2048]{1,0:T(8,128)(2,1)S(1)}, u32[]{:S(2)}, u32[]{:S(2)}) collective-permute-start(bf16[64,2048]{1,0:T(8,128)(2,1)S(1)} %get-tuple-element.25), channel_id=1, source_target_pairs={{0,8},{1,9},{2,10},{3,11},{4,12},{5,13},{6,14},{7,15},{8,0},{9,1},... | collective-permute-start | bytes 786440 | tf_op jit(solution)/shard_map/ppermute | solution.py:383
  94.1 7.6 %copy-start = (bf16[4,2048,1408]{2,1,0:T(8,128)(2,1)S(1)}, bf16[4,2048,1408]{2,1,0:T(8,128)(2,1)}, u32[]{:S(2)}) copy-start(bf16[4,2048,1408]{2,1,0:T(8,128)(2,1)} %refs_1_.3) | copy-start | bytes 69206016
  122.7 0.7 copy-start.6
  123.4 1.2 copy-start.2
  124.6 33.9 %all-to-all-start.3 = ((bf16[8,48,2048]{2,1,0:T(8,128)(2,1)}), bf16[8,48,2048]{2,1,0:T(8,128)(2,1)S(1)}, u32[]{:S(2)}, u32[]{:S(2)}) async-start(bf16[8,48,2048]{2,1,0:T(8,128)(2,1)} %ordered.2.refs_0_), calls=%async_computation.3 | async-start | bytes 3145728 | tf_op jit(solution)/shard_map/all_to_all | solution.py:348
  128.8 29.7 %collective-permute-start.2 = (bf16[64,2048]{1,0:T(8,128)(2,1)}, bf16[64,2048]{1,0:T(8,128)(2,1)S(1)}, u32[]{:S(2)}, u32[]{:S(2)}) collective-permute-start(bf16[64,2048]{1,0:T(8,128)(2,1)} %get-tuple-element.28), channel_id=1, source_target_pairs={{0,8},{1,9},{2,10},{3,11},{4,12},{5,13},{6,14},{7,15},{8,0},{9,1},... | collective-permute-start | bytes 786440 | tf_op jit(solution)/shard_map/ppermute | solution.py:383
  131.1 7.6 %copy-start.1 = (bf16[4,2048,1408]{2,1,0:T(8,128)(2,1)S(1)}, bf16[4,2048,1408]{2,1,0:T(8,128)(2,1)}, u32[]{:S(2)}) copy-start(bf16[4,2048,1408]{2,1,0:T(8,128)(2,1)} %refs_1_.3) | copy-start | bytes 69206016
  138.7 1.4 copy-start.3
  158.6 24.5 %copy-start.7 = (bf16[64,2048]{1,0:T(8,128)(2,1)S(1)}, bf16[64,2048]{1,0:T(8,128)(2,1)}, u32[]{:S(2)}) copy-start(bf16[64,2048]{1,0:T(8,128)(2,1)} %copy-done.6) | copy-start | bytes 786436
  158.6 24.5 %copy-start.9 = (f32[128,128]{1,0:T(8,128)S(1)}, f32[128,128]{1,0:T(8,128)}, u32[]{:S(2)}) copy-start(f32[128,128]{1,0:T(8,128)} %copy-done.8) | copy-start | bytes 196612
  183.1 4.2 %copy-start.12 = (bf16[128,2048]{1,0:T(8,128)(2,1)S(1)}, bf16[128,2048]{1,0:T(8,128)(2,1)}, u32[]{:S(2)}) copy-start(bf16[128,2048]{1,0:T(8,128)(2,1)} %refs_0_.1) | copy-start | bytes 1572868
  184.3 26.6 %collective-permute-start.3 = (bf16[128,2048]{1,0:T(8,128)(2,1)S(1)}, bf16[128,2048]{1,0:T(8,128)(2,1)S(1)}, u32[]{:S(2)}, u32[]{:S(2)}) collective-permute-start(bf16[128,2048]{1,0:T(8,128)(2,1)S(1)} %get-tuple-element.29), channel_id=1, source_target_pairs={{0,8},{1,9},{2,10},{3,11},{4,12},{5,13},{6,14},{7,15},{8,0},{9,1},... | collective-permute-start | bytes 1572872 | tf_op jit(solution)/shard_map/ppermute | solution.py:383
  185.0 25.3 %collective-permute-start.4 = (f32[8,128]{1,0:T(8,128)S(1)}, f32[8,128]{1,0:T(8,128)S(1)}, u32[]{:S(2)}, u32[]{:S(2)}) collective-permute-start(f32[8,128]{1,0:T(8,128)S(1)} %get-tuple-element.31), channel_id=1, source_target_pairs={{0,8},{1,9},{2,10},{3,11},{4,12},{5,13},{6,14},{7,15},{8,0},{9,1},... | collective-permute-start | bytes 12296 | tf_op jit(solution)/shard_map/ppermute | solution.py:383

commit v10 on v9

--- a/solution.py
+++ b/solution.py
@@ -20,6 +20,10 @@
 
 def dot(a, b):
     return jnp.dot(a, b, preferred_element_type=F32)
+
+
+def in_hbm(array):
+    return pltpu.with_memory_space_constraint(array, pltpu.HBM)
 
 
 def iota(shape, dimension):
@@ -203,32 +207,38 @@
         copy.wait()
 
 
-def expert_kernel(after, rows_ref, *refs):
+def expert_kernel(after, rows_hbm, *refs):
     wg_hbm, wu_hbm, wd_hbm, out_ref = refs[after : after + 4]
-    x_ref, wg_ref, wu_ref, wd_ref, hidden_ref, result_ref, sem = refs[after + 4 :]
-    exp_dev = wg_hbm.shape[0]
-    held, features, width = wg_ref.shape
+    rows_ref, x_ref, wg_ref, wu_ref, both_ref, wd_ref, hidden_ref, result_ref, sem, rows_sem = refs[
+        after + 4 :
+    ]
+    exp_dev, features, width = wg_hbm.shape
     half = rows_ref.shape[0]
-    up_cuts = ((0, 512), (512, 512), (1024, width - 1024))
+    wide = wg_ref.shape[1]
+    rest = width - wide
+    up_cuts = ((0, 512), (512, 512), (1024, wide - 1024))
     down_cuts = tuple((at, 512) for at in range(0, features, 512))
 
-    def weight_copies(j, place):
+    def weight_copies(j):
         copies = []
         for at, size in up_cuts:
-            for hbm, ref in ((wg_hbm, wg_ref), (wu_hbm, wu_ref)):
-                cols = pl.ds(at, size)
-                copies.append((hbm.at[j, :, cols], ref.at[place, :, cols]))
+            cols = pl.ds(at, size)
+            copies.append((wg_hbm.at[j, :, cols], wg_ref.at[:, cols]))
+            copies.append((wu_hbm.at[j, :, cols], wu_ref.at[:, cols]))
+        for n, hbm in enumerate((wg_hbm, wu_hbm)):
+            copies.append((hbm.at[j, :, pl.ds(wide, rest)], both_ref.at[:, pl.ds(n * rest, rest)]))
         for at, size in down_cuts:
             cols = pl.ds(at, size)
-            copies.append((wd_hbm.at[j, :, cols], wd_ref.at[place, :, cols]))
+            copies.append((wd_hbm.at[j, :, cols], wd_ref.at[:, cols]))
         return [
-            pltpu.make_async_copy(src, dst, sem.at[place, n])
-            for n, (src, dst) in enumerate(copies)
+            pltpu.make_async_copy(src, dst, sem.at[n]) for n, (src, dst) in enumerate(copies)
         ]
 
-    for j in range(held):
-        for copy in weight_copies(j, j):
-            copy.start()
+    rows_copy = pltpu.make_async_copy(rows_hbm, rows_ref, rows_sem)
+    rows_copy.start()
+    for copy in weight_copies(0):
+        copy.start()
+    rows_copy.wait()
 
     low = iota((PAIR, features), 0) < CAP
     for chunk in range(exp_dev // 2):
@@ -247,31 +257,37 @@
 
     @pl.loop(0, exp_dev)
     def _(j):
-        place = j % held
-        copies = weight_copies(j, place)
-        later = weight_copies(jnp.minimum(j + held, exp_dev - 1), place)
+        copies = weight_copies(j)
+        later = weight_copies(jnp.minimum(j + 1, exp_dev - 1))
 
         def refill(first, count):
-            @pl.when(j + held < exp_dev)
+            @pl.when(j + 1 < exp_dev)
             def _():
                 for n in range(first, first + count):
                     later[n].start()
+
+        def hide(gate, up, at):
+            hidden = gate / (1.0 + jnp.exp(-gate)) * up
+            hidden_ref[:, at : at + gate.shape[1]] = hidden.astype(BF16)
 
         n = 0
         for at, size in up_cuts:
             copies[n].wait()
             copies[n + 1].wait()
-            x = x_ref[j]
-            gate = dot(x, wg_ref[place, :, at : at + size])
-            up = dot(x, wu_ref[place, :, at : at + size])
-            hidden_ref[:, at : at + size] = (gate / (1.0 + jnp.exp(-gate)) * up).astype(BF16)
+            gate = dot(x_ref[j], wg_ref[:, at : at + size])
+            up = dot(x_ref[j], wu_ref[:, at : at + size])
+            hide(gate, up, at)
             refill(n, 2)
             n += 2
+        copies[n].wait()
+        copies[n + 1].wait()
+        both = dot(x_ref[j], both_ref[...])
+        hide(both[:, :rest], both[:, rest:], wide)
+        refill(n, 2)
+        n += 2
         for at, size in down_cuts:
             copies[n].wait()
-            result_ref[j, :, at : at + size] = dot(
-                hidden_ref[...], wd_ref[place, :, at : at + size]
-            )
+            result_ref[j, :, at : at + size] = dot(hidden_ref[...], wd_ref[:, at : at + size])
             refill(n, 1)
             n += 1
 
@@ -289,32 +305,37 @@
     w_gate, w_up, w_down = weights
     exp_dev, features, width = w_gate.shape
     half = rows_in.shape[0]
-    held = 1
     rows = half * CAP
+    rest = 128
+    wide = width - rest
     anywhere = pl.BlockSpec(memory_space=pl.ANY)
+    hbm = pl.BlockSpec(memory_space=pltpu.HBM)
     vmem = pl.BlockSpec(memory_space=VMEM)
     return pl.pallas_call(
         functools.partial(expert_kernel, len(after)),
         out_shape=jax.ShapeDtypeStruct((half, exp_dev * CAP, features), BF16),
-        in_specs=[vmem] + [anywhere] * (3 + len(after)),
+        in_specs=[hbm] + [anywhere] * len(after) + [hbm] * 3,
         out_specs=vmem,
         scratch_shapes=[
+            VMEM(rows_in.shape, BF16),
             VMEM((exp_dev, rows, features), BF16),
-            VMEM((held, features, width), BF16),
-            VMEM((held, features, width), BF16),
-            VMEM((held, width, features), BF16),
+            VMEM((features, wide), BF16),
+            VMEM((features, wide), BF16),
+            VMEM((features, 2 * rest), BF16),
+            VMEM((width, features), BF16),
             VMEM((rows, width), BF16),
             VMEM((exp_dev, rows, features), F32),
-            pltpu.SemaphoreType.DMA((held, 10)),
+            pltpu.SemaphoreType.DMA((12,)),
+            pltpu.SemaphoreType.DMA,
         ],
-        compiler_params=pltpu.CompilerParams(vmem_limit_bytes=27 * 1024 * 1024),
+        compiler_params=pltpu.CompilerParams(vmem_limit_bytes=28 * 1024 * 1024),
         cost_estimate=pl.CostEstimate(
             flops=12 * exp_dev * rows * features * width,
             bytes_accessed=6 * exp_dev * features * width,
             transcendentals=exp_dev * rows * width,
         ),
         name=name,
-    )(rows_in, *after, w_gate, w_up, w_down)
+    )(in_hbm(rows_in), *[in_hbm(array) for array in after], in_hbm(w_gate), in_hbm(w_up), in_hbm(w_down))
 
 
 def mix_kernel(first_column, slots_ref, columns_ref, back_ref, *refs):
@@ -410,7 +431,7 @@
         scratch_shapes=[VMEM(table.shape, BF16), pltpu.SemaphoreType.DMA((4,))],
         compiler_params=SMALL,
         name="fetch_rows",
-    )(place, packed, table)
+    )(place, packed, in_hbm(table))
     returned = swap(fetched.reshape(device_count, look_cap, features))
     put, near_pick, far_pick, near_of, far_of, columns = pl.pallas_call(
         plan_kernel,

time: 212 us -> 205 us (0.967)
  local copies, waits for them, and re-layouts: 20.3 us -> 2.52 us
  Pallas kernels: 51.5 us -> 62.1 us
    unnamed x30 -> x20, local copies, waits for them, and re-layouts: 19.7 us -> 1.94 us
    pallas_call x2, Pallas kernels: 39.5 us -> 49.6 us  [expert_call(): pl.pallas_call(functools.partial(expert_kernel, len(after)), out_shape=ja...]
  transfers between devices with their start and end apart: 10 -> 10, of which waited for: 5 -> 5; matrix products, arithmetic and copies ran while one was open for 0% -> 0% of each run, Pallas kernels for 21% -> 26%
where the time goes in v10:
time: 205 us
  waiting for transfers between devices  79.3 us (39%)
  Pallas kernels  62.1 us (30%)
  starting transfers between devices  34.3 us (17%)
  blocking collectives  24.4 us (12%)
  local copies, waits for them, and re-layouts  2.52 us (1%)
    pallas_call x2, Pallas kernels, expert_call(): pl.pallas_call(functools.partial(expert_kernel, len(after)), out_shape=ja...  49.6 us
    ppermute x5, waiting for transfers between devices, mirrored(): return lax.ppermute(array, 'expert', pairs)  40.4 us
    all_to_all x5, waiting for transfers between devices, swap(): lax.all_to_all(array, 'expert', split_axis=0, concat_axis=0, tiled=True,...  38.9 us
    all_to_all x1, blocking collectives, swap(): lax.all_to_all(array, 'expert', split_axis=0, concat_axis=0, tiled=True,...  24.4 us
    all_to_all x5, starting transfers between devices, swap(): lax.all_to_all(array, 'expert', split_axis=0, concat_axis=0, tiled=True,...  23.4 us
    ppermute x5, starting transfers between devices, mirrored(): return lax.ppermute(array, 'expert', pairs)  10.9 us
  transfers between devices with their start and end apart: 10, of which 5 were waited for; matrix products, arithmetic and copies ran while one was open for 0% of the time, Pallas kernels for 26%

profile of v10, /device:TPU:0, one launch (start us, length us, event | category | flops | bytes accessed | tf_op | source)
XLA Modules:
  0.0 204.5 jit_solution(15259923085755604991)
XLA Ops:
  0.6 1.4 pack.1
  2.0 7.4 %all-to-all-start = ((f32[16,16,128]{2,1,0:T(8,128)}), f32[16,16,128]{2,1,0:T(8,128)S(1)}, u32[]{:S(2)}, u32[]{:S(2)}) async-start(f32[16,16,128]{2,1,0:T(8,128)} %pack.1), calls=%async_computation | async-start | bytes 262144 | tf_op jit(solution)/shard_map/all_to_all | solution.py:369
  9.4 0.1 pad_add_fusion.me_ref
  9.5 7.9 %all-to-all-done.packed_ref = f32[16,16,128]{2,1,0:T(8,128)S(1)} async-done(((f32[16,16,128]{2,1,0:T(8,128)}), f32[16,16,128]{2,1,0:T(8,128)S(1)}, u32[]{:S(2)}, u32[]{:S(2)}) %all-to-all-start) | async-done | bytes 131104 | tf_op jit(solution)/shard_map/all_to_all | solution.py:369
  17.3 3.5 %fetch_rows.1.fetched_ref = bf16[256,2048]{1,0:T(8,128)(2,1)} custom-call(s32[2]{0:T(128)S(1)} %pad_add_fusion.me_ref, f32[16,16,128]{2,1,0:T(8,128)S(1)} %all-to-all-done.packed_ref, bf16[256,2048]{1,0:T(8,128)(2,1)} %table_hbm.1), custom_call_target="tpu_custom_call" | custom-call | tf_op jit(solution)/shard_map/fetch_rows/pallas_call | solution.py:426
  20.8 0.0 copy-start.9
  20.8 0.0 copy-start.7
  20.8 0.0 copy-start.4
  20.8 3.8 %all-to-all-start.1 = ((bf16[16,16,2048]{2,1,0:T(8,128)(2,1)}), bf16[16,16,2048]{2,1,0:T(8,128)(2,1)S(1)}, u32[]{:S(2)}, u32[]{:S(2)}) async-start(bf16[16,16,2048]{2,1,0:T(8,128)(2,1)} %bitcast.5), calls=%async_computation.1 | async-start | bytes 2097152 | tf_op jit(solution)/shard_map/all_to_all | solution.py:369
  24.6 0.0 copy-done.9
  24.7 0.0 copy-done.7
  24.7 0.9 plan.1
  25.6 0.0 copy-start.2
  25.6 22.0 %all-to-all-done.1 = bf16[16,16,2048]{2,1,0:T(8,128)(2,1)S(1)} async-done(((bf16[16,16,2048]{2,1,0:T(8,128)(2,1)}), bf16[16,16,2048]{2,1,0:T(8,128)(2,1)S(1)}, u32[]{:S(2)}, u32[]{:S(2)}) %all-to-all-start.1) | async-done | bytes 1048608 | tf_op jit(solution)/shard_map/all_to_all | solution.py:369
  47.5 0.0 copy-done.4
  47.5 2.2 %token_state.1 = (bf16[128,2048]{1,0:T(8,128)(2,1)S(1)}, bf16[384,2048]{1,0:T(8,128)(2,1)}) custom-call(bf16[128,256]{1,0:T(8,128)(2,1)S(1)} %get-tuple-element.19.put_ref, bf16[384,128]{1,0:T(8,128)(2,1)S(1)} %get-tuple-element.20.pick_ref, bf16[256,2048]{1,0:T(8,128)(2,1)S(1)} %bitcast.16, bf16[128,2048]{1,0:T(8,128)(2,1)S(1)} %copy-done.4, ...), custom_call_target="tpu_custom_call" | custom-call | tf_op jit(solution)/shard_map/token_state/pallas_call | solution.py:453
  49.7 5.1 %collective-permute-start = (bf16[128,2048]{1,0:T(8,128)(2,1)S(1)}, bf16[128,2048]{1,0:T(8,128)(2,1)S(1)}, u32[]{:S(2)}, u32[]{:S(2)}) collective-permute-start(bf16[128,2048]{1,0:T(8,128)(2,1)S(1)} %get-tuple-element.23), channel_id=1, source_target_pairs={{0,8},{1,9},{2,10},{3,11},{4,12},{5,13},{6,14},{7,15},{8,0},{9,1},... | collective-permute-start | bytes 1572872 | tf_op jit(solution)/shard_map/ppermute | solution.py:404
  54.8 0.0 copy-done.2
  54.8 4.4 %all-to-all-start.2 = ((bf16[8,48,2048]{2,1,0:T(8,128)(2,1)}), bf16[8,48,2048]{2,1,0:T(8,128)(2,1)}, u32[]{:S(2)}, u32[]{:S(2)}) async-start(bf16[8,48,2048]{2,1,0:T(8,128)(2,1)} %bitcast.21), calls=%async_computation.2 | async-start | bytes 3145728 | tf_op jit(solution)/shard_map/all_to_all | solution.py:369
  59.2 18.6 %collective-permute-done.state_ref = bf16[128,2048]{1,0:T(8,128)(2,1)S(1)} collective-permute-done((bf16[128,2048]{1,0:T(8,128)(2,1)S(1)}, bf16[128,2048]{1,0:T(8,128)(2,1)S(1)}, u32[]{:S(2)}, u32[]{:S(2)}) %collective-permute-start) | collective-permute-done | bytes 524320 | tf_op jit(solution)/shard_map/ppermute | solution.py:404
  77.9 0.0 copy-done.5
  77.9 2.1 %far_slots.1 = (bf16[384,2048]{1,0:T(8,128)(2,1)}, bf16[64,2048]{1,0:T(8,128)(2,1)S(1)}, bf16[64,2048]{1,0:T(8,128)(2,1)}) custom-call(bf16[384,128]{1,0:T(8,128)(2,1)S(1)} %get-tuple-element.22.pick_ref, bf16[128,2048]{1,0:T(8,128)(2,1)S(1)} %collective-permute-done.state_ref, bf16[128,2048]{1,0:T(8,128)(2,1)S(1)} %copy-done.5), custom_call_target="tpu_custom_call" | custom-call | flops 399999991808 | bytes 3145728 | tf_op jit(solution)/shard_map/far_slots/pallas_call | solution.py:464
  80.0 9.1 %all-to-all-done.2.rows_hbm = bf16[8,48,2048]{2,1,0:T(8,128)(2,1)} async-done(((bf16[8,48,2048]{2,1,0:T(8,128)(2,1)}), bf16[8,48,2048]{2,1,0:T(8,128)(2,1)}, u32[]{:S(2)}, u32[]{:S(2)}) %all-to-all-start.2) | async-done | bytes 1572896 | tf_op jit(solution)/shard_map/all_to_all | solution.py:369
  89.1 3.6 %all-to-all-start.4 = ((bf16[8,48,2048]{2,1,0:T(8,128)(2,1)}), bf16[8,48,2048]{2,1,0:T(8,128)(2,1)S(1)}, u32[]{:S(2)}, u32[]{:S(2)}) async-start(bf16[8,48,2048]{2,1,0:T(8,128)(2,1)} %bitcast.19), calls=%async_computation.4 | async-start | bytes 3145728 | tf_op jit(solution)/shard_map/all_to_all | solution.py:369
  92.7 0.5 collective-permute-start.1
  93.2 25.4 %near_experts.1.refs_0_ = bf16[8,48,2048]{2,1,0:T(8,128)(2,1)} custom-call(bf16[8,48,2048]{2,1,0:T(8,128)(2,1)} %all-to-all-done.2.rows_hbm, bf16[8,48,2048]{2,1,0:T(8,128)(2,1)} %bitcast.20, bf16[4,2048,1408]{2,1,0:T(8,128)(2,1)} %refs_1_.3, bf16[4,2048,1408]{2,1,0:T(8,128)(2,1)} %refs_2_.3, bf16[4,1408,2048]{2,1,0:T(8,128)(2,1)} %refs_3_.3), custom_call_target="tpu_custom_call" | custom-call | flops 13287555072 | bytes 69206016 | tf_op jit(solution)/shard_map/near_experts/pallas_call | solution.py:314
  118.6 0.0 collective-permute-done.1.refs_1_.refs_0_
  118.7 0.0 copy-start
  118.7 0.7 copy-done
  119.4 0.0 all-to-all-done.4.rows_hbm
  119.4 1.2 copy-done.8
  120.6 4.2 %all-to-all-start.3 = ((bf16[8,48,2048]{2,1,0:T(8,128)(2,1)}), bf16[8,48,2048]{2,1,0:T(8,128)(2,1)S(1)}, u32[]{:S(2)}, u32[]{:S(2)}) async-start(bf16[8,48,2048]{2,1,0:T(8,128)(2,1)} %ordered.2.refs_0_), calls=%async_computation.3 | async-start | bytes 3145728 | tf_op jit(solution)/shard_map/all_to_all | solution.py:369
  124.8 2.3 %collective-permute-start.2 = (bf16[64,2048]{1,0:T(8,128)(2,1)}, bf16[64,2048]{1,0:T(8,128)(2,1)S(1)}, u32[]{:S(2)}, u32[]{:S(2)}) collective-permute-start(bf16[64,2048]{1,0:T(8,128)(2,1)} %get-tuple-element.28), channel_id=1, source_target_pairs={{0,8},{1,9},{2,10},{3,11},{4,12},{5,13},{6,14},{7,15},{8,0},{9,1},... | collective-permute-start | bytes 786440 | tf_op jit(solution)/shard_map/ppermute | solution.py:404
  127.1 24.2 %far_experts.1.refs_0_ = bf16[8,48,2048]{2,1,0:T(8,128)(2,1)S(1)} custom-call(bf16[8,48,2048]{2,1,0:T(8,128)(2,1)} %copy-done.8, bf16[8,48,2048]{2,1,0:T(8,128)(2,1)} %ordered.2.refs_0_, bf16[4,2048,1408]{2,1,0:T(8,128)(2,1)} %refs_1_.3, bf16[4,2048,1408]{2,1,0:T(8,128)(2,1)} %refs_2_.3, bf16[4,1408,2048]{2,1,0:T(8,128)(2,1)} %refs_3_.3), custom_call_target="tpu_custom_call" | custom-call | flops 13287555072 | bytes 69206016 | tf_op jit(solution)/shard_map/far_experts/pallas_call | solution.py:314
  151.3 0.0 collective-permute-done.2.refs_2_.refs_1_
  151.3 0.0 all-to-all-done.3.refs_1_
  151.4 0.0 copy-start.1
  151.4 0.0 copy-start.3
  151.4 24.4 %all_to_all.30 = bf16[8,48,2048]{2,1,0:T(8,128)(2,1)S(1)} all-to-all(bf16[8,48,2048]{2,1,0:T(8,128)(2,1)S(1)} %ordered.3), channel_id=1, replica_groups={{0,1,2,3,4,5,6,7},{8,9,10,11,12,13,14,15},{16,17,18,19,20,21,22,23},{24..., dimensions={0} | all-to-all | bytes 3145728 | tf_op jit(solution)/shard_map/all_to_all | solution.py:369
  175.8 0.0 copy-done.1
  175.8 1.3 mix_far.1
  177.1 0.7 collective-permute-start.3
  177.7 2.3 %collective-permute-start.4 = (f32[8,128]{1,0:T(8,128)S(1)}, f32[8,128]{1,0:T(8,128)S(1)}, u32[]{:S(2)}, u32[]{:S(2)}) collective-permute-start(f32[8,128]{1,0:T(8,128)S(1)} %get-tuple-element.31), channel_id=1, source_target_pairs={{0,8},{1,9},{2,10},{3,11},{4,12},{5,13},{6,14},{7,15},{8,0},{9,1},... | collective-permute-start | bytes 12296 | tf_op jit(solution)/shard_map/ppermute | solution.py:404
  180.1 1.2 mix_near.1
  181.3 21.8 %collective-permute-done.4 = f32[8,128]{1,0:T(8,128)S(1)} collective-permute-done((f32[8,128]{1,0:T(8,128)S(1)}, f32[8,128]{1,0:T(8,128)S(1)}, u32[]{:S(2)}, u32[]{:S(2)}) %collective-permute-start.4) | collective-permute-done | bytes 4128 | tf_op jit(solution)/shard_map/ppermute | solution.py:404
  203.0 0.6 slice_bitcast_fusion
  203.6 0.0 collective-permute-done.3
  203.6 0.9 add_convert_fusion
  (9 shorter events, 0.0 us)
Async XLA Ops:
  2.0 15.3 %all-to-all-start = ((f32[16,16,128]{2,1,0:T(8,128)}), f32[16,16,128]{2,1,0:T(8,128)S(1)}, u32[]{:S(2)}, u32[]{:S(2)}) async-start(f32[16,16,128]{2,1,0:T(8,128)} %pack.1), calls=%async_computation | async-start | bytes 262144 | tf_op jit(solution)/shard_map/all_to_all | solution.py:369
  20.8 3.8 %copy-start.9 = (s32[128,16]{0,1:T(8,128)S(1)}, s32[128,16]{0,1:T(8,128)}, u32[]{:S(2)}) copy-start(s32[128,16]{0,1:T(8,128)} %param.11) | copy-start | bytes 24580
  20.8 3.9 %copy-start.7 = (s32[128]{0:T(128)S(1)}, s32[128]{0:T(128)}, u32[]{:S(2)}) copy-start(s32[128]{0:T(128)} %param.12) | copy-start | bytes 1540
  20.8 26.7 %copy-start.4 = (bf16[128,2048]{1,0:T(8,128)(2,1)S(1)}, bf16[128,2048]{1,0:T(8,128)(2,1)}, u32[]{:S(2)}) copy-start(bf16[128,2048]{1,0:T(8,128)(2,1)} %values_ref.1) | copy-start | bytes 1572868
  20.8 26.7 %all-to-all-start.1 = ((bf16[16,16,2048]{2,1,0:T(8,128)(2,1)}), bf16[16,16,2048]{2,1,0:T(8,128)(2,1)S(1)}, u32[]{:S(2)}, u32[]{:S(2)}) async-start(bf16[16,16,2048]{2,1,0:T(8,128)(2,1)} %bitcast.5), calls=%async_computation.1 | async-start | bytes 2097152 | tf_op jit(solution)/shard_map/all_to_all | solution.py:369
  25.6 29.2 %copy-start.2 = (f32[128,128]{1,0:T(8,128)}, f32[128,128]{1,0:T(8,128)S(1)}, u32[]{:S(2)}) copy-start(f32[128,128]{1,0:T(8,128)S(1)} %get-tuple-element.18.columns_ref) | copy-start | bytes 196612
  49.7 28.2 %collective-permute-start = (bf16[128,2048]{1,0:T(8,128)(2,1)S(1)}, bf16[128,2048]{1,0:T(8,128)(2,1)S(1)}, u32[]{:S(2)}, u32[]{:S(2)}) collective-permute-start(bf16[128,2048]{1,0:T(8,128)(2,1)S(1)} %get-tuple-element.23), channel_id=1, source_target_pairs={{0,8},{1,9},{2,10},{3,11},{4,12},{5,13},{6,14},{7,15},{8,0},{9,1},... | collective-permute-start | bytes 1572872 | tf_op jit(solution)/shard_map/ppermute | solution.py:404
  54.8 23.1 %copy-start.5 = (bf16[128,2048]{1,0:T(8,128)(2,1)S(1)}, bf16[128,2048]{1,0:T(8,128)(2,1)}, u32[]{:S(2)}) copy-start(bf16[128,2048]{1,0:T(8,128)(2,1)} %refs_0_.1) | copy-start | bytes 1572868
  54.8 34.3 %all-to-all-start.2 = ((bf16[8,48,2048]{2,1,0:T(8,128)(2,1)}), bf16[8,48,2048]{2,1,0:T(8,128)(2,1)}, u32[]{:S(2)}, u32[]{:S(2)}) async-start(bf16[8,48,2048]{2,1,0:T(8,128)(2,1)} %bitcast.21), calls=%async_computation.2 | async-start | bytes 3145728 | tf_op jit(solution)/shard_map/all_to_all | solution.py:369
  89.1 30.3 %all-to-all-start.4 = ((bf16[8,48,2048]{2,1,0:T(8,128)(2,1)}), bf16[8,48,2048]{2,1,0:T(8,128)(2,1)S(1)}, u32[]{:S(2)}, u32[]{:S(2)}) async-start(bf16[8,48,2048]{2,1,0:T(8,128)(2,1)} %bitcast.19), calls=%async_computation.4 | async-start | bytes 3145728 | tf_op jit(solution)/shard_map/all_to_all | solution.py:369
  92.7 26.0 %collective-permute-start.1 = (bf16[64,2048]{1,0:T(8,128)(2,1)S(1)}, bf16[64,2048]{1,0:T(8,128)(2,1)S(1)}, u32[]{:S(2)}, u32[]{:S(2)}) collective-permute-start(bf16[64,2048]{1,0:T(8,128)(2,1)S(1)} %get-tuple-element.25), channel_id=1, source_target_pairs={{0,8},{1,9},{2,10},{3,11},{4,12},{5,13},{6,14},{7,15},{8,0},{9,1},... | collective-permute-start | bytes 786440 | tf_op jit(solution)/shard_map/ppermute | solution.py:404
  118.7 0.7 copy-start
  119.4 1.2 copy-start.8
  120.6 30.8 %all-to-all-start.3 = ((bf16[8,48,2048]{2,1,0:T(8,128)(2,1)}), bf16[8,48,2048]{2,1,0:T(8,128)(2,1)S(1)}, u32[]{:S(2)}, u32[]{:S(2)}) async-start(bf16[8,48,2048]{2,1,0:T(8,128)(2,1)} %ordered.2.refs_0_), calls=%async_computation.3 | async-start | bytes 3145728 | tf_op jit(solution)/shard_map/all_to_all | solution.py:369
  124.8 26.5 %collective-permute-start.2 = (bf16[64,2048]{1,0:T(8,128)(2,1)}, bf16[64,2048]{1,0:T(8,128)(2,1)S(1)}, u32[]{:S(2)}, u32[]{:S(2)}) collective-permute-start(bf16[64,2048]{1,0:T(8,128)(2,1)} %get-tuple-element.28), channel_id=1, source_target_pairs={{0,8},{1,9},{2,10},{3,11},{4,12},{5,13},{6,14},{7,15},{8,0},{9,1},... | collective-permute-start | bytes 786440 | tf_op jit(solution)/shard_map/ppermute | solution.py:404
  151.4 24.4 %copy-start.1 = (bf16[64,2048]{1,0:T(8,128)(2,1)S(1)}, bf16[64,2048]{1,0:T(8,128)(2,1)}, u32[]{:S(2)}) copy-start(bf16[64,2048]{1,0:T(8,128)(2,1)} %copy-done) | copy-start | bytes 786436
  151.4 24.4 %copy-start.3 = (f32[128,128]{1,0:T(8,128)S(1)}, f32[128,128]{1,0:T(8,128)}, u32[]{:S(2)}) copy-start(f32[128,128]{1,0:T(8,128)} %copy-done.2) | copy-start | bytes 196612
  175.8 4.3 %copy-start.6 = (bf16[128,2048]{1,0:T(8,128)(2,1)S(1)}, bf16[128,2048]{1,0:T(8,128)(2,1)}, u32[]{:S(2)}) copy-start(bf16[128,2048]{1,0:T(8,128)(2,1)} %refs_0_.1) | copy-start | bytes 1572868
  177.1 26.6 %collective-permute-start.3 = (bf16[128,2048]{1,0:T(8,128)(2,1)S(1)}, bf16[128,2048]{1,0:T(8,128)(2,1)S(1)}, u32[]{:S(2)}, u32[]{:S(2)}) collective-permute-start(bf16[128,2048]{1,0:T(8,128)(2,1)S(1)} %get-tuple-element.29), channel_id=1, source_target_pairs={{0,8},{1,9},{2,10},{3,11},{4,12},{5,13},{6,14},{7,15},{8,0},{9,1},... | collective-permute-start | bytes 1572872 | tf_op jit(solution)/shard_map/ppermute | solution.py:404
  177.7 25.3 %collective-permute-start.4 = (f32[8,128]{1,0:T(8,128)S(1)}, f32[8,128]{1,0:T(8,128)S(1)}, u32[]{:S(2)}, u32[]{:S(2)}) collective-permute-start(f32[8,128]{1,0:T(8,128)S(1)} %get-tuple-element.31), channel_id=1, source_target_pairs={{0,8},{1,9},{2,10},{3,11},{4,12},{5,13},{6,14},{7,15},{8,0},{9,1},... | collective-permute-start | bytes 12296 | tf_op jit(solution)/shard_map/ppermute | solution.py:404

commit v11 on v8

--- a/solution.py
+++ b/solution.py
@@ -22,6 +22,10 @@
     return jnp.dot(a, b, preferred_element_type=F32)
 
 
+def in_hbm(array):
+    return pltpu.with_memory_space_constraint(array, pltpu.HBM)
+
+
 def iota(shape, dimension):
     return lax.broadcasted_iota(jnp.int32, shape, dimension)
 
@@ -34,26 +38,18 @@
     return flags(iota((length, length), 0) < iota((length, length), 1))
 
 
-def pack_kernel(rows_ref, ids_ref, weights_ref, out_ref):
-    count, lines, tok_rows = out_ref.shape
-    packed = jnp.concatenate(
-        [
-            rows_ref[...].astype(F32),
-            ids_ref[...].astype(F32),
-            weights_ref[...],
-            jnp.zeros((lines - 1 - 2 * TOP, tok_rows), F32),
-        ],
-        axis=0,
-    )
-    for n in range(count):
-        out_ref[n] = packed
-
-
-def fetch_kernel(me_ref, packed_ref, table_ref, out_ref):
-    device_count, _, tok_rows = packed_ref.shape
+def repeat_kernel(rows_ref, out_ref):
+    for n in range(out_ref.shape[0]):
+        out_ref[n] = rows_ref[...]
+
+
+def fetch_kernel(me_ref, rows_ref, table_hbm, out_ref, table_ref, sem):
+    copy = pltpu.make_async_copy(table_hbm, table_ref, sem)
+    copy.start()
+    device_count, _, tok_rows = rows_ref.shape
     held = table_ref.shape[0]
     look_cap = out_ref.shape[0] // device_count
-    local = packed_ref[:, 0, :].astype(jnp.int32) - me_ref[0] * held
+    local = rows_ref[:, 0, :] - me_ref[0] * held
     hit = (local >= 0) & (local < held)
     rank = dot(flags(hit), earlier(tok_rows)).astype(jnp.int32)
     rank = jnp.where(hit, rank, -1)
@@ -64,7 +60,9 @@
         mine = jnp.where(slot == rank[source : source + 1], local[source : source + 1], 0)
         wanted = jnp.sum(mine, axis=1, keepdims=True)
         picks.append(flags(place == wanted))
-    out_ref[...] = dot(jnp.concatenate(picks, axis=0), table_ref[...]).astype(BF16)
+    pick = jnp.concatenate(picks, axis=0)
+    copy.wait()
+    out_ref[...] = dot(pick, table_ref[...]).astype(BF16)
 
 
 def turned(rows):
@@ -72,76 +70,67 @@
     return jnp.concatenate([rows, jnp.zeros((length - count, length), F32)], axis=0).T
 
 
-def plan_kernel(
+def plan_slots(me, ids_ref, pick_ref, slots_ref):
+    tok_rows = ids_ref.shape[1]
+    half = pick_ref.shape[0] // (2 * PAIR)
+    exp_dev = EXPERTS // (2 * half)
+    flip = me % 2
+    inside = iota((half * exp_dev, tok_rows), 0)
+    expert = inside + me // half * half * exp_dev
+    place = iota((PAIR, tok_rows), 0)
+    ids = ids_ref[...]
+    chosen = [ids[k : k + 1] == expert for k in range(TOP)]
+    hit = functools.reduce(jnp.logical_or, chosen)
+    rank = jnp.where(hit, dot(flags(hit), earlier(tok_rows)).astype(jnp.int32), -1000)
+    lines = []
+    for at in range(0, half * exp_dev, 2):
+        one, two = rank[at : at + 1], rank[at + 1 : at + 2]
+        upper = jnp.where(flip == 0, one, two)
+        lower = jnp.where(flip == 0, two, one) + CAP
+        here = ((place < CAP) & (place == upper)) | ((place >= CAP) & (place == lower))
+        lines.append(here.astype(F32))
+    pick_ref[...] = jnp.concatenate(lines, axis=0).astype(BF16)
+    slot = (inside // 2) * PAIR + ((inside + flip) & 1) * CAP + rank
+    found = [
+        jnp.sum(jnp.where(chosen[k], slot + 1, 0), axis=0, keepdims=True) - 1 for k in range(TOP)
+    ]
+    slots_ref[...] = turned(jnp.concatenate(found, axis=0).astype(F32)).astype(jnp.int32)
+
+
+def near_plan_kernel(
     me_ref,
     rows_ref,
-    packed_ref,
+    ids_ref,
+    weights_ref,
     scales_ref,
-    fetched_ref,
+    _,
     put_ref,
-    near_ref,
-    far_ref,
-    near_slots_ref,
-    far_slots_ref,
+    pick_ref,
+    slots_ref,
     columns_ref,
+    ids_out_ref,
+    weights_out_ref,
 ):
+    ids_out_ref[...] = ids_ref[...]
+    weights_out_ref[...] = weights_ref[...]
     tok_rows = rows_ref.shape[1]
-    slots = put_ref.shape[1]
-    half = near_ref.shape[0] // (2 * PAIR)
-    device_count = 2 * half
-    exp_dev = EXPERTS // device_count
-    look_cap = slots // device_count
     me, held = me_ref[0], me_ref[1]
-    flip = me % 2
-    start = me // half * half * exp_dev
-    before = earlier(tok_rows)
-
+    device_count = pick_ref.shape[0] // PAIR
+    look_cap = put_ref.shape[1] // device_count
     row = jnp.broadcast_to(rows_ref[...], (device_count, tok_rows))
     low = iota((device_count, tok_rows), 0) * held
     hit = (row >= low) & (row < low + held)
-    rank = jnp.where(hit, dot(flags(hit), before).astype(jnp.int32), -1)
+    rank = jnp.where(hit, dot(flags(hit), earlier(tok_rows)).astype(jnp.int32), -1)
     slot = iota((look_cap, tok_rows), 0)
     put = [(slot == rank[o : o + 1]).astype(F32) for o in range(device_count)]
     put_ref[...] = jnp.concatenate(put, axis=0).T.astype(BF16)
-
-    expert = iota((half * exp_dev, tok_rows), 0) + start
-    place = iota((PAIR, tok_rows), 0)
-    inside = iota((half * exp_dev, tok_rows), 0)
-    flipped = ((inside + flip) & 1) * CAP
-    device = inside // exp_dev
-    chunk = (inside % exp_dev) // 2
-    mine = packed_ref[me]
-    other = packed_ref[(me + half) % device_count]
-    for far, packed in enumerate((mine, other)):
-        ids = [packed[1 + k : 2 + k].astype(jnp.int32) for k in range(TOP)]
-        chosen = [ids[k] == expert for k in range(TOP)]
-        hit = functools.reduce(jnp.logical_or, chosen)
-        rank = jnp.where(hit, dot(flags(hit), before).astype(jnp.int32), -1000)
-        lines = [[], []]
-        for d in range(half):
-            for c in range(2):
-                at = d * exp_dev + 2 * c
-                one, two = rank[at : at + 1], rank[at + 1 : at + 2]
-                upper = jnp.where(flip == 0, one, two)
-                lower = jnp.where(flip == 0, two, one) + CAP
-                here = ((place < CAP) & (place == upper)) | ((place >= CAP) & (place == lower))
-                lines[c].append(here.astype(F32))
-        both = [line for pair in zip(*lines) for line in pair]
-        pick_ref = far_ref if far else near_ref
-        pick_ref[...] = jnp.concatenate(both, axis=0).astype(BF16)
-        slot = device * (2 * PAIR) + chunk * PAIR + flipped + rank
-        found = [
-            jnp.sum(jnp.where(chosen[k], slot + 1, 0), axis=0, keepdims=True) - 1
-            for k in range(TOP)
-        ]
-        slots_out = far_slots_ref if far else near_slots_ref
-        found = turned(jnp.concatenate(found, axis=0).astype(F32))
-        slots_out[...] = found.astype(jnp.int32)
-    columns_ref[...] = turned(
-        jnp.concatenate(
-            [mine[1 + TOP : 1 + 2 * TOP], other[1 + TOP : 1 + 2 * TOP], scales_ref[...]], axis=0
-        )
-    )
+    plan_slots(me, ids_ref, pick_ref, slots_ref)
+    columns_ref[...] = turned(jnp.concatenate([weights_ref[...], scales_ref[...]], axis=0))
+
+
+def far_plan_kernel(me_ref, ids_ref, weights_ref, pick_ref, slots_ref, columns_ref):
+    plan_slots(me_ref[0], ids_ref, pick_ref, slots_ref)
+    columns_ref[...] = turned(weights_ref[...])
 
 
 def pick_slots(pick_ref, state_ref, out_hbm, sent_ref, sem, left, width):
@@ -155,7 +144,7 @@
 
 
 def state_kernel(
-    put_ref, pick_ref, returned_ref, values_ref, columns_ref, state_ref, out_hbm, sent_ref, sem
+    put_ref, pick_ref, returned_ref, values_ref, columns_ref, _, state_ref, out_hbm, sent_ref, sem
 ):
     features = values_ref.shape[1]
     width = features // sem.shape[0]
@@ -166,7 +155,7 @@
             at = left + b * BLOCK
             scaled = (
                 values_ref[:, at : at + BLOCK].astype(F32)
-                * columns_ref[:, 2 * TOP + at // BLOCK : 2 * TOP + at // BLOCK + 1]
+                * columns_ref[:, TOP + at // BLOCK : TOP + at // BLOCK + 1]
             )
             state_ref[:, at : at + BLOCK] = (
                 scaled + found[:, b * BLOCK : (b + 1) * BLOCK]
@@ -187,21 +176,28 @@
         copy.wait()
 
 
-def expert_kernel(after, rows_ref, *refs):
+def expert_kernel(after, rows_hbm, *refs):
     wg_hbm, wu_hbm, wd_hbm, out_ref = refs[after : after + 4]
-    x_ref, wg_ref, wu_ref, wd_ref, hidden_ref, result_ref, sem = refs[after + 4 :]
-    exp_dev = wg_hbm.shape[0]
-    held, features, width = wg_ref.shape
+    rows_ref, x_ref, wg_ref, wu_ref, both_ref, wd_ref, hidden_ref, result_ref, sem, rows_sem = refs[
+        after + 4 :
+    ]
+    exp_dev, features, width = wg_hbm.shape
     half = rows_ref.shape[0]
-    up_cuts = ((0, 512), (512, 512), (1024, width - 1024))
+    held = wg_ref.shape[0]
+    wide = wg_ref.shape[2]
+    rest = width - wide
+    up_cuts = ((0, 512), (512, 512), (1024, wide - 1024))
     down_cuts = tuple((at, 512) for at in range(0, features, 512))
 
     def weight_copies(j, place):
         copies = []
         for at, size in up_cuts:
-            for hbm, ref in ((wg_hbm, wg_ref), (wu_hbm, wu_ref)):
-                cols = pl.ds(at, size)
-                copies.append((hbm.at[j, :, cols], ref.at[place, :, cols]))
+            cols = pl.ds(at, size)
+            copies.append((wg_hbm.at[j, :, cols], wg_ref.at[place, :, cols]))
+            copies.append((wu_hbm.at[j, :, cols], wu_ref.at[place, :, cols]))
+        for n, hbm in enumerate((wg_hbm, wu_hbm)):
+            last = both_ref.at[place, :, pl.ds(n * rest, rest)]
+            copies.append((hbm.at[j, :, pl.ds(wide, rest)], last))
         for at, size in down_cuts:
             cols = pl.ds(at, size)
             copies.append((wd_hbm.at[j, :, cols], wd_ref.at[place, :, cols]))
@@ -210,9 +206,12 @@
             for n, (src, dst) in enumerate(copies)
         ]
 
+    rows_copy = pltpu.make_async_copy(rows_hbm, rows_ref, rows_sem)
+    rows_copy.start()
     for j in range(held):
         for copy in weight_copies(j, j):
             copy.start()
+    rows_copy.wait()
 
     low = iota((PAIR, features), 0) < CAP
     for chunk in range(exp_dev // 2):
@@ -241,16 +240,25 @@
                 for n in range(first, first + count):
                     later[n].start()
 
+        def hide(gate, up, at):
+            hidden = gate / (1.0 + jnp.exp(-gate)) * up
+            hidden_ref[:, at : at + gate.shape[1]] = hidden.astype(BF16)
+
         n = 0
         for at, size in up_cuts:
             copies[n].wait()
             copies[n + 1].wait()
-            x = x_ref[j]
-            gate = dot(x, wg_ref[place, :, at : at + size])
-            up = dot(x, wu_ref[place, :, at : at + size])
-            hidden_ref[:, at : at + size] = (gate / (1.0 + jnp.exp(-gate)) * up).astype(BF16)
+            gate = dot(x_ref[j], wg_ref[place, :, at : at + size])
+            up = dot(x_ref[j], wu_ref[place, :, at : at + size])
+            hide(gate, up, at)
             refill(n, 2)
             n += 2
+        copies[n].wait()
+        copies[n + 1].wait()
+        both = dot(x_ref[j], both_ref[place])
+        hide(both[:, :rest], both[:, rest:], wide)
+        refill(n, 2)
+        n += 2
         for at, size in down_cuts:
             copies[n].wait()
             result_ref[j, :, at : at + size] = dot(
@@ -273,59 +281,75 @@
     w_gate, w_up, w_down = weights
     exp_dev, features, width = w_gate.shape
     half = rows_in.shape[0]
+    rows = half * CAP
     held = 2
-    rows = half * CAP
+    rest = 128
+    wide = width - rest
     anywhere = pl.BlockSpec(memory_space=pl.ANY)
+    hbm = pl.BlockSpec(memory_space=pltpu.HBM)
     vmem = pl.BlockSpec(memory_space=VMEM)
     return pl.pallas_call(
         functools.partial(expert_kernel, len(after)),
-        out_shape=jax.ShapeDtypeStruct((half, exp_dev * CAP, features), BF16),
-        in_specs=[vmem] + [anywhere] * (3 + len(after)),
+        out_shape=pltpu.HBM((half, exp_dev * CAP, features), BF16),
+        in_specs=[hbm] + [anywhere] * len(after) + [hbm] * 3,
         out_specs=vmem,
         scratch_shapes=[
+            VMEM(rows_in.shape, BF16),
             VMEM((exp_dev, rows, features), BF16),
-            VMEM((held, features, width), BF16),
-            VMEM((held, features, width), BF16),
+            VMEM((held, features, wide), BF16),
+            VMEM((held, features, wide), BF16),
+            VMEM((held, features, 2 * rest), BF16),
             VMEM((held, width, features), BF16),
             VMEM((rows, width), BF16),
             VMEM((exp_dev, rows, features), F32),
-            pltpu.SemaphoreType.DMA((held, 10)),
+            pltpu.SemaphoreType.DMA((held, 12)),
+            pltpu.SemaphoreType.DMA,
         ],
-        compiler_params=pltpu.CompilerParams(vmem_limit_bytes=43 * 1024 * 1024),
+        compiler_params=pltpu.CompilerParams(vmem_limit_bytes=46 * 1024 * 1024),
         cost_estimate=pl.CostEstimate(
             flops=12 * exp_dev * rows * features * width,
             bytes_accessed=6 * exp_dev * features * width,
             transcendentals=exp_dev * rows * width,
         ),
         name=name,
-    )(rows_in, *after, w_gate, w_up, w_down)
-
-
-def mix_kernel(first_column, slots_ref, columns_ref, back_ref, *refs):
+    )(in_hbm(rows_in), *[in_hbm(array) for array in after], in_hbm(w_gate), in_hbm(w_up), in_hbm(w_down))
+
+
+def mix_kernel(after, slots_ref, columns_ref, back_ref, grad_ref, *refs):
+    refs = refs[after:]
     mixed_ref, grads_ref = refs[-2:]
-    tok_rows = slots_ref.shape[0]
-    count, features = back_ref.shape
-    grad = jnp.concatenate([ref[...] for ref in refs[:-2]], axis=0)
+    tok_rows, features = grad_ref.shape
+    count = back_ref.shape[0]
     column = iota((tok_rows, count), 1)
     inner = lax.dot_general(
-        grad, back_ref[...], (((1,), (1,)), ((), ())), preferred_element_type=F32
+        grad_ref[...], back_ref[...], (((1,), (1,)), ((), ())), preferred_element_type=F32
     )
     total = jnp.zeros((tok_rows, count), F32)
     place = iota((tok_rows, tok_rows), 1)
     wide = jnp.zeros((tok_rows, tok_rows), F32)
     for k in range(TOP):
         here = column == slots_ref[:, k : k + 1]
-        weight = columns_ref[:, first_column + k : first_column + k + 1]
-        total = total + jnp.where(here, weight, 0.0)
+        total = total + jnp.where(here, columns_ref[:, k : k + 1], 0.0)
         value = jnp.sum(jnp.where(here, inner, 0.0), axis=1, keepdims=True)
         wide = wide + jnp.where(place == k, value, 0.0)
     high = total.astype(BF16)
     rest = (total - high.astype(F32)).astype(BF16)
     width = 512
     for at in range(0, features, width):
-        rows = back_ref[:, at : at + width]
-        mixed_ref[:, at : at + width] = (dot(high, rows) + dot(rest, rows)).astype(mixed_ref.dtype)
-    grads_ref[...] = wide.T[: grads_ref.shape[0], :]
+        cols = slice(at, at + width)
+        value = dot(high, back_ref[:, cols]) + dot(rest, back_ref[:, cols])
+        if len(refs) > 2:
+            value = value + refs[0][:, cols].astype(F32)
+        mixed_ref[:, cols] = value.astype(BF16)
+    lines = grads_ref.shape[0]
+    grads = wide.T[:lines, :]
+    if len(refs) > 2:
+        grads = grads + refs[1][:lines, :]
+    grads_ref[...] = grads
+
+
+def after_far_kernel(sent_hbm, far_hbm, grad_ref, sent_out_hbm, grad_out_ref):
+    grad_out_ref[...] = grad_ref[...]
 
 
 def swap(array, groups=None):
@@ -366,7 +390,7 @@
         pairs = [(i, (i + half) % device_count) for i in range(device_count)]
         return lax.ppermute(array, "expert", pairs)
 
-    def ordered(array, *earlier_arrays):
+    def ordered(array, *earlier_arrays, flops=0):
         return pl.pallas_call(
             lambda *refs: None,
             out_shape=shape(array.shape, array.dtype),
@@ -374,56 +398,79 @@
             out_specs=anywhere,
             input_output_aliases={0: 0},
             compiler_params=SMALL,
+            cost_estimate=pl.CostEstimate(flops=flops, bytes_accessed=0, transcendentals=0),
             name="ordered",
         )(array, *earlier_arrays)
 
-    split = tok_rows // 2
-    other_grads = (mirrored(out_grad[:split]), mirrored(out_grad[split:]))
-    packed = pl.pallas_call(
-        pack_kernel,
-        out_shape=shape((device_count, 16, tok_rows), F32),
-        in_specs=[vmem] * 3,
+    all_rows = pl.pallas_call(
+        repeat_kernel,
+        out_shape=shape((device_count, 1, tok_rows), jnp.int32),
+        in_specs=[vmem],
         out_specs=vmem,
-        name="pack",
-    )(row_ids[None, :], expert_ids.T, gate_weights.T)
-    packed = swap(packed)
+        name="repeat_rows",
+    )(row_ids[None, :])
     fetched = pl.pallas_call(
         fetch_kernel,
         out_shape=shape((device_count * look_cap, features), BF16),
-        in_specs=[smem, vmem, vmem],
+        in_specs=[smem, vmem, pl.BlockSpec(memory_space=pltpu.HBM)],
         out_specs=vmem,
+        scratch_shapes=[VMEM(table.shape, BF16), pltpu.SemaphoreType.DMA],
         compiler_params=SMALL,
         name="fetch_rows",
-    )(place, packed, table)
+    )(place, swap(all_rows), in_hbm(table))
     returned = swap(fetched.reshape(device_count, look_cap, features))
-    put, near_pick, far_pick, near_of, far_of, columns = pl.pallas_call(
-        plan_kernel,
+    turned_ids, turned_weights = expert_ids.T, gate_weights.T
+    pick_shape = shape((slots, tok_rows), BF16)
+    square = (tok_rows, tok_rows)
+    put, near_pick, near_of, near_columns, sent_ids, sent_weights = pl.pallas_call(
+        near_plan_kernel,
         out_shape=(
             shape((tok_rows, device_count * look_cap), BF16),
-            shape((slots, tok_rows), BF16),
-            shape((slots, tok_rows), BF16),
-            shape((tok_rows, tok_rows), jnp.int32),
-            shape((tok_rows, tok_rows), jnp.int32),
-            shape((tok_rows, tok_rows), F32),
+            pick_shape,
+            shape(square, jnp.int32),
+            shape(square, F32),
+            shape(turned_ids.shape, jnp.int32),
+            shape(turned_weights.shape, F32),
         ),
-        in_specs=[smem, vmem, vmem, vmem, anywhere],
+        in_specs=[smem, vmem, vmem, vmem, vmem, anywhere],
         out_specs=(vmem,) * 6,
         compiler_params=SMALL,
-        name="plan",
-    )(place, row_ids[None, :], packed, jnp.exp2(block_exps.T.astype(F32)), fetched)
+        name="near_plan",
+    )(
+        place,
+        row_ids[None, :],
+        turned_ids,
+        turned_weights,
+        jnp.exp2(block_exps.T.astype(F32)),
+        fetched,
+    )
+    far_pick, far_of, far_columns = pl.pallas_call(
+        far_plan_kernel,
+        out_shape=(pick_shape, shape(square, jnp.int32), shape(square, F32)),
+        in_specs=[smem, vmem, vmem],
+        out_specs=(vmem,) * 3,
+        compiler_params=SMALL,
+        name="far_plan",
+    )(place, mirrored(sent_ids), mirrored(sent_weights))
+
     sent_shape = pltpu.HBM((slots, features), BF16)
     sent_scratch = [VMEM((slots, features), BF16), pltpu.SemaphoreType.DMA((4,))]
     state, near_sent = pl.pallas_call(
         state_kernel,
         out_shape=(shape((tok_rows, features), BF16), sent_shape),
-        in_specs=[vmem] * 5,
+        in_specs=[vmem] * 5 + [anywhere],
         out_specs=(vmem, anywhere),
         scratch_shapes=sent_scratch,
         compiler_params=SMALL,
         name="token_state",
-    )(put, near_pick, returned.reshape(device_count * look_cap, features), block_values, columns)
-    other_state = mirrored(state)
-    near_rows = swap(near_sent.reshape(half, 2 * PAIR, features), halves)
+    )(
+        put,
+        near_pick,
+        returned.reshape(device_count * look_cap, features),
+        block_values,
+        near_columns,
+        far_pick,
+    )
     far_sent = pl.pallas_call(
         pick_kernel,
         out_shape=sent_shape,
@@ -431,33 +478,51 @@
         out_specs=anywhere,
         scratch_shapes=sent_scratch,
         compiler_params=SMALL,
-        cost_estimate=pl.CostEstimate(
-            flops=20_000_000_000, bytes_accessed=4 * slots * features, transcendentals=0
-        ),
         name="far_slots",
-    )(far_pick, other_state).reshape(half, 2 * PAIR, features)
-    far_rows = swap(far_sent, halves)
+    )(far_pick, mirrored(state))
+    rows_shape = (half, 2 * PAIR, features)
+    far_rows = swap(far_sent.reshape(rows_shape), halves)
+    near_sent, sent_grad = pl.pallas_call(
+        after_far_kernel,
+        out_shape=(shape(rows_shape, BF16), shape((tok_rows, features), BF16)),
+        in_specs=[anywhere, anywhere, vmem],
+        out_specs=(anywhere, vmem),
+        input_output_aliases={0: 0},
+        compiler_params=SMALL,
+        name="after_far",
+    )(in_hbm(near_sent.reshape(rows_shape)), in_hbm(far_rows), out_grad)
+    near_rows = swap(near_sent, halves)
 
     weights = (w_gate, w_up, w_down)
-    near_out = expert_call("near_experts", near_rows, weights, after=(far_sent,))
-    far_out = expert_call("far_experts", far_rows, weights, after=(near_out,))
-    near_back = swap(ordered(near_out, other_grads[0]), halves)
-    far_back = swap(ordered(far_out, near_back, other_grads[1]), halves)
-
-    def mixed_rows(name, first_column, slot_of, back, grads, kind):
+    other_grad = mirrored(sent_grad)
+    far_out = expert_call("far_experts", far_rows, weights)
+    far_out = ordered(in_hbm(far_out), in_hbm(near_rows), other_grad)
+    near_out = expert_call("near_experts", near_rows, weights, after=(far_out,))
+    far_back = swap(far_out, halves)
+
+    def mixed_rows(name, slot_of, columns, back, grad, lines, more=(), after=()):
         return pl.pallas_call(
-            functools.partial(mix_kernel, first_column),
-            out_shape=(shape((tok_rows, features), kind), shape((2 * TOP, tok_rows), F32)),
-            in_specs=[vmem] * (3 + len(grads)),
+            functools.partial(mix_kernel, len(after)),
+            out_shape=(shape((tok_rows, features), BF16), shape((lines, tok_rows), F32)),
+            in_specs=[vmem] * 4 + [anywhere] * len(after) + [vmem] * len(more),
             out_specs=(vmem, vmem),
             compiler_params=SMALL,
             name=name,
-        )(slot_of, columns, back.reshape(slots, features), *grads)
-
-    near_mixed, near_grads = mixed_rows("mix_near", 0, near_of, near_back, (out_grad,), F32)
-    far_mixed, far_grads = mixed_rows("mix_far", TOP, far_of, far_back, other_grads, BF16)
-    mixed = (near_mixed + mirrored(far_mixed).astype(F32)).astype(BF16)
-    grads = (near_grads + mirrored(far_grads))[:TOP]
+        )(slot_of, columns, back.reshape(slots, features), grad, *after, *more)
+
+    far_mixed, far_grads = mixed_rows(
+        "mix_far", far_of, far_columns, far_back, other_grad, 2 * TOP, after=(in_hbm(near_out),)
+    )
+    near_back = swap(ordered(in_hbm(near_out), far_mixed), halves)
+    mixed, grads = mixed_rows(
+        "mix_near",
+        near_of,
+        near_columns,
+        near_back,
+        out_grad,
+        TOP,
+        more=(ordered(mirrored(far_mixed), flops=400_000_000_000), mirrored(far_grads)),
+    )
     return mixed, grads.T
 
 

time: 208 us -> 215 us (1.034)
  Pallas kernels: 55.2 us -> 74.6 us
  local copies, waits for them, and re-layouts: 12 us -> 1.2 us
  starting transfers between devices: 36.3 us -> 29.6 us
  waiting for transfers between devices: 78 us -> 83.6 us
    ppermute x5 -> x6, waiting for transfers between devices: 48.2 us -> 70.6 us  [mirrored(): return lax.ppermute(array, 'expert', pairs)]
    pallas_call x6 -> x8, Pallas kernels: 49.4 us -> 67.7 us  [the longest x2 59.6 us: expert_call(): pl.pallas_call(functools.partial(expert_kernel, len(after)), out_shape=pl...]
    all_to_all x5, waiting for transfers between devices: 29.8 us -> 13 us  [swap(): lax.all_to_all(array, 'expert', split_axis=0, concat_axis=0, tiled=True,...]
    unnamed x29 -> x20, local copies, waits for them, and re-layouts: 9.64 us -> 1.2 us
    all_to_all x5, starting transfers between devices: 27.5 us -> 22.7 us  [swap(): lax.all_to_all(array, 'expert', split_axis=0, concat_axis=0, tiled=True,...]
    ppermute x5 -> x6, starting transfers between devices: 8.76 us -> 6.9 us  [mirrored(): return lax.ppermute(array, 'expert', pairs)]
  transfers between devices with their start and end apart: 10 -> 11, of which waited for: 5 -> 7; matrix products, arithmetic and copies ran while one was open for 2% -> 0% of each run, Pallas kernels for 23% -> 29%
where the time goes in v11:
time: 215 us
  waiting for transfers between devices  83.6 us (39%)
  Pallas kernels  74.6 us (35%)
  starting transfers between devices  29.6 us (14%)
  blocking collectives  24.7 us (11%)
    ppermute x6, waiting for transfers between devices, mirrored(): return lax.ppermute(array, 'expert', pairs)  70.6 us
    pallas_call x2, Pallas kernels, expert_call(): pl.pallas_call(functools.partial(expert_kernel, len(after)), out_shape=pl...  59.6 us
    all_to_all x1, blocking collectives, swap(): lax.all_to_all(array, 'expert', split_axis=0, concat_axis=0, tiled=True,...  24.7 us
    all_to_all x5, starting transfers between devices, swap(): lax.all_to_all(array, 'expert', split_axis=0, concat_axis=0, tiled=True,...  22.7 us
    all_to_all x5, waiting for transfers between devices, swap(): lax.all_to_all(array, 'expert', split_axis=0, concat_axis=0, tiled=True,...  13 us
    ppermute x6, starting transfers between devices, mirrored(): return lax.ppermute(array, 'expert', pairs)  6.9 us
    pallas_call x2, Pallas kernels, mixed_rows(): pl.pallas_call(functools.partial(mix_kernel, len(after)), out_shape=(shap...  5.09 us
  transfers between devices with their start and end apart: 11, of which 7 were waited for; matrix products, arithmetic and copies ran while one was open for 0% of the time, Pallas kernels for 29%

profile of v11, /device:TPU:0, one launch (start us, length us, event | category | flops | bytes accessed | tf_op | source)
XLA Modules:
  0.0 214.7 jit_solution(11860276706660892282)
XLA Ops:
  0.6 1.3 repeat_rows.1
  1.9 7.4 %all-to-all-start = ((s32[16,1,128]{2,1,0:T(1,128)}), s32[16,1,128]{2,1,0:T(1,128)S(1)}, u32[]{:S(2)}, u32[]{:S(2)}) async-start(s32[16,1,128]{2,1,0:T(1,128)} %repeat_rows.1), calls=%async_computation | async-start | bytes 16384 | tf_op jit(solution)/shard_map/all_to_all | solution.py:356
  9.3 0.1 pad_add_fusion.me_ref
  9.4 6.3 %all-to-all-done.rows_ref = s32[16,1,128]{2,1,0:T(1,128)S(1)} async-done(((s32[16,1,128]{2,1,0:T(1,128)}), s32[16,1,128]{2,1,0:T(1,128)S(1)}, u32[]{:S(2)}, u32[]{:S(2)}) %all-to-all-start) | async-done | bytes 8224 | tf_op jit(solution)/shard_map/all_to_all | solution.py:356
  15.6 3.2 %fetch_rows.1._ = bf16[256,2048]{1,0:T(8,128)(2,1)} custom-call(s32[2]{0:T(128)S(1)} %pad_add_fusion.me_ref, s32[16,1,128]{2,1,0:T(1,128)S(1)} %all-to-all-done.rows_ref, bf16[256,2048]{1,0:T(8,128)(2,1)} %table_hbm.1), custom_call_target="tpu_custom_call" | custom-call | tf_op jit(solution)/shard_map/fetch_rows/pallas_call | solution.py:412
  18.8 0.0 copy-start.9
  18.8 0.0 copy-start.5
  18.9 0.0 copy-start.6
  18.9 0.0 copy-start.7
  18.9 0.0 copy-start.2
  18.9 3.8 %all-to-all-start.1 = ((bf16[16,16,2048]{2,1,0:T(8,128)(2,1)}), bf16[16,16,2048]{2,1,0:T(8,128)(2,1)S(1)}, u32[]{:S(2)}, u32[]{:S(2)}) async-start(bf16[16,16,2048]{2,1,0:T(8,128)(2,1)} %bitcast.5), calls=%async_computation.1 | async-start | bytes 2097152 | tf_op jit(solution)/shard_map/all_to_all | solution.py:356
  22.7 0.0 copy-done.9
  22.7 0.0 copy-done.5
  22.7 0.0 copy-done.6
  22.7 0.0 copy-done.7
  22.8 0.9 near_plan.1
  23.6 0.0 copy-start.3
  23.6 2.8 %collective-permute-start = (s32[4,128]{1,0:T(4,128)S(1)}, s32[4,128]{1,0:T(4,128)S(1)}, u32[]{:S(2)}, u32[]{:S(2)}) collective-permute-start(s32[4,128]{1,0:T(4,128)S(1)} %get-tuple-element.23), channel_id=1, source_target_pairs={{0,8},{1,9},{2,10},{3,11},{4,12},{5,13},{6,14},{7,15},{8,0},{9,1},... | collective-permute-start | bytes 6152 | tf_op jit(solution)/shard_map/ppermute | solution.py:391
  26.4 0.2 collective-permute-start.1
  26.6 22.7 %collective-permute-done.ids_ref = s32[4,128]{1,0:T(4,128)S(1)} collective-permute-done((s32[4,128]{1,0:T(4,128)S(1)}, s32[4,128]{1,0:T(4,128)S(1)}, u32[]{:S(2)}, u32[]{:S(2)}) %collective-permute-start) | collective-permute-done | bytes 2080 | tf_op jit(solution)/shard_map/ppermute | solution.py:391
  49.3 0.0 collective-permute-done.1.weights_ref
  49.3 0.8 far_plan.1
  50.2 0.0 all-to-all-done.1
  50.2 0.0 copy-done.2
  50.2 2.2 %token_state.1 = (bf16[128,2048]{1,0:T(8,128)(2,1)S(1)}, bf16[384,2048]{1,0:T(8,128)(2,1)}) custom-call(bf16[128,256]{1,0:T(8,128)(2,1)S(1)} %get-tuple-element.21.put_ref, bf16[384,128]{1,0:T(8,128)(2,1)S(1)} %get-tuple-element.22.pick_ref, bf16[256,2048]{1,0:T(8,128)(2,1)S(1)} %bitcast.14, bf16[128,2048]{1,0:T(8,128)(2,1)S(1)} %copy-done.2, ...), custom_call_target="tpu_custom_call" | custom-call | tf_op jit(solution)/shard_map/token_state/pallas_call | solution.py:458
  52.4 0.6 collective-permute-start.2
  53.0 24.3 %collective-permute-done.2.state_ref = bf16[128,2048]{1,0:T(8,128)(2,1)S(1)} collective-permute-done((bf16[128,2048]{1,0:T(8,128)(2,1)S(1)}, bf16[128,2048]{1,0:T(8,128)(2,1)S(1)}, u32[]{:S(2)}, u32[]{:S(2)}) %collective-permute-start.2) | collective-permute-done | bytes 524320 | tf_op jit(solution)/shard_map/ppermute | solution.py:391
  77.3 1.5 far_slots.1
  78.8 0.0 copy-done.3
  78.9 0.0 copy-start
  78.9 24.7 %all_to_all.30.far_hbm.rows_hbm = bf16[8,48,2048]{2,1,0:T(8,128)(2,1)} all-to-all(bf16[8,48,2048]{2,1,0:T(8,128)(2,1)} %bitcast.20), channel_id=1, replica_groups={{0,1,2,3,4,5,6,7},{8,9,10,11,12,13,14,15},{16,17,18,19,20,21,22,23},{24..., dimensions={0} | all-to-all | bytes 3145728 | tf_op jit(solution)/shard_map/all_to_all | solution.py:356
  103.6 3.6 %all-to-all-start.3 = ((bf16[8,48,2048]{2,1,0:T(8,128)(2,1)}), bf16[8,48,2048]{2,1,0:T(8,128)(2,1)S(1)}, u32[]{:S(2)}, u32[]{:S(2)}) async-start(bf16[8,48,2048]{2,1,0:T(8,128)(2,1)} %get-tuple-element.28), calls=%async_computation.3 | async-start | bytes 3145728 | tf_op jit(solution)/shard_map/all_to_all | solution.py:356
  107.2 0.3 collective-permute-start.3
  107.5 29.8 %far_experts.1.refs_0_ = bf16[8,48,2048]{2,1,0:T(8,128)(2,1)} custom-call(bf16[8,48,2048]{2,1,0:T(8,128)(2,1)} %all_to_all.30.far_hbm.rows_hbm, bf16[4,2048,1408]{2,1,0:T(8,128)(2,1)} %refs_1_.3, bf16[4,2048,1408]{2,1,0:T(8,128)(2,1)} %refs_2_.3, bf16[4,1408,2048]{2,1,0:T(8,128)(2,1)} %refs_3_.1), custom_call_target="tpu_custom_call" | custom-call | flops 13287555072 | bytes 69206016 | tf_op jit(solution)/shard_map/far_experts/pallas_call | solution.py:291
  137.3 0.0 collective-permute-done.3.refs_2_.grad_ref
  137.3 1.1 all-to-all-done.3.refs_1_.rows_hbm
  138.5 1.1 copy-done.8
  139.6 3.6 %all-to-all-start.4 = ((bf16[8,48,2048]{2,1,0:T(8,128)(2,1)}), bf16[8,48,2048]{2,1,0:T(8,128)(2,1)S(1)}, u32[]{:S(2)}, u32[]{:S(2)}) async-start(bf16[8,48,2048]{2,1,0:T(8,128)(2,1)} %ordered.3.refs_0_), calls=%async_computation.4 | async-start | bytes 3145728 | tf_op jit(solution)/shard_map/all_to_all | solution.py:356
  143.2 29.8 %near_experts.1.refs_0_ = bf16[8,48,2048]{2,1,0:T(8,128)(2,1)} custom-call(bf16[8,48,2048]{2,1,0:T(8,128)(2,1)} %copy-done.8, bf16[8,48,2048]{2,1,0:T(8,128)(2,1)} %ordered.3.refs_0_, bf16[4,2048,1408]{2,1,0:T(8,128)(2,1)} %refs_1_.3, bf16[4,2048,1408]{2,1,0:T(8,128)(2,1)} %refs_2_.3, bf16[4,1408,2048]{2,1,0:T(8,128)(2,1)} %refs_3_.1), custom_call_target="tpu_custom_call" | custom-call | flops 13287555072 | bytes 69206016 | tf_op jit(solution)/shard_map/near_experts/pallas_call | solution.py:291
  173.0 0.0 all-to-all-done.4
  173.0 1.6 mix_far.1
  174.7 2.0 collective-permute-start.4
  176.7 4.3 %all-to-all-start.5 = ((bf16[8,48,2048]{2,1,0:T(8,128)(2,1)}), bf16[8,48,2048]{2,1,0:T(8,128)(2,1)}, u32[]{:S(2)}, u32[]{:S(2)}) async-start(bf16[8,48,2048]{2,1,0:T(8,128)(2,1)} %ordered.4), calls=%async_computation.5 | async-start | bytes 3145728 | tf_op jit(solution)/shard_map/all_to_all | solution.py:356
  181.0 1.0 collective-permute-start.5
  182.0 19.2 %collective-permute-done.4.refs_0_ = bf16[128,2048]{1,0:T(8,128)(2,1)S(1)} collective-permute-done((bf16[128,2048]{1,0:T(8,128)(2,1)S(1)}, bf16[128,2048]{1,0:T(8,128)(2,1)S(1)}, u32[]{:S(2)}, u32[]{:S(2)}) %collective-permute-start.4) | collective-permute-done | bytes 524320 | tf_op jit(solution)/shard_map/ppermute | solution.py:391
  201.2 4.4 %collective-permute-done.5.refs_1_ = f32[8,128]{1,0:T(8,128)} collective-permute-done((f32[8,128]{1,0:T(8,128)}, f32[8,128]{1,0:T(8,128)}, u32[]{:S(2)}, u32[]{:S(2)}) %collective-permute-start.5) | collective-permute-done | bytes 4128 | tf_op jit(solution)/shard_map/ppermute | solution.py:391
  205.6 5.6 %all-to-all-done.5 = bf16[8,48,2048]{2,1,0:T(8,128)(2,1)} async-done(((bf16[8,48,2048]{2,1,0:T(8,128)(2,1)}), bf16[8,48,2048]{2,1,0:T(8,128)(2,1)}, u32[]{:S(2)}, u32[]{:S(2)}) %all-to-all-start.5) | async-done | bytes 1572896 | tf_op jit(solution)/shard_map/all_to_all | solution.py:356
  211.2 3.4 %mix_near.1 = (bf16[128,2048]{1,0:T(8,128)(2,1)}, f32[4,128]{1,0:T(4,128)}) custom-call(s32[128,128]{1,0:T(8,128)S(1)} %get-tuple-element.19.slots_ref, f32[128,128]{1,0:T(8,128)S(1)} %copy-done.4, bf16[384,2048]{1,0:T(8,128)(2,1)} %bitcast.10.back_ref, bf16[128,2048]{1,0:T(8,128)(2,1)S(1)} %copy-done.1, bf16[128,2048]{1,0:T(8,128)(2,1)S(1)} %ordered.5.refs_0_, ...), custom_call_target="tpu_custom_call" | custom-call | tf_op jit(solution)/shard_map/mix_near/pallas_call | solution.py:504
  (11 shorter events, 0.1 us)
Async XLA Ops:
  1.9 13.7 %all-to-all-start = ((s32[16,1,128]{2,1,0:T(1,128)}), s32[16,1,128]{2,1,0:T(1,128)S(1)}, u32[]{:S(2)}, u32[]{:S(2)}) async-start(s32[16,1,128]{2,1,0:T(1,128)} %repeat_rows.1), calls=%async_computation | async-start | bytes 16384 | tf_op jit(solution)/shard_map/all_to_all | solution.py:356
  18.8 3.9 %copy-start.9 = (s32[128,16]{0,1:T(8,128)S(1)}, s32[128,16]{0,1:T(8,128)}, u32[]{:S(2)}) copy-start(s32[128,16]{0,1:T(8,128)} %param.11) | copy-start | bytes 24580
  18.8 3.9 %copy-start.5 = (s32[128]{0:T(128)S(1)}, s32[128]{0:T(128)}, u32[]{:S(2)}) copy-start(s32[128]{0:T(128)} %param.12) | copy-start | bytes 1540
  18.9 3.9 %copy-start.6 = (s32[128,4]{0,1:T(4,128)S(1)}, s32[128,4]{0,1:T(4,128)}, u32[]{:S(2)}) copy-start(s32[128,4]{0,1:T(4,128)} %param.13) | copy-start | bytes 6148
  18.9 3.9 %copy-start.7 = (f32[128,4]{0,1:T(4,128)S(1)}, f32[128,4]{0,1:T(4,128)}, u32[]{:S(2)}) copy-start(f32[128,4]{0,1:T(4,128)} %param.14) | copy-start | bytes 6148
  18.9 31.3 %copy-start.2 = (bf16[128,2048]{1,0:T(8,128)(2,1)S(1)}, bf16[128,2048]{1,0:T(8,128)(2,1)}, u32[]{:S(2)}) copy-start(bf16[128,2048]{1,0:T(8,128)(2,1)} %values_ref.1) | copy-start | bytes 1572868
  18.9 31.3 %all-to-all-start.1 = ((bf16[16,16,2048]{2,1,0:T(8,128)(2,1)}), bf16[16,16,2048]{2,1,0:T(8,128)(2,1)S(1)}, u32[]{:S(2)}, u32[]{:S(2)}) async-start(bf16[16,16,2048]{2,1,0:T(8,128)(2,1)} %bitcast.5), calls=%async_computation.1 | async-start | bytes 2097152 | tf_op jit(solution)/shard_map/all_to_all | solution.py:356
  23.6 55.2 %copy-start.3 = (f32[128,128]{1,0:T(8,128)}, f32[128,128]{1,0:T(8,128)S(1)}, u32[]{:S(2)}) copy-start(f32[128,128]{1,0:T(8,128)S(1)} %get-tuple-element.20.columns_ref) | copy-start | bytes 196612
  23.6 25.7 %collective-permute-start = (s32[4,128]{1,0:T(4,128)S(1)}, s32[4,128]{1,0:T(4,128)S(1)}, u32[]{:S(2)}, u32[]{:S(2)}) collective-permute-start(s32[4,128]{1,0:T(4,128)S(1)} %get-tuple-element.23), channel_id=1, source_target_pairs={{0,8},{1,9},{2,10},{3,11},{4,12},{5,13},{6,14},{7,15},{8,0},{9,1},... | collective-permute-start | bytes 6152 | tf_op jit(solution)/shard_map/ppermute | solution.py:391
  26.4 22.9 %collective-permute-start.1 = (f32[4,128]{1,0:T(4,128)S(1)}, f32[4,128]{1,0:T(4,128)S(1)}, u32[]{:S(2)}, u32[]{:S(2)}) collective-permute-start(f32[4,128]{1,0:T(4,128)S(1)} %get-tuple-element.24), channel_id=1, source_target_pairs={{0,8},{1,9},{2,10},{3,11},{4,12},{5,13},{6,14},{7,15},{8,0},{9,1},... | collective-permute-start | bytes 6152 | tf_op jit(solution)/shard_map/ppermute | solution.py:391
  52.4 24.9 %collective-permute-start.2 = (bf16[128,2048]{1,0:T(8,128)(2,1)S(1)}, bf16[128,2048]{1,0:T(8,128)(2,1)S(1)}, u32[]{:S(2)}, u32[]{:S(2)}) collective-permute-start(bf16[128,2048]{1,0:T(8,128)(2,1)S(1)} %get-tuple-element.27), channel_id=1, source_target_pairs={{0,8},{1,9},{2,10},{3,11},{4,12},{5,13},{6,14},{7,15},{8,0},{9,1},... | collective-permute-start | bytes 1572872 | tf_op jit(solution)/shard_map/ppermute | solution.py:391
  78.9 24.7 %copy-start = (bf16[128,2048]{1,0:T(8,128)(2,1)S(1)}, bf16[128,2048]{1,0:T(8,128)(2,1)}, u32[]{:S(2)}) copy-start(bf16[128,2048]{1,0:T(8,128)(2,1)} %grad_ref.3) | copy-start | bytes 1572868
  103.6 34.8 %all-to-all-start.3 = ((bf16[8,48,2048]{2,1,0:T(8,128)(2,1)}), bf16[8,48,2048]{2,1,0:T(8,128)(2,1)S(1)}, u32[]{:S(2)}, u32[]{:S(2)}) async-start(bf16[8,48,2048]{2,1,0:T(8,128)(2,1)} %get-tuple-element.28), calls=%async_computation.3 | async-start | bytes 3145728 | tf_op jit(solution)/shard_map/all_to_all | solution.py:356
  107.2 30.1 %collective-permute-start.3 = (bf16[128,2048]{1,0:T(8,128)(2,1)S(1)}, bf16[128,2048]{1,0:T(8,128)(2,1)S(1)}, u32[]{:S(2)}, u32[]{:S(2)}) collective-permute-start(bf16[128,2048]{1,0:T(8,128)(2,1)S(1)} %get-tuple-element.29), channel_id=1, source_target_pairs={{0,8},{1,9},{2,10},{3,11},{4,12},{5,13},{6,14},{7,15},{8,0},{9,1},... | collective-permute-start | bytes 1572872 | tf_op jit(solution)/shard_map/ppermute | solution.py:391
  138.5 1.1 copy-start.8
  139.6 33.4 %all-to-all-start.4 = ((bf16[8,48,2048]{2,1,0:T(8,128)(2,1)}), bf16[8,48,2048]{2,1,0:T(8,128)(2,1)S(1)}, u32[]{:S(2)}, u32[]{:S(2)}) async-start(bf16[8,48,2048]{2,1,0:T(8,128)(2,1)} %ordered.3.refs_0_), calls=%async_computation.4 | async-start | bytes 3145728 | tf_op jit(solution)/shard_map/all_to_all | solution.py:356
  174.7 26.5 %collective-permute-start.4 = (bf16[128,2048]{1,0:T(8,128)(2,1)S(1)}, bf16[128,2048]{1,0:T(8,128)(2,1)S(1)}, u32[]{:S(2)}, u32[]{:S(2)}) collective-permute-start(bf16[128,2048]{1,0:T(8,128)(2,1)S(1)} %get-tuple-element.32.refs_1_), channel_id=1, source_target_pairs={{0,8},{1,9},{2,10},{3,11},{4,12},{5,13},{6,14},{7,15},{8,0},{9,1},... | collective-permute-start | bytes 1572872 | tf_op jit(solution)/shard_map/ppermute | solution.py:391
  176.7 34.5 %all-to-all-start.5 = ((bf16[8,48,2048]{2,1,0:T(8,128)(2,1)}), bf16[8,48,2048]{2,1,0:T(8,128)(2,1)}, u32[]{:S(2)}, u32[]{:S(2)}) async-start(bf16[8,48,2048]{2,1,0:T(8,128)(2,1)} %ordered.4), calls=%async_computation.5 | async-start | bytes 3145728 | tf_op jit(solution)/shard_map/all_to_all | solution.py:356
  181.0 24.6 %collective-permute-start.5 = (f32[8,128]{1,0:T(8,128)}, f32[8,128]{1,0:T(8,128)}, u32[]{:S(2)}, u32[]{:S(2)}) collective-permute-start(f32[8,128]{1,0:T(8,128)} %get-tuple-element.33), channel_id=1, source_target_pairs={{0,8},{1,9},{2,10},{3,11},{4,12},{5,13},{6,14},{7,15},{8,0},{9,1},... | collective-permute-start | bytes 12296 | tf_op jit(solution)/shard_map/ppermute | solution.py:391
  201.2 10.0 %copy-start.1 = (bf16[128,2048]{1,0:T(8,128)(2,1)S(1)}, bf16[128,2048]{1,0:T(8,128)(2,1)}, u32[]{:S(2)}) copy-start(bf16[128,2048]{1,0:T(8,128)(2,1)} %grad_ref.3) | copy-start | bytes 1572868
  201.2 10.0 %copy-start.4 = (f32[128,128]{1,0:T(8,128)S(1)}, f32[128,128]{1,0:T(8,128)}, u32[]{:S(2)}) copy-start(f32[128,128]{1,0:T(8,128)} %copy-done.3) | copy-start | bytes 196612

commit v12 on v11

--- a/solution.py
+++ b/solution.py
@@ -133,22 +133,14 @@
     columns_ref[...] = turned(weights_ref[...])
 
 
-def pick_slots(pick_ref, state_ref, out_hbm, sent_ref, sem, left, width):
-    cols = pl.ds(left, width)
-    sent_ref[:, cols] = dot(pick_ref[...], state_ref[:, cols]).astype(BF16)
-    copy = pltpu.make_async_copy(
-        sent_ref.at[:, cols], out_hbm.at[:, cols], sem.at[left // width]
-    )
-    copy.start()
-    return copy
-
-
 def state_kernel(
-    put_ref, pick_ref, returned_ref, values_ref, columns_ref, _, state_ref, out_hbm, sent_ref, sem
+    me_ref, put_ref, pick_ref, returned_ref, values_ref, columns_ref, _, state_ref, *refs
 ):
+    out_hbms, (sent_ref, sem) = refs[:-2], refs[-2:]
     features = values_ref.shape[1]
-    width = features // sem.shape[0]
-    copies = []
+    half = len(out_hbms)
+    block = sent_ref.shape[0] // half
+    width = 512
     for left in range(0, features, width):
         found = dot(put_ref[...], returned_ref[:, left : left + width])
         for b in range(width // BLOCK):
@@ -160,33 +152,47 @@
             state_ref[:, at : at + BLOCK] = (
                 scaled + found[:, b * BLOCK : (b + 1) * BLOCK]
             ).astype(BF16)
-        copies.append(pick_slots(pick_ref, state_ref, out_hbm, sent_ref, sem, left, width))
+        cols = slice(left, left + width)
+        sent_ref[:, cols] = dot(pick_ref[...], state_ref[:, cols]).astype(BF16)
+    copies = []
+    for k in range(half):
+        partner = (me_ref[0] & (half - 1)) ^ k
+        rows = pl.ds(pl.multiple_of(partner * block, block), block)
+        copies.append(pltpu.make_async_copy(sent_ref.at[rows], out_hbms[k], sem.at[k]))
+        copies[-1].start()
     for copy in copies:
         copy.wait()
 
 
-def pick_kernel(pick_ref, state_ref, out_hbm, sent_ref, sem):
-    features = state_ref.shape[1]
+def pick_kernel(
+    pick_ref, state_ref, grad_ref, out_hbm, upper_grad_ref, lower_grad_ref, sent_ref, sem
+):
+    tok_rows, features = state_ref.shape
     width = features // sem.shape[0]
-    copies = [
-        pick_slots(pick_ref, state_ref, out_hbm, sent_ref, sem, left, width)
-        for left in range(0, features, width)
-    ]
+    copies = []
+    for n in range(sem.shape[0]):
+        cols = pl.ds(n * width, width)
+        sent_ref[:, cols] = dot(pick_ref[...], state_ref[:, cols]).astype(BF16)
+        copies.append(
+            pltpu.make_async_copy(sent_ref.at[:, cols], out_hbm.at[:, cols], sem.at[n])
+        )
+        copies[-1].start()
+    upper_grad_ref[...] = grad_ref[: tok_rows // 2, :]
+    lower_grad_ref[...] = grad_ref[tok_rows // 2 :, :]
     for copy in copies:
         copy.wait()
 
 
-def expert_kernel(after, rows_hbm, *refs):
-    wg_hbm, wu_hbm, wd_hbm, out_ref = refs[after : after + 4]
-    rows_ref, x_ref, wg_ref, wu_ref, both_ref, wd_ref, hidden_ref, result_ref, sem, rows_sem = refs[
-        after + 4 :
+def expert_kernel(parts, after, me_ref, *refs):
+    rows_hbms = refs[:parts]
+    wg_hbm, wu_hbm, wd_hbm, out_ref = refs[parts + after : parts + after + 4]
+    rows_ref, x_ref, wg_ref, wu_ref, wd_ref, hidden_ref, result_ref, sem, rows_sem = refs[
+        parts + after + 4 :
     ]
     exp_dev, features, width = wg_hbm.shape
+    held = wg_ref.shape[0]
     half = rows_ref.shape[0]
-    held = wg_ref.shape[0]
-    wide = wg_ref.shape[2]
-    rest = width - wide
-    up_cuts = ((0, 512), (512, 512), (1024, wide - 1024))
+    up_cuts = ((0, 512), (512, 512), (1024, width - 1024))
     down_cuts = tuple((at, 512) for at in range(0, features, 512))
 
     def weight_copies(j, place):
@@ -195,9 +201,6 @@
             cols = pl.ds(at, size)
             copies.append((wg_hbm.at[j, :, cols], wg_ref.at[place, :, cols]))
             copies.append((wu_hbm.at[j, :, cols], wu_ref.at[place, :, cols]))
-        for n, hbm in enumerate((wg_hbm, wu_hbm)):
-            last = both_ref.at[place, :, pl.ds(n * rest, rest)]
-            copies.append((hbm.at[j, :, pl.ds(wide, rest)], last))
         for at, size in down_cuts:
             cols = pl.ds(at, size)
             copies.append((wd_hbm.at[j, :, cols], wd_ref.at[place, :, cols]))
@@ -206,12 +209,22 @@
             for n, (src, dst) in enumerate(copies)
         ]
 
-    rows_copy = pltpu.make_async_copy(rows_hbm, rows_ref, rows_sem)
-    rows_copy.start()
+    if parts == 1:
+        rows_copies = [pltpu.make_async_copy(rows_hbms[0], rows_ref, rows_sem.at[0])]
+    else:
+        rows_copies = [
+            pltpu.make_async_copy(
+                rows_hbms[k], rows_ref.at[(me_ref[0] & (half - 1)) ^ k], rows_sem.at[k]
+            )
+            for k in range(parts)
+        ]
+    for copy in rows_copies:
+        copy.start()
     for j in range(held):
         for copy in weight_copies(j, j):
             copy.start()
-    rows_copy.wait()
+    for copy in rows_copies:
+        copy.wait()
 
     low = iota((PAIR, features), 0) < CAP
     for chunk in range(exp_dev // 2):
@@ -253,12 +266,6 @@
             hide(gate, up, at)
             refill(n, 2)
             n += 2
-        copies[n].wait()
-        copies[n + 1].wait()
-        both = dot(x_ref[j], both_ref[place])
-        hide(both[:, :rest], both[:, rest:], wide)
-        refill(n, 2)
-        n += 2
         for at, size in down_cuts:
             copies[n].wait()
             result_ref[j, :, at : at + size] = dot(
@@ -277,33 +284,35 @@
             out_ref[2 * pair + odd] = jnp.concatenate(parts, axis=0).astype(BF16)
 
 
-def expert_call(name, rows_in, weights, after=()):
+def expert_call(name, place, rows_in, weights, after=()):
     w_gate, w_up, w_down = weights
     exp_dev, features, width = w_gate.shape
-    half = rows_in.shape[0]
+    parts = len(rows_in)
+    half = EXPERTS // exp_dev // 2
     rows = half * CAP
     held = 2
-    rest = 128
-    wide = width - rest
+    slots = exp_dev * CAP
     anywhere = pl.BlockSpec(memory_space=pl.ANY)
     hbm = pl.BlockSpec(memory_space=pltpu.HBM)
-    vmem = pl.BlockSpec(memory_space=VMEM)
+    operands = [in_hbm(array) for array in (*rows_in, *after, w_gate, w_up, w_down)]
     return pl.pallas_call(
-        functools.partial(expert_kernel, len(after)),
-        out_shape=pltpu.HBM((half, exp_dev * CAP, features), BF16),
-        in_specs=[hbm] + [anywhere] * len(after) + [hbm] * 3,
-        out_specs=vmem,
+        functools.partial(expert_kernel, parts, len(after)),
+        out_shape=pltpu.HBM((half, slots, features), BF16),
+        in_specs=[pl.BlockSpec(memory_space=pltpu.SMEM)]
+        + [hbm] * parts
+        + [anywhere] * len(after)
+        + [hbm] * 3,
+        out_specs=pl.BlockSpec(memory_space=VMEM),
         scratch_shapes=[
-            VMEM(rows_in.shape, BF16),
+            VMEM((half, slots, features), BF16),
             VMEM((exp_dev, rows, features), BF16),
-            VMEM((held, features, wide), BF16),
-            VMEM((held, features, wide), BF16),
-            VMEM((held, features, 2 * rest), BF16),
+            VMEM((held, features, width), BF16),
+            VMEM((held, features, width), BF16),
             VMEM((held, width, features), BF16),
             VMEM((rows, width), BF16),
             VMEM((exp_dev, rows, features), F32),
-            pltpu.SemaphoreType.DMA((held, 12)),
-            pltpu.SemaphoreType.DMA,
+            pltpu.SemaphoreType.DMA((held, 10)),
+            pltpu.SemaphoreType.DMA((half,)),
         ],
         compiler_params=pltpu.CompilerParams(vmem_limit_bytes=46 * 1024 * 1024),
         cost_estimate=pl.CostEstimate(
@@ -312,17 +321,17 @@
             transcendentals=exp_dev * rows * width,
         ),
         name=name,
-    )(in_hbm(rows_in), *[in_hbm(array) for array in after], in_hbm(w_gate), in_hbm(w_up), in_hbm(w_down))
-
-
-def mix_kernel(after, slots_ref, columns_ref, back_ref, grad_ref, *refs):
-    refs = refs[after:]
+    )(place, *operands)
+
+
+def mix_kernel(slots_ref, columns_ref, back_ref, *refs):
     mixed_ref, grads_ref = refs[-2:]
-    tok_rows, features = grad_ref.shape
-    count = back_ref.shape[0]
+    tok_rows = slots_ref.shape[0]
+    count, features = back_ref.shape
+    grad = jnp.concatenate([ref[...] for ref in refs[:-2]], axis=0)
     column = iota((tok_rows, count), 1)
     inner = lax.dot_general(
-        grad_ref[...], back_ref[...], (((1,), (1,)), ((), ())), preferred_element_type=F32
+        grad, back_ref[...], (((1,), (1,)), ((), ())), preferred_element_type=F32
     )
     total = jnp.zeros((tok_rows, count), F32)
     place = iota((tok_rows, tok_rows), 1)
@@ -336,20 +345,9 @@
     rest = (total - high.astype(F32)).astype(BF16)
     width = 512
     for at in range(0, features, width):
-        cols = slice(at, at + width)
-        value = dot(high, back_ref[:, cols]) + dot(rest, back_ref[:, cols])
-        if len(refs) > 2:
-            value = value + refs[0][:, cols].astype(F32)
-        mixed_ref[:, cols] = value.astype(BF16)
-    lines = grads_ref.shape[0]
-    grads = wide.T[:lines, :]
-    if len(refs) > 2:
-        grads = grads + refs[1][:lines, :]
-    grads_ref[...] = grads
-
-
-def after_far_kernel(sent_hbm, far_hbm, grad_ref, sent_out_hbm, grad_out_ref):
-    grad_out_ref[...] = grad_ref[...]
+        rows = back_ref[:, at : at + width]
+        mixed_ref[:, at : at + width] = (dot(high, rows) + dot(rest, rows)).astype(mixed_ref.dtype)
+    grads_ref[...] = wide.T[: grads_ref.shape[0], :]
 
 
 def swap(array, groups=None):
@@ -453,17 +451,19 @@
         name="far_plan",
     )(place, mirrored(sent_ids), mirrored(sent_weights))
 
-    sent_shape = pltpu.HBM((slots, features), BF16)
-    sent_scratch = [VMEM((slots, features), BF16), pltpu.SemaphoreType.DMA((4,))]
-    state, near_sent = pl.pallas_call(
+    state, *near_sent = pl.pallas_call(
         state_kernel,
-        out_shape=(shape((tok_rows, features), BF16), sent_shape),
-        in_specs=[vmem] * 5 + [anywhere],
-        out_specs=(vmem, anywhere),
-        scratch_shapes=sent_scratch,
+        out_shape=(
+            shape((tok_rows, features), BF16),
+            *[pltpu.HBM((2 * PAIR, features), BF16)] * half,
+        ),
+        in_specs=[smem] + [vmem] * 5 + [anywhere],
+        out_specs=(vmem,) + (anywhere,) * half,
+        scratch_shapes=[VMEM((slots, features), BF16), pltpu.SemaphoreType.DMA((half,))],
         compiler_params=SMALL,
         name="token_state",
     )(
+        place,
         put,
         near_pick,
         returned.reshape(device_count * look_cap, features),
@@ -471,58 +471,56 @@
         near_columns,
         far_pick,
     )
-    far_sent = pl.pallas_call(
+    split = shape((tok_rows // 2, features), BF16)
+    far_sent, *grad_halves = pl.pallas_call(
         pick_kernel,
-        out_shape=sent_shape,
-        in_specs=[vmem, vmem],
-        out_specs=anywhere,
-        scratch_shapes=sent_scratch,
+        out_shape=(pltpu.HBM((slots, features), BF16), split, split),
+        in_specs=[vmem, vmem, vmem],
+        out_specs=(anywhere, vmem, vmem),
+        scratch_shapes=[VMEM((slots, features), BF16), pltpu.SemaphoreType.DMA((4,))],
         compiler_params=SMALL,
+        cost_estimate=pl.CostEstimate(
+            flops=400_000_000_000, bytes_accessed=4 * slots * features, transcendentals=0
+        ),
         name="far_slots",
-    )(far_pick, mirrored(state))
-    rows_shape = (half, 2 * PAIR, features)
-    far_rows = swap(far_sent.reshape(rows_shape), halves)
-    near_sent, sent_grad = pl.pallas_call(
-        after_far_kernel,
-        out_shape=(shape(rows_shape, BF16), shape((tok_rows, features), BF16)),
-        in_specs=[anywhere, anywhere, vmem],
-        out_specs=(anywhere, vmem),
-        input_output_aliases={0: 0},
-        compiler_params=SMALL,
-        name="after_far",
-    )(in_hbm(near_sent.reshape(rows_shape)), in_hbm(far_rows), out_grad)
-    near_rows = swap(near_sent, halves)
+    )(far_pick, mirrored(state), out_grad)
+    near_rows = near_sent[:1] + [
+        lax.ppermute(
+            near_sent[k],
+            "expert",
+            [(i, i // half * half + (i % half ^ k)) for i in range(device_count)],
+        )
+        for k in range(1, half)
+    ]
+    far_sent = far_sent.reshape(half, 2 * PAIR, features)
+    far_rows = swap(far_sent, halves)
+    other_grads = [mirrored(array) for array in grad_halves]
 
     weights = (w_gate, w_up, w_down)
-    other_grad = mirrored(sent_grad)
-    far_out = expert_call("far_experts", far_rows, weights)
-    far_out = ordered(in_hbm(far_out), in_hbm(near_rows), other_grad)
-    near_out = expert_call("near_experts", near_rows, weights, after=(far_out,))
-    far_back = swap(far_out, halves)
-
-    def mixed_rows(name, slot_of, columns, back, grad, lines, more=(), after=()):
+    near_out = expert_call("near_experts", place, near_rows, weights, after=(far_sent,))
+    near_out = ordered(in_hbm(near_out), other_grads[0])
+    far_out = expert_call("far_experts", place, [far_rows], weights, after=(near_out,))
+    near_back = swap(near_out, halves)
+    far_back = swap(ordered(in_hbm(far_out), near_back, other_grads[1]), halves)
+
+    def mixed_rows(name, slot_of, columns, back, grads, kind):
         return pl.pallas_call(
-            functools.partial(mix_kernel, len(after)),
-            out_shape=(shape((tok_rows, features), BF16), shape((lines, tok_rows), F32)),
-            in_specs=[vmem] * 4 + [anywhere] * len(after) + [vmem] * len(more),
+            mix_kernel,
+            out_shape=(shape((tok_rows, features), kind), shape((2 * TOP, tok_rows), F32)),
+            in_specs=[vmem] * (3 + len(grads)),
             out_specs=(vmem, vmem),
             compiler_params=SMALL,
             name=name,
-        )(slot_of, columns, back.reshape(slots, features), grad, *after, *more)
-
+        )(slot_of, columns, back.reshape(slots, features), *grads)
+
+    near_mixed, near_grads = mixed_rows(
+        "mix_near", near_of, near_columns, near_back, (out_grad,), F32
+    )
     far_mixed, far_grads = mixed_rows(
-        "mix_far", far_of, far_columns, far_back, other_grad, 2 * TOP, after=(in_hbm(near_out),)
-    )
-    near_back = swap(ordered(in_hbm(near_out), far_mixed), halves)
-    mixed, grads = mixed_rows(
-        "mix_near",
-        near_of,
-        near_columns,
-        near_back,
-        out_grad,
-        TOP,
-        more=(ordered(mirrored(far_mixed), flops=400_000_000_000), mirrored(far_grads)),
-    )
+        "mix_far", far_of, far_columns, far_back, other_grads, BF16
+    )
+    mixed = (near_mixed + mirrored(far_mixed).astype(F32)).astype(BF16)
+    grads = (near_grads + mirrored(far_grads))[:TOP]
     return mixed, grads.T
 
 

time: 215 us -> 243 us (1.13)
  waiting for transfers between devices: 83.6 us -> 110 us
  Pallas kernels: 74.6 us -> 70.4 us
  starting transfers between devices: 29.6 us -> 33.2 us
    ppermute x0 -> x7, waiting for transfers between devices: none -> 34.9 us  [near_path(): lax.ppermute(near_sent[k], 'expert', [(i, i // half * half + (i % half ^...]
    ppermute x0 -> x7, starting transfers between devices: none -> 7.01 us  [near_path(): lax.ppermute(near_sent[k], 'expert', [(i, i // half * half + (i % half ^...]
    all_to_all x5 -> x4, waiting for transfers between devices: 13 us -> 6.26 us  [swap(): lax.all_to_all(array, 'expert', split_axis=0, concat_axis=0, tiled=True,...]
    pallas_call x6 -> x5, Pallas kernels: 66.2 us -> 61.2 us  [the longest x2 57.2 us: expert_call(): pl.pallas_call(functools.partial(expert_kernel, parts, len(after)), out_s...]
    all_to_all x5 -> x4, starting transfers between devices: 22.7 us -> 18.5 us  [swap(): lax.all_to_all(array, 'expert', split_axis=0, concat_axis=0, tiled=True,...]
    ppermute x6 -> x7, waiting for transfers between devices: 70.6 us -> 69 us  [mirrored(): return lax.ppermute(array, 'expert', pairs)]
    ppermute x6 -> x7, starting transfers between devices: 6.9 us -> 7.68 us  [mirrored(): return lax.ppermute(array, 'expert', pairs)]
  transfers between devices with their start and end apart: 11 -> 18, of which waited for: 7 -> 8; matrix products, arithmetic and copies ran while one was open for 0% -> 0% of each run, Pallas kernels for 29% -> 25%
where the time goes in v12:
time: 243 us
  waiting for transfers between devices  110 us (45%)
  Pallas kernels  70.4 us (29%)
  starting transfers between devices  33.2 us (14%)
  blocking collectives  24.4 us (10%)
  local copies, waits for them, and re-layouts  2.48 us (1%)
    ppermute x7, waiting for transfers between devices, mirrored(): return lax.ppermute(array, 'expert', pairs)  69 us
    pallas_call x2, Pallas kernels, expert_call(): pl.pallas_call(functools.partial(expert_kernel, parts, len(after)), out_s...  57.2 us
    ppermute x7, waiting for transfers between devices, near_path(): lax.ppermute(near_sent[k], 'expert', [(i, i // half * half + (i % half ^...  34.9 us
    all_to_all x1, blocking collectives, swap(): lax.all_to_all(array, 'expert', split_axis=0, concat_axis=0, tiled=True,...  24.4 us
    all_to_all x4, starting transfers between devices, swap(): lax.all_to_all(array, 'expert', split_axis=0, concat_axis=0, tiled=True,...  18.5 us
    ppermute x7, starting transfers between devices, mirrored(): return lax.ppermute(array, 'expert', pairs)  7.68 us
    ppermute x7, starting transfers between devices, near_path(): lax.ppermute(near_sent[k], 'expert', [(i, i // half * half + (i % half ^...  7.01 us
    all_to_all x4, waiting for transfers between devices, swap(): lax.all_to_all(array, 'expert', split_axis=0, concat_axis=0, tiled=True,...  6.26 us
  transfers between devices with their start and end apart: 18, of which 8 were waited for; matrix products, arithmetic and copies ran while one was open for 0% of the time, Pallas kernels for 25%

profile of v12, /device:TPU:0, one launch (start us, length us, event | category | flops | bytes accessed | tf_op | source)
XLA Modules:
  0.0 242.6 jit_solution(9198974845503476751)
XLA Ops:
  0.6 1.3 repeat_rows.1
  1.9 7.4 %all-to-all-start = ((s32[16,1,128]{2,1,0:T(1,128)}), s32[16,1,128]{2,1,0:T(1,128)S(1)}, u32[]{:S(2)}, u32[]{:S(2)}) async-start(s32[16,1,128]{2,1,0:T(1,128)} %repeat_rows.1), calls=%async_computation | async-start | bytes 16384 | tf_op jit(solution)/shard_map/all_to_all | solution.py:354
  9.3 0.1 pad_add_fusion.me_ref
  9.4 6.2 %all-to-all-done.rows_ref = s32[16,1,128]{2,1,0:T(1,128)S(1)} async-done(((s32[16,1,128]{2,1,0:T(1,128)}), s32[16,1,128]{2,1,0:T(1,128)S(1)}, u32[]{:S(2)}, u32[]{:S(2)}) %all-to-all-start) | async-done | bytes 8224 | tf_op jit(solution)/shard_map/all_to_all | solution.py:354
  15.6 3.2 %fetch_rows.1._ = bf16[256,2048]{1,0:T(8,128)(2,1)} custom-call(s32[2]{0:T(128)S(1)} %pad_add_fusion.me_ref, s32[16,1,128]{2,1,0:T(1,128)S(1)} %all-to-all-done.rows_ref, bf16[256,2048]{1,0:T(8,128)(2,1)} %table_hbm.1), custom_call_target="tpu_custom_call" | custom-call | tf_op jit(solution)/shard_map/fetch_rows/pallas_call | solution.py:410
  18.9 0.0 copy-start.17
  18.9 0.0 copy-start.6
  18.9 0.0 copy-start.7
  18.9 0.0 copy-start.1
  18.9 3.8 %all-to-all-start.1 = ((bf16[16,16,2048]{2,1,0:T(8,128)(2,1)}), bf16[16,16,2048]{2,1,0:T(8,128)(2,1)S(1)}, u32[]{:S(2)}, u32[]{:S(2)}) async-start(bf16[16,16,2048]{2,1,0:T(8,128)(2,1)} %bitcast.5), calls=%async_computation.1 | async-start | bytes 2097152 | tf_op jit(solution)/shard_map/all_to_all | solution.py:354
  22.7 0.0 copy-start
  22.8 0.9 near_plan.1
  23.6 2.8 %collective-permute-start = (s32[4,128]{1,0:T(4,128)S(1)}, s32[4,128]{1,0:T(4,128)S(1)}, u32[]{:S(2)}, u32[]{:S(2)}) collective-permute-start(s32[4,128]{1,0:T(4,128)S(1)} %get-tuple-element.31), channel_id=1, source_target_pairs={{0,8},{1,9},{2,10},{3,11},{4,12},{5,13},{6,14},{7,15},{8,0},{9,1},... | collective-permute-start | bytes 6152 | tf_op jit(solution)/shard_map/ppermute | solution.py:389
  26.5 0.2 collective-permute-start.1
  26.6 22.7 %collective-permute-done.ids_ref = s32[4,128]{1,0:T(4,128)S(1)} collective-permute-done((s32[4,128]{1,0:T(4,128)S(1)}, s32[4,128]{1,0:T(4,128)S(1)}, u32[]{:S(2)}, u32[]{:S(2)}) %collective-permute-start) | collective-permute-done | bytes 2080 | tf_op jit(solution)/shard_map/ppermute | solution.py:389
  49.3 0.0 collective-permute-done.1.weights_ref
  49.4 0.8 far_plan.1
  50.2 3.1 %token_state.1 = (bf16[128,2048]{1,0:T(8,128)(2,1)S(1)}, bf16[48,2048]{1,0:T(8,128)(2,1)}, bf16[48,2048]{1,0:T(8,128)(2,1)}, bf16[48,2048]{1,0:T(8,128)(2,1)}, b...) custom-call(s32[2]{0:T(128)S(1)} %pad_add_fusion.me_ref, ...), custom_call_target="tpu_custom_call" | custom-call | tf_op jit(solution)/shard_map/token_state/pallas_call | solution.py:454
  53.3 0.6 collective-permute-start.9
  53.9 24.3 %collective-permute-done.9.state_ref = bf16[128,2048]{1,0:T(8,128)(2,1)S(1)} collective-permute-done((bf16[128,2048]{1,0:T(8,128)(2,1)S(1)}, bf16[128,2048]{1,0:T(8,128)(2,1)S(1)}, u32[]{:S(2)}, u32[]{:S(2)}) %collective-permute-start.9) | collective-permute-done | bytes 524320 | tf_op jit(solution)/shard_map/ppermute | solution.py:389
  78.2 1.5 far_slots.1
  79.7 0.0 copy-start.5
  79.8 3.7 %all-to-all-start.3 = ((bf16[8,48,2048]{2,1,0:T(8,128)(2,1)}), bf16[8,48,2048]{2,1,0:T(8,128)(2,1)S(1)}, u32[]{:S(2)}, u32[]{:S(2)}) async-start(bf16[8,48,2048]{2,1,0:T(8,128)(2,1)} %bitcast.20), calls=%async_computation.3 | async-start | bytes 3145728 | tf_op jit(solution)/shard_map/all_to_all | solution.py:354
  83.5 0.4 collective-permute-start.2
  83.9 1.7 collective-permute-start.3
  85.6 1.7 collective-permute-start.5
  87.3 0.1 collective-permute-start.6
  87.4 2.7 %collective-permute-start.7 = (bf16[48,2048]{1,0:T(8,128)(2,1)S(1)}, bf16[48,2048]{1,0:T(8,128)(2,1)S(1)}, u32[]{:S(2)}, u32[]{:S(2)}) collective-permute-start(bf16[48,2048]{1,0:T(8,128)(2,1)S(1)} %copy-done.19), channel_id=1, source_target_pairs={{0,6},{1,7},{2,4},{3,5},{4,2},{5,3},{6,0},{7,1},{8,14},{9,15},{10,... | collective-permute-start | bytes 589832 | tf_op jit(solution)/shard_map/ppermute | solution.py:488
  90.1 18.1 %collective-permute-done.3.refs_2_ = bf16[48,2048]{1,0:T(8,128)(2,1)S(1)} collective-permute-done((bf16[48,2048]{1,0:T(8,128)(2,1)}, bf16[48,2048]{1,0:T(8,128)(2,1)S(1)}, u32[]{:S(2)}, u32[]{:S(2)}) %collective-permute-start.3) | collective-permute-done | bytes 196640 | tf_op jit(solution)/shard_map/ppermute | solution.py:488
  108.2 0.4 collective-permute-start.8
  108.6 2.8 %collective-permute-done.4.refs_3_ = bf16[48,2048]{1,0:T(8,128)(2,1)S(1)} collective-permute-done((bf16[48,2048]{1,0:T(8,128)(2,1)S(1)}, bf16[48,2048]{1,0:T(8,128)(2,1)S(1)}, u32[]{:S(2)}, u32[]{:S(2)}) %collective-permute-start.4) | collective-permute-done | bytes 196640 | tf_op jit(solution)/shard_map/ppermute | solution.py:488
  111.4 1.0 collective-permute-start.10
  112.4 10.7 %collective-permute-done.7.refs_6_ = bf16[48,2048]{1,0:T(8,128)(2,1)S(1)} collective-permute-done((bf16[48,2048]{1,0:T(8,128)(2,1)S(1)}, bf16[48,2048]{1,0:T(8,128)(2,1)S(1)}, u32[]{:S(2)}, u32[]{:S(2)}) %collective-permute-start.7) | collective-permute-done | bytes 196640 | tf_op jit(solution)/shard_map/ppermute | solution.py:488
  123.1 3.3 %collective-permute-done.8.refs_7_ = bf16[48,2048]{1,0:T(8,128)(2,1)S(1)} collective-permute-done((bf16[48,2048]{1,0:T(8,128)(2,1)S(1)}, bf16[48,2048]{1,0:T(8,128)(2,1)S(1)}, u32[]{:S(2)}, u32[]{:S(2)}) %collective-permute-start.8) | collective-permute-done | bytes 196640 | tf_op jit(solution)/shard_map/ppermute | solution.py:488
  126.4 0.7 copy-done.16
  127.1 28.5 %near_experts.1.refs_0_ = bf16[8,48,2048]{2,1,0:T(8,128)(2,1)} custom-call(s32[2]{0:T(128)S(1)} %copy-done.5, bf16[48,2048]{1,0:T(8,128)(2,1)} %get-tuple-element.34.refs_0_, bf16[48,2048]{1,0:T(8,128)(2,1)} %copy-done.10, bf16[48,2048]{1,0:T(8,128)(2,1)} %copy-done.11, bf16[48,2048]{1,0:T(8,128)(2,1)} %copy-done.12, bf16[48,2048]{1,0:T(8,128)(2,1)} %copy-done.13, ...), custom_call_target="tpu_custom_call" | custom-call | flops 13287555072 | bytes 69206016 | tf_op jit(solution)/shard_map/near_experts/pallas_call | solution.py:298
  155.7 1.1 copy-done.9
  156.8 3.6 %all-to-all-start.2 = ((bf16[8,48,2048]{2,1,0:T(8,128)(2,1)}), bf16[8,48,2048]{2,1,0:T(8,128)(2,1)S(1)}, u32[]{:S(2)}, u32[]{:S(2)}) async-start(bf16[8,48,2048]{2,1,0:T(8,128)(2,1)} %ordered.2.refs_1_), calls=%async_computation.2 | async-start | bytes 3145728 | tf_op jit(solution)/shard_map/all_to_all | solution.py:354
  160.4 0.1 collective-permute-start.11
  160.5 28.7 %far_experts.1.refs_0_ = bf16[8,48,2048]{2,1,0:T(8,128)(2,1)} custom-call(s32[2]{0:T(128)S(1)} %copy-done.5, bf16[8,48,2048]{2,1,0:T(8,128)(2,1)} %copy-done.9, bf16[8,48,2048]{2,1,0:T(8,128)(2,1)} %ordered.2.refs_1_, bf16[4,2048,1408]{2,1,0:T(8,128)(2,1)} %refs_2_.1, bf16[4,2048,1408]{2,1,0:T(8,128)(2,1)} %refs_3_.1, bf16[4,1408,2048]{2,1,0:T(8,128)(2,1)} %refs_4_.1), custom_call_target="tpu_custom_call" | custom-call | flops 13287555072 | bytes 69206016 | tf_op jit(solution)/shard_map/far_experts/pallas_call | solution.py:298
  189.2 24.4 %all_to_all.25 = bf16[8,48,2048]{2,1,0:T(8,128)(2,1)S(1)} all-to-all(bf16[8,48,2048]{2,1,0:T(8,128)(2,1)} %ordered.3), channel_id=1, replica_groups={{0,1,2,3,4,5,6,7},{8,9,10,11,12,13,14,15},{16,17,18,19,20,21,22,23},{24..., dimensions={0} | all-to-all | bytes 3145728 | tf_op jit(solution)/shard_map/all_to_all | solution.py:354
  213.6 1.3 mix_far.1
  214.8 3.0 %collective-permute-start.12 = (bf16[128,2048]{1,0:T(8,128)(2,1)S(1)}, bf16[128,2048]{1,0:T(8,128)(2,1)S(1)}, u32[]{:S(2)}, u32[]{:S(2)}) collective-permute-start(bf16[128,2048]{1,0:T(8,128)(2,1)S(1)} %get-tuple-element.49), channel_id=1, source_target_pairs={{0,8},{1,9},{2,10},{3,11},{4,12},{5,13},{6,14},{7,15},{8,0},{9,1},... | collective-permute-start | bytes 1572872 | tf_op jit(solution)/shard_map/ppermute | solution.py:389
  217.8 0.1 collective-permute-start.13
  217.9 1.2 mix_near.1
  219.1 21.9 %collective-permute-done.13 = f32[8,128]{1,0:T(8,128)S(1)} collective-permute-done((f32[8,128]{1,0:T(8,128)S(1)}, f32[8,128]{1,0:T(8,128)S(1)}, u32[]{:S(2)}, u32[]{:S(2)}) %collective-permute-start.13) | collective-permute-done | bytes 4128 | tf_op jit(solution)/shard_map/ppermute | solution.py:389
  241.1 0.6 slice_bitcast_fusion
  241.7 0.9 add_convert_fusion
  (48 shorter events, 0.1 us)
Async XLA Ops:
  1.9 13.7 %all-to-all-start = ((s32[16,1,128]{2,1,0:T(1,128)}), s32[16,1,128]{2,1,0:T(1,128)S(1)}, u32[]{:S(2)}, u32[]{:S(2)}) async-start(s32[16,1,128]{2,1,0:T(1,128)} %repeat_rows.1), calls=%async_computation | async-start | bytes 16384 | tf_op jit(solution)/shard_map/all_to_all | solution.py:354
  9.4 40.9 %copy-start.4 = (s32[2]{0:T(128)}, s32[2]{0:T(128)S(1)}, u32[]{:S(2)}) copy-start(s32[2]{0:T(128)S(1)} %pad_add_fusion.me_ref) | copy-start | bytes 28
  18.9 3.9 %copy-start.17 = (s32[128,16]{0,1:T(8,128)S(1)}, s32[128,16]{0,1:T(8,128)}, u32[]{:S(2)}) copy-start(s32[128,16]{0,1:T(8,128)} %param.11) | copy-start | bytes 24580
  18.9 3.9 %copy-start.6 = (s32[128]{0:T(128)S(1)}, s32[128]{0:T(128)}, u32[]{:S(2)}) copy-start(s32[128]{0:T(128)} %param.12) | copy-start | bytes 1540
  18.9 3.9 %copy-start.7 = (s32[128,4]{0,1:T(4,128)S(1)}, s32[128,4]{0,1:T(4,128)}, u32[]{:S(2)}) copy-start(s32[128,4]{0,1:T(4,128)} %param.13) | copy-start | bytes 6148
  18.9 3.9 %copy-start.8 = (f32[128,4]{0,1:T(4,128)S(1)}, f32[128,4]{0,1:T(4,128)}, u32[]{:S(2)}) copy-start(f32[128,4]{0,1:T(4,128)} %param.14) | copy-start | bytes 6148
  18.9 31.3 %copy-start.1 = (bf16[128,2048]{1,0:T(8,128)(2,1)S(1)}, bf16[128,2048]{1,0:T(8,128)(2,1)}, u32[]{:S(2)}) copy-start(bf16[128,2048]{1,0:T(8,128)(2,1)} %values_ref.1) | copy-start | bytes 1572868
  18.9 31.3 %all-to-all-start.1 = ((bf16[16,16,2048]{2,1,0:T(8,128)(2,1)}), bf16[16,16,2048]{2,1,0:T(8,128)(2,1)S(1)}, u32[]{:S(2)}, u32[]{:S(2)}) async-start(bf16[16,16,2048]{2,1,0:T(8,128)(2,1)} %bitcast.5), calls=%async_computation.1 | async-start | bytes 2097152 | tf_op jit(solution)/shard_map/all_to_all | solution.py:354
  22.7 55.5 %copy-start = (bf16[128,2048]{1,0:T(8,128)(2,1)S(1)}, bf16[128,2048]{1,0:T(8,128)(2,1)}, u32[]{:S(2)}) copy-start(bf16[128,2048]{1,0:T(8,128)(2,1)} %refs_0_.1) | copy-start | bytes 1572868
  23.6 56.1 %copy-start.2 = (f32[128,128]{1,0:T(8,128)}, f32[128,128]{1,0:T(8,128)S(1)}, u32[]{:S(2)}) copy-start(f32[128,128]{1,0:T(8,128)S(1)} %get-tuple-element.28.columns_ref) | copy-start | bytes 196612
  23.6 25.7 %collective-permute-start = (s32[4,128]{1,0:T(4,128)S(1)}, s32[4,128]{1,0:T(4,128)S(1)}, u32[]{:S(2)}, u32[]{:S(2)}) collective-permute-start(s32[4,128]{1,0:T(4,128)S(1)} %get-tuple-element.31), channel_id=1, source_target_pairs={{0,8},{1,9},{2,10},{3,11},{4,12},{5,13},{6,14},{7,15},{8,0},{9,1},... | collective-permute-start | bytes 6152 | tf_op jit(solution)/shard_map/ppermute | solution.py:389
  26.5 22.9 %collective-permute-start.1 = (f32[4,128]{1,0:T(4,128)S(1)}, f32[4,128]{1,0:T(4,128)S(1)}, u32[]{:S(2)}, u32[]{:S(2)}) collective-permute-start(f32[4,128]{1,0:T(4,128)S(1)} %get-tuple-element.32), channel_id=1, source_target_pairs={{0,8},{1,9},{2,10},{3,11},{4,12},{5,13},{6,14},{7,15},{8,0},{9,1},... | collective-permute-start | bytes 6152 | tf_op jit(solution)/shard_map/ppermute | solution.py:389
  53.3 24.9 %collective-permute-start.9 = (bf16[128,2048]{1,0:T(8,128)(2,1)S(1)}, bf16[128,2048]{1,0:T(8,128)(2,1)S(1)}, u32[]{:S(2)}, u32[]{:S(2)}) collective-permute-start(bf16[128,2048]{1,0:T(8,128)(2,1)S(1)} %get-tuple-element.42), channel_id=1, source_target_pairs={{0,8},{1,9},{2,10},{3,11},{4,12},{5,13},{6,14},{7,15},{8,0},{9,1},... | collective-permute-start | bytes 1572872 | tf_op jit(solution)/shard_map/ppermute | solution.py:389
  79.7 5.9 %copy-start.20 = (bf16[48,2048]{1,0:T(8,128)(2,1)S(1)}, bf16[48,2048]{1,0:T(8,128)(2,1)}, u32[]{:S(2)}) copy-start(bf16[48,2048]{1,0:T(8,128)(2,1)} %get-tuple-element.37) | copy-start | bytes 589828
  79.7 7.7 %copy-start.19 = (bf16[48,2048]{1,0:T(8,128)(2,1)S(1)}, bf16[48,2048]{1,0:T(8,128)(2,1)}, u32[]{:S(2)}) copy-start(bf16[48,2048]{1,0:T(8,128)(2,1)} %get-tuple-element.40) | copy-start | bytes 589828
  79.7 28.4 %copy-start.18 = (bf16[48,2048]{1,0:T(8,128)(2,1)S(1)}, bf16[48,2048]{1,0:T(8,128)(2,1)}, u32[]{:S(2)}) copy-start(bf16[48,2048]{1,0:T(8,128)(2,1)} %get-tuple-element.41) | copy-start | bytes 589828
  79.7 47.3 %copy-start.5 = (s32[2]{0:T(128)S(1)}, s32[2]{0:T(128)}, u32[]{:S(2)}) copy-start(s32[2]{0:T(128)} %copy-done.4) | copy-start | bytes 28
  79.8 75.9 %all-to-all-start.3 = ((bf16[8,48,2048]{2,1,0:T(8,128)(2,1)}), bf16[8,48,2048]{2,1,0:T(8,128)(2,1)S(1)}, u32[]{:S(2)}, u32[]{:S(2)}) async-start(bf16[8,48,2048]{2,1,0:T(8,128)(2,1)} %bitcast.20), calls=%async_computation.3 | async-start | bytes 3145728 | tf_op jit(solution)/shard_map/all_to_all | solution.py:354
  83.5 3.9 %collective-permute-start.2 = (bf16[48,2048]{1,0:T(8,128)(2,1)}, bf16[48,2048]{1,0:T(8,128)(2,1)S(1)}, u32[]{:S(2)}, u32[]{:S(2)}) collective-permute-start(bf16[48,2048]{1,0:T(8,128)(2,1)} %get-tuple-element.35), channel_id=1, source_target_pairs={{0,1},{1,0},{2,3},{3,2},{4,5},{5,4},{6,7},{7,6},{8,9},{9,8},{10,11... | collective-permute-start | bytes 589832 | tf_op jit(solution)/shard_map/ppermute | solution.py:488
  83.9 24.3 %collective-permute-start.3 = (bf16[48,2048]{1,0:T(8,128)(2,1)}, bf16[48,2048]{1,0:T(8,128)(2,1)S(1)}, u32[]{:S(2)}, u32[]{:S(2)}) collective-permute-start(bf16[48,2048]{1,0:T(8,128)(2,1)} %get-tuple-element.36), channel_id=1, source_target_pairs={{0,2},{1,3},{2,0},{3,1},{4,6},{5,7},{6,4},{7,5},{8,10},{9,11},{10,... | collective-permute-start | bytes 589832 | tf_op jit(solution)/shard_map/ppermute | solution.py:488
  85.6 25.8 %collective-permute-start.4 = (bf16[48,2048]{1,0:T(8,128)(2,1)S(1)}, bf16[48,2048]{1,0:T(8,128)(2,1)S(1)}, u32[]{:S(2)}, u32[]{:S(2)}) collective-permute-start(bf16[48,2048]{1,0:T(8,128)(2,1)S(1)} %copy-done.20), channel_id=1, source_target_pairs={{0,3},{1,2},{2,1},{3,0},{4,7},{5,6},{6,5},{7,4},{8,11},{9,10},{10,... | collective-permute-start | bytes 589832 | tf_op jit(solution)/shard_map/ppermute | solution.py:488
  85.6 26.8 %collective-permute-start.5 = (bf16[48,2048]{1,0:T(8,128)(2,1)}, bf16[48,2048]{1,0:T(8,128)(2,1)S(1)}, u32[]{:S(2)}, u32[]{:S(2)}) collective-permute-start(bf16[48,2048]{1,0:T(8,128)(2,1)} %get-tuple-element.38), channel_id=1, source_target_pairs={{0,4},{1,5},{2,6},{3,7},{4,0},{5,1},{6,2},{7,3},{8,12},{9,13},{10,... | collective-permute-start | bytes 589832 | tf_op jit(solution)/shard_map/ppermute | solution.py:488
  87.3 25.1 %collective-permute-start.6 = (bf16[48,2048]{1,0:T(8,128)(2,1)}, bf16[48,2048]{1,0:T(8,128)(2,1)S(1)}, u32[]{:S(2)}, u32[]{:S(2)}) collective-permute-start(bf16[48,2048]{1,0:T(8,128)(2,1)} %get-tuple-element.39), channel_id=1, source_target_pairs={{0,5},{1,4},{2,7},{3,6},{4,1},{5,0},{6,3},{7,2},{8,13},{9,12},{10,... | collective-permute-start | bytes 589832 | tf_op jit(solution)/shard_map/ppermute | solution.py:488
  87.4 39.0 %copy-start.10 = (bf16[48,2048]{1,0:T(8,128)(2,1)}, bf16[48,2048]{1,0:T(8,128)(2,1)S(1)}, u32[]{:S(2)}) copy-start(bf16[48,2048]{1,0:T(8,128)(2,1)S(1)} %collective-permute-done.2.refs_1_) | copy-start | bytes 589828
  87.4 35.7 %collective-permute-start.7 = (bf16[48,2048]{1,0:T(8,128)(2,1)S(1)}, bf16[48,2048]{1,0:T(8,128)(2,1)S(1)}, u32[]{:S(2)}, u32[]{:S(2)}) collective-permute-start(bf16[48,2048]{1,0:T(8,128)(2,1)S(1)} %copy-done.19), channel_id=1, source_target_pairs={{0,6},{1,7},{2,4},{3,5},{4,2},{5,3},{6,0},{7,1},{8,14},{9,15},{10,... | collective-permute-start | bytes 589832 | tf_op jit(solution)/shard_map/ppermute | solution.py:488
  108.2 18.2 %copy-start.11 = (bf16[48,2048]{1,0:T(8,128)(2,1)}, bf16[48,2048]{1,0:T(8,128)(2,1)S(1)}, u32[]{:S(2)}) copy-start(bf16[48,2048]{1,0:T(8,128)(2,1)S(1)} %collective-permute-done.3.refs_2_) | copy-start | bytes 589828
  108.2 18.2 %collective-permute-start.8 = (bf16[48,2048]{1,0:T(8,128)(2,1)S(1)}, bf16[48,2048]{1,0:T(8,128)(2,1)S(1)}, u32[]{:S(2)}, u32[]{:S(2)}) collective-permute-start(bf16[48,2048]{1,0:T(8,128)(2,1)S(1)} %copy-done.18), channel_id=1, source_target_pairs={{0,7},{1,6},{2,5},{3,4},{4,3},{5,2},{6,1},{7,0},{8,15},{9,14},{10,... | collective-permute-start | bytes 589832 | tf_op jit(solution)/shard_map/ppermute | solution.py:488
  111.4 15.0 %copy-start.12 = (bf16[48,2048]{1,0:T(8,128)(2,1)}, bf16[48,2048]{1,0:T(8,128)(2,1)S(1)}, u32[]{:S(2)}) copy-start(bf16[48,2048]{1,0:T(8,128)(2,1)S(1)} %collective-permute-done.4.refs_3_) | copy-start | bytes 589828
  111.4 44.2 %collective-permute-start.10 = (bf16[64,2048]{1,0:T(8,128)(2,1)S(1)}, bf16[64,2048]{1,0:T(8,128)(2,1)S(1)}, u32[]{:S(2)}, u32[]{:S(2)}) collective-permute-start(bf16[64,2048]{1,0:T(8,128)(2,1)S(1)} %get-tuple-element.44), channel_id=1, source_target_pairs={{0,8},{1,9},{2,10},{3,11},{4,12},{5,13},{6,14},{7,15},{8,0},{9,1},... | collective-permute-start | bytes 786440 | tf_op jit(solution)/shard_map/ppermute | solution.py:389
  112.4 14.0 %copy-start.13 = (bf16[48,2048]{1,0:T(8,128)(2,1)}, bf16[48,2048]{1,0:T(8,128)(2,1)S(1)}, u32[]{:S(2)}) copy-start(bf16[48,2048]{1,0:T(8,128)(2,1)S(1)} %collective-permute-done.5.refs_4_) | copy-start | bytes 589828
  112.4 14.0 %copy-start.14 = (bf16[48,2048]{1,0:T(8,128)(2,1)}, bf16[48,2048]{1,0:T(8,128)(2,1)S(1)}, u32[]{:S(2)}) copy-start(bf16[48,2048]{1,0:T(8,128)(2,1)S(1)} %collective-permute-done.6.refs_5_) | copy-start | bytes 589828
  123.1 3.3 %copy-start.15 = (bf16[48,2048]{1,0:T(8,128)(2,1)}, bf16[48,2048]{1,0:T(8,128)(2,1)S(1)}, u32[]{:S(2)}) copy-start(bf16[48,2048]{1,0:T(8,128)(2,1)S(1)} %collective-permute-done.7.refs_6_) | copy-start | bytes 589828
  126.4 0.7 copy-start.16
  155.7 1.2 copy-start.9
  156.8 32.4 %all-to-all-start.2 = ((bf16[8,48,2048]{2,1,0:T(8,128)(2,1)}), bf16[8,48,2048]{2,1,0:T(8,128)(2,1)S(1)}, u32[]{:S(2)}, u32[]{:S(2)}) async-start(bf16[8,48,2048]{2,1,0:T(8,128)(2,1)} %ordered.2.refs_1_), calls=%async_computation.2 | async-start | bytes 3145728 | tf_op jit(solution)/shard_map/all_to_all | solution.py:354
  160.4 28.8 %collective-permute-start.11 = (bf16[64,2048]{1,0:T(8,128)(2,1)S(1)}, bf16[64,2048]{1,0:T(8,128)(2,1)S(1)}, u32[]{:S(2)}, u32[]{:S(2)}) collective-permute-start(bf16[64,2048]{1,0:T(8,128)(2,1)S(1)} %get-tuple-element.48), channel_id=1, source_target_pairs={{0,8},{1,9},{2,10},{3,11},{4,12},{5,13},{6,14},{7,15},{8,0},{9,1},... | collective-permute-start | bytes 786440 | tf_op jit(solution)/shard_map/ppermute | solution.py:389
  213.6 4.3 %copy-start.3 = (f32[128,128]{1,0:T(8,128)S(1)}, f32[128,128]{1,0:T(8,128)}, u32[]{:S(2)}) copy-start(f32[128,128]{1,0:T(8,128)} %copy-done.2) | copy-start | bytes 196612
  214.8 26.8 %collective-permute-start.12 = (bf16[128,2048]{1,0:T(8,128)(2,1)S(1)}, bf16[128,2048]{1,0:T(8,128)(2,1)S(1)}, u32[]{:S(2)}, u32[]{:S(2)}) collective-permute-start(bf16[128,2048]{1,0:T(8,128)(2,1)S(1)} %get-tuple-element.49), channel_id=1, source_target_pairs={{0,8},{1,9},{2,10},{3,11},{4,12},{5,13},{6,14},{7,15},{8,0},{9,1},... | collective-permute-start | bytes 1572872 | tf_op jit(solution)/shard_map/ppermute | solution.py:389
  217.8 23.3 %collective-permute-start.13 = (f32[8,128]{1,0:T(8,128)S(1)}, f32[8,128]{1,0:T(8,128)S(1)}, u32[]{:S(2)}, u32[]{:S(2)}) collective-permute-start(f32[8,128]{1,0:T(8,128)S(1)} %get-tuple-element.51), channel_id=1, source_target_pairs={{0,8},{1,9},{2,10},{3,11},{4,12},{5,13},{6,14},{7,15},{8,0},{9,1},... | collective-permute-start | bytes 12296 | tf_op jit(solution)/shard_map/ppermute | solution.py:389

commit v13 on v12

--- a/solution.py
+++ b/solution.py
@@ -134,14 +134,13 @@
 
 
 def state_kernel(
-    me_ref, put_ref, pick_ref, returned_ref, values_ref, columns_ref, _, state_ref, *refs
+    put_ref, pick_ref, returned_ref, values_ref, columns_ref, _, state_ref, out_hbm, sent_ref, sem
 ):
-    out_hbms, (sent_ref, sem) = refs[:-2], refs[-2:]
     features = values_ref.shape[1]
-    half = len(out_hbms)
-    block = sent_ref.shape[0] // half
-    width = 512
-    for left in range(0, features, width):
+    width = features // sem.shape[0]
+    copies = []
+    for n in range(sem.shape[0]):
+        left = n * width
         found = dot(put_ref[...], returned_ref[:, left : left + width])
         for b in range(width // BLOCK):
             at = left + b * BLOCK
@@ -152,13 +151,11 @@
             state_ref[:, at : at + BLOCK] = (
                 scaled + found[:, b * BLOCK : (b + 1) * BLOCK]
             ).astype(BF16)
-        cols = slice(left, left + width)
+        cols = pl.ds(left, width)
         sent_ref[:, cols] = dot(pick_ref[...], state_ref[:, cols]).astype(BF16)
-    copies = []
-    for k in range(half):
-        partner = (me_ref[0] & (half - 1)) ^ k
-        rows = pl.ds(pl.multiple_of(partner * block, block), block)
-        copies.append(pltpu.make_async_copy(sent_ref.at[rows], out_hbms[k], sem.at[k]))
+        copies.append(
+            pltpu.make_async_copy(sent_ref.at[:, cols], out_hbm.at[:, cols], sem.at[n])
+        )
         copies[-1].start()
     for copy in copies:
         copy.wait()
@@ -183,48 +180,41 @@
         copy.wait()
 
 
-def expert_kernel(parts, after, me_ref, *refs):
-    rows_hbms = refs[:parts]
-    wg_hbm, wu_hbm, wd_hbm, out_ref = refs[parts + after : parts + after + 4]
+def expert_kernel(after, rows_hbm, *refs):
+    wg_hbm, wu_hbm, wd_hbm, out_ref = refs[after : after + 4]
     rows_ref, x_ref, wg_ref, wu_ref, wd_ref, hidden_ref, result_ref, sem, rows_sem = refs[
-        parts + after + 4 :
+        after + 4 :
     ]
     exp_dev, features, width = wg_hbm.shape
-    held = wg_ref.shape[0]
     half = rows_ref.shape[0]
-    up_cuts = ((0, 512), (512, 512), (1024, width - 1024))
+    up_cuts = ((0, 256), (256, 256), (512, 512), (1024, width - 1024))
     down_cuts = tuple((at, 512) for at in range(0, features, 512))
-
-    def weight_copies(j, place):
-        copies = []
-        for at, size in up_cuts:
+    ahead = 4
+
+    def part_copies(j, n):
+        if n < len(up_cuts):
+            at, size = up_cuts[n]
             cols = pl.ds(at, size)
-            copies.append((wg_hbm.at[j, :, cols], wg_ref.at[place, :, cols]))
-            copies.append((wu_hbm.at[j, :, cols], wu_ref.at[place, :, cols]))
-        for at, size in down_cuts:
+            pairs = ((wg_hbm, wg_ref), (wu_hbm, wu_ref))
+        else:
+            at, size = down_cuts[n - len(up_cuts)]
             cols = pl.ds(at, size)
-            copies.append((wd_hbm.at[j, :, cols], wd_ref.at[place, :, cols]))
+            pairs = ((wd_hbm, wd_ref),)
         return [
-            pltpu.make_async_copy(src, dst, sem.at[place, n])
-            for n, (src, dst) in enumerate(copies)
+            pltpu.make_async_copy(hbm.at[j, :, cols], ref.at[:, cols], sem.at[n, m])
+            for m, (hbm, ref) in enumerate(pairs)
         ]
 
-    if parts == 1:
-        rows_copies = [pltpu.make_async_copy(rows_hbms[0], rows_ref, rows_sem.at[0])]
-    else:
-        rows_copies = [
-            pltpu.make_async_copy(
-                rows_hbms[k], rows_ref.at[(me_ref[0] & (half - 1)) ^ k], rows_sem.at[k]
-            )
-            for k in range(parts)
-        ]
-    for copy in rows_copies:
+    part_count = len(up_cuts) + len(down_cuts)
+
+    rows_copy = pltpu.make_async_copy(rows_hbm, rows_ref, rows_sem)
+    rows_copy.start()
+    for copy in part_copies(0, 0):
         copy.start()
-    for j in range(held):
-        for copy in weight_copies(j, j):
+    rows_copy.wait()
+    for n in range(1, ahead):
+        for copy in part_copies(0, n):
             copy.start()
-    for copy in rows_copies:
-        copy.wait()
 
     low = iota((PAIR, features), 0) < CAP
     for chunk in range(exp_dev // 2):
@@ -243,35 +233,30 @@
 
     @pl.loop(0, exp_dev)
     def _(j):
-        place = j % held
-        copies = weight_copies(j, place)
-        later = weight_copies(jnp.minimum(j + held, exp_dev - 1), place)
-
-        def refill(first, count):
-            @pl.when(j + held < exp_dev)
-            def _():
-                for n in range(first, first + count):
-                    later[n].start()
-
-        def hide(gate, up, at):
-            hidden = gate / (1.0 + jnp.exp(-gate)) * up
-            hidden_ref[:, at : at + gate.shape[1]] = hidden.astype(BF16)
+        def arrive(n):
+            for copy in part_copies(j, n):
+                copy.wait()
+            if n + ahead < part_count:
+                for copy in part_copies(j, n + ahead):
+                    copy.start()
+            else:
+
+                @pl.when(j + 1 < exp_dev)
+                def _():
+                    for copy in part_copies(j + 1, n + ahead - part_count):
+                        copy.start()
 
         n = 0
         for at, size in up_cuts:
-            copies[n].wait()
-            copies[n + 1].wait()
-            gate = dot(x_ref[j], wg_ref[place, :, at : at + size])
-            up = dot(x_ref[j], wu_ref[place, :, at : at + size])
-            hide(gate, up, at)
-            refill(n, 2)
-            n += 2
+            arrive(n)
+            gate = dot(x_ref[j], wg_ref[:, at : at + size])
+            up = dot(x_ref[j], wu_ref[:, at : at + size])
+            hidden = gate / (1.0 + jnp.exp(-gate)) * up
+            hidden_ref[:, at : at + size] = hidden.astype(BF16)
+            n += 1
         for at, size in down_cuts:
-            copies[n].wait()
-            result_ref[j, :, at : at + size] = dot(
-                hidden_ref[...], wd_ref[place, :, at : at + size]
-            )
-            refill(n, 1)
+            arrive(n)
+            result_ref[j, :, at : at + size] = dot(hidden_ref[...], wd_ref[:, at : at + size])
             n += 1
 
     for pair in range(half // 2):
@@ -284,44 +269,38 @@
             out_ref[2 * pair + odd] = jnp.concatenate(parts, axis=0).astype(BF16)
 
 
-def expert_call(name, place, rows_in, weights, after=()):
+def expert_call(name, rows_in, weights, after=()):
     w_gate, w_up, w_down = weights
     exp_dev, features, width = w_gate.shape
-    parts = len(rows_in)
-    half = EXPERTS // exp_dev // 2
+    half = rows_in.shape[0]
     rows = half * CAP
-    held = 2
-    slots = exp_dev * CAP
     anywhere = pl.BlockSpec(memory_space=pl.ANY)
     hbm = pl.BlockSpec(memory_space=pltpu.HBM)
-    operands = [in_hbm(array) for array in (*rows_in, *after, w_gate, w_up, w_down)]
+    operands = [in_hbm(array) for array in (rows_in, *after, w_gate, w_up, w_down)]
     return pl.pallas_call(
-        functools.partial(expert_kernel, parts, len(after)),
-        out_shape=pltpu.HBM((half, slots, features), BF16),
-        in_specs=[pl.BlockSpec(memory_space=pltpu.SMEM)]
-        + [hbm] * parts
-        + [anywhere] * len(after)
-        + [hbm] * 3,
+        functools.partial(expert_kernel, len(after)),
+        out_shape=pltpu.HBM(rows_in.shape, BF16),
+        in_specs=[hbm] + [anywhere] * len(after) + [hbm] * 3,
         out_specs=pl.BlockSpec(memory_space=VMEM),
         scratch_shapes=[
-            VMEM((half, slots, features), BF16),
+            VMEM(rows_in.shape, BF16),
             VMEM((exp_dev, rows, features), BF16),
-            VMEM((held, features, width), BF16),
-            VMEM((held, features, width), BF16),
-            VMEM((held, width, features), BF16),
+            VMEM((features, width), BF16),
+            VMEM((features, width), BF16),
+            VMEM((width, features), BF16),
             VMEM((rows, width), BF16),
             VMEM((exp_dev, rows, features), F32),
-            pltpu.SemaphoreType.DMA((held, 10)),
-            pltpu.SemaphoreType.DMA((half,)),
+            pltpu.SemaphoreType.DMA((8, 2)),
+            pltpu.SemaphoreType.DMA,
         ],
-        compiler_params=pltpu.CompilerParams(vmem_limit_bytes=46 * 1024 * 1024),
+        compiler_params=pltpu.CompilerParams(vmem_limit_bytes=30 * 1024 * 1024),
         cost_estimate=pl.CostEstimate(
             flops=12 * exp_dev * rows * features * width,
             bytes_accessed=6 * exp_dev * features * width,
             transcendentals=exp_dev * rows * width,
         ),
         name=name,
-    )(place, *operands)
+    )(*operands)
 
 
 def mix_kernel(slots_ref, columns_ref, back_ref, *refs):
@@ -451,19 +430,17 @@
         name="far_plan",
     )(place, mirrored(sent_ids), mirrored(sent_weights))
 
-    state, *near_sent = pl.pallas_call(
+    sent_shape = pltpu.HBM((slots, features), BF16)
+    sent_scratch = [VMEM((slots, features), BF16), pltpu.SemaphoreType.DMA((4,))]
+    state, near_sent = pl.pallas_call(
         state_kernel,
-        out_shape=(
-            shape((tok_rows, features), BF16),
-            *[pltpu.HBM((2 * PAIR, features), BF16)] * half,
-        ),
-        in_specs=[smem] + [vmem] * 5 + [anywhere],
-        out_specs=(vmem,) + (anywhere,) * half,
-        scratch_shapes=[VMEM((slots, features), BF16), pltpu.SemaphoreType.DMA((half,))],
+        out_shape=(shape((tok_rows, features), BF16), sent_shape),
+        in_specs=[vmem] * 5 + [anywhere],
+        out_specs=(vmem, anywhere),
+        scratch_shapes=sent_scratch,
         compiler_params=SMALL,
         name="token_state",
     )(
-        place,
         put,
         near_pick,
         returned.reshape(device_count * look_cap, features),
@@ -474,32 +451,25 @@
     split = shape((tok_rows // 2, features), BF16)
     far_sent, *grad_halves = pl.pallas_call(
         pick_kernel,
-        out_shape=(pltpu.HBM((slots, features), BF16), split, split),
+        out_shape=(sent_shape, split, split),
         in_specs=[vmem, vmem, vmem],
         out_specs=(anywhere, vmem, vmem),
-        scratch_shapes=[VMEM((slots, features), BF16), pltpu.SemaphoreType.DMA((4,))],
+        scratch_shapes=sent_scratch,
         compiler_params=SMALL,
         cost_estimate=pl.CostEstimate(
             flops=400_000_000_000, bytes_accessed=4 * slots * features, transcendentals=0
         ),
         name="far_slots",
     )(far_pick, mirrored(state), out_grad)
-    near_rows = near_sent[:1] + [
-        lax.ppermute(
-            near_sent[k],
-            "expert",
-            [(i, i // half * half + (i % half ^ k)) for i in range(device_count)],
-        )
-        for k in range(1, half)
-    ]
+    near_rows = swap(near_sent.reshape(half, 2 * PAIR, features), halves)
     far_sent = far_sent.reshape(half, 2 * PAIR, features)
     far_rows = swap(far_sent, halves)
     other_grads = [mirrored(array) for array in grad_halves]
 
     weights = (w_gate, w_up, w_down)
-    near_out = expert_call("near_experts", place, near_rows, weights, after=(far_sent,))
+    near_out = expert_call("near_experts", near_rows, weights, after=(far_sent,))
     near_out = ordered(in_hbm(near_out), other_grads[0])
-    far_out = expert_call("far_experts", place, [far_rows], weights, after=(near_out,))
+    far_out = expert_call("far_experts", far_rows, weights, after=(near_out,))
     near_back = swap(near_out, halves)
     far_back = swap(ordered(in_hbm(far_out), near_back, other_grads[1]), halves)
 

time: 243 us -> 204 us (0.84)
  waiting for transfers between devices: 110 us -> 80.5 us
  Pallas kernels: 70.4 us -> 62.5 us
    ppermute x7 -> x0, waiting for transfers between devices: 34.9 us -> none  [near_path(): lax.ppermute(near_sent[k], 'expert', [(i, i // half * half + (i % half ^...]
    all_to_all x4 -> x5, waiting for transfers between devices: 6.26 us -> 16 us  [swap(): lax.all_to_all(array, 'expert', split_axis=0, concat_axis=0, tiled=True,...]
    pallas_call x3, Pallas kernels: 58.7 us -> 51.6 us  [the longest x2 50.2 us: expert_call(): pl.pallas_call(functools.partial(expert_kernel, len(after)), out_shape=pl...]
    ppermute x7 -> x0, starting transfers between devices: 7.01 us -> none  [near_path(): lax.ppermute(near_sent[k], 'expert', [(i, i // half * half + (i % half ^...]
    all_to_all x4 -> x5, starting transfers between devices: 18.5 us -> 24.3 us  [swap(): lax.all_to_all(array, 'expert', split_axis=0, concat_axis=0, tiled=True,...]
    ppermute x7, waiting for transfers between devices: 69 us -> 64.4 us  [mirrored(): return lax.ppermute(array, 'expert', pairs)]
  transfers between devices with their start and end apart: 18 -> 12, of which waited for: 8 -> 5; matrix products, arithmetic and copies ran while one was open for 0% -> 0% of each run, Pallas kernels for 25% -> 27%
where the time goes in v13:
time: 204 us
  waiting for transfers between devices  80.5 us (39%)
  Pallas kernels  62.5 us (31%)
  starting transfers between devices  33.6 us (16%)
  blocking collectives  24.5 us (12%)
    ppermute x7, waiting for transfers between devices, mirrored(): return lax.ppermute(array, 'expert', pairs)  64.4 us
    pallas_call x2, Pallas kernels, expert_call(): pl.pallas_call(functools.partial(expert_kernel, len(after)), out_shape=pl...  50.2 us
    all_to_all x1, blocking collectives, swap(): lax.all_to_all(array, 'expert', split_axis=0, concat_axis=0, tiled=True,...  24.5 us
    all_to_all x5, starting transfers between devices, swap(): lax.all_to_all(array, 'expert', split_axis=0, concat_axis=0, tiled=True,...  24.3 us
    all_to_all x5, waiting for transfers between devices, swap(): lax.all_to_all(array, 'expert', split_axis=0, concat_axis=0, tiled=True,...  16 us
    ppermute x7, starting transfers between devices, mirrored(): return lax.ppermute(array, 'expert', pairs)  9.3 us
  transfers between devices with their start and end apart: 12, of which 5 were waited for; matrix products, arithmetic and copies ran while one was open for 0% of the time, Pallas kernels for 27%

profile of v13, /device:TPU:0, one launch (start us, length us, event | category | flops | bytes accessed | tf_op | source)
XLA Modules:
  0.0 203.5 jit_solution(11139317166310788710)
XLA Ops:
  0.6 1.3 repeat_rows.1
  1.9 7.4 %all-to-all-start = ((s32[16,1,128]{2,1,0:T(1,128)}), s32[16,1,128]{2,1,0:T(1,128)S(1)}, u32[]{:S(2)}, u32[]{:S(2)}) async-start(s32[16,1,128]{2,1,0:T(1,128)} %repeat_rows.1), calls=%async_computation | async-start | bytes 16384 | tf_op jit(solution)/shard_map/all_to_all | solution.py:333
  9.3 0.1 pad_add_fusion.me_ref
  9.4 6.3 %all-to-all-done.rows_ref = s32[16,1,128]{2,1,0:T(1,128)S(1)} async-done(((s32[16,1,128]{2,1,0:T(1,128)}), s32[16,1,128]{2,1,0:T(1,128)S(1)}, u32[]{:S(2)}, u32[]{:S(2)}) %all-to-all-start) | async-done | bytes 8224 | tf_op jit(solution)/shard_map/all_to_all | solution.py:333
  15.6 3.2 %fetch_rows.1._ = bf16[256,2048]{1,0:T(8,128)(2,1)} custom-call(s32[2]{0:T(128)S(1)} %pad_add_fusion.me_ref, s32[16,1,128]{2,1,0:T(1,128)S(1)} %all-to-all-done.rows_ref, bf16[256,2048]{1,0:T(8,128)(2,1)} %table_hbm.1), custom_call_target="tpu_custom_call" | custom-call | tf_op jit(solution)/shard_map/fetch_rows/pallas_call | solution.py:389
  18.8 0.0 copy-start.7
  18.8 0.0 copy-start.4
  18.9 0.0 copy-start.5
  18.9 0.0 copy-start.6
  18.9 0.0 copy-start.1
  18.9 3.8 %all-to-all-start.1 = ((bf16[16,16,2048]{2,1,0:T(8,128)(2,1)}), bf16[16,16,2048]{2,1,0:T(8,128)(2,1)S(1)}, u32[]{:S(2)}, u32[]{:S(2)}) async-start(bf16[16,16,2048]{2,1,0:T(8,128)(2,1)} %bitcast.5), calls=%async_computation.1 | async-start | bytes 2097152 | tf_op jit(solution)/shard_map/all_to_all | solution.py:333
  22.7 0.0 copy-done.7
  22.7 0.0 copy-done.4
  22.7 0.0 copy-done.5
  22.7 0.0 copy-done.6
  22.8 0.9 near_plan.1
  23.6 0.0 copy-start.2
  23.6 2.8 %collective-permute-start = (s32[4,128]{1,0:T(4,128)S(1)}, s32[4,128]{1,0:T(4,128)S(1)}, u32[]{:S(2)}, u32[]{:S(2)}) collective-permute-start(s32[4,128]{1,0:T(4,128)S(1)} %get-tuple-element.24), channel_id=1, source_target_pairs={{0,8},{1,9},{2,10},{3,11},{4,12},{5,13},{6,14},{7,15},{8,0},{9,1},... | collective-permute-start | bytes 6152 | tf_op jit(solution)/shard_map/ppermute | solution.py:368
  26.4 0.2 collective-permute-start.1
  26.6 22.7 %collective-permute-done.ids_ref = s32[4,128]{1,0:T(4,128)S(1)} collective-permute-done((s32[4,128]{1,0:T(4,128)S(1)}, s32[4,128]{1,0:T(4,128)S(1)}, u32[]{:S(2)}, u32[]{:S(2)}) %collective-permute-start) | collective-permute-done | bytes 2080 | tf_op jit(solution)/shard_map/ppermute | solution.py:368
  49.3 0.0 collective-permute-done.1.weights_ref
  49.3 0.8 far_plan.1
  50.2 0.0 all-to-all-done.1
  50.2 2.2 %token_state.1 = (bf16[128,2048]{1,0:T(8,128)(2,1)S(1)}, bf16[384,2048]{1,0:T(8,128)(2,1)}) custom-call(bf16[128,256]{1,0:T(8,128)(2,1)S(1)} %get-tuple-element.22.put_ref, bf16[384,128]{1,0:T(8,128)(2,1)S(1)} %get-tuple-element.23.pick_ref, bf16[256,2048]{1,0:T(8,128)(2,1)S(1)} %bitcast.16, bf16[128,2048]{1,0:T(8,128)(2,1)S(1)} %copy-done.1, ...), custom_call_target="tpu_custom_call" | custom-call | tf_op jit(solution)/shard_map/token_state/pallas_call | solution.py:435
  52.4 0.6 collective-permute-start.2
  53.0 4.4 %all-to-all-start.2 = ((bf16[8,48,2048]{2,1,0:T(8,128)(2,1)}), bf16[8,48,2048]{2,1,0:T(8,128)(2,1)}, u32[]{:S(2)}, u32[]{:S(2)}) async-start(bf16[8,48,2048]{2,1,0:T(8,128)(2,1)} %bitcast.23), calls=%async_computation.2 | async-start | bytes 3145728 | tf_op jit(solution)/shard_map/all_to_all | solution.py:333
  57.5 20.0 %collective-permute-done.2.state_ref = bf16[128,2048]{1,0:T(8,128)(2,1)S(1)} collective-permute-done((bf16[128,2048]{1,0:T(8,128)(2,1)S(1)}, bf16[128,2048]{1,0:T(8,128)(2,1)S(1)}, u32[]{:S(2)}, u32[]{:S(2)}) %collective-permute-start.2) | collective-permute-done | bytes 524320 | tf_op jit(solution)/shard_map/ppermute | solution.py:368
  77.4 1.5 far_slots.1
  78.9 9.8 %all-to-all-done.2.rows_hbm = bf16[8,48,2048]{2,1,0:T(8,128)(2,1)} async-done(((bf16[8,48,2048]{2,1,0:T(8,128)(2,1)}), bf16[8,48,2048]{2,1,0:T(8,128)(2,1)}, u32[]{:S(2)}, u32[]{:S(2)}) %all-to-all-start.2) | async-done | bytes 1572896 | tf_op jit(solution)/shard_map/all_to_all | solution.py:333
  88.7 4.3 %all-to-all-start.4 = ((bf16[8,48,2048]{2,1,0:T(8,128)(2,1)}), bf16[8,48,2048]{2,1,0:T(8,128)(2,1)}, u32[]{:S(2)}, u32[]{:S(2)}) async-start(bf16[8,48,2048]{2,1,0:T(8,128)(2,1)} %bitcast.21), calls=%async_computation.4 | async-start | bytes 3145728 | tf_op jit(solution)/shard_map/all_to_all | solution.py:333
  93.0 0.8 collective-permute-start.3
  93.8 25.1 %near_experts.1.refs_0_ = bf16[8,48,2048]{2,1,0:T(8,128)(2,1)} custom-call(bf16[8,48,2048]{2,1,0:T(8,128)(2,1)} %all-to-all-done.2.rows_hbm, bf16[8,48,2048]{2,1,0:T(8,128)(2,1)} %bitcast.22, bf16[4,2048,1408]{2,1,0:T(8,128)(2,1)} %refs_1_.3, bf16[4,2048,1408]{2,1,0:T(8,128)(2,1)} %refs_2_.3, bf16[4,1408,2048]{2,1,0:T(8,128)(2,1)} %refs_3_.3), custom_call_target="tpu_custom_call" | custom-call | flops 13287555072 | bytes 69206016 | tf_op jit(solution)/shard_map/near_experts/pallas_call | solution.py:280
  118.9 0.0 collective-permute-done.3.refs_1_.refs_0_
  118.9 0.0 all-to-all-done.4.rows_hbm
  118.9 4.4 %all-to-all-start.3 = ((bf16[8,48,2048]{2,1,0:T(8,128)(2,1)}), bf16[8,48,2048]{2,1,0:T(8,128)(2,1)S(1)}, u32[]{:S(2)}, u32[]{:S(2)}) async-start(bf16[8,48,2048]{2,1,0:T(8,128)(2,1)} %ordered.2.refs_0_), calls=%async_computation.3 | async-start | bytes 3145728 | tf_op jit(solution)/shard_map/all_to_all | solution.py:333
  123.3 1.9 collective-permute-start.4
  125.2 25.1 %far_experts.1.refs_0_ = bf16[8,48,2048]{2,1,0:T(8,128)(2,1)} custom-call(bf16[8,48,2048]{2,1,0:T(8,128)(2,1)} %all-to-all-done.4.rows_hbm, bf16[8,48,2048]{2,1,0:T(8,128)(2,1)} %ordered.2.refs_0_, bf16[4,2048,1408]{2,1,0:T(8,128)(2,1)} %refs_1_.3, bf16[4,2048,1408]{2,1,0:T(8,128)(2,1)} %refs_2_.3, bf16[4,1408,2048]{2,1,0:T(8,128)(2,1)} %refs_3_.3), custom_call_target="tpu_custom_call" | custom-call | flops 13287555072 | bytes 69206016 | tf_op jit(solution)/shard_map/far_experts/pallas_call | solution.py:280
  150.3 0.0 collective-permute-done.4.refs_2_.refs_1_
  150.3 0.0 all-to-all-done.3.refs_1_
  150.3 24.5 %all_to_all.30 = bf16[8,48,2048]{2,1,0:T(8,128)(2,1)S(1)} all-to-all(bf16[8,48,2048]{2,1,0:T(8,128)(2,1)} %ordered.3), channel_id=1, replica_groups={{0,1,2,3,4,5,6,7},{8,9,10,11,12,13,14,15},{16,17,18,19,20,21,22,23},{24..., dimensions={0} | all-to-all | bytes 3145728 | tf_op jit(solution)/shard_map/all_to_all | solution.py:333
  174.8 1.3 mix_far.1
  176.1 1.1 collective-permute-start.5
  177.2 1.9 collective-permute-start.6
  179.1 1.2 mix_near.1
  180.3 21.8 %collective-permute-done.6 = f32[8,128]{1,0:T(8,128)S(1)} collective-permute-done((f32[8,128]{1,0:T(8,128)S(1)}, f32[8,128]{1,0:T(8,128)S(1)}, u32[]{:S(2)}, u32[]{:S(2)}) %collective-permute-start.6) | collective-permute-done | bytes 4128 | tf_op jit(solution)/shard_map/ppermute | solution.py:368
  202.1 0.6 slice_bitcast_fusion
  202.6 0.0 collective-permute-done.5
  202.6 0.9 add_convert_fusion
  (10 shorter events, 0.0 us)
Async XLA Ops:
  1.9 13.7 %all-to-all-start = ((s32[16,1,128]{2,1,0:T(1,128)}), s32[16,1,128]{2,1,0:T(1,128)S(1)}, u32[]{:S(2)}, u32[]{:S(2)}) async-start(s32[16,1,128]{2,1,0:T(1,128)} %repeat_rows.1), calls=%async_computation | async-start | bytes 16384 | tf_op jit(solution)/shard_map/all_to_all | solution.py:333
  18.8 3.9 %copy-start.7 = (s32[128,16]{0,1:T(8,128)S(1)}, s32[128,16]{0,1:T(8,128)}, u32[]{:S(2)}) copy-start(s32[128,16]{0,1:T(8,128)} %param.11) | copy-start | bytes 24580
  18.8 3.9 %copy-start.4 = (s32[128]{0:T(128)S(1)}, s32[128]{0:T(128)}, u32[]{:S(2)}) copy-start(s32[128]{0:T(128)} %param.12) | copy-start | bytes 1540
  18.9 3.9 %copy-start.5 = (s32[128,4]{0,1:T(4,128)S(1)}, s32[128,4]{0,1:T(4,128)}, u32[]{:S(2)}) copy-start(s32[128,4]{0,1:T(4,128)} %param.13) | copy-start | bytes 6148
  18.9 3.9 %copy-start.6 = (f32[128,4]{0,1:T(4,128)S(1)}, f32[128,4]{0,1:T(4,128)}, u32[]{:S(2)}) copy-start(f32[128,4]{0,1:T(4,128)} %param.14) | copy-start | bytes 6148
  18.9 31.3 %copy-start.1 = (bf16[128,2048]{1,0:T(8,128)(2,1)S(1)}, bf16[128,2048]{1,0:T(8,128)(2,1)}, u32[]{:S(2)}) copy-start(bf16[128,2048]{1,0:T(8,128)(2,1)} %values_ref.1) | copy-start | bytes 1572868
  18.9 31.3 %all-to-all-start.1 = ((bf16[16,16,2048]{2,1,0:T(8,128)(2,1)}), bf16[16,16,2048]{2,1,0:T(8,128)(2,1)S(1)}, u32[]{:S(2)}, u32[]{:S(2)}) async-start(bf16[16,16,2048]{2,1,0:T(8,128)(2,1)} %bitcast.5), calls=%async_computation.1 | async-start | bytes 2097152 | tf_op jit(solution)/shard_map/all_to_all | solution.py:333
  23.6 29.4 %copy-start.2 = (f32[128,128]{1,0:T(8,128)}, f32[128,128]{1,0:T(8,128)S(1)}, u32[]{:S(2)}) copy-start(f32[128,128]{1,0:T(8,128)S(1)} %get-tuple-element.21.columns_ref) | copy-start | bytes 196612
  23.6 25.7 %collective-permute-start = (s32[4,128]{1,0:T(4,128)S(1)}, s32[4,128]{1,0:T(4,128)S(1)}, u32[]{:S(2)}, u32[]{:S(2)}) collective-permute-start(s32[4,128]{1,0:T(4,128)S(1)} %get-tuple-element.24), channel_id=1, source_target_pairs={{0,8},{1,9},{2,10},{3,11},{4,12},{5,13},{6,14},{7,15},{8,0},{9,1},... | collective-permute-start | bytes 6152 | tf_op jit(solution)/shard_map/ppermute | solution.py:368
  26.4 22.9 %collective-permute-start.1 = (f32[4,128]{1,0:T(4,128)S(1)}, f32[4,128]{1,0:T(4,128)S(1)}, u32[]{:S(2)}, u32[]{:S(2)}) collective-permute-start(f32[4,128]{1,0:T(4,128)S(1)} %get-tuple-element.25), channel_id=1, source_target_pairs={{0,8},{1,9},{2,10},{3,11},{4,12},{5,13},{6,14},{7,15},{8,0},{9,1},... | collective-permute-start | bytes 6152 | tf_op jit(solution)/shard_map/ppermute | solution.py:368
  52.4 25.0 %collective-permute-start.2 = (bf16[128,2048]{1,0:T(8,128)(2,1)S(1)}, bf16[128,2048]{1,0:T(8,128)(2,1)S(1)}, u32[]{:S(2)}, u32[]{:S(2)}) collective-permute-start(bf16[128,2048]{1,0:T(8,128)(2,1)S(1)} %get-tuple-element.28), channel_id=1, source_target_pairs={{0,8},{1,9},{2,10},{3,11},{4,12},{5,13},{6,14},{7,15},{8,0},{9,1},... | collective-permute-start | bytes 1572872 | tf_op jit(solution)/shard_map/ppermute | solution.py:368
  53.0 24.4 %copy-start = (bf16[128,2048]{1,0:T(8,128)(2,1)S(1)}, bf16[128,2048]{1,0:T(8,128)(2,1)}, u32[]{:S(2)}) copy-start(bf16[128,2048]{1,0:T(8,128)(2,1)} %refs_0_.1) | copy-start | bytes 1572868
  53.0 35.7 %all-to-all-start.2 = ((bf16[8,48,2048]{2,1,0:T(8,128)(2,1)}), bf16[8,48,2048]{2,1,0:T(8,128)(2,1)}, u32[]{:S(2)}, u32[]{:S(2)}) async-start(bf16[8,48,2048]{2,1,0:T(8,128)(2,1)} %bitcast.23), calls=%async_computation.2 | async-start | bytes 3145728 | tf_op jit(solution)/shard_map/all_to_all | solution.py:333
  88.7 30.3 %all-to-all-start.4 = ((bf16[8,48,2048]{2,1,0:T(8,128)(2,1)}), bf16[8,48,2048]{2,1,0:T(8,128)(2,1)}, u32[]{:S(2)}, u32[]{:S(2)}) async-start(bf16[8,48,2048]{2,1,0:T(8,128)(2,1)} %bitcast.21), calls=%async_computation.4 | async-start | bytes 3145728 | tf_op jit(solution)/shard_map/all_to_all | solution.py:333
  93.0 25.9 %collective-permute-start.3 = (bf16[64,2048]{1,0:T(8,128)(2,1)S(1)}, bf16[64,2048]{1,0:T(8,128)(2,1)S(1)}, u32[]{:S(2)}, u32[]{:S(2)}) collective-permute-start(bf16[64,2048]{1,0:T(8,128)(2,1)S(1)} %get-tuple-element.30), channel_id=1, source_target_pairs={{0,8},{1,9},{2,10},{3,11},{4,12},{5,13},{6,14},{7,15},{8,0},{9,1},... | collective-permute-start | bytes 786440 | tf_op jit(solution)/shard_map/ppermute | solution.py:368
  118.9 31.3 %all-to-all-start.3 = ((bf16[8,48,2048]{2,1,0:T(8,128)(2,1)}), bf16[8,48,2048]{2,1,0:T(8,128)(2,1)S(1)}, u32[]{:S(2)}, u32[]{:S(2)}) async-start(bf16[8,48,2048]{2,1,0:T(8,128)(2,1)} %ordered.2.refs_0_), calls=%async_computation.3 | async-start | bytes 3145728 | tf_op jit(solution)/shard_map/all_to_all | solution.py:333
  123.3 27.0 %collective-permute-start.4 = (bf16[64,2048]{1,0:T(8,128)(2,1)S(1)}, bf16[64,2048]{1,0:T(8,128)(2,1)S(1)}, u32[]{:S(2)}, u32[]{:S(2)}) collective-permute-start(bf16[64,2048]{1,0:T(8,128)(2,1)S(1)} %get-tuple-element.34), channel_id=1, source_target_pairs={{0,8},{1,9},{2,10},{3,11},{4,12},{5,13},{6,14},{7,15},{8,0},{9,1},... | collective-permute-start | bytes 786440 | tf_op jit(solution)/shard_map/ppermute | solution.py:368
  174.8 4.3 %copy-start.3 = (f32[128,128]{1,0:T(8,128)S(1)}, f32[128,128]{1,0:T(8,128)}, u32[]{:S(2)}) copy-start(f32[128,128]{1,0:T(8,128)} %copy-done.2) | copy-start | bytes 196612
  176.1 26.6 %collective-permute-start.5 = (bf16[128,2048]{1,0:T(8,128)(2,1)S(1)}, bf16[128,2048]{1,0:T(8,128)(2,1)S(1)}, u32[]{:S(2)}, u32[]{:S(2)}) collective-permute-start(bf16[128,2048]{1,0:T(8,128)(2,1)S(1)} %get-tuple-element.35), channel_id=1, source_target_pairs={{0,8},{1,9},{2,10},{3,11},{4,12},{5,13},{6,14},{7,15},{8,0},{9,1},... | collective-permute-start | bytes 1572872 | tf_op jit(solution)/shard_map/ppermute | solution.py:368
  177.2 24.9 %collective-permute-start.6 = (f32[8,128]{1,0:T(8,128)S(1)}, f32[8,128]{1,0:T(8,128)S(1)}, u32[]{:S(2)}, u32[]{:S(2)}) collective-permute-start(f32[8,128]{1,0:T(8,128)S(1)} %get-tuple-element.37), channel_id=1, source_target_pairs={{0,8},{1,9},{2,10},{3,11},{4,12},{5,13},{6,14},{7,15},{8,0},{9,1},... | collective-permute-start | bytes 12296 | tf_op jit(solution)/shard_map/ppermute | solution.py:368

commit v14 on v13

--- a/solution.py
+++ b/solution.py
@@ -70,9 +70,9 @@
     return jnp.concatenate([rows, jnp.zeros((length - count, length), F32)], axis=0).T
 
 
-def plan_slots(me, ids_ref, pick_ref, slots_ref):
+def plan_slots(me, ids_ref, pick_refs, slots_ref):
     tok_rows = ids_ref.shape[1]
-    half = pick_ref.shape[0] // (2 * PAIR)
+    half = sum(ref.shape[0] for ref in pick_refs) // (2 * PAIR)
     exp_dev = EXPERTS // (2 * half)
     flip = me % 2
     inside = iota((half * exp_dev, tok_rows), 0)
@@ -89,8 +89,18 @@
         lower = jnp.where(flip == 0, two, one) + CAP
         here = ((place < CAP) & (place == upper)) | ((place >= CAP) & (place == lower))
         lines.append(here.astype(F32))
-    pick_ref[...] = jnp.concatenate(lines, axis=0).astype(BF16)
-    slot = (inside // 2) * PAIR + ((inside + flip) & 1) * CAP + rank
+    pairs = exp_dev // 2
+    slot = ((inside + flip) & 1) * CAP + rank
+    if len(pick_refs) == 1:
+        pick_refs[0][...] = jnp.concatenate(lines, axis=0).astype(BF16)
+        slot = slot + (inside // 2) * PAIR
+    else:
+        for n, ref in enumerate(pick_refs):
+            ref[...] = jnp.concatenate(lines[n::pairs], axis=0).astype(BF16)
+        device = inside // exp_dev
+        first = device * (2 * PAIR) + PAIR
+        second = half * 2 * PAIR + device * PAIR
+        slot = slot + jnp.where((inside & 2) == 0, first, second)
     found = [
         jnp.sum(jnp.where(chosen[k], slot + 1, 0), axis=0, keepdims=True) - 1 for k in range(TOP)
     ]
@@ -105,7 +115,8 @@
     scales_ref,
     _,
     put_ref,
-    pick_ref,
+    first_pick_ref,
+    second_pick_ref,
     slots_ref,
     columns_ref,
     ids_out_ref,
@@ -115,7 +126,7 @@
     weights_out_ref[...] = weights_ref[...]
     tok_rows = rows_ref.shape[1]
     me, held = me_ref[0], me_ref[1]
-    device_count = pick_ref.shape[0] // PAIR
+    device_count = first_pick_ref.shape[0] // PAIR * 2
     look_cap = put_ref.shape[1] // device_count
     row = jnp.broadcast_to(rows_ref[...], (device_count, tok_rows))
     low = iota((device_count, tok_rows), 0) * held
@@ -124,12 +135,12 @@
     slot = iota((look_cap, tok_rows), 0)
     put = [(slot == rank[o : o + 1]).astype(F32) for o in range(device_count)]
     put_ref[...] = jnp.concatenate(put, axis=0).T.astype(BF16)
-    plan_slots(me, ids_ref, pick_ref, slots_ref)
+    plan_slots(me, ids_ref, (first_pick_ref, second_pick_ref), slots_ref)
     columns_ref[...] = turned(jnp.concatenate([weights_ref[...], scales_ref[...]], axis=0))
 
 
 def far_plan_kernel(me_ref, ids_ref, weights_ref, pick_ref, slots_ref, columns_ref):
-    plan_slots(me_ref[0], ids_ref, pick_ref, slots_ref)
+    plan_slots(me_ref[0], ids_ref, (pick_ref,), slots_ref)
     columns_ref[...] = turned(weights_ref[...])
 
 
@@ -161,6 +172,10 @@
         copy.wait()
 
 
+def later_kernel(pick_ref, state_ref, _, out_ref):
+    out_ref[...] = dot(pick_ref[...], state_ref[...]).astype(BF16)
+
+
 def pick_kernel(
     pick_ref, state_ref, grad_ref, out_hbm, upper_grad_ref, lower_grad_ref, sent_ref, sem
 ):
@@ -180,44 +195,36 @@
         copy.wait()
 
 
-def expert_kernel(after, rows_hbm, *refs):
+def expert_kernel(first, count, join, after, rows_ref, *refs):
+    if join:
+        front_ref, refs = refs[0], refs[1:]
     wg_hbm, wu_hbm, wd_hbm, out_ref = refs[after : after + 4]
-    rows_ref, x_ref, wg_ref, wu_ref, wd_ref, hidden_ref, result_ref, sem, rows_sem = refs[
-        after + 4 :
-    ]
-    exp_dev, features, width = wg_hbm.shape
+    x_ref, wg_ref, wu_ref, wd_ref, hidden_ref, result_ref, sem = refs[after + 4 :]
+    held, features, width = wg_ref.shape
     half = rows_ref.shape[0]
-    up_cuts = ((0, 256), (256, 256), (512, 512), (1024, width - 1024))
+    up_cuts = ((0, 512), (512, 512), (1024, width - 1024))
     down_cuts = tuple((at, 512) for at in range(0, features, 512))
-    ahead = 4
-
-    def part_copies(j, n):
-        if n < len(up_cuts):
-            at, size = up_cuts[n]
+
+    def weight_copies(j, place):
+        copies = []
+        for at, size in up_cuts:
             cols = pl.ds(at, size)
-            pairs = ((wg_hbm, wg_ref), (wu_hbm, wu_ref))
-        else:
-            at, size = down_cuts[n - len(up_cuts)]
+            copies.append((wg_hbm.at[first + j, :, cols], wg_ref.at[place, :, cols]))
+            copies.append((wu_hbm.at[first + j, :, cols], wu_ref.at[place, :, cols]))
+        for at, size in down_cuts:
             cols = pl.ds(at, size)
-            pairs = ((wd_hbm, wd_ref),)
+            copies.append((wd_hbm.at[first + j, :, cols], wd_ref.at[place, :, cols]))
         return [
-            pltpu.make_async_copy(hbm.at[j, :, cols], ref.at[:, cols], sem.at[n, m])
-            for m, (hbm, ref) in enumerate(pairs)
+            pltpu.make_async_copy(src, dst, sem.at[place, n])
+            for n, (src, dst) in enumerate(copies)
         ]
 
-    part_count = len(up_cuts) + len(down_cuts)
-
-    rows_copy = pltpu.make_async_copy(rows_hbm, rows_ref, rows_sem)
-    rows_copy.start()
-    for copy in part_copies(0, 0):
-        copy.start()
-    rows_copy.wait()
-    for n in range(1, ahead):
-        for copy in part_copies(0, n):
+    for j in range(held):
+        for copy in weight_copies(j, j):
             copy.start()
 
     low = iota((PAIR, features), 0) < CAP
-    for chunk in range(exp_dev // 2):
+    for chunk in range(count // 2):
         here = slice(chunk * PAIR, (chunk + 1) * PAIR)
         for quad in range(half // 4):
             ones, twos = [], []
@@ -231,101 +238,116 @@
             x_ref[2 * chunk, rows, :] = jnp.concatenate(ones, axis=0).astype(BF16)
             x_ref[2 * chunk + 1, rows, :] = jnp.concatenate(twos, axis=0).astype(BF16)
 
-    @pl.loop(0, exp_dev)
+    @pl.loop(0, count)
     def _(j):
-        def arrive(n):
-            for copy in part_copies(j, n):
-                copy.wait()
-            if n + ahead < part_count:
-                for copy in part_copies(j, n + ahead):
+        place = j % held
+        copies = weight_copies(j, place)
+
+        def refill(n, parts):
+            @pl.when(j + held < count)
+            def _():
+                for copy in weight_copies(j + held, place)[n : n + parts]:
                     copy.start()
-            else:
-
-                @pl.when(j + 1 < exp_dev)
-                def _():
-                    for copy in part_copies(j + 1, n + ahead - part_count):
-                        copy.start()
 
         n = 0
         for at, size in up_cuts:
-            arrive(n)
-            gate = dot(x_ref[j], wg_ref[:, at : at + size])
-            up = dot(x_ref[j], wu_ref[:, at : at + size])
+            copies[n].wait()
+            copies[n + 1].wait()
+            gate = dot(x_ref[j], wg_ref[place, :, at : at + size])
+            up = dot(x_ref[j], wu_ref[place, :, at : at + size])
             hidden = gate / (1.0 + jnp.exp(-gate)) * up
             hidden_ref[:, at : at + size] = hidden.astype(BF16)
-            n += 1
+            if count > held:
+                refill(n, 2)
+            n += 2
         for at, size in down_cuts:
-            arrive(n)
-            result_ref[j, :, at : at + size] = dot(hidden_ref[...], wd_ref[:, at : at + size])
+            copies[n].wait()
+            result_ref[j, :, at : at + size] = dot(
+                hidden_ref[...], wd_ref[place, :, at : at + size]
+            )
+            if count > held:
+                refill(n, 1)
             n += 1
 
     for pair in range(half // 2):
         rows = slice(pair * PAIR, (pair + 1) * PAIR)
-        values = [result_ref[j, rows, :] for j in range(exp_dev)]
+        values = [result_ref[j, rows, :] for j in range(count)]
         for odd in range(2):
             parts = [
-                jnp.where(low, values[j + odd], values[j + 1 - odd]) for j in range(0, exp_dev, 2)
+                jnp.where(low, values[j + odd], values[j + 1 - odd]) for j in range(0, count, 2)
             ]
+            if join:
+                parts = [front_ref[2 * pair + odd].astype(F32)] + parts
             out_ref[2 * pair + odd] = jnp.concatenate(parts, axis=0).astype(BF16)
 
 
-def expert_call(name, rows_in, weights, after=()):
+def expert_call(name, first, count, rows_in, weights, front=(), after=()):
     w_gate, w_up, w_down = weights
-    exp_dev, features, width = w_gate.shape
+    _, features, width = w_gate.shape
     half = rows_in.shape[0]
     rows = half * CAP
+    held = 2
     anywhere = pl.BlockSpec(memory_space=pl.ANY)
     hbm = pl.BlockSpec(memory_space=pltpu.HBM)
-    operands = [in_hbm(array) for array in (rows_in, *after, w_gate, w_up, w_down)]
+    vmem = pl.BlockSpec(memory_space=VMEM)
     return pl.pallas_call(
-        functools.partial(expert_kernel, len(after)),
-        out_shape=pltpu.HBM(rows_in.shape, BF16),
-        in_specs=[hbm] + [anywhere] * len(after) + [hbm] * 3,
-        out_specs=pl.BlockSpec(memory_space=VMEM),
+        functools.partial(expert_kernel, first, count, bool(front), len(after)),
+        out_shape=pltpu.HBM((half, count * CAP + len(front) * PAIR, features), BF16),
+        in_specs=[vmem] * (1 + len(front)) + [anywhere] * len(after) + [hbm] * 3,
+        out_specs=vmem,
         scratch_shapes=[
-            VMEM(rows_in.shape, BF16),
-            VMEM((exp_dev, rows, features), BF16),
-            VMEM((features, width), BF16),
-            VMEM((features, width), BF16),
-            VMEM((width, features), BF16),
+            VMEM((count, rows, features), BF16),
+            VMEM((held, features, width), BF16),
+            VMEM((held, features, width), BF16),
+            VMEM((held, width, features), BF16),
             VMEM((rows, width), BF16),
-            VMEM((exp_dev, rows, features), F32),
-            pltpu.SemaphoreType.DMA((8, 2)),
-            pltpu.SemaphoreType.DMA,
+            VMEM((count, rows, features), F32),
+            pltpu.SemaphoreType.DMA((held, 10)),
         ],
-        compiler_params=pltpu.CompilerParams(vmem_limit_bytes=30 * 1024 * 1024),
+        compiler_params=pltpu.CompilerParams(vmem_limit_bytes=46 * 1024 * 1024),
         cost_estimate=pl.CostEstimate(
-            flops=12 * exp_dev * rows * features * width,
-            bytes_accessed=6 * exp_dev * features * width,
-            transcendentals=exp_dev * rows * width,
+            flops=12 * count * rows * features * width,
+            bytes_accessed=6 * count * features * width,
+            transcendentals=count * rows * width,
         ),
         name=name,
-    )(*operands)
-
-
-def mix_kernel(slots_ref, columns_ref, back_ref, *refs):
+    )(
+        *[in_hbm(array) for array in (rows_in, *front, *after, w_gate, w_up, w_down)],
+    )
+
+
+def mix_kernel(parts, grads, slots_ref, columns_ref, *refs):
     mixed_ref, grads_ref = refs[-2:]
+    back_refs, grad_refs = refs[:parts], refs[parts : parts + grads]
     tok_rows = slots_ref.shape[0]
-    count, features = back_ref.shape
-    grad = jnp.concatenate([ref[...] for ref in refs[:-2]], axis=0)
-    column = iota((tok_rows, count), 1)
-    inner = lax.dot_general(
-        grad, back_ref[...], (((1,), (1,)), ((), ())), preferred_element_type=F32
-    )
-    total = jnp.zeros((tok_rows, count), F32)
+    features = back_refs[0].shape[1]
+    grad = jnp.concatenate([ref[...] for ref in grad_refs], axis=0)
     place = iota((tok_rows, tok_rows), 1)
     wide = jnp.zeros((tok_rows, tok_rows), F32)
-    for k in range(TOP):
-        here = column == slots_ref[:, k : k + 1]
-        total = total + jnp.where(here, columns_ref[:, k : k + 1], 0.0)
-        value = jnp.sum(jnp.where(here, inner, 0.0), axis=1, keepdims=True)
-        wide = wide + jnp.where(place == k, value, 0.0)
-    high = total.astype(BF16)
-    rest = (total - high.astype(F32)).astype(BF16)
+    spread = []
+    start = 0
+    for ref in back_refs:
+        count = ref.shape[0]
+        column = iota((tok_rows, count), 1) + start
+        start += count
+        inner = lax.dot_general(
+            grad, ref[...], (((1,), (1,)), ((), ())), preferred_element_type=F32
+        )
+        total = jnp.zeros((tok_rows, count), F32)
+        for k in range(TOP):
+            here = column == slots_ref[:, k : k + 1]
+            total = total + jnp.where(here, columns_ref[:, k : k + 1], 0.0)
+            value = jnp.sum(jnp.where(here, inner, 0.0), axis=1, keepdims=True)
+            wide = wide + jnp.where(place == k, value, 0.0)
+        high = total.astype(BF16)
+        spread.append((high, (total - high.astype(F32)).astype(BF16)))
     width = 512
     for at in range(0, features, width):
-        rows = back_ref[:, at : at + width]
-        mixed_ref[:, at : at + width] = (dot(high, rows) + dot(rest, rows)).astype(mixed_ref.dtype)
+        cols = slice(at, at + width)
+        value = jnp.zeros((tok_rows, width), F32)
+        for (high, rest), ref in zip(spread, back_refs):
+            value = value + dot(high, ref[:, cols]) + dot(rest, ref[:, cols])
+        mixed_ref[:, cols] = value.astype(mixed_ref.dtype)
     grads_ref[...] = wide.T[: grads_ref.shape[0], :]
 
 
@@ -398,19 +420,21 @@
     returned = swap(fetched.reshape(device_count, look_cap, features))
     turned_ids, turned_weights = expert_ids.T, gate_weights.T
     pick_shape = shape((slots, tok_rows), BF16)
+    pair_shape = shape((slots // 2, tok_rows), BF16)
     square = (tok_rows, tok_rows)
-    put, near_pick, near_of, near_columns, sent_ids, sent_weights = pl.pallas_call(
+    put, first_pick, second_pick, near_of, near_columns, sent_ids, sent_weights = pl.pallas_call(
         near_plan_kernel,
         out_shape=(
             shape((tok_rows, device_count * look_cap), BF16),
-            pick_shape,
+            pair_shape,
+            pair_shape,
             shape(square, jnp.int32),
             shape(square, F32),
             shape(turned_ids.shape, jnp.int32),
             shape(turned_weights.shape, F32),
         ),
         in_specs=[smem, vmem, vmem, vmem, vmem, anywhere],
-        out_specs=(vmem,) * 6,
+        out_specs=(vmem,) * 7,
         compiler_params=SMALL,
         name="near_plan",
     )(
@@ -430,19 +454,20 @@
         name="far_plan",
     )(place, mirrored(sent_ids), mirrored(sent_weights))
 
-    sent_shape = pltpu.HBM((slots, features), BF16)
-    sent_scratch = [VMEM((slots, features), BF16), pltpu.SemaphoreType.DMA((4,))]
+    def sent_scratch(count):
+        return [VMEM((count, features), BF16), pltpu.SemaphoreType.DMA((4,))]
+
     state, near_sent = pl.pallas_call(
         state_kernel,
-        out_shape=(shape((tok_rows, features), BF16), sent_shape),
+        out_shape=(shape((tok_rows, features), BF16), pltpu.HBM((slots // 2, features), BF16)),
         in_specs=[vmem] * 5 + [anywhere],
         out_specs=(vmem, anywhere),
-        scratch_shapes=sent_scratch,
+        scratch_shapes=sent_scratch(slots // 2),
         compiler_params=SMALL,
         name="token_state",
     )(
         put,
-        near_pick,
+        first_pick,
         returned.reshape(device_count * look_cap, features),
         block_values,
         near_columns,
@@ -451,45 +476,60 @@
     split = shape((tok_rows // 2, features), BF16)
     far_sent, *grad_halves = pl.pallas_call(
         pick_kernel,
-        out_shape=(sent_shape, split, split),
+        out_shape=(pltpu.HBM((slots, features), BF16), split, split),
         in_specs=[vmem, vmem, vmem],
         out_specs=(anywhere, vmem, vmem),
-        scratch_shapes=sent_scratch,
+        scratch_shapes=sent_scratch(slots),
         compiler_params=SMALL,
         cost_estimate=pl.CostEstimate(
             flops=400_000_000_000, bytes_accessed=4 * slots * features, transcendentals=0
         ),
         name="far_slots",
     )(far_pick, mirrored(state), out_grad)
-    near_rows = swap(near_sent.reshape(half, 2 * PAIR, features), halves)
+    pair_rows = (half, PAIR, features)
+    near_rows = swap(near_sent.reshape(pair_rows), halves)
     far_sent = far_sent.reshape(half, 2 * PAIR, features)
     far_rows = swap(far_sent, halves)
+    later_sent = pl.pallas_call(
+        later_kernel,
+        out_shape=pltpu.HBM((slots // 2, features), BF16),
+        in_specs=[vmem, vmem, anywhere],
+        out_specs=vmem,
+        compiler_params=SMALL,
+        name="later_slots",
+    )(second_pick, state, in_hbm(far_sent)).reshape(pair_rows)
     other_grads = [mirrored(array) for array in grad_halves]
 
     weights = (w_gate, w_up, w_down)
-    near_out = expert_call("near_experts", near_rows, weights, after=(far_sent,))
-    near_out = ordered(in_hbm(near_out), other_grads[0])
-    far_out = expert_call("far_experts", far_rows, weights, after=(near_out,))
-    near_back = swap(near_out, halves)
-    far_back = swap(ordered(in_hbm(far_out), near_back, other_grads[1]), halves)
-
-    def mixed_rows(name, slot_of, columns, back, grads, kind):
+    sent_both = expert_call(
+        "near_first", 0, 2, near_rows, weights, front=(later_sent,), after=(far_sent,)
+    )
+    sent_both = ordered(in_hbm(sent_both), other_grads[0])
+    far_out = expert_call("far_experts", 0, 4, far_rows, weights, after=(sent_both,))
+    both = swap(sent_both, halves)
+    far_back = swap(ordered(in_hbm(far_out), in_hbm(both), other_grads[1]), halves)
+    near_out = expert_call("near_second", 2, 2, both, weights)
+
+    def mixed_rows(name, slot_of, columns, backs, grads, kind, after=()):
+        backs = [back.reshape(-1, features) for back in backs]
         return pl.pallas_call(
-            mix_kernel,
+            functools.partial(mix_kernel, len(backs), len(grads)),
             out_shape=(shape((tok_rows, features), kind), shape((2 * TOP, tok_rows), F32)),
-            in_specs=[vmem] * (3 + len(grads)),
+            in_specs=[vmem] * (2 + len(backs) + len(grads)) + [anywhere] * len(after),
             out_specs=(vmem, vmem),
             compiler_params=SMALL,
             name=name,
-        )(slot_of, columns, back.reshape(slots, features), *grads)
-
+        )(slot_of, columns, *backs, *grads, *after)
+
+    far_mixed, far_grads = mixed_rows(
+        "mix_far", far_of, far_columns, (far_back,), other_grads, BF16, after=(in_hbm(near_out),)
+    )
+    near_back = swap(ordered(in_hbm(near_out), far_mixed), halves)
     near_mixed, near_grads = mixed_rows(
-        "mix_near", near_of, near_columns, near_back, (out_grad,), F32
-    )
-    far_mixed, far_grads = mixed_rows(
-        "mix_far", far_of, far_columns, far_back, other_grads, BF16
-    )
-    mixed = (near_mixed + mirrored(far_mixed).astype(F32)).astype(BF16)
+        "mix_near", near_of, near_columns, (both, near_back), (out_grad,), F32
+    )
+    arrived = ordered(mirrored(far_mixed), flops=400_000_000_000)
+    mixed = (near_mixed + arrived.astype(F32)).astype(BF16)
     grads = (near_grads + mirrored(far_grads))[:TOP]
     return mixed, grads.T
 

time: 204 us -> 201 us (0.985)
  blocking collectives: 24.5 us -> 0 us
  starting transfers between devices: 33.6 us -> 40.2 us
  Pallas kernels: 62.5 us -> 68.8 us
  waiting for transfers between devices: 80.5 us -> 86.8 us
    all_to_all x1 -> x0, blocking collectives: 24.5 us -> none  [swap(): lax.all_to_all(array, 'expert', split_axis=0, concat_axis=0, tiled=True,...]
    all_to_all x5 -> x7, starting transfers between devices: 24.3 us -> 31.5 us  [swap(): lax.all_to_all(array, 'expert', split_axis=0, concat_axis=0, tiled=True,...]
    pallas_call x5 -> x7, Pallas kernels: 54.1 us -> 60.8 us  [the longest x3 53.6 us: expert_call(): pl.pallas_call(functools.partial(expert_kernel, first, count, bool(front)...]
    ppermute x7, waiting for transfers between devices: 64.4 us -> 68.4 us  [mirrored(): return lax.ppermute(array, 'expert', pairs)]
    all_to_all x5 -> x7, waiting for transfers between devices: 16 us -> 18.4 us  [swap(): lax.all_to_all(array, 'expert', split_axis=0, concat_axis=0, tiled=True,...]
  transfers between devices with their start and end apart: 12 -> 14, of which waited for: 5 -> 9; matrix products, arithmetic and copies ran while one was open for 0% -> 0% of each run, Pallas kernels for 27% -> 30%
where the time goes in v14:
time: 201 us; the launch traced here: 200 us
  waiting for transfers between devices  86.8 us (43%)
  Pallas kernels  68.8 us (34%)
  starting transfers between devices  40.2 us (20%)
    ppermute x7, waiting for transfers between devices, mirrored(): return lax.ppermute(array, 'expert', pairs)  68.4 us
    pallas_call x3, Pallas kernels, expert_call(): pl.pallas_call(functools.partial(expert_kernel, first, count, bool(front)...  53.6 us
    all_to_all x7, starting transfers between devices, swap(): lax.all_to_all(array, 'expert', split_axis=0, concat_axis=0, tiled=True,...  31.5 us
    all_to_all x7, waiting for transfers between devices, swap(): lax.all_to_all(array, 'expert', split_axis=0, concat_axis=0, tiled=True,...  18.4 us
    ppermute x7, starting transfers between devices, mirrored(): return lax.ppermute(array, 'expert', pairs)  8.65 us
    pallas_call x2, Pallas kernels, mixed_rows(): pl.pallas_call(functools.partial(mix_kernel, len(backs), len(grads)), out...  4.5 us
  transfers between devices with their start and end apart: 14, of which 9 were waited for; matrix products, arithmetic and copies ran while one was open for 0% of the time, Pallas kernels for 30%

profile of v14, /device:TPU:0, one launch (start us, length us, event | category | flops | bytes accessed | tf_op | source)
XLA Modules:
  0.0 200.2 jit_solution(15062318490520557252)
XLA Ops:
  0.6 1.3 repeat_rows.1
  1.9 7.4 %all-to-all-start = ((s32[16,1,128]{2,1,0:T(1,128)}), s32[16,1,128]{2,1,0:T(1,128)S(1)}, u32[]{:S(2)}, u32[]{:S(2)}) async-start(s32[16,1,128]{2,1,0:T(1,128)} %repeat_rows.1), calls=%async_computation | async-start | bytes 16384 | tf_op jit(solution)/shard_map/all_to_all | solution.py:355
  9.3 0.1 pad_add_fusion.me_ref
  9.4 6.3 %all-to-all-done.rows_ref = s32[16,1,128]{2,1,0:T(1,128)S(1)} async-done(((s32[16,1,128]{2,1,0:T(1,128)}), s32[16,1,128]{2,1,0:T(1,128)S(1)}, u32[]{:S(2)}, u32[]{:S(2)}) %all-to-all-start) | async-done | bytes 8224 | tf_op jit(solution)/shard_map/all_to_all | solution.py:355
  15.6 3.2 %fetch_rows.1._ = bf16[256,2048]{1,0:T(8,128)(2,1)} custom-call(s32[2]{0:T(128)S(1)} %pad_add_fusion.me_ref, s32[16,1,128]{2,1,0:T(1,128)S(1)} %all-to-all-done.rows_ref, bf16[256,2048]{1,0:T(8,128)(2,1)} %table_hbm.1), custom_call_target="tpu_custom_call" | custom-call | tf_op jit(solution)/shard_map/fetch_rows/pallas_call | solution.py:411
  18.8 0.0 copy-start.10
  18.8 0.0 copy-start.7
  18.8 0.0 copy-start.8
  18.9 0.0 copy-start.9
  18.9 0.0 copy-start.2
  18.9 3.8 %all-to-all-start.1 = ((bf16[16,16,2048]{2,1,0:T(8,128)(2,1)}), bf16[16,16,2048]{2,1,0:T(8,128)(2,1)S(1)}, u32[]{:S(2)}, u32[]{:S(2)}) async-start(bf16[16,16,2048]{2,1,0:T(8,128)(2,1)} %bitcast.5), calls=%async_computation.1 | async-start | bytes 2097152 | tf_op jit(solution)/shard_map/all_to_all | solution.py:355
  22.7 0.9 near_plan.1
  23.6 0.0 copy-start.5
  23.6 2.8 %collective-permute-start = (s32[4,128]{1,0:T(4,128)S(1)}, s32[4,128]{1,0:T(4,128)S(1)}, u32[]{:S(2)}, u32[]{:S(2)}) collective-permute-start(s32[4,128]{1,0:T(4,128)S(1)} %get-tuple-element.25), channel_id=1, source_target_pairs={{0,8},{1,9},{2,10},{3,11},{4,12},{5,13},{6,14},{7,15},{8,0},{9,1},... | collective-permute-start | bytes 6152 | tf_op jit(solution)/shard_map/ppermute | solution.py:390
  26.4 0.2 collective-permute-start.1
  26.6 22.7 %collective-permute-done.ids_ref = s32[4,128]{1,0:T(4,128)S(1)} collective-permute-done((s32[4,128]{1,0:T(4,128)S(1)}, s32[4,128]{1,0:T(4,128)S(1)}, u32[]{:S(2)}, u32[]{:S(2)}) %collective-permute-start) | collective-permute-done | bytes 2080 | tf_op jit(solution)/shard_map/ppermute | solution.py:390
  49.3 0.0 collective-permute-done.1.weights_ref
  49.3 0.8 far_plan.1
  50.2 0.0 copy-start.3
  50.2 1.9 token_state.1
  52.1 0.6 collective-permute-start.2
  52.7 4.2 %all-to-all-start.2 = ((bf16[8,24,2048]{2,1,0:T(8,128)(2,1)}), bf16[8,24,2048]{2,1,0:T(8,128)(2,1)}, u32[]{:S(2)}, u32[]{:S(2)}) async-start(bf16[8,24,2048]{2,1,0:T(8,128)(2,1)} %bitcast.27), calls=%async_computation.2 | async-start | bytes 1572864 | tf_op jit(solution)/shard_map/all_to_all | solution.py:355
  56.9 20.2 %collective-permute-done.2.state_ref = bf16[128,2048]{1,0:T(8,128)(2,1)S(1)} collective-permute-done((bf16[128,2048]{1,0:T(8,128)(2,1)S(1)}, bf16[128,2048]{1,0:T(8,128)(2,1)S(1)}, u32[]{:S(2)}, u32[]{:S(2)}) %collective-permute-start.2) | collective-permute-done | bytes 524320 | tf_op jit(solution)/shard_map/ppermute | solution.py:390
  77.1 1.5 far_slots.1
  78.6 1.1 all-to-all-done.2.rows_ref
  79.7 4.3 %all-to-all-start.4 = ((bf16[8,48,2048]{2,1,0:T(8,128)(2,1)}), bf16[8,48,2048]{2,1,0:T(8,128)(2,1)}, u32[]{:S(2)}, u32[]{:S(2)}) async-start(bf16[8,48,2048]{2,1,0:T(8,128)(2,1)} %bitcast.23), calls=%async_computation.4 | async-start | bytes 3145728 | tf_op jit(solution)/shard_map/all_to_all | solution.py:355
  84.0 1.2 later_slots.1
  85.2 0.8 collective-permute-start.3
  86.0 14.5 %near_first.1.refs_0_ = bf16[8,48,2048]{2,1,0:T(8,128)(2,1)} custom-call(bf16[8,24,2048]{2,1,0:T(8,128)(2,1)} %all-to-all-done.2.rows_ref, bf16[8,24,2048]{2,1,0:T(8,128)(2,1)} %bitcast.26, bf16[8,48,2048]{2,1,0:T(8,128)(2,1)} %bitcast.25, bf16[4,2048,1408]{2,1,0:T(8,128)(2,1)} %refs_1_.3, bf16[4,2048,1408]{2,1,0:T(8,128)(2,1)} %refs_2_.6, ...), custom_call_target="tpu_custom_call" | custom-call | flops 6643777536 | bytes 34603008 | tf_op jit(solution)/shard_map/near_first/pallas_call | solution.py:293
  100.5 6.9 %collective-permute-done.3.refs_1_ = bf16[64,2048]{1,0:T(8,128)(2,1)S(1)} collective-permute-done((bf16[64,2048]{1,0:T(8,128)(2,1)S(1)}, bf16[64,2048]{1,0:T(8,128)(2,1)S(1)}, u32[]{:S(2)}, u32[]{:S(2)}) %collective-permute-start.3) | collective-permute-done | bytes 262176 | tf_op jit(solution)/shard_map/ppermute | solution.py:390
  107.5 2.2 %all-to-all-done.4.rows_ref = bf16[8,48,2048]{2,1,0:T(8,128)(2,1)} async-done(((bf16[8,48,2048]{2,1,0:T(8,128)(2,1)}), bf16[8,48,2048]{2,1,0:T(8,128)(2,1)}, u32[]{:S(2)}, u32[]{:S(2)}) %all-to-all-start.4) | async-done | bytes 1572896 | tf_op jit(solution)/shard_map/all_to_all | solution.py:355
  109.7 3.6 %all-to-all-start.3 = ((bf16[8,48,2048]{2,1,0:T(8,128)(2,1)}), bf16[8,48,2048]{2,1,0:T(8,128)(2,1)S(1)}, u32[]{:S(2)}, u32[]{:S(2)}) async-start(bf16[8,48,2048]{2,1,0:T(8,128)(2,1)} %ordered.4.refs_0_), calls=%async_computation.3 | async-start | bytes 3145728 | tf_op jit(solution)/shard_map/all_to_all | solution.py:355
  113.3 1.3 collective-permute-start.4
  114.5 24.9 %far_experts.1.refs_0_ = bf16[8,48,2048]{2,1,0:T(8,128)(2,1)} custom-call(bf16[8,48,2048]{2,1,0:T(8,128)(2,1)} %all-to-all-done.4.rows_ref, bf16[8,48,2048]{2,1,0:T(8,128)(2,1)} %ordered.4.refs_0_, bf16[4,2048,1408]{2,1,0:T(8,128)(2,1)} %refs_1_.3, bf16[4,2048,1408]{2,1,0:T(8,128)(2,1)} %refs_2_.6, bf16[4,1408,2048]{2,1,0:T(8,128)(2,1)} %refs_3_.3), custom_call_target="tpu_custom_call" | custom-call | flops 13287555072 | bytes 69206016 | tf_op jit(solution)/shard_map/far_experts/pallas_call | solution.py:293
  139.4 1.2 copy-done
  140.6 4.1 %all-to-all-start.5 = ((bf16[8,48,2048]{2,1,0:T(8,128)(2,1)}), bf16[8,48,2048]{2,1,0:T(8,128)(2,1)S(1)}, u32[]{:S(2)}, u32[]{:S(2)}) async-start(bf16[8,48,2048]{2,1,0:T(8,128)(2,1)} %ordered.5), calls=%async_computation.5 | async-start | bytes 3145728 | tf_op jit(solution)/shard_map/all_to_all | solution.py:355
  144.7 14.2 %near_second.1.refs_3_.refs_0_ = bf16[8,24,2048]{2,1,0:T(8,128)(2,1)} custom-call(bf16[8,48,2048]{2,1,0:T(8,128)(2,1)} %copy-done, bf16[4,2048,1408]{2,1,0:T(8,128)(2,1)} %refs_1_.3, bf16[4,2048,1408]{2,1,0:T(8,128)(2,1)} %refs_2_.6, bf16[4,1408,2048]{2,1,0:T(8,128)(2,1)} %refs_3_.3), custom_call_target="tpu_custom_call" | custom-call | flops 6643777536 | bytes 34603008 | tf_op jit(solution)/shard_map/near_second/pallas_call | solution.py:293
  158.9 5.9 %all-to-all-done.5 = bf16[8,48,2048]{2,1,0:T(8,128)(2,1)S(1)} async-done(((bf16[8,48,2048]{2,1,0:T(8,128)(2,1)}), bf16[8,48,2048]{2,1,0:T(8,128)(2,1)S(1)}, u32[]{:S(2)}, u32[]{:S(2)}) %all-to-all-start.5) | async-done | bytes 1572896 | tf_op jit(solution)/shard_map/all_to_all | solution.py:355
  164.8 1.6 mix_far.1
  166.4 1.7 collective-permute-start.5
  168.2 4.2 %all-to-all-start.6 = ((bf16[8,24,2048]{2,1,0:T(8,128)(2,1)}), bf16[8,24,2048]{2,1,0:T(8,128)(2,1)}, u32[]{:S(2)}, u32[]{:S(2)}) async-start(bf16[8,24,2048]{2,1,0:T(8,128)(2,1)} %ordered.6), calls=%async_computation.6 | async-start | bytes 1572864 | tf_op jit(solution)/shard_map/all_to_all | solution.py:355
  172.4 1.2 collective-permute-start.6
  173.6 18.6 %collective-permute-done.5.refs_0_ = bf16[128,2048]{1,0:T(8,128)(2,1)S(1)} collective-permute-done((bf16[128,2048]{1,0:T(8,128)(2,1)S(1)}, bf16[128,2048]{1,0:T(8,128)(2,1)S(1)}, u32[]{:S(2)}, u32[]{:S(2)}) %collective-permute-start.5) | collective-permute-done | bytes 524320 | tf_op jit(solution)/shard_map/ppermute | solution.py:390
  192.2 2.9 %all-to-all-done.6 = bf16[8,24,2048]{2,1,0:T(8,128)(2,1)} async-done(((bf16[8,24,2048]{2,1,0:T(8,128)(2,1)}), bf16[8,24,2048]{2,1,0:T(8,128)(2,1)}, u32[]{:S(2)}, u32[]{:S(2)}) %all-to-all-start.6) | async-done | bytes 786464 | tf_op jit(solution)/shard_map/all_to_all | solution.py:355
  195.1 2.9 %mix_near.1 = (f32[128,2048]{1,0:T(8,128)S(1)}, f32[8,128]{1,0:T(8,128)S(1)}) custom-call(s32[128,128]{1,0:T(8,128)S(1)} %get-tuple-element.21.slots_ref, f32[128,128]{1,0:T(8,128)S(1)} %copy-done.6, bf16[384,2048]{1,0:T(8,128)(2,1)S(1)} %bitcast.16, bf16[192,2048]{1,0:T(8,128)(2,1)} %bitcast.12.refs_1_, bf16[128,2048]{1,0:T(8,128)(2,1)S(1)} %copy-done.4), custom_call_target="tpu_custom_call" | custom-call | tf_op jit(solution)/shard_map/mix_near/pallas_call | solution.py:515
  198.0 0.7 add.7
  198.7 0.6 slice_bitcast_fusion
  199.3 0.9 add_convert_fusion
  (23 shorter events, 0.0 us)
Async XLA Ops:
  1.9 13.7 %all-to-all-start = ((s32[16,1,128]{2,1,0:T(1,128)}), s32[16,1,128]{2,1,0:T(1,128)S(1)}, u32[]{:S(2)}, u32[]{:S(2)}) async-start(s32[16,1,128]{2,1,0:T(1,128)} %repeat_rows.1), calls=%async_computation | async-start | bytes 16384 | tf_op jit(solution)/shard_map/all_to_all | solution.py:355
  18.8 3.9 %copy-start.10 = (s32[128,16]{0,1:T(8,128)S(1)}, s32[128,16]{0,1:T(8,128)}, u32[]{:S(2)}) copy-start(s32[128,16]{0,1:T(8,128)} %param.11) | copy-start | bytes 24580
  18.8 3.9 %copy-start.7 = (s32[128]{0:T(128)S(1)}, s32[128]{0:T(128)}, u32[]{:S(2)}) copy-start(s32[128]{0:T(128)} %param.12) | copy-start | bytes 1540
  18.8 3.9 %copy-start.8 = (s32[128,4]{0,1:T(4,128)S(1)}, s32[128,4]{0,1:T(4,128)}, u32[]{:S(2)}) copy-start(s32[128,4]{0,1:T(4,128)} %param.13) | copy-start | bytes 6148
  18.9 3.9 %copy-start.9 = (f32[128,4]{0,1:T(4,128)S(1)}, f32[128,4]{0,1:T(4,128)}, u32[]{:S(2)}) copy-start(f32[128,4]{0,1:T(4,128)} %param.14) | copy-start | bytes 6148
  18.9 31.3 %copy-start.2 = (bf16[128,2048]{1,0:T(8,128)(2,1)S(1)}, bf16[128,2048]{1,0:T(8,128)(2,1)}, u32[]{:S(2)}) copy-start(bf16[128,2048]{1,0:T(8,128)(2,1)} %values_ref.1) | copy-start | bytes 1572868
  18.9 31.3 %all-to-all-start.1 = ((bf16[16,16,2048]{2,1,0:T(8,128)(2,1)}), bf16[16,16,2048]{2,1,0:T(8,128)(2,1)S(1)}, u32[]{:S(2)}, u32[]{:S(2)}) async-start(bf16[16,16,2048]{2,1,0:T(8,128)(2,1)} %bitcast.5), calls=%async_computation.1 | async-start | bytes 2097152 | tf_op jit(solution)/shard_map/all_to_all | solution.py:355
  23.6 29.1 %copy-start.5 = (f32[128,128]{1,0:T(8,128)}, f32[128,128]{1,0:T(8,128)S(1)}, u32[]{:S(2)}) copy-start(f32[128,128]{1,0:T(8,128)S(1)} %get-tuple-element.22.columns_ref) | copy-start | bytes 196612
  23.6 25.7 %collective-permute-start = (s32[4,128]{1,0:T(4,128)S(1)}, s32[4,128]{1,0:T(4,128)S(1)}, u32[]{:S(2)}, u32[]{:S(2)}) collective-permute-start(s32[4,128]{1,0:T(4,128)S(1)} %get-tuple-element.25), channel_id=1, source_target_pairs={{0,8},{1,9},{2,10},{3,11},{4,12},{5,13},{6,14},{7,15},{8,0},{9,1},... | collective-permute-start | bytes 6152 | tf_op jit(solution)/shard_map/ppermute | solution.py:390
  26.4 22.9 %collective-permute-start.1 = (f32[4,128]{1,0:T(4,128)S(1)}, f32[4,128]{1,0:T(4,128)S(1)}, u32[]{:S(2)}, u32[]{:S(2)}) collective-permute-start(f32[4,128]{1,0:T(4,128)S(1)} %get-tuple-element.26), channel_id=1, source_target_pairs={{0,8},{1,9},{2,10},{3,11},{4,12},{5,13},{6,14},{7,15},{8,0},{9,1},... | collective-permute-start | bytes 6152 | tf_op jit(solution)/shard_map/ppermute | solution.py:390
  50.2 26.9 %copy-start.3 = (bf16[128,2048]{1,0:T(8,128)(2,1)S(1)}, bf16[128,2048]{1,0:T(8,128)(2,1)}, u32[]{:S(2)}) copy-start(bf16[128,2048]{1,0:T(8,128)(2,1)} %refs_2_.7) | copy-start | bytes 1572868
  52.1 25.0 %collective-permute-start.2 = (bf16[128,2048]{1,0:T(8,128)(2,1)S(1)}, bf16[128,2048]{1,0:T(8,128)(2,1)S(1)}, u32[]{:S(2)}, u32[]{:S(2)}) collective-permute-start(bf16[128,2048]{1,0:T(8,128)(2,1)S(1)} %get-tuple-element.30.state_ref), channel_id=1, source_target_pairs={{0,8},{1,9},{2,10},{3,11},{4,12},{5,13},{6,14},{7,15},{8,0},{9,1},... | collective-permute-start | bytes 1572872 | tf_op jit(solution)/shard_map/ppermute | solution.py:390
  52.7 27.0 %all-to-all-start.2 = ((bf16[8,24,2048]{2,1,0:T(8,128)(2,1)}), bf16[8,24,2048]{2,1,0:T(8,128)(2,1)}, u32[]{:S(2)}, u32[]{:S(2)}) async-start(bf16[8,24,2048]{2,1,0:T(8,128)(2,1)} %bitcast.27), calls=%async_computation.2 | async-start | bytes 1572864 | tf_op jit(solution)/shard_map/all_to_all | solution.py:355
  79.7 30.0 %all-to-all-start.4 = ((bf16[8,48,2048]{2,1,0:T(8,128)(2,1)}), bf16[8,48,2048]{2,1,0:T(8,128)(2,1)}, u32[]{:S(2)}, u32[]{:S(2)}) async-start(bf16[8,48,2048]{2,1,0:T(8,128)(2,1)} %bitcast.23), calls=%async_computation.4 | async-start | bytes 3145728 | tf_op jit(solution)/shard_map/all_to_all | solution.py:355
  85.2 22.2 %collective-permute-start.3 = (bf16[64,2048]{1,0:T(8,128)(2,1)S(1)}, bf16[64,2048]{1,0:T(8,128)(2,1)S(1)}, u32[]{:S(2)}, u32[]{:S(2)}) collective-permute-start(bf16[64,2048]{1,0:T(8,128)(2,1)S(1)} %get-tuple-element.32), channel_id=1, source_target_pairs={{0,8},{1,9},{2,10},{3,11},{4,12},{5,13},{6,14},{7,15},{8,0},{9,1},... | collective-permute-start | bytes 786440 | tf_op jit(solution)/shard_map/ppermute | solution.py:390
  109.7 29.8 %all-to-all-start.3 = ((bf16[8,48,2048]{2,1,0:T(8,128)(2,1)}), bf16[8,48,2048]{2,1,0:T(8,128)(2,1)S(1)}, u32[]{:S(2)}, u32[]{:S(2)}) async-start(bf16[8,48,2048]{2,1,0:T(8,128)(2,1)} %ordered.4.refs_0_), calls=%async_computation.3 | async-start | bytes 3145728 | tf_op jit(solution)/shard_map/all_to_all | solution.py:355
  113.3 26.2 %collective-permute-start.4 = (bf16[64,2048]{1,0:T(8,128)(2,1)S(1)}, bf16[64,2048]{1,0:T(8,128)(2,1)S(1)}, u32[]{:S(2)}, u32[]{:S(2)}) collective-permute-start(bf16[64,2048]{1,0:T(8,128)(2,1)S(1)} %get-tuple-element.35), channel_id=1, source_target_pairs={{0,8},{1,9},{2,10},{3,11},{4,12},{5,13},{6,14},{7,15},{8,0},{9,1},... | collective-permute-start | bytes 786440 | tf_op jit(solution)/shard_map/ppermute | solution.py:390
  139.4 1.2 copy-start
  140.6 24.1 %all-to-all-start.5 = ((bf16[8,48,2048]{2,1,0:T(8,128)(2,1)}), bf16[8,48,2048]{2,1,0:T(8,128)(2,1)S(1)}, u32[]{:S(2)}, u32[]{:S(2)}) async-start(bf16[8,48,2048]{2,1,0:T(8,128)(2,1)} %ordered.5), calls=%async_computation.5 | async-start | bytes 3145728 | tf_op jit(solution)/shard_map/all_to_all | solution.py:355
  166.4 25.8 %collective-permute-start.5 = (bf16[128,2048]{1,0:T(8,128)(2,1)S(1)}, bf16[128,2048]{1,0:T(8,128)(2,1)S(1)}, u32[]{:S(2)}, u32[]{:S(2)}) collective-permute-start(bf16[128,2048]{1,0:T(8,128)(2,1)S(1)} %get-tuple-element.36.refs_1_), channel_id=1, source_target_pairs={{0,8},{1,9},{2,10},{3,11},{4,12},{5,13},{6,14},{7,15},{8,0},{9,1},... | collective-permute-start | bytes 1572872 | tf_op jit(solution)/shard_map/ppermute | solution.py:390
  168.2 27.0 %all-to-all-start.6 = ((bf16[8,24,2048]{2,1,0:T(8,128)(2,1)}), bf16[8,24,2048]{2,1,0:T(8,128)(2,1)}, u32[]{:S(2)}, u32[]{:S(2)}) async-start(bf16[8,24,2048]{2,1,0:T(8,128)(2,1)} %ordered.6), calls=%async_computation.6 | async-start | bytes 1572864 | tf_op jit(solution)/shard_map/all_to_all | solution.py:355
  172.4 25.6 %collective-permute-start.6 = (f32[8,128]{1,0:T(8,128)}, f32[8,128]{1,0:T(8,128)}, u32[]{:S(2)}, u32[]{:S(2)}) collective-permute-start(f32[8,128]{1,0:T(8,128)} %get-tuple-element.39), channel_id=1, source_target_pairs={{0,8},{1,9},{2,10},{3,11},{4,12},{5,13},{6,14},{7,15},{8,0},{9,1},... | collective-permute-start | bytes 12296 | tf_op jit(solution)/shard_map/ppermute | solution.py:390
  192.2 2.9 %copy-start.1 = (bf16[8,48,2048]{2,1,0:T(8,128)(2,1)S(1)}, bf16[8,48,2048]{2,1,0:T(8,128)(2,1)}, u32[]{:S(2)}) copy-start(bf16[8,48,2048]{2,1,0:T(8,128)(2,1)} %copy-done) | copy-start | bytes 4718596
  192.2 2.9 %copy-start.4 = (bf16[128,2048]{1,0:T(8,128)(2,1)S(1)}, bf16[128,2048]{1,0:T(8,128)(2,1)}, u32[]{:S(2)}) copy-start(bf16[128,2048]{1,0:T(8,128)(2,1)} %refs_2_.7) | copy-start | bytes 1572868
  192.2 2.9 %copy-start.6 = (f32[128,128]{1,0:T(8,128)S(1)}, f32[128,128]{1,0:T(8,128)}, u32[]{:S(2)}) copy-start(f32[128,128]{1,0:T(8,128)} %copy-done.5) | copy-start | bytes 196612

commit v15 on v14

--- a/solution.py
+++ b/solution.py
@@ -38,12 +38,15 @@
     return flags(iota((length, length), 0) < iota((length, length), 1))
 
 
-def repeat_kernel(rows_ref, out_ref):
+def repeat_kernel(rows_ref, grad_hbm, out_ref, upper_hbm, sem):
+    copy = pltpu.make_async_copy(grad_hbm.at[pl.ds(0, upper_hbm.shape[0])], upper_hbm, sem)
+    copy.start()
     for n in range(out_ref.shape[0]):
         out_ref[n] = rows_ref[...]
-
-
-def fetch_kernel(me_ref, rows_ref, table_hbm, out_ref, table_ref, sem):
+    copy.wait()
+
+
+def fetch_kernel(me_ref, rows_ref, table_hbm, _, out_ref, table_ref, sem):
     copy = pltpu.make_async_copy(table_hbm, table_ref, sem)
     copy.start()
     device_count, _, tok_rows = rows_ref.shape
@@ -177,7 +180,7 @@
 
 
 def pick_kernel(
-    pick_ref, state_ref, grad_ref, out_hbm, upper_grad_ref, lower_grad_ref, sent_ref, sem
+    pick_ref, state_ref, grad_ref, out_hbm, lower_grad_ref, sent_ref, sem
 ):
     tok_rows, features = state_ref.shape
     width = features // sem.shape[0]
@@ -189,7 +192,6 @@
             pltpu.make_async_copy(sent_ref.at[:, cols], out_hbm.at[:, cols], sem.at[n])
         )
         copies[-1].start()
-    upper_grad_ref[...] = grad_ref[: tok_rows // 2, :]
     lower_grad_ref[...] = grad_ref[tok_rows // 2 :, :]
     for copy in copies:
         copy.wait()
@@ -316,39 +318,38 @@
     )
 
 
-def mix_kernel(parts, grads, slots_ref, columns_ref, *refs):
+def mix_kernel(grads, added, start, slots_ref, columns_ref, back_ref, *refs):
     mixed_ref, grads_ref = refs[-2:]
-    back_refs, grad_refs = refs[:parts], refs[parts : parts + grads]
+    grad_refs, added_refs = refs[:grads], refs[grads : grads + 2 * added]
     tok_rows = slots_ref.shape[0]
-    features = back_refs[0].shape[1]
+    count, features = back_ref.shape
     grad = jnp.concatenate([ref[...] for ref in grad_refs], axis=0)
     place = iota((tok_rows, tok_rows), 1)
     wide = jnp.zeros((tok_rows, tok_rows), F32)
-    spread = []
-    start = 0
-    for ref in back_refs:
-        count = ref.shape[0]
-        column = iota((tok_rows, count), 1) + start
-        start += count
-        inner = lax.dot_general(
-            grad, ref[...], (((1,), (1,)), ((), ())), preferred_element_type=F32
-        )
-        total = jnp.zeros((tok_rows, count), F32)
-        for k in range(TOP):
-            here = column == slots_ref[:, k : k + 1]
-            total = total + jnp.where(here, columns_ref[:, k : k + 1], 0.0)
-            value = jnp.sum(jnp.where(here, inner, 0.0), axis=1, keepdims=True)
-            wide = wide + jnp.where(place == k, value, 0.0)
-        high = total.astype(BF16)
-        spread.append((high, (total - high.astype(F32)).astype(BF16)))
+    column = iota((tok_rows, count), 1) + start
+    inner = lax.dot_general(
+        grad, back_ref[...], (((1,), (1,)), ((), ())), preferred_element_type=F32
+    )
+    total = jnp.zeros((tok_rows, count), F32)
+    for k in range(TOP):
+        here = column == slots_ref[:, k : k + 1]
+        total = total + jnp.where(here, columns_ref[:, k : k + 1], 0.0)
+        value = jnp.sum(jnp.where(here, inner, 0.0), axis=1, keepdims=True)
+        wide = wide + jnp.where(place == k, value, 0.0)
+    high = total.astype(BF16)
+    rest = (total - high.astype(F32)).astype(BF16)
     width = 512
     for at in range(0, features, width):
         cols = slice(at, at + width)
-        value = jnp.zeros((tok_rows, width), F32)
-        for (high, rest), ref in zip(spread, back_refs):
-            value = value + dot(high, ref[:, cols]) + dot(rest, ref[:, cols])
+        value = dot(high, back_ref[:, cols]) + dot(rest, back_ref[:, cols])
+        for ref in added_refs[::2]:
+            value = value + ref[:, cols].astype(F32)
         mixed_ref[:, cols] = value.astype(mixed_ref.dtype)
-    grads_ref[...] = wide.T[: grads_ref.shape[0], :]
+    lines = grads_ref.shape[0]
+    sums = wide.T[:lines, :]
+    for ref in added_refs[1::2]:
+        sums = sums + ref[:lines, :]
+    grads_ref[...] = sums
 
 
 def swap(array, groups=None):
@@ -401,22 +402,28 @@
             name="ordered",
         )(array, *earlier_arrays)
 
-    all_rows = pl.pallas_call(
+    upper = tok_rows // 2
+    all_rows, upper_grad = pl.pallas_call(
         repeat_kernel,
-        out_shape=shape((device_count, 1, tok_rows), jnp.int32),
-        in_specs=[vmem],
-        out_specs=vmem,
+        out_shape=(
+            shape((device_count, 1, tok_rows), jnp.int32),
+            pltpu.HBM((upper, features), BF16),
+        ),
+        in_specs=[vmem, anywhere],
+        out_specs=(vmem, anywhere),
+        scratch_shapes=[pltpu.SemaphoreType.DMA],
         name="repeat_rows",
-    )(row_ids[None, :])
+    )(row_ids[None, :], in_hbm(out_grad))
+    other_upper = mirrored(upper_grad)
     fetched = pl.pallas_call(
         fetch_kernel,
         out_shape=shape((device_count * look_cap, features), BF16),
-        in_specs=[smem, vmem, pl.BlockSpec(memory_space=pltpu.HBM)],
+        in_specs=[smem, vmem, pl.BlockSpec(memory_space=pltpu.HBM), anywhere],
         out_specs=vmem,
         scratch_shapes=[VMEM(table.shape, BF16), pltpu.SemaphoreType.DMA],
         compiler_params=SMALL,
         name="fetch_rows",
-    )(place, swap(all_rows), in_hbm(table))
+    )(place, swap(all_rows), in_hbm(table), in_hbm(other_upper))
     returned = swap(fetched.reshape(device_count, look_cap, features))
     turned_ids, turned_weights = expert_ids.T, gate_weights.T
     pick_shape = shape((slots, tok_rows), BF16)
@@ -473,12 +480,14 @@
         near_columns,
         far_pick,
     )
-    split = shape((tok_rows // 2, features), BF16)
-    far_sent, *grad_halves = pl.pallas_call(
+    far_sent, lower_grad = pl.pallas_call(
         pick_kernel,
-        out_shape=(pltpu.HBM((slots, features), BF16), split, split),
+        out_shape=(
+            pltpu.HBM((slots, features), BF16),
+            shape((tok_rows - upper, features), BF16),
+        ),
         in_specs=[vmem, vmem, vmem],
-        out_specs=(anywhere, vmem, vmem),
+        out_specs=(anywhere, vmem),
         scratch_shapes=sent_scratch(slots),
         compiler_params=SMALL,
         cost_estimate=pl.CostEstimate(
@@ -498,39 +507,48 @@
         compiler_params=SMALL,
         name="later_slots",
     )(second_pick, state, in_hbm(far_sent)).reshape(pair_rows)
-    other_grads = [mirrored(array) for array in grad_halves]
+    other_grads = (in_hbm(other_upper), mirrored(lower_grad))
 
     weights = (w_gate, w_up, w_down)
     sent_both = expert_call(
         "near_first", 0, 2, near_rows, weights, front=(later_sent,), after=(far_sent,)
     )
-    sent_both = ordered(in_hbm(sent_both), other_grads[0])
     far_out = expert_call("far_experts", 0, 4, far_rows, weights, after=(sent_both,))
     both = swap(sent_both, halves)
     far_back = swap(ordered(in_hbm(far_out), in_hbm(both), other_grads[1]), halves)
     near_out = expert_call("near_second", 2, 2, both, weights)
 
-    def mixed_rows(name, slot_of, columns, backs, grads, kind, after=()):
-        backs = [back.reshape(-1, features) for back in backs]
+    def mixed_rows(
+        name, slot_of, columns, back, grads, kind, start=0, lines=2 * TOP, added=(), after=()
+    ):
         return pl.pallas_call(
-            functools.partial(mix_kernel, len(backs), len(grads)),
-            out_shape=(shape((tok_rows, features), kind), shape((2 * TOP, tok_rows), F32)),
-            in_specs=[vmem] * (2 + len(backs) + len(grads)) + [anywhere] * len(after),
+            functools.partial(mix_kernel, len(grads), len(added) // 2, start),
+            out_shape=(shape((tok_rows, features), kind), shape((lines, tok_rows), F32)),
+            in_specs=[vmem] * (3 + len(grads) + len(added)) + [anywhere] * len(after),
             out_specs=(vmem, vmem),
             compiler_params=SMALL,
             name=name,
-        )(slot_of, columns, *backs, *grads, *after)
+        )(slot_of, columns, back.reshape(-1, features), *grads, *added, *after)
 
     far_mixed, far_grads = mixed_rows(
-        "mix_far", far_of, far_columns, (far_back,), other_grads, BF16, after=(in_hbm(near_out),)
+        "mix_far", far_of, far_columns, far_back, other_grads, BF16, after=(in_hbm(near_out),)
     )
     near_back = swap(ordered(in_hbm(near_out), far_mixed), halves)
-    near_mixed, near_grads = mixed_rows(
-        "mix_near", near_of, near_columns, (both, near_back), (out_grad,), F32
-    )
-    arrived = ordered(mirrored(far_mixed), flops=400_000_000_000)
-    mixed = (near_mixed + arrived.astype(F32)).astype(BF16)
-    grads = (near_grads + mirrored(far_grads))[:TOP]
+    near_sums = mixed_rows(
+        "mix_first", near_of, near_columns, in_hbm(both.reshape(slots, features)), (out_grad,), F32
+    )
+    far_sums = (ordered(mirrored(far_mixed), flops=400_000_000_000), mirrored(far_grads))
+    mixed, grads = mixed_rows(
+        "mix_second",
+        near_of,
+        near_columns,
+        near_back,
+        (out_grad,),
+        BF16,
+        start=slots,
+        lines=TOP,
+        added=(*near_sums, *far_sums),
+    )
     return mixed, grads.T
 
 

time: 201 us -> 211 us (1.050)
  Pallas kernels: 68.8 us -> 81.5 us
    pallas_call x3 -> x4, Pallas kernels: 5.76 us -> 18.3 us  [the longest x1 10.3 us: near_path(): pl.pallas_call(repeat_kernel, out_shape=(shape((device_count, 1, tok_rows...]
    ppermute x7, waiting for transfers between devices: 68.4 us -> 59.1 us  [mirrored(): return lax.ppermute(array, 'expert', pairs)]
    all_to_all x7, waiting for transfers between devices: 18.4 us -> 26.3 us  [swap(): lax.all_to_all(array, 'expert', split_axis=0, concat_axis=0, tiled=True,...]
    ppermute x7, starting transfers between devices: 8.65 us -> 11.7 us  [mirrored(): return lax.ppermute(array, 'expert', pairs)]
  transfers between devices with their start and end apart: 14 -> 14, of which waited for: 9 -> 9; matrix products, arithmetic and copies ran while one was open for 0% -> 0% of each run, Pallas kernels for 30% -> 29%
where the time goes in v15:
time: 211 us; the launch traced here: 210 us
  waiting for transfers between devices  85.4 us (40%)
  Pallas kernels  81.5 us (39%)
  starting transfers between devices  41.7 us (20%)
    ppermute x7, waiting for transfers between devices, mirrored(): return lax.ppermute(array, 'expert', pairs)  59.1 us
    pallas_call x3, Pallas kernels, expert_call(): pl.pallas_call(functools.partial(expert_kernel, first, count, bool(front)...  53.7 us
    all_to_all x7, starting transfers between devices, swap(): lax.all_to_all(array, 'expert', split_axis=0, concat_axis=0, tiled=True,...  30.1 us
    all_to_all x7, waiting for transfers between devices, swap(): lax.all_to_all(array, 'expert', split_axis=0, concat_axis=0, tiled=True,...  26.3 us
    ppermute x7, starting transfers between devices, mirrored(): return lax.ppermute(array, 'expert', pairs)  11.7 us
    pallas_call x1, Pallas kernels, near_path(): pl.pallas_call(repeat_kernel, out_shape=(shape((device_count, 1, tok_rows...  10.3 us
    pallas_call x3, Pallas kernels, mixed_rows(): pl.pallas_call(functools.partial(mix_kernel, len(grads), len(added) // 2,...  8.05 us
  transfers between devices with their start and end apart: 14, of which 9 were waited for; matrix products, arithmetic and copies ran while one was open for 0% of the time, Pallas kernels for 29%

profile of v15, /device:TPU:0, one launch (start us, length us, event | category | flops | bytes accessed | tf_op | source)
XLA Modules:
  0.0 210.3 jit_solution(9212008348629078501)
XLA Ops:
  0.6 10.3 %repeat_rows.1 = (s32[16,1,128]{2,1,0:T(1,128)}, bf16[64,2048]{1,0:T(8,128)(2,1)}) custom-call(s32[1,128]{1,0:T(1,128)} %bitcast.17, bf16[128,2048]{1,0:T(8,128)(2,1)} %refs_0_.5), custom_call_target="tpu_custom_call" | custom-call | tf_op jit(solution)/shard_map/repeat_rows/pallas_call | solution.py:406
  10.9 4.1 %collective-permute-start = (bf16[64,2048]{1,0:T(8,128)(2,1)}, bf16[64,2048]{1,0:T(8,128)(2,1)S(1)}, u32[]{:S(2)}, u32[]{:S(2)}) collective-permute-start(bf16[64,2048]{1,0:T(8,128)(2,1)} %get-tuple-element.25), channel_id=1, source_target_pairs={{0,8},{1,9},{2,10},{3,11},{4,12},{5,13},{6,14},{7,15},{8,0},{9,1},... | collective-permute-start | bytes 786440 | tf_op jit(solution)/shard_map/ppermute | solution.py:391
  15.0 3.9 %all-to-all-start = ((s32[16,1,128]{2,1,0:T(1,128)}), s32[16,1,128]{2,1,0:T(1,128)S(1)}, u32[]{:S(2)}, u32[]{:S(2)}) async-start(s32[16,1,128]{2,1,0:T(1,128)} %get-tuple-element.24), calls=%async_computation | async-start | bytes 16384 | tf_op jit(solution)/shard_map/all_to_all | solution.py:356
  19.0 0.1 pad_add_fusion.me_ref
  19.0 9.2 %all-to-all-done.rows_ref = s32[16,1,128]{2,1,0:T(1,128)S(1)} async-done(((s32[16,1,128]{2,1,0:T(1,128)}), s32[16,1,128]{2,1,0:T(1,128)S(1)}, u32[]{:S(2)}, u32[]{:S(2)}) %all-to-all-start) | async-done | bytes 8224 | tf_op jit(solution)/shard_map/all_to_all | solution.py:356
  28.3 0.0 collective-permute-done._.refs_0_
  28.3 0.7 copy-done.7
  29.0 3.2 %fetch_rows.1._ = bf16[256,2048]{1,0:T(8,128)(2,1)} custom-call(s32[2]{0:T(128)S(1)} %pad_add_fusion.me_ref, s32[16,1,128]{2,1,0:T(1,128)S(1)} %all-to-all-done.rows_ref, bf16[256,2048]{1,0:T(8,128)(2,1)} %table_hbm.1, bf16[64,2048]{1,0:T(8,128)(2,1)} %copy-done.7), custom_call_target="tpu_custom_call" | custom-call | tf_op jit(solution)/shard_map/fetch_rows/pallas_call | solution.py:418
  32.2 0.0 copy-start.8
  32.2 0.0 copy-start.4
  32.2 0.0 copy-start.5
  32.2 0.0 copy-start.6
  32.2 0.0 copy-start.3
  32.3 5.1 %all-to-all-start.1 = ((bf16[16,16,2048]{2,1,0:T(8,128)(2,1)}), bf16[16,16,2048]{2,1,0:T(8,128)(2,1)S(1)}, u32[]{:S(2)}, u32[]{:S(2)}) async-start(bf16[16,16,2048]{2,1,0:T(8,128)(2,1)} %bitcast.5), calls=%async_computation.1 | async-start | bytes 2097152 | tf_op jit(solution)/shard_map/all_to_all | solution.py:356
  37.4 0.9 near_plan.1
  38.3 2.9 %collective-permute-start.1 = (s32[4,128]{1,0:T(4,128)S(1)}, s32[4,128]{1,0:T(4,128)S(1)}, u32[]{:S(2)}, u32[]{:S(2)}) collective-permute-start(s32[4,128]{1,0:T(4,128)S(1)} %get-tuple-element.30), channel_id=1, source_target_pairs={{0,8},{1,9},{2,10},{3,11},{4,12},{5,13},{6,14},{7,15},{8,0},{9,1},... | collective-permute-start | bytes 6152 | tf_op jit(solution)/shard_map/ppermute | solution.py:391
  41.2 0.1 collective-permute-start.2
  41.3 22.8 %collective-permute-done.1.ids_ref = s32[4,128]{1,0:T(4,128)S(1)} collective-permute-done((s32[4,128]{1,0:T(4,128)S(1)}, s32[4,128]{1,0:T(4,128)S(1)}, u32[]{:S(2)}, u32[]{:S(2)}) %collective-permute-start.1) | collective-permute-done | bytes 2080 | tf_op jit(solution)/shard_map/ppermute | solution.py:391
  64.1 0.0 collective-permute-done.2.weights_ref
  64.1 0.8 far_plan.1
  64.9 0.0 all-to-all-done.1
  65.0 0.0 copy-start
  65.0 1.9 token_state.1
  66.8 0.6 collective-permute-start.3
  67.5 4.2 %all-to-all-start.2 = ((bf16[8,24,2048]{2,1,0:T(8,128)(2,1)}), bf16[8,24,2048]{2,1,0:T(8,128)(2,1)}, u32[]{:S(2)}, u32[]{:S(2)}) async-start(bf16[8,24,2048]{2,1,0:T(8,128)(2,1)} %bitcast.25), calls=%async_computation.2 | async-start | bytes 1572864 | tf_op jit(solution)/shard_map/all_to_all | solution.py:356
  71.7 20.2 %collective-permute-done.3.state_ref = bf16[128,2048]{1,0:T(8,128)(2,1)S(1)} collective-permute-done((bf16[128,2048]{1,0:T(8,128)(2,1)S(1)}, bf16[128,2048]{1,0:T(8,128)(2,1)S(1)}, u32[]{:S(2)}, u32[]{:S(2)}) %collective-permute-start.3) | collective-permute-done | bytes 524320 | tf_op jit(solution)/shard_map/ppermute | solution.py:391
  91.8 1.5 far_slots.1
  93.3 1.2 all-to-all-done.2.rows_ref
  94.5 4.3 %all-to-all-start.4 = ((bf16[8,48,2048]{2,1,0:T(8,128)(2,1)}), bf16[8,48,2048]{2,1,0:T(8,128)(2,1)}, u32[]{:S(2)}, u32[]{:S(2)}) async-start(bf16[8,48,2048]{2,1,0:T(8,128)(2,1)} %bitcast.21), calls=%async_computation.4 | async-start | bytes 3145728 | tf_op jit(solution)/shard_map/all_to_all | solution.py:356
  98.8 1.3 later_slots.1
  100.0 14.5 %near_first.1.refs_0_ = bf16[8,48,2048]{2,1,0:T(8,128)(2,1)} custom-call(bf16[8,24,2048]{2,1,0:T(8,128)(2,1)} %all-to-all-done.2.rows_ref, bf16[8,24,2048]{2,1,0:T(8,128)(2,1)} %bitcast.24, bf16[8,48,2048]{2,1,0:T(8,128)(2,1)} %bitcast.23, bf16[4,2048,1408]{2,1,0:T(8,128)(2,1)} %refs_1_.3, bf16[4,2048,1408]{2,1,0:T(8,128)(2,1)} %refs_2_.5, ...), custom_call_target="tpu_custom_call" | custom-call | flops 6643777536 | bytes 34603008 | tf_op jit(solution)/shard_map/near_first/pallas_call | solution.py:295
  114.5 4.3 %all-to-all-done.4.rows_ref = bf16[8,48,2048]{2,1,0:T(8,128)(2,1)} async-done(((bf16[8,48,2048]{2,1,0:T(8,128)(2,1)}), bf16[8,48,2048]{2,1,0:T(8,128)(2,1)}, u32[]{:S(2)}, u32[]{:S(2)}) %all-to-all-start.4) | async-done | bytes 1572896 | tf_op jit(solution)/shard_map/all_to_all | solution.py:356
  118.8 4.3 %all-to-all-start.3 = ((bf16[8,48,2048]{2,1,0:T(8,128)(2,1)}), bf16[8,48,2048]{2,1,0:T(8,128)(2,1)}, u32[]{:S(2)}, u32[]{:S(2)}) async-start(bf16[8,48,2048]{2,1,0:T(8,128)(2,1)} %near_first.1.refs_0_), calls=%async_computation.3 | async-start | bytes 3145728 | tf_op jit(solution)/shard_map/all_to_all | solution.py:356
  123.1 1.0 collective-permute-start.4
  124.1 25.0 %far_experts.1.refs_0_ = bf16[8,48,2048]{2,1,0:T(8,128)(2,1)} custom-call(bf16[8,48,2048]{2,1,0:T(8,128)(2,1)} %all-to-all-done.4.rows_ref, bf16[8,48,2048]{2,1,0:T(8,128)(2,1)} %near_first.1.refs_0_, bf16[4,2048,1408]{2,1,0:T(8,128)(2,1)} %refs_1_.3, bf16[4,2048,1408]{2,1,0:T(8,128)(2,1)} %refs_2_.5, bf16[4,1408,2048]{2,1,0:T(8,128)(2,1)} %refs_3_.3), custom_call_target="tpu_custom_call" | custom-call | flops 13287555072 | bytes 69206016 | tf_op jit(solution)/shard_map/far_experts/pallas_call | solution.py:295
  149.1 0.0 all-to-all-done.3.rows_ref.refs_1_
  149.1 4.0 %all-to-all-start.5 = ((bf16[8,48,2048]{2,1,0:T(8,128)(2,1)}), bf16[8,48,2048]{2,1,0:T(8,128)(2,1)S(1)}, u32[]{:S(2)}, u32[]{:S(2)}) async-start(bf16[8,48,2048]{2,1,0:T(8,128)(2,1)} %ordered.3), calls=%async_computation.5 | async-start | bytes 3145728 | tf_op jit(solution)/shard_map/all_to_all | solution.py:356
  153.2 14.2 %near_second.1.refs_2_.refs_0_ = bf16[8,24,2048]{2,1,0:T(8,128)(2,1)} custom-call(bf16[8,48,2048]{2,1,0:T(8,128)(2,1)} %all-to-all-done.3.rows_ref.refs_1_, bf16[4,2048,1408]{2,1,0:T(8,128)(2,1)} %refs_1_.3, bf16[4,2048,1408]{2,1,0:T(8,128)(2,1)} %refs_2_.5, bf16[4,1408,2048]{2,1,0:T(8,128)(2,1)} %refs_3_.3), custom_call_target="tpu_custom_call" | custom-call | flops 6643777536 | bytes 34603008 | tf_op jit(solution)/shard_map/near_second/pallas_call | solution.py:295
  167.4 5.9 %all-to-all-done.5 = bf16[8,48,2048]{2,1,0:T(8,128)(2,1)S(1)} async-done(((bf16[8,48,2048]{2,1,0:T(8,128)(2,1)}), bf16[8,48,2048]{2,1,0:T(8,128)(2,1)S(1)}, u32[]{:S(2)}, u32[]{:S(2)}) %all-to-all-start.5) | async-done | bytes 1572896 | tf_op jit(solution)/shard_map/all_to_all | solution.py:356
  173.2 2.6 %mix_far.1 = (bf16[128,2048]{1,0:T(8,128)(2,1)S(1)}, f32[8,128]{1,0:T(8,128)}) custom-call(s32[128,128]{1,0:T(8,128)S(1)} %get-tuple-element.37.slots_ref, f32[128,128]{1,0:T(8,128)S(1)} %get-tuple-element.38.columns_ref, bf16[384,2048]{1,0:T(8,128)(2,1)S(1)} %bitcast.15, bf16[64,2048]{1,0:T(8,128)(2,1)} %copy-done.7, ...), custom_call_target="tpu_custom_call" | custom-call | tf_op jit(solution)/shard_map/mix_far/pallas_call | solution.py:524
  175.9 2.0 collective-permute-start.5
  177.9 2.6 %mix_first.1 = (f32[128,2048]{1,0:T(8,128)S(1)}, f32[8,128]{1,0:T(8,128)S(1)}) custom-call(s32[128,128]{1,0:T(8,128)S(1)} %get-tuple-element.26.slots_ref, f32[128,128]{1,0:T(8,128)S(1)} %copy-done.2, bf16[384,2048]{1,0:T(8,128)(2,1)} %bitcast.12.back_ref, bf16[128,2048]{1,0:T(8,128)(2,1)S(1)} %copy-done), custom_call_target="tpu_custom_call" | custom-call | tf_op jit(solution)/shard_map/mix_first/pallas_call | solution.py:524
  180.5 4.2 %all-to-all-start.6 = ((bf16[8,24,2048]{2,1,0:T(8,128)(2,1)}), bf16[8,24,2048]{2,1,0:T(8,128)(2,1)}, u32[]{:S(2)}, u32[]{:S(2)}) async-start(bf16[8,24,2048]{2,1,0:T(8,128)(2,1)} %ordered.4), calls=%async_computation.6 | async-start | bytes 1572864 | tf_op jit(solution)/shard_map/all_to_all | solution.py:356
  184.7 1.0 collective-permute-start.6
  185.7 15.9 %collective-permute-done.5.refs_0_ = bf16[128,2048]{1,0:T(8,128)(2,1)S(1)} collective-permute-done((bf16[128,2048]{1,0:T(8,128)(2,1)S(1)}, bf16[128,2048]{1,0:T(8,128)(2,1)S(1)}, u32[]{:S(2)}, u32[]{:S(2)}) %collective-permute-start.5) | collective-permute-done | bytes 524320 | tf_op jit(solution)/shard_map/ppermute | solution.py:391
  201.6 0.1 collective-permute-done.6.refs_4_
  201.8 5.7 %all-to-all-done.6 = bf16[8,24,2048]{2,1,0:T(8,128)(2,1)} async-done(((bf16[8,24,2048]{2,1,0:T(8,128)(2,1)}), bf16[8,24,2048]{2,1,0:T(8,128)(2,1)}, u32[]{:S(2)}, u32[]{:S(2)}) %all-to-all-start.6) | async-done | bytes 786464 | tf_op jit(solution)/shard_map/all_to_all | solution.py:356
  207.5 2.8 %mix_second.1 = (bf16[128,2048]{1,0:T(8,128)(2,1)}, f32[4,128]{1,0:T(4,128)}) custom-call(s32[128,128]{1,0:T(8,128)S(1)} %get-tuple-element.26.slots_ref, f32[128,128]{1,0:T(8,128)S(1)} %copy-done.2, bf16[192,2048]{1,0:T(8,128)(2,1)} %bitcast.11.back_ref, bf16[128,2048]{1,0:T(8,128)(2,1)S(1)} %copy-done, f32[128,2048]{1,0:T(8,128)S(1)} %get-tuple-element.41.refs_1_, ...), custom_call_target="tpu_custom_call" | custom-call | tf_op jit(solution)/shard_map/mix_second/pallas_call | solution.py:524
  (16 shorter events, 0.0 us)
Async XLA Ops:
  10.9 17.4 %collective-permute-start = (bf16[64,2048]{1,0:T(8,128)(2,1)}, bf16[64,2048]{1,0:T(8,128)(2,1)S(1)}, u32[]{:S(2)}, u32[]{:S(2)}) collective-permute-start(bf16[64,2048]{1,0:T(8,128)(2,1)} %get-tuple-element.25), channel_id=1, source_target_pairs={{0,8},{1,9},{2,10},{3,11},{4,12},{5,13},{6,14},{7,15},{8,0},{9,1},... | collective-permute-start | bytes 786440 | tf_op jit(solution)/shard_map/ppermute | solution.py:391
  15.0 13.2 %all-to-all-start = ((s32[16,1,128]{2,1,0:T(1,128)}), s32[16,1,128]{2,1,0:T(1,128)S(1)}, u32[]{:S(2)}, u32[]{:S(2)}) async-start(s32[16,1,128]{2,1,0:T(1,128)} %get-tuple-element.24), calls=%async_computation | async-start | bytes 16384 | tf_op jit(solution)/shard_map/all_to_all | solution.py:356
  28.3 0.7 copy-start.7
  32.2 5.2 %copy-start.8 = (s32[128,16]{0,1:T(8,128)S(1)}, s32[128,16]{0,1:T(8,128)}, u32[]{:S(2)}) copy-start(s32[128,16]{0,1:T(8,128)} %param.11) | copy-start | bytes 24580
  32.2 5.2 %copy-start.4 = (s32[128]{0:T(128)S(1)}, s32[128]{0:T(128)}, u32[]{:S(2)}) copy-start(s32[128]{0:T(128)} %param.12) | copy-start | bytes 1540
  32.2 5.2 %copy-start.5 = (s32[128,4]{0,1:T(4,128)S(1)}, s32[128,4]{0,1:T(4,128)}, u32[]{:S(2)}) copy-start(s32[128,4]{0,1:T(4,128)} %param.13) | copy-start | bytes 6148
  32.2 5.2 %copy-start.6 = (f32[128,4]{0,1:T(4,128)S(1)}, f32[128,4]{0,1:T(4,128)}, u32[]{:S(2)}) copy-start(f32[128,4]{0,1:T(4,128)} %param.14) | copy-start | bytes 6148
  32.2 32.7 %copy-start.3 = (bf16[128,2048]{1,0:T(8,128)(2,1)S(1)}, bf16[128,2048]{1,0:T(8,128)(2,1)}, u32[]{:S(2)}) copy-start(bf16[128,2048]{1,0:T(8,128)(2,1)} %values_ref.1) | copy-start | bytes 1572868
  32.3 32.7 %all-to-all-start.1 = ((bf16[16,16,2048]{2,1,0:T(8,128)(2,1)}), bf16[16,16,2048]{2,1,0:T(8,128)(2,1)S(1)}, u32[]{:S(2)}, u32[]{:S(2)}) async-start(bf16[16,16,2048]{2,1,0:T(8,128)(2,1)} %bitcast.5), calls=%async_computation.1 | async-start | bytes 2097152 | tf_op jit(solution)/shard_map/all_to_all | solution.py:356
  38.3 29.2 %copy-start.1 = (f32[128,128]{1,0:T(8,128)}, f32[128,128]{1,0:T(8,128)S(1)}, u32[]{:S(2)}) copy-start(f32[128,128]{1,0:T(8,128)S(1)} %get-tuple-element.27.columns_ref) | copy-start | bytes 196612
  38.3 25.8 %collective-permute-start.1 = (s32[4,128]{1,0:T(4,128)S(1)}, s32[4,128]{1,0:T(4,128)S(1)}, u32[]{:S(2)}, u32[]{:S(2)}) collective-permute-start(s32[4,128]{1,0:T(4,128)S(1)} %get-tuple-element.30), channel_id=1, source_target_pairs={{0,8},{1,9},{2,10},{3,11},{4,12},{5,13},{6,14},{7,15},{8,0},{9,1},... | collective-permute-start | bytes 6152 | tf_op jit(solution)/shard_map/ppermute | solution.py:391
  41.2 22.9 %collective-permute-start.2 = (f32[4,128]{1,0:T(4,128)S(1)}, f32[4,128]{1,0:T(4,128)S(1)}, u32[]{:S(2)}, u32[]{:S(2)}) collective-permute-start(f32[4,128]{1,0:T(4,128)S(1)} %get-tuple-element.31), channel_id=1, source_target_pairs={{0,8},{1,9},{2,10},{3,11},{4,12},{5,13},{6,14},{7,15},{8,0},{9,1},... | collective-permute-start | bytes 6152 | tf_op jit(solution)/shard_map/ppermute | solution.py:391
  65.0 26.9 %copy-start = (bf16[128,2048]{1,0:T(8,128)(2,1)S(1)}, bf16[128,2048]{1,0:T(8,128)(2,1)}, u32[]{:S(2)}) copy-start(bf16[128,2048]{1,0:T(8,128)(2,1)} %refs_0_.5) | copy-start | bytes 1572868
  66.8 25.0 %collective-permute-start.3 = (bf16[128,2048]{1,0:T(8,128)(2,1)S(1)}, bf16[128,2048]{1,0:T(8,128)(2,1)S(1)}, u32[]{:S(2)}, u32[]{:S(2)}) collective-permute-start(bf16[128,2048]{1,0:T(8,128)(2,1)S(1)} %get-tuple-element.35.state_ref), channel_id=1, source_target_pairs={{0,8},{1,9},{2,10},{3,11},{4,12},{5,13},{6,14},{7,15},{8,0},{9,1},... | collective-permute-start | bytes 1572872 | tf_op jit(solution)/shard_map/ppermute | solution.py:391
  67.5 27.0 %all-to-all-start.2 = ((bf16[8,24,2048]{2,1,0:T(8,128)(2,1)}), bf16[8,24,2048]{2,1,0:T(8,128)(2,1)}, u32[]{:S(2)}, u32[]{:S(2)}) async-start(bf16[8,24,2048]{2,1,0:T(8,128)(2,1)} %bitcast.25), calls=%async_computation.2 | async-start | bytes 1572864 | tf_op jit(solution)/shard_map/all_to_all | solution.py:356
  94.5 24.4 %all-to-all-start.4 = ((bf16[8,48,2048]{2,1,0:T(8,128)(2,1)}), bf16[8,48,2048]{2,1,0:T(8,128)(2,1)}, u32[]{:S(2)}, u32[]{:S(2)}) async-start(bf16[8,48,2048]{2,1,0:T(8,128)(2,1)} %bitcast.21), calls=%async_computation.4 | async-start | bytes 3145728 | tf_op jit(solution)/shard_map/all_to_all | solution.py:356
  118.8 30.3 %all-to-all-start.3 = ((bf16[8,48,2048]{2,1,0:T(8,128)(2,1)}), bf16[8,48,2048]{2,1,0:T(8,128)(2,1)}, u32[]{:S(2)}, u32[]{:S(2)}) async-start(bf16[8,48,2048]{2,1,0:T(8,128)(2,1)} %near_first.1.refs_0_), calls=%async_computation.3 | async-start | bytes 3145728 | tf_op jit(solution)/shard_map/all_to_all | solution.py:356
  123.1 26.0 %collective-permute-start.4 = (bf16[64,2048]{1,0:T(8,128)(2,1)S(1)}, bf16[64,2048]{1,0:T(8,128)(2,1)S(1)}, u32[]{:S(2)}, u32[]{:S(2)}) collective-permute-start(bf16[64,2048]{1,0:T(8,128)(2,1)S(1)} %get-tuple-element.39), channel_id=1, source_target_pairs={{0,8},{1,9},{2,10},{3,11},{4,12},{5,13},{6,14},{7,15},{8,0},{9,1},... | collective-permute-start | bytes 786440 | tf_op jit(solution)/shard_map/ppermute | solution.py:391
  149.1 24.1 %all-to-all-start.5 = ((bf16[8,48,2048]{2,1,0:T(8,128)(2,1)}), bf16[8,48,2048]{2,1,0:T(8,128)(2,1)S(1)}, u32[]{:S(2)}, u32[]{:S(2)}) async-start(bf16[8,48,2048]{2,1,0:T(8,128)(2,1)} %ordered.3), calls=%async_computation.5 | async-start | bytes 3145728 | tf_op jit(solution)/shard_map/all_to_all | solution.py:356
  167.4 10.5 %copy-start.2 = (f32[128,128]{1,0:T(8,128)S(1)}, f32[128,128]{1,0:T(8,128)}, u32[]{:S(2)}) copy-start(f32[128,128]{1,0:T(8,128)} %copy-done.1) | copy-start | bytes 196612
  175.9 25.8 %collective-permute-start.5 = (bf16[128,2048]{1,0:T(8,128)(2,1)S(1)}, bf16[128,2048]{1,0:T(8,128)(2,1)S(1)}, u32[]{:S(2)}, u32[]{:S(2)}) collective-permute-start(bf16[128,2048]{1,0:T(8,128)(2,1)S(1)} %get-tuple-element.40.refs_1_), channel_id=1, source_target_pairs={{0,8},{1,9},{2,10},{3,11},{4,12},{5,13},{6,14},{7,15},{8,0},{9,1},... | collective-permute-start | bytes 1572872 | tf_op jit(solution)/shard_map/ppermute | solution.py:391
  180.5 27.0 %all-to-all-start.6 = ((bf16[8,24,2048]{2,1,0:T(8,128)(2,1)}), bf16[8,24,2048]{2,1,0:T(8,128)(2,1)}, u32[]{:S(2)}, u32[]{:S(2)}) async-start(bf16[8,24,2048]{2,1,0:T(8,128)(2,1)} %ordered.4), calls=%async_computation.6 | async-start | bytes 1572864 | tf_op jit(solution)/shard_map/all_to_all | solution.py:356
  184.7 17.0 %collective-permute-start.6 = (f32[8,128]{1,0:T(8,128)}, f32[8,128]{1,0:T(8,128)}, u32[]{:S(2)}, u32[]{:S(2)}) collective-permute-start(f32[8,128]{1,0:T(8,128)} %get-tuple-element.43), channel_id=1, source_target_pairs={{0,8},{1,9},{2,10},{3,11},{4,12},{5,13},{6,14},{7,15},{8,0},{9,1},... | collective-permute-start | bytes 12296 | tf_op jit(solution)/shard_map/ppermute | solution.py:391

commit v16 on v15

--- a/solution.py
+++ b/solution.py
@@ -38,12 +38,10 @@
     return flags(iota((length, length), 0) < iota((length, length), 1))
 
 
-def repeat_kernel(rows_ref, grad_hbm, out_ref, upper_hbm, sem):
-    copy = pltpu.make_async_copy(grad_hbm.at[pl.ds(0, upper_hbm.shape[0])], upper_hbm, sem)
-    copy.start()
+def repeat_kernel(rows_ref, grad_ref, out_ref, upper_ref):
     for n in range(out_ref.shape[0]):
         out_ref[n] = rows_ref[...]
-    copy.wait()
+    upper_ref[...] = grad_ref[...]
 
 
 def fetch_kernel(me_ref, rows_ref, table_hbm, _, out_ref, table_ref, sem):
@@ -142,13 +140,23 @@
     columns_ref[...] = turned(jnp.concatenate([weights_ref[...], scales_ref[...]], axis=0))
 
 
-def far_plan_kernel(me_ref, ids_ref, weights_ref, pick_ref, slots_ref, columns_ref):
+def far_plan_kernel(me_ref, ids_ref, weights_ref, _, pick_ref, slots_ref, columns_ref):
     plan_slots(me_ref[0], ids_ref, (pick_ref,), slots_ref)
     columns_ref[...] = turned(weights_ref[...])
 
 
 def state_kernel(
-    put_ref, pick_ref, returned_ref, values_ref, columns_ref, _, state_ref, out_hbm, sent_ref, sem
+    put_ref,
+    pick_ref,
+    returned_ref,
+    values_ref,
+    columns_ref,
+    ids_ref,
+    weights_ref,
+    state_ref,
+    out_hbm,
+    sent_ref,
+    sem,
 ):
     features = values_ref.shape[1]
     width = features // sem.shape[0]
@@ -197,11 +205,13 @@
         copy.wait()
 
 
-def expert_kernel(first, count, join, after, rows_ref, *refs):
+def expert_kernel(first, count, join, after, rows_hbm, *refs):
     if join:
         front_ref, refs = refs[0], refs[1:]
     wg_hbm, wu_hbm, wd_hbm, out_ref = refs[after : after + 4]
-    x_ref, wg_ref, wu_ref, wd_ref, hidden_ref, result_ref, sem = refs[after + 4 :]
+    rows_ref, x_ref, wg_ref, wu_ref, wd_ref, hidden_ref, result_ref, sem, rows_sem = refs[
+        after + 4 :
+    ]
     held, features, width = wg_ref.shape
     half = rows_ref.shape[0]
     up_cuts = ((0, 512), (512, 512), (1024, width - 1024))
@@ -221,9 +231,14 @@
             for n, (src, dst) in enumerate(copies)
         ]
 
-    for j in range(held):
-        for copy in weight_copies(j, j):
-            copy.start()
+    rows_copy = pltpu.make_async_copy(rows_hbm, rows_ref, rows_sem)
+    rows_copy.start()
+    weights = weight_copies(0, 0) + weight_copies(1, 1)
+    for copy in weights[:4]:
+        copy.start()
+    rows_copy.wait()
+    for copy in weights[4:]:
+        copy.start()
 
     low = iota((PAIR, features), 0) < CAP
     for chunk in range(count // 2):
@@ -295,9 +310,10 @@
     return pl.pallas_call(
         functools.partial(expert_kernel, first, count, bool(front), len(after)),
         out_shape=pltpu.HBM((half, count * CAP + len(front) * PAIR, features), BF16),
-        in_specs=[vmem] * (1 + len(front)) + [anywhere] * len(after) + [hbm] * 3,
+        in_specs=[hbm] + [vmem] * len(front) + [anywhere] * len(after) + [hbm] * 3,
         out_specs=vmem,
         scratch_shapes=[
+            VMEM(rows_in.shape, BF16),
             VMEM((count, rows, features), BF16),
             VMEM((held, features, width), BF16),
             VMEM((held, features, width), BF16),
@@ -305,6 +321,7 @@
             VMEM((rows, width), BF16),
             VMEM((count, rows, features), F32),
             pltpu.SemaphoreType.DMA((held, 10)),
+            pltpu.SemaphoreType.DMA,
         ],
         compiler_params=pltpu.CompilerParams(vmem_limit_bytes=46 * 1024 * 1024),
         cost_estimate=pl.CostEstimate(
@@ -407,13 +424,19 @@
         repeat_kernel,
         out_shape=(
             shape((device_count, 1, tok_rows), jnp.int32),
-            pltpu.HBM((upper, features), BF16),
+            shape((upper, features), BF16),
         ),
-        in_specs=[vmem, anywhere],
-        out_specs=(vmem, anywhere),
-        scratch_shapes=[pltpu.SemaphoreType.DMA],
+        grid=(1,),
+        in_specs=[
+            pl.BlockSpec((1, tok_rows), lambda i: (0, 0)),
+            pl.BlockSpec((upper, features), lambda i: (0, 0)),
+        ],
+        out_specs=(
+            pl.BlockSpec((device_count, 1, tok_rows), lambda i: (0, 0, 0)),
+            pl.BlockSpec((upper, features), lambda i: (0, 0)),
+        ),
         name="repeat_rows",
-    )(row_ids[None, :], in_hbm(out_grad))
+    )(row_ids[None, :], out_grad)
     other_upper = mirrored(upper_grad)
     fetched = pl.pallas_call(
         fetch_kernel,
@@ -423,7 +446,7 @@
         scratch_shapes=[VMEM(table.shape, BF16), pltpu.SemaphoreType.DMA],
         compiler_params=SMALL,
         name="fetch_rows",
-    )(place, swap(all_rows), in_hbm(table), in_hbm(other_upper))
+    )(place, swap(all_rows), in_hbm(table), other_upper)
     returned = swap(fetched.reshape(device_count, look_cap, features))
     turned_ids, turned_weights = expert_ids.T, gate_weights.T
     pick_shape = shape((slots, tok_rows), BF16)
@@ -452,14 +475,7 @@
         jnp.exp2(block_exps.T.astype(F32)),
         fetched,
     )
-    far_pick, far_of, far_columns = pl.pallas_call(
-        far_plan_kernel,
-        out_shape=(pick_shape, shape(square, jnp.int32), shape(square, F32)),
-        in_specs=[smem, vmem, vmem],
-        out_specs=(vmem,) * 3,
-        compiler_params=SMALL,
-        name="far_plan",
-    )(place, mirrored(sent_ids), mirrored(sent_weights))
+    other_ids, other_weights = mirrored(sent_ids), mirrored(sent_weights)
 
     def sent_scratch(count):
         return [VMEM((count, features), BF16), pltpu.SemaphoreType.DMA((4,))]
@@ -467,7 +483,7 @@
     state, near_sent = pl.pallas_call(
         state_kernel,
         out_shape=(shape((tok_rows, features), BF16), pltpu.HBM((slots // 2, features), BF16)),
-        in_specs=[vmem] * 5 + [anywhere],
+        in_specs=[vmem] * 5 + [anywhere] * 2,
         out_specs=(vmem, anywhere),
         scratch_shapes=sent_scratch(slots // 2),
         compiler_params=SMALL,
@@ -478,8 +494,17 @@
         returned.reshape(device_count * look_cap, features),
         block_values,
         near_columns,
-        far_pick,
-    )
+        other_ids,
+        other_weights,
+    )
+    far_pick, far_of, far_columns = pl.pallas_call(
+        far_plan_kernel,
+        out_shape=(pick_shape, shape(square, jnp.int32), shape(square, F32)),
+        in_specs=[smem, vmem, vmem, anywhere],
+        out_specs=(vmem,) * 3,
+        compiler_params=SMALL,
+        name="far_plan",
+    )(place, other_ids, other_weights, state)
     far_sent, lower_grad = pl.pallas_call(
         pick_kernel,
         out_shape=(
@@ -507,7 +532,7 @@
         compiler_params=SMALL,
         name="later_slots",
     )(second_pick, state, in_hbm(far_sent)).reshape(pair_rows)
-    other_grads = (in_hbm(other_upper), mirrored(lower_grad))
+    other_grads = (other_upper, mirrored(lower_grad))
 
     weights = (w_gate, w_up, w_down)
     sent_both = expert_call(
@@ -534,10 +559,16 @@
         "mix_far", far_of, far_columns, far_back, other_grads, BF16, after=(in_hbm(near_out),)
     )
     near_back = swap(ordered(in_hbm(near_out), far_mixed), halves)
-    near_sums = mixed_rows(
-        "mix_first", near_of, near_columns, in_hbm(both.reshape(slots, features)), (out_grad,), F32
-    )
     far_sums = (ordered(mirrored(far_mixed), flops=400_000_000_000), mirrored(far_grads))
+    sums = mixed_rows(
+        "mix_first",
+        near_of,
+        near_columns,
+        in_hbm(both.reshape(slots, features)),
+        (out_grad,),
+        F32,
+        added=far_sums,
+    )
     mixed, grads = mixed_rows(
         "mix_second",
         near_of,
@@ -547,7 +578,7 @@
         BF16,
         start=slots,
         lines=TOP,
-        added=(*near_sums, *far_sums),
+        added=sums,
     )
     return mixed, grads.T
 

time: 211 us -> 197 us (0.934)
  Pallas kernels: 81.5 us -> 71.5 us
  waiting for transfers between devices: 85.4 us -> 81.5 us
    pallas_call x1, Pallas kernels: 10.3 us -> 1.69 us  [near_path(): pl.pallas_call(repeat_kernel, out_shape=(shape((device_count, 1, tok_rows...]
    all_to_all x7, waiting for transfers between devices: 26.3 us -> 20.9 us  [swap(): lax.all_to_all(array, 'expert', split_axis=0, concat_axis=0, tiled=True,...]
  transfers between devices with their start and end apart: 14 -> 14, of which waited for: 9 -> 10; matrix products, arithmetic and copies ran while one was open for 0% -> 0% of each run, Pallas kernels for 29% -> 31%
where the time goes in v16:
time: 197 us
  waiting for transfers between devices  81.5 us (41%)
  Pallas kernels  71.5 us (36%)
  starting transfers between devices  41.8 us (21%)
    ppermute x7, waiting for transfers between devices, mirrored(): return lax.ppermute(array, 'expert', pairs)  60.6 us
    pallas_call x3, Pallas kernels, expert_call(): pl.pallas_call(functools.partial(expert_kernel, first, count, bool(front)...  53.2 us
    all_to_all x7, starting transfers between devices, swap(): lax.all_to_all(array, 'expert', split_axis=0, concat_axis=0, tiled=True,...  29.2 us
    all_to_all x7, waiting for transfers between devices, swap(): lax.all_to_all(array, 'expert', split_axis=0, concat_axis=0, tiled=True,...  20.9 us
    ppermute x7, starting transfers between devices, mirrored(): return lax.ppermute(array, 'expert', pairs)  12.6 us
    pallas_call x3, Pallas kernels, mixed_rows(): pl.pallas_call(functools.partial(mix_kernel, len(grads), len(added) // 2,...  7.09 us
  transfers between devices with their start and end apart: 14, of which 10 were waited for; matrix products, arithmetic and copies ran while one was open for 0% of the time, Pallas kernels for 31%

profile of v16, /device:TPU:0, one launch (start us, length us, event | category | flops | bytes accessed | tf_op | source)
XLA Modules:
  0.0 196.7 jit_solution(16761845997715191646)
XLA Ops:
  0.6 1.7 repeat_rows.1
  2.3 4.0 %collective-permute-start = (bf16[64,2048]{1,0:T(8,128)(2,1)}, bf16[64,2048]{1,0:T(8,128)(2,1)S(1)}, u32[]{:S(2)}, u32[]{:S(2)}) collective-permute-start(bf16[64,2048]{1,0:T(8,128)(2,1)} %get-tuple-element.25), channel_id=1, source_target_pairs={{0,8},{1,9},{2,10},{3,11},{4,12},{5,13},{6,14},{7,15},{8,0},{9,1},... | collective-permute-start | bytes 786440 | tf_op jit(solution)/shard_map/ppermute | solution.py:408
  6.4 3.9 %all-to-all-start = ((s32[16,1,128]{2,1,0:T(1,128)}), s32[16,1,128]{2,1,0:T(1,128)S(1)}, u32[]{:S(2)}, u32[]{:S(2)}) async-start(s32[16,1,128]{2,1,0:T(1,128)} %get-tuple-element.24), calls=%async_computation | async-start | bytes 16384 | tf_op jit(solution)/shard_map/all_to_all | solution.py:373
  10.3 0.1 pad_add_fusion.me_ref
  10.4 9.2 %all-to-all-done.rows_ref = s32[16,1,128]{2,1,0:T(1,128)S(1)} async-done(((s32[16,1,128]{2,1,0:T(1,128)}), s32[16,1,128]{2,1,0:T(1,128)S(1)}, u32[]{:S(2)}, u32[]{:S(2)}) %all-to-all-start) | async-done | bytes 8224 | tf_op jit(solution)/shard_map/all_to_all | solution.py:373
  19.6 0.0 collective-permute-done._.refs_0_
  19.6 3.2 %fetch_rows.1._ = bf16[256,2048]{1,0:T(8,128)(2,1)} custom-call(s32[2]{0:T(128)S(1)} %pad_add_fusion.me_ref, s32[16,1,128]{2,1,0:T(1,128)S(1)} %all-to-all-done.rows_ref, bf16[256,2048]{1,0:T(8,128)(2,1)} %table_hbm.1, bf16[64,2048]{1,0:T(8,128)(2,1)S(1)} %collective-permute-done._.refs_0_), custom_call_target="tpu_custom_call" | custom-call | tf_op jit(solution)/shard_map/fetch_rows/pallas_call | solution.py:441
  22.8 0.0 copy-start.9
  22.8 0.0 copy-start.5
  22.8 0.0 copy-start.6
  22.9 0.0 copy-start.7
  22.9 0.0 copy-start.4
  22.9 5.1 %all-to-all-start.1 = ((bf16[16,16,2048]{2,1,0:T(8,128)(2,1)}), bf16[16,16,2048]{2,1,0:T(8,128)(2,1)S(1)}, u32[]{:S(2)}, u32[]{:S(2)}) async-start(bf16[16,16,2048]{2,1,0:T(8,128)(2,1)} %bitcast.5), calls=%async_computation.1 | async-start | bytes 2097152 | tf_op jit(solution)/shard_map/all_to_all | solution.py:373
  28.1 0.9 near_plan.1
  28.9 2.9 %collective-permute-start.1 = (s32[4,128]{1,0:T(4,128)S(1)}, s32[4,128]{1,0:T(4,128)S(1)}, u32[]{:S(2)}, u32[]{:S(2)}) collective-permute-start(s32[4,128]{1,0:T(4,128)S(1)} %get-tuple-element.30), channel_id=1, source_target_pairs={{0,8},{1,9},{2,10},{3,11},{4,12},{5,13},{6,14},{7,15},{8,0},{9,1},... | collective-permute-start | bytes 6152 | tf_op jit(solution)/shard_map/ppermute | solution.py:408
  31.8 0.1 collective-permute-start.2
  31.9 22.8 %collective-permute-done.1.ids_ref = s32[4,128]{1,0:T(4,128)S(1)} collective-permute-done((s32[4,128]{1,0:T(4,128)S(1)}, s32[4,128]{1,0:T(4,128)S(1)}, u32[]{:S(2)}, u32[]{:S(2)}) %collective-permute-start.1) | collective-permute-done | bytes 2080 | tf_op jit(solution)/shard_map/ppermute | solution.py:408
  54.7 0.0 collective-permute-done.2.weights_ref
  54.7 0.0 all-to-all-done.1
  54.7 1.9 token_state.1
  56.7 1.5 collective-permute-start.3
  58.1 4.2 %all-to-all-start.2 = ((bf16[8,24,2048]{2,1,0:T(8,128)(2,1)}), bf16[8,24,2048]{2,1,0:T(8,128)(2,1)}, u32[]{:S(2)}, u32[]{:S(2)}) async-start(bf16[8,24,2048]{2,1,0:T(8,128)(2,1)} %bitcast.25), calls=%async_computation.2 | async-start | bytes 1572864 | tf_op jit(solution)/shard_map/all_to_all | solution.py:373
  62.4 0.8 far_plan.1
  63.2 18.9 %collective-permute-done.3.state_ref = bf16[128,2048]{1,0:T(8,128)(2,1)S(1)} collective-permute-done((bf16[128,2048]{1,0:T(8,128)(2,1)S(1)}, bf16[128,2048]{1,0:T(8,128)(2,1)S(1)}, u32[]{:S(2)}, u32[]{:S(2)}) %collective-permute-start.3) | collective-permute-done | bytes 524320 | tf_op jit(solution)/shard_map/ppermute | solution.py:408
  82.1 1.5 far_slots.1
  83.6 1.1 all-to-all-done.2.rows_hbm
  84.8 3.6 %all-to-all-start.4 = ((bf16[8,48,2048]{2,1,0:T(8,128)(2,1)}), bf16[8,48,2048]{2,1,0:T(8,128)(2,1)S(1)}, u32[]{:S(2)}, u32[]{:S(2)}) async-start(bf16[8,48,2048]{2,1,0:T(8,128)(2,1)} %bitcast.21), calls=%async_computation.4 | async-start | bytes 3145728 | tf_op jit(solution)/shard_map/all_to_all | solution.py:373
  88.4 1.2 later_slots.1
  89.6 15.0 %near_first.1.refs_0_ = bf16[8,48,2048]{2,1,0:T(8,128)(2,1)} custom-call(bf16[8,24,2048]{2,1,0:T(8,128)(2,1)} %all-to-all-done.2.rows_hbm, bf16[8,24,2048]{2,1,0:T(8,128)(2,1)} %bitcast.24, bf16[8,48,2048]{2,1,0:T(8,128)(2,1)} %bitcast.23, bf16[4,2048,1408]{2,1,0:T(8,128)(2,1)} %refs_1_.3, bf16[4,2048,1408]{2,1,0:T(8,128)(2,1)} %refs_2_.5, ...), custom_call_target="tpu_custom_call" | custom-call | flops 6643777536 | bytes 34603008 | tf_op jit(solution)/shard_map/near_first/pallas_call | solution.py:310
  104.6 3.8 %all-to-all-done.4.rows_hbm = bf16[8,48,2048]{2,1,0:T(8,128)(2,1)S(1)} async-done(((bf16[8,48,2048]{2,1,0:T(8,128)(2,1)}), bf16[8,48,2048]{2,1,0:T(8,128)(2,1)S(1)}, u32[]{:S(2)}, u32[]{:S(2)}) %all-to-all-start.4) | async-done | bytes 1572896 | tf_op jit(solution)/shard_map/all_to_all | solution.py:373
  108.4 4.3 %all-to-all-start.3 = ((bf16[8,48,2048]{2,1,0:T(8,128)(2,1)}), bf16[8,48,2048]{2,1,0:T(8,128)(2,1)}, u32[]{:S(2)}, u32[]{:S(2)}) async-start(bf16[8,48,2048]{2,1,0:T(8,128)(2,1)} %near_first.1.refs_0_), calls=%async_computation.3 | async-start | bytes 3145728 | tf_op jit(solution)/shard_map/all_to_all | solution.py:373
  112.7 1.2 collective-permute-start.4
  113.8 24.4 %far_experts.1.refs_0_ = bf16[8,48,2048]{2,1,0:T(8,128)(2,1)} custom-call(bf16[8,48,2048]{2,1,0:T(8,128)(2,1)} %copy-done.8, bf16[8,48,2048]{2,1,0:T(8,128)(2,1)} %near_first.1.refs_0_, bf16[4,2048,1408]{2,1,0:T(8,128)(2,1)} %refs_1_.3, bf16[4,2048,1408]{2,1,0:T(8,128)(2,1)} %refs_2_.5, bf16[4,1408,2048]{2,1,0:T(8,128)(2,1)} %refs_3_.3), custom_call_target="tpu_custom_call" | custom-call | flops 13287555072 | bytes 69206016 | tf_op jit(solution)/shard_map/far_experts/pallas_call | solution.py:310
  138.2 0.0 collective-permute-done.4.refs_2_.refs_1_
  138.2 0.1 all-to-all-done.3.rows_hbm.refs_1_
  138.4 3.9 %all-to-all-start.5 = ((bf16[8,48,2048]{2,1,0:T(8,128)(2,1)}), bf16[8,48,2048]{2,1,0:T(8,128)(2,1)S(1)}, u32[]{:S(2)}, u32[]{:S(2)}) async-start(bf16[8,48,2048]{2,1,0:T(8,128)(2,1)} %ordered.3), calls=%async_computation.5 | async-start | bytes 3145728 | tf_op jit(solution)/shard_map/all_to_all | solution.py:373
  142.3 13.8 %near_second.1.refs_2_.refs_0_ = bf16[8,24,2048]{2,1,0:T(8,128)(2,1)} custom-call(bf16[8,48,2048]{2,1,0:T(8,128)(2,1)} %all-to-all-done.3.rows_hbm.refs_1_, bf16[4,2048,1408]{2,1,0:T(8,128)(2,1)} %refs_1_.3, bf16[4,2048,1408]{2,1,0:T(8,128)(2,1)} %refs_2_.5, bf16[4,1408,2048]{2,1,0:T(8,128)(2,1)} %refs_3_.3), custom_call_target="tpu_custom_call" | custom-call | flops 6643777536 | bytes 34603008 | tf_op jit(solution)/shard_map/near_second/pallas_call | solution.py:310
  156.1 6.2 %all-to-all-done.5 = bf16[8,48,2048]{2,1,0:T(8,128)(2,1)S(1)} async-done(((bf16[8,48,2048]{2,1,0:T(8,128)(2,1)}), bf16[8,48,2048]{2,1,0:T(8,128)(2,1)S(1)}, u32[]{:S(2)}, u32[]{:S(2)}) %all-to-all-start.5) | async-done | bytes 1572896 | tf_op jit(solution)/shard_map/all_to_all | solution.py:373
  162.4 1.6 mix_far.1
  164.0 1.8 collective-permute-start.5
  165.8 1.1 collective-permute-start.6
  166.9 4.2 %all-to-all-start.6 = ((bf16[8,24,2048]{2,1,0:T(8,128)(2,1)}), bf16[8,24,2048]{2,1,0:T(8,128)(2,1)}, u32[]{:S(2)}, u32[]{:S(2)}) async-start(bf16[8,24,2048]{2,1,0:T(8,128)(2,1)} %ordered.4), calls=%async_computation.6 | async-start | bytes 1572864 | tf_op jit(solution)/shard_map/all_to_all | solution.py:373
  171.1 18.7 %collective-permute-done.5.refs_0_ = bf16[128,2048]{1,0:T(8,128)(2,1)S(1)} collective-permute-done((bf16[128,2048]{1,0:T(8,128)(2,1)S(1)}, bf16[128,2048]{1,0:T(8,128)(2,1)S(1)}, u32[]{:S(2)}, u32[]{:S(2)}) %collective-permute-start.5) | collective-permute-done | bytes 524320 | tf_op jit(solution)/shard_map/ppermute | solution.py:408
  189.8 0.1 collective-permute-done.6.refs_2_
  190.0 0.9 copy-done.1
  190.9 2.6 %mix_first.1 = (f32[128,2048]{1,0:T(8,128)S(1)}, f32[8,128]{1,0:T(8,128)S(1)}) custom-call(s32[128,128]{1,0:T(8,128)S(1)} %get-tuple-element.26.slots_ref, f32[128,128]{1,0:T(8,128)S(1)} %get-tuple-element.27.columns_ref, bf16[384,2048]{1,0:T(8,128)(2,1)} %bitcast.12.back_ref, bf16[128,2048]{1,0:T(8,128)(2,1)S(1)} %copy-done.1, ...), custom_call_target="tpu_custom_call" | custom-call | tf_op jit(solution)/shard_map/mix_first/pallas_call | solution.py:549
  193.5 0.4 all-to-all-done.6
  193.9 2.8 %mix_second.1 = (bf16[128,2048]{1,0:T(8,128)(2,1)}, f32[4,128]{1,0:T(4,128)}) custom-call(s32[128,128]{1,0:T(8,128)S(1)} %get-tuple-element.26.slots_ref, f32[128,128]{1,0:T(8,128)S(1)} %get-tuple-element.27.columns_ref, bf16[192,2048]{1,0:T(8,128)(2,1)} %bitcast.11.back_ref, bf16[128,2048]{1,0:T(8,128)(2,1)S(1)} %copy-done.1, ...), custom_call_target="tpu_custom_call" | custom-call | tf_op jit(solution)/shard_map/mix_second/pallas_call | solution.py:549
  (18 shorter events, 0.0 us)
Async XLA Ops:
  2.3 17.3 %collective-permute-start = (bf16[64,2048]{1,0:T(8,128)(2,1)}, bf16[64,2048]{1,0:T(8,128)(2,1)S(1)}, u32[]{:S(2)}, u32[]{:S(2)}) collective-permute-start(bf16[64,2048]{1,0:T(8,128)(2,1)} %get-tuple-element.25), channel_id=1, source_target_pairs={{0,8},{1,9},{2,10},{3,11},{4,12},{5,13},{6,14},{7,15},{8,0},{9,1},... | collective-permute-start | bytes 786440 | tf_op jit(solution)/shard_map/ppermute | solution.py:408
  6.4 13.2 %all-to-all-start = ((s32[16,1,128]{2,1,0:T(1,128)}), s32[16,1,128]{2,1,0:T(1,128)S(1)}, u32[]{:S(2)}, u32[]{:S(2)}) async-start(s32[16,1,128]{2,1,0:T(1,128)} %get-tuple-element.24), calls=%async_computation | async-start | bytes 16384 | tf_op jit(solution)/shard_map/all_to_all | solution.py:373
  19.6 3.3 %copy-start.2 = (bf16[64,2048]{1,0:T(8,128)(2,1)}, bf16[64,2048]{1,0:T(8,128)(2,1)S(1)}, u32[]{:S(2)}) copy-start(bf16[64,2048]{1,0:T(8,128)(2,1)S(1)} %collective-permute-done._.refs_0_) | copy-start | bytes 786436
  22.8 5.2 %copy-start.9 = (s32[128,16]{0,1:T(8,128)S(1)}, s32[128,16]{0,1:T(8,128)}, u32[]{:S(2)}) copy-start(s32[128,16]{0,1:T(8,128)} %param.11) | copy-start | bytes 24580
  22.8 5.2 %copy-start.5 = (s32[128]{0:T(128)S(1)}, s32[128]{0:T(128)}, u32[]{:S(2)}) copy-start(s32[128]{0:T(128)} %param.12) | copy-start | bytes 1540
  22.8 5.2 %copy-start.6 = (s32[128,4]{0,1:T(4,128)S(1)}, s32[128,4]{0,1:T(4,128)}, u32[]{:S(2)}) copy-start(s32[128,4]{0,1:T(4,128)} %param.13) | copy-start | bytes 6148
  22.9 5.2 %copy-start.7 = (f32[128,4]{0,1:T(4,128)S(1)}, f32[128,4]{0,1:T(4,128)}, u32[]{:S(2)}) copy-start(f32[128,4]{0,1:T(4,128)} %param.14) | copy-start | bytes 6148
  22.9 31.9 %copy-start.4 = (bf16[128,2048]{1,0:T(8,128)(2,1)S(1)}, bf16[128,2048]{1,0:T(8,128)(2,1)}, u32[]{:S(2)}) copy-start(bf16[128,2048]{1,0:T(8,128)(2,1)} %values_ref.1) | copy-start | bytes 1572868
  22.9 31.8 %all-to-all-start.1 = ((bf16[16,16,2048]{2,1,0:T(8,128)(2,1)}), bf16[16,16,2048]{2,1,0:T(8,128)(2,1)S(1)}, u32[]{:S(2)}, u32[]{:S(2)}) async-start(bf16[16,16,2048]{2,1,0:T(8,128)(2,1)} %bitcast.5), calls=%async_computation.1 | async-start | bytes 2097152 | tf_op jit(solution)/shard_map/all_to_all | solution.py:373
  28.9 25.8 %collective-permute-start.1 = (s32[4,128]{1,0:T(4,128)S(1)}, s32[4,128]{1,0:T(4,128)S(1)}, u32[]{:S(2)}, u32[]{:S(2)}) collective-permute-start(s32[4,128]{1,0:T(4,128)S(1)} %get-tuple-element.30), channel_id=1, source_target_pairs={{0,8},{1,9},{2,10},{3,11},{4,12},{5,13},{6,14},{7,15},{8,0},{9,1},... | collective-permute-start | bytes 6152 | tf_op jit(solution)/shard_map/ppermute | solution.py:408
  31.8 22.9 %collective-permute-start.2 = (f32[4,128]{1,0:T(4,128)S(1)}, f32[4,128]{1,0:T(4,128)S(1)}, u32[]{:S(2)}, u32[]{:S(2)}) collective-permute-start(f32[4,128]{1,0:T(4,128)S(1)} %get-tuple-element.31), channel_id=1, source_target_pairs={{0,8},{1,9},{2,10},{3,11},{4,12},{5,13},{6,14},{7,15},{8,0},{9,1},... | collective-permute-start | bytes 6152 | tf_op jit(solution)/shard_map/ppermute | solution.py:408
  54.7 27.4 %copy-start = (bf16[128,2048]{1,0:T(8,128)(2,1)S(1)}, bf16[128,2048]{1,0:T(8,128)(2,1)}, u32[]{:S(2)}) copy-start(bf16[128,2048]{1,0:T(8,128)(2,1)} %refs_0_.5) | copy-start | bytes 1572868
  56.7 25.5 %collective-permute-start.3 = (bf16[128,2048]{1,0:T(8,128)(2,1)S(1)}, bf16[128,2048]{1,0:T(8,128)(2,1)S(1)}, u32[]{:S(2)}, u32[]{:S(2)}) collective-permute-start(bf16[128,2048]{1,0:T(8,128)(2,1)S(1)} %get-tuple-element.34._.state_ref), channel_id=1, source_target_pairs={{0,8},{1,9},{2,10},{3,11},{4,12},{5,13},{6,14},{7,15},{8,0},{9,1},... | collective-permute-start | bytes 1572872 | tf_op jit(solution)/shard_map/ppermute | solution.py:408
  58.1 26.7 %all-to-all-start.2 = ((bf16[8,24,2048]{2,1,0:T(8,128)(2,1)}), bf16[8,24,2048]{2,1,0:T(8,128)(2,1)}, u32[]{:S(2)}, u32[]{:S(2)}) async-start(bf16[8,24,2048]{2,1,0:T(8,128)(2,1)} %bitcast.25), calls=%async_computation.2 | async-start | bytes 1572864 | tf_op jit(solution)/shard_map/all_to_all | solution.py:373
  84.8 23.6 %all-to-all-start.4 = ((bf16[8,48,2048]{2,1,0:T(8,128)(2,1)}), bf16[8,48,2048]{2,1,0:T(8,128)(2,1)S(1)}, u32[]{:S(2)}, u32[]{:S(2)}) async-start(bf16[8,48,2048]{2,1,0:T(8,128)(2,1)} %bitcast.21), calls=%async_computation.4 | async-start | bytes 3145728 | tf_op jit(solution)/shard_map/all_to_all | solution.py:373
  108.4 4.3 %copy-start.8 = (bf16[8,48,2048]{2,1,0:T(8,128)(2,1)}, bf16[8,48,2048]{2,1,0:T(8,128)(2,1)S(1)}, u32[]{:S(2)}) copy-start(bf16[8,48,2048]{2,1,0:T(8,128)(2,1)S(1)} %all-to-all-done.4.rows_hbm) | copy-start | bytes 4718596
  108.4 30.0 %all-to-all-start.3 = ((bf16[8,48,2048]{2,1,0:T(8,128)(2,1)}), bf16[8,48,2048]{2,1,0:T(8,128)(2,1)}, u32[]{:S(2)}, u32[]{:S(2)}) async-start(bf16[8,48,2048]{2,1,0:T(8,128)(2,1)} %near_first.1.refs_0_), calls=%async_computation.3 | async-start | bytes 3145728 | tf_op jit(solution)/shard_map/all_to_all | solution.py:373
  112.7 25.5 %collective-permute-start.4 = (bf16[64,2048]{1,0:T(8,128)(2,1)S(1)}, bf16[64,2048]{1,0:T(8,128)(2,1)S(1)}, u32[]{:S(2)}, u32[]{:S(2)}) collective-permute-start(bf16[64,2048]{1,0:T(8,128)(2,1)S(1)} %get-tuple-element.39), channel_id=1, source_target_pairs={{0,8},{1,9},{2,10},{3,11},{4,12},{5,13},{6,14},{7,15},{8,0},{9,1},... | collective-permute-start | bytes 786440 | tf_op jit(solution)/shard_map/ppermute | solution.py:408
  138.4 24.0 %all-to-all-start.5 = ((bf16[8,48,2048]{2,1,0:T(8,128)(2,1)}), bf16[8,48,2048]{2,1,0:T(8,128)(2,1)S(1)}, u32[]{:S(2)}, u32[]{:S(2)}) async-start(bf16[8,48,2048]{2,1,0:T(8,128)(2,1)} %ordered.3), calls=%async_computation.5 | async-start | bytes 3145728 | tf_op jit(solution)/shard_map/all_to_all | solution.py:373
  142.3 20.1 %copy-start.3 = (bf16[64,2048]{1,0:T(8,128)(2,1)S(1)}, bf16[64,2048]{1,0:T(8,128)(2,1)}, u32[]{:S(2)}) copy-start(bf16[64,2048]{1,0:T(8,128)(2,1)} %copy-done.2) | copy-start | bytes 786436
  164.0 25.8 %collective-permute-start.5 = (bf16[128,2048]{1,0:T(8,128)(2,1)S(1)}, bf16[128,2048]{1,0:T(8,128)(2,1)S(1)}, u32[]{:S(2)}, u32[]{:S(2)}) collective-permute-start(bf16[128,2048]{1,0:T(8,128)(2,1)S(1)} %get-tuple-element.40.refs_1_), channel_id=1, source_target_pairs={{0,8},{1,9},{2,10},{3,11},{4,12},{5,13},{6,14},{7,15},{8,0},{9,1},... | collective-permute-start | bytes 1572872 | tf_op jit(solution)/shard_map/ppermute | solution.py:408
  165.8 24.2 %collective-permute-start.6 = (f32[8,128]{1,0:T(8,128)}, f32[8,128]{1,0:T(8,128)}, u32[]{:S(2)}, u32[]{:S(2)}) collective-permute-start(f32[8,128]{1,0:T(8,128)} %get-tuple-element.41), channel_id=1, source_target_pairs={{0,8},{1,9},{2,10},{3,11},{4,12},{5,13},{6,14},{7,15},{8,0},{9,1},... | collective-permute-start | bytes 12296 | tf_op jit(solution)/shard_map/ppermute | solution.py:408
  166.9 27.0 %all-to-all-start.6 = ((bf16[8,24,2048]{2,1,0:T(8,128)(2,1)}), bf16[8,24,2048]{2,1,0:T(8,128)(2,1)}, u32[]{:S(2)}, u32[]{:S(2)}) async-start(bf16[8,24,2048]{2,1,0:T(8,128)(2,1)} %ordered.4), calls=%async_computation.6 | async-start | bytes 1572864 | tf_op jit(solution)/shard_map/all_to_all | solution.py:373
  189.8 1.0 copy-start.1

commit v17 on v16

--- a/solution.py
+++ b/solution.py
@@ -44,7 +44,7 @@
     upper_ref[...] = grad_ref[...]
 
 
-def fetch_kernel(me_ref, rows_ref, table_hbm, _, out_ref, table_ref, sem):
+def fetch_kernel(me_ref, rows_ref, table_hbm, _, out_hbm, table_ref, out_ref, sem, out_sem):
     copy = pltpu.make_async_copy(table_hbm, table_ref, sem)
     copy.start()
     device_count, _, tok_rows = rows_ref.shape
@@ -63,7 +63,17 @@
         picks.append(flags(place == wanted))
     pick = jnp.concatenate(picks, axis=0)
     copy.wait()
-    out_ref[...] = dot(pick, table_ref[...]).astype(BF16)
+    width = out_ref.shape[1] // out_sem.shape[0]
+    copies = []
+    for n in range(out_sem.shape[0]):
+        cols = pl.ds(n * width, width)
+        out_ref[:, cols] = dot(pick, table_ref[:, cols]).astype(BF16)
+        copies.append(
+            pltpu.make_async_copy(out_ref.at[:, cols], out_hbm.at[:, cols], out_sem.at[n])
+        )
+        copies[-1].start()
+    for copy in copies:
+        copy.wait()
 
 
 def turned(rows):
@@ -146,23 +156,11 @@
 
 
 def state_kernel(
-    put_ref,
-    pick_ref,
-    returned_ref,
-    values_ref,
-    columns_ref,
-    ids_ref,
-    weights_ref,
-    state_ref,
-    out_hbm,
-    sent_ref,
-    sem,
+    put_ref, returned_ref, values_ref, columns_ref, ids_ref, weights_ref, state_ref
 ):
     features = values_ref.shape[1]
-    width = features // sem.shape[0]
-    copies = []
-    for n in range(sem.shape[0]):
-        left = n * width
+    width = 512
+    for left in range(0, features, width):
         found = dot(put_ref[...], returned_ref[:, left : left + width])
         for b in range(width // BLOCK):
             at = left + b * BLOCK
@@ -173,17 +171,10 @@
             state_ref[:, at : at + BLOCK] = (
                 scaled + found[:, b * BLOCK : (b + 1) * BLOCK]
             ).astype(BF16)
-        cols = pl.ds(left, width)
-        sent_ref[:, cols] = dot(pick_ref[...], state_ref[:, cols]).astype(BF16)
-        copies.append(
-            pltpu.make_async_copy(sent_ref.at[:, cols], out_hbm.at[:, cols], sem.at[n])
-        )
-        copies[-1].start()
-    for copy in copies:
-        copy.wait()
-
-
-def later_kernel(pick_ref, state_ref, _, out_ref):
+
+
+def pair_kernel(pick_ref, state_ref, *refs):
+    out_ref = refs[-1]
     out_ref[...] = dot(pick_ref[...], state_ref[...]).astype(BF16)
 
 
@@ -335,9 +326,11 @@
     )
 
 
-def mix_kernel(grads, added, start, slots_ref, columns_ref, back_ref, *refs):
+def mix_kernel(grads, added, added_grads, start, slots_ref, columns_ref, back_ref, *refs):
     mixed_ref, grads_ref = refs[-2:]
-    grad_refs, added_refs = refs[:grads], refs[grads : grads + 2 * added]
+    grad_refs = refs[:grads]
+    added_refs = refs[grads : grads + added]
+    added_grad_refs = refs[grads + added : grads + added + added_grads]
     tok_rows = slots_ref.shape[0]
     count, features = back_ref.shape
     grad = jnp.concatenate([ref[...] for ref in grad_refs], axis=0)
@@ -359,12 +352,12 @@
     for at in range(0, features, width):
         cols = slice(at, at + width)
         value = dot(high, back_ref[:, cols]) + dot(rest, back_ref[:, cols])
-        for ref in added_refs[::2]:
+        for ref in added_refs:
             value = value + ref[:, cols].astype(F32)
         mixed_ref[:, cols] = value.astype(mixed_ref.dtype)
     lines = grads_ref.shape[0]
     sums = wide.T[:lines, :]
-    for ref in added_refs[1::2]:
+    for ref in added_grad_refs:
         sums = sums + ref[:lines, :]
     grads_ref[...] = sums
 
@@ -440,10 +433,15 @@
     other_upper = mirrored(upper_grad)
     fetched = pl.pallas_call(
         fetch_kernel,
-        out_shape=shape((device_count * look_cap, features), BF16),
+        out_shape=pltpu.HBM((device_count * look_cap, features), BF16),
         in_specs=[smem, vmem, pl.BlockSpec(memory_space=pltpu.HBM), anywhere],
-        out_specs=vmem,
-        scratch_shapes=[VMEM(table.shape, BF16), pltpu.SemaphoreType.DMA],
+        out_specs=anywhere,
+        scratch_shapes=[
+            VMEM(table.shape, BF16),
+            VMEM((device_count * look_cap, features), BF16),
+            pltpu.SemaphoreType.DMA,
+            pltpu.SemaphoreType.DMA((4,)),
+        ],
         compiler_params=SMALL,
         name="fetch_rows",
     )(place, swap(all_rows), in_hbm(table), other_upper)
@@ -473,30 +471,39 @@
         turned_ids,
         turned_weights,
         jnp.exp2(block_exps.T.astype(F32)),
-        fetched,
+        in_hbm(fetched),
     )
     other_ids, other_weights = mirrored(sent_ids), mirrored(sent_weights)
 
     def sent_scratch(count):
         return [VMEM((count, features), BF16), pltpu.SemaphoreType.DMA((4,))]
 
-    state, near_sent = pl.pallas_call(
+    state = pl.pallas_call(
         state_kernel,
-        out_shape=(shape((tok_rows, features), BF16), pltpu.HBM((slots // 2, features), BF16)),
-        in_specs=[vmem] * 5 + [anywhere] * 2,
-        out_specs=(vmem, anywhere),
-        scratch_shapes=sent_scratch(slots // 2),
+        out_shape=shape((tok_rows, features), BF16),
+        in_specs=[vmem] * 4 + [anywhere] * 2,
+        out_specs=vmem,
         compiler_params=SMALL,
         name="token_state",
     )(
         put,
-        first_pick,
         returned.reshape(device_count * look_cap, features),
         block_values,
         near_columns,
         other_ids,
         other_weights,
     )
+
+    def pair_sent(name, pick, *after):
+        return pl.pallas_call(
+            pair_kernel,
+            out_shape=pltpu.HBM((slots // 2, features), BF16),
+            in_specs=[vmem, vmem] + [anywhere] * len(after),
+            out_specs=vmem,
+            compiler_params=SMALL,
+            name=name,
+        )(pick, state, *after).reshape(half, PAIR, features)
+
     far_pick, far_of, far_columns = pl.pallas_call(
         far_plan_kernel,
         out_shape=(pick_shape, shape(square, jnp.int32), shape(square, F32)),
@@ -520,18 +527,10 @@
         ),
         name="far_slots",
     )(far_pick, mirrored(state), out_grad)
-    pair_rows = (half, PAIR, features)
-    near_rows = swap(near_sent.reshape(pair_rows), halves)
+    near_rows = swap(pair_sent("first_slots", first_pick), halves)
     far_sent = far_sent.reshape(half, 2 * PAIR, features)
     far_rows = swap(far_sent, halves)
-    later_sent = pl.pallas_call(
-        later_kernel,
-        out_shape=pltpu.HBM((slots // 2, features), BF16),
-        in_specs=[vmem, vmem, anywhere],
-        out_specs=vmem,
-        compiler_params=SMALL,
-        name="later_slots",
-    )(second_pick, state, in_hbm(far_sent)).reshape(pair_rows)
+    later_sent = pair_sent("later_slots", second_pick, in_hbm(far_sent))
     other_grads = (other_upper, mirrored(lower_grad))
 
     weights = (w_gate, w_up, w_down)
@@ -544,30 +543,42 @@
     near_out = expert_call("near_second", 2, 2, both, weights)
 
     def mixed_rows(
-        name, slot_of, columns, back, grads, kind, start=0, lines=2 * TOP, added=(), after=()
+        name,
+        slot_of,
+        columns,
+        back,
+        grads,
+        kind,
+        start=0,
+        lines=2 * TOP,
+        added=(),
+        added_grads=(),
+        after=(),
     ):
+        operands = (*grads, *added, *added_grads)
+
         return pl.pallas_call(
-            functools.partial(mix_kernel, len(grads), len(added) // 2, start),
+            functools.partial(mix_kernel, len(grads), len(added), len(added_grads), start),
             out_shape=(shape((tok_rows, features), kind), shape((lines, tok_rows), F32)),
-            in_specs=[vmem] * (3 + len(grads) + len(added)) + [anywhere] * len(after),
+            in_specs=[vmem] * (3 + len(operands)) + [anywhere] * len(after),
             out_specs=(vmem, vmem),
             compiler_params=SMALL,
             name=name,
-        )(slot_of, columns, back.reshape(-1, features), *grads, *added, *after)
+        )(slot_of, columns, back.reshape(-1, features), *operands, *after)
 
     far_mixed, far_grads = mixed_rows(
         "mix_far", far_of, far_columns, far_back, other_grads, BF16, after=(in_hbm(near_out),)
     )
     near_back = swap(ordered(in_hbm(near_out), far_mixed), halves)
-    far_sums = (ordered(mirrored(far_mixed), flops=400_000_000_000), mirrored(far_grads))
-    sums = mixed_rows(
+    far_sums = ordered(mirrored(far_mixed), flops=400_000_000_000)
+    sums, sum_grads = mixed_rows(
         "mix_first",
         near_of,
         near_columns,
         in_hbm(both.reshape(slots, features)),
         (out_grad,),
         F32,
-        added=far_sums,
+        added=(far_sums,),
     )
     mixed, grads = mixed_rows(
         "mix_second",
@@ -578,7 +589,8 @@
         BF16,
         start=slots,
         lines=TOP,
-        added=sums,
+        added=(sums,),
+        added_grads=(sum_grads, mirrored(far_grads)),
     )
     return mixed, grads.T
 

time: 197 us -> 198 us (level)
  local copies, waits for them, and re-layouts: 0.94 us -> 3.41 us
    unnamed x20 -> x26, local copies, waits for them, and re-layouts: 0.94 us -> 3.41 us
    pallas_call x6 -> x7, Pallas kernels: 13.4 us -> 13 us  [the longest x3 7.09 us: mixed_rows(): pl.pallas_call(functools.partial(mix_kernel, len(grads), len(added), len(...]
  transfers between devices with their start and end apart: 14 -> 14, of which waited for: 10 -> 8; matrix products, arithmetic and copies ran while one was open for 0% -> 0% of each run, Pallas kernels for 31% -> 31%
where the time goes in v17:
time: 198 us; the launch traced here: 197 us
  waiting for transfers between devices  80.8 us (41%)
  Pallas kernels  71.1 us (36%)
  starting transfers between devices  41.3 us (21%)
  local copies, waits for them, and re-layouts  3.41 us (2%)
    ppermute x7, waiting for transfers between devices, mirrored(): return lax.ppermute(array, 'expert', pairs)  59.1 us
    pallas_call x3, Pallas kernels, expert_call(): pl.pallas_call(functools.partial(expert_kernel, first, count, bool(front)...  53.2 us
    all_to_all x7, starting transfers between devices, swap(): lax.all_to_all(array, 'expert', split_axis=0, concat_axis=0, tiled=True,...  28.6 us
    all_to_all x7, waiting for transfers between devices, swap(): lax.all_to_all(array, 'expert', split_axis=0, concat_axis=0, tiled=True,...  21.7 us
    ppermute x7, starting transfers between devices, mirrored(): return lax.ppermute(array, 'expert', pairs)  12.7 us
    pallas_call x3, Pallas kernels, mixed_rows(): pl.pallas_call(functools.partial(mix_kernel, len(grads), len(added), len(...  7.09 us
  transfers between devices with their start and end apart: 14, of which 8 were waited for; matrix products, arithmetic and copies ran while one was open for 0% of the time, Pallas kernels for 31%

profile of v17, /device:TPU:0, one launch (start us, length us, event | category | flops | bytes accessed | tf_op | source)
XLA Modules:
  0.0 197.5 jit_solution(9879957964368889019)
XLA Ops:
  0.6 1.7 repeat_rows.1
  2.3 4.0 %collective-permute-start = (bf16[64,2048]{1,0:T(8,128)(2,1)}, bf16[64,2048]{1,0:T(8,128)(2,1)S(1)}, u32[]{:S(2)}, u32[]{:S(2)}) collective-permute-start(bf16[64,2048]{1,0:T(8,128)(2,1)} %get-tuple-element.23), channel_id=1, source_target_pairs={{0,8},{1,9},{2,10},{3,11},{4,12},{5,13},{6,14},{7,15},{8,0},{9,1},... | collective-permute-start | bytes 786440 | tf_op jit(solution)/shard_map/ppermute | solution.py:401
  6.4 3.9 %all-to-all-start = ((s32[16,1,128]{2,1,0:T(1,128)}), s32[16,1,128]{2,1,0:T(1,128)S(1)}, u32[]{:S(2)}, u32[]{:S(2)}) async-start(s32[16,1,128]{2,1,0:T(1,128)} %get-tuple-element.22), calls=%async_computation | async-start | bytes 16384 | tf_op jit(solution)/shard_map/all_to_all | solution.py:366
  10.3 0.1 pad_add_fusion.me_ref
  10.4 9.2 %all-to-all-done.rows_ref = s32[16,1,128]{2,1,0:T(1,128)S(1)} async-done(((s32[16,1,128]{2,1,0:T(1,128)}), s32[16,1,128]{2,1,0:T(1,128)S(1)}, u32[]{:S(2)}, u32[]{:S(2)}) %all-to-all-start) | async-done | bytes 8224 | tf_op jit(solution)/shard_map/all_to_all | solution.py:366
  19.6 3.0 %fetch_rows.1._ = bf16[256,2048]{1,0:T(8,128)(2,1)} custom-call(s32[2]{0:T(128)S(1)} %pad_add_fusion.me_ref, s32[16,1,128]{2,1,0:T(1,128)S(1)} %all-to-all-done.rows_ref, bf16[256,2048]{1,0:T(8,128)(2,1)} %table_hbm.1, bf16[64,2048]{1,0:T(8,128)(2,1)S(1)} %collective-permute-done._.refs_0_), custom_call_target="tpu_custom_call" | custom-call | tf_op jit(solution)/shard_map/fetch_rows/pallas_call | solution.py:434
  22.7 0.0 copy-start.12
  22.7 0.0 copy-start.7
  22.7 0.0 copy-start.8
  22.7 0.0 copy-start.9
  22.7 0.0 copy-start.6
  22.7 5.1 %all-to-all-start.1 = ((bf16[16,16,2048]{2,1,0:T(8,128)(2,1)}), bf16[16,16,2048]{2,1,0:T(8,128)(2,1)S(1)}, u32[]{:S(2)}, u32[]{:S(2)}) async-start(bf16[16,16,2048]{2,1,0:T(8,128)(2,1)} %bitcast.25), calls=%async_computation.1 | async-start | bytes 2097152 | tf_op jit(solution)/shard_map/all_to_all | solution.py:366
  27.9 0.9 near_plan.1
  28.8 2.9 %collective-permute-start.1 = (s32[4,128]{1,0:T(4,128)S(1)}, s32[4,128]{1,0:T(4,128)S(1)}, u32[]{:S(2)}, u32[]{:S(2)}) collective-permute-start(s32[4,128]{1,0:T(4,128)S(1)} %get-tuple-element.28), channel_id=1, source_target_pairs={{0,8},{1,9},{2,10},{3,11},{4,12},{5,13},{6,14},{7,15},{8,0},{9,1},... | collective-permute-start | bytes 6152 | tf_op jit(solution)/shard_map/ppermute | solution.py:401
  31.7 0.1 collective-permute-start.2
  31.8 22.8 %collective-permute-done.1.ids_ref = s32[4,128]{1,0:T(4,128)S(1)} collective-permute-done((s32[4,128]{1,0:T(4,128)S(1)}, s32[4,128]{1,0:T(4,128)S(1)}, u32[]{:S(2)}, u32[]{:S(2)}) %collective-permute-start.1) | collective-permute-done | bytes 2080 | tf_op jit(solution)/shard_map/ppermute | solution.py:401
  54.5 0.0 collective-permute-done.2.weights_ref
  54.6 0.4 token_state.1.state_ref._
  55.0 1.5 collective-permute-start.3
  56.5 1.2 first_slots.1
  57.7 4.2 %all-to-all-start.2 = ((bf16[8,24,2048]{2,1,0:T(8,128)(2,1)}), bf16[8,24,2048]{2,1,0:T(8,128)(2,1)}, u32[]{:S(2)}, u32[]{:S(2)}) async-start(bf16[8,24,2048]{2,1,0:T(8,128)(2,1)} %bitcast.27), calls=%async_computation.2 | async-start | bytes 1572864 | tf_op jit(solution)/shard_map/all_to_all | solution.py:366
  61.9 0.8 far_plan.1
  62.8 17.7 %collective-permute-done.3.state_ref = bf16[128,2048]{1,0:T(8,128)(2,1)S(1)} collective-permute-done((bf16[128,2048]{1,0:T(8,128)(2,1)S(1)}, bf16[128,2048]{1,0:T(8,128)(2,1)S(1)}, u32[]{:S(2)}, u32[]{:S(2)}) %collective-permute-start.3) | collective-permute-done | bytes 524320 | tf_op jit(solution)/shard_map/ppermute | solution.py:401
  80.5 1.5 far_slots.1
  81.9 2.4 %all-to-all-done.2.rows_hbm = bf16[8,24,2048]{2,1,0:T(8,128)(2,1)} async-done(((bf16[8,24,2048]{2,1,0:T(8,128)(2,1)}), bf16[8,24,2048]{2,1,0:T(8,128)(2,1)}, u32[]{:S(2)}, u32[]{:S(2)}) %all-to-all-start.2) | async-done | bytes 786464 | tf_op jit(solution)/shard_map/all_to_all | solution.py:366
  84.3 3.6 %all-to-all-start.4 = ((bf16[8,48,2048]{2,1,0:T(8,128)(2,1)}), bf16[8,48,2048]{2,1,0:T(8,128)(2,1)S(1)}, u32[]{:S(2)}, u32[]{:S(2)}) async-start(bf16[8,48,2048]{2,1,0:T(8,128)(2,1)} %bitcast.22), calls=%async_computation.4 | async-start | bytes 3145728 | tf_op jit(solution)/shard_map/all_to_all | solution.py:366
  87.9 1.2 later_slots.1
  89.2 15.0 %near_first.1.refs_0_ = bf16[8,48,2048]{2,1,0:T(8,128)(2,1)} custom-call(bf16[8,24,2048]{2,1,0:T(8,128)(2,1)} %all-to-all-done.2.rows_hbm, bf16[8,24,2048]{2,1,0:T(8,128)(2,1)} %bitcast.26, bf16[8,48,2048]{2,1,0:T(8,128)(2,1)} %bitcast.24, bf16[4,2048,1408]{2,1,0:T(8,128)(2,1)} %refs_1_.3, bf16[4,2048,1408]{2,1,0:T(8,128)(2,1)} %refs_2_.5, ...), custom_call_target="tpu_custom_call" | custom-call | flops 6643777536 | bytes 34603008 | tf_op jit(solution)/shard_map/near_first/pallas_call | solution.py:301
  104.2 3.8 %all-to-all-done.4.rows_hbm = bf16[8,48,2048]{2,1,0:T(8,128)(2,1)S(1)} async-done(((bf16[8,48,2048]{2,1,0:T(8,128)(2,1)}), bf16[8,48,2048]{2,1,0:T(8,128)(2,1)S(1)}, u32[]{:S(2)}, u32[]{:S(2)}) %all-to-all-start.4) | async-done | bytes 1572896 | tf_op jit(solution)/shard_map/all_to_all | solution.py:366
  107.9 1.1 copy-done.11
  109.1 3.6 %all-to-all-start.3 = ((bf16[8,48,2048]{2,1,0:T(8,128)(2,1)}), bf16[8,48,2048]{2,1,0:T(8,128)(2,1)S(1)}, u32[]{:S(2)}, u32[]{:S(2)}) async-start(bf16[8,48,2048]{2,1,0:T(8,128)(2,1)} %near_first.1.refs_0_), calls=%async_computation.3 | async-start | bytes 3145728 | tf_op jit(solution)/shard_map/all_to_all | solution.py:366
  112.7 1.2 collective-permute-start.4
  113.8 24.3 %far_experts.1.refs_0_ = bf16[8,48,2048]{2,1,0:T(8,128)(2,1)} custom-call(bf16[8,48,2048]{2,1,0:T(8,128)(2,1)} %copy-done.11, bf16[8,48,2048]{2,1,0:T(8,128)(2,1)} %near_first.1.refs_0_, bf16[4,2048,1408]{2,1,0:T(8,128)(2,1)} %refs_1_.3, bf16[4,2048,1408]{2,1,0:T(8,128)(2,1)} %refs_2_.5, bf16[4,1408,2048]{2,1,0:T(8,128)(2,1)} %refs_3_.3), custom_call_target="tpu_custom_call" | custom-call | flops 13287555072 | bytes 69206016 | tf_op jit(solution)/shard_map/far_experts/pallas_call | solution.py:301
  138.2 0.1 all-to-all-done.3.rows_hbm.refs_1_
  138.3 1.2 copy-done.10
  139.5 4.0 %all-to-all-start.5 = ((bf16[8,48,2048]{2,1,0:T(8,128)(2,1)}), bf16[8,48,2048]{2,1,0:T(8,128)(2,1)S(1)}, u32[]{:S(2)}, u32[]{:S(2)}) async-start(bf16[8,48,2048]{2,1,0:T(8,128)(2,1)} %ordered.3), calls=%async_computation.5 | async-start | bytes 3145728 | tf_op jit(solution)/shard_map/all_to_all | solution.py:366
  143.5 13.8 %near_second.1.refs_2_.refs_0_ = bf16[8,24,2048]{2,1,0:T(8,128)(2,1)} custom-call(bf16[8,48,2048]{2,1,0:T(8,128)(2,1)} %copy-done.10, bf16[4,2048,1408]{2,1,0:T(8,128)(2,1)} %refs_1_.3, bf16[4,2048,1408]{2,1,0:T(8,128)(2,1)} %refs_2_.5, bf16[4,1408,2048]{2,1,0:T(8,128)(2,1)} %refs_3_.3), custom_call_target="tpu_custom_call" | custom-call | flops 6643777536 | bytes 34603008 | tf_op jit(solution)/shard_map/near_second/pallas_call | solution.py:301
  157.3 6.2 %all-to-all-done.5 = bf16[8,48,2048]{2,1,0:T(8,128)(2,1)S(1)} async-done(((bf16[8,48,2048]{2,1,0:T(8,128)(2,1)}), bf16[8,48,2048]{2,1,0:T(8,128)(2,1)S(1)}, u32[]{:S(2)}, u32[]{:S(2)}) %all-to-all-start.5) | async-done | bytes 1572896 | tf_op jit(solution)/shard_map/all_to_all | solution.py:366
  163.5 1.6 mix_far.1
  165.2 1.8 collective-permute-start.5
  167.0 4.2 %all-to-all-start.6 = ((bf16[8,24,2048]{2,1,0:T(8,128)(2,1)}), bf16[8,24,2048]{2,1,0:T(8,128)(2,1)}, u32[]{:S(2)}, u32[]{:S(2)}) async-start(bf16[8,24,2048]{2,1,0:T(8,128)(2,1)} %ordered.4), calls=%async_computation.6 | async-start | bytes 1572864 | tf_op jit(solution)/shard_map/all_to_all | solution.py:366
  171.2 1.2 collective-permute-start.6
  172.4 18.6 %collective-permute-done.5.refs_0_ = bf16[128,2048]{1,0:T(8,128)(2,1)S(1)} collective-permute-done((bf16[128,2048]{1,0:T(8,128)(2,1)S(1)}, bf16[128,2048]{1,0:T(8,128)(2,1)S(1)}, u32[]{:S(2)}, u32[]{:S(2)}) %collective-permute-start.5) | collective-permute-done | bytes 524320 | tf_op jit(solution)/shard_map/ppermute | solution.py:401
  191.0 1.0 copy-done.1
  192.0 2.6 %mix_first.1 = (f32[128,2048]{1,0:T(8,128)S(1)}, f32[8,128]{1,0:T(8,128)S(1)}) custom-call(s32[128,128]{1,0:T(8,128)S(1)} %get-tuple-element.24.slots_ref, f32[128,128]{1,0:T(8,128)S(1)} %copy-done.5, bf16[384,2048]{1,0:T(8,128)(2,1)} %bitcast.21, bf16[128,2048]{1,0:T(8,128)(2,1)S(1)} %copy-done.1, bf16[128,2048]{1,0:T(8,128)(2,1)S(1)} %ordered.5.refs_1_), custom_call_target="tpu_custom_call" | custom-call | tf_op jit(solution)/shard_map/mix_first/pallas_call | solution.py:560
  194.6 0.0 collective-permute-done.6.refs_3_
  194.7 0.0 all-to-all-done.6
  194.7 2.8 %mix_second.1 = (bf16[128,2048]{1,0:T(8,128)(2,1)}, f32[4,128]{1,0:T(4,128)}) custom-call(s32[128,128]{1,0:T(8,128)S(1)} %get-tuple-element.24.slots_ref, f32[128,128]{1,0:T(8,128)S(1)} %copy-done.5, bf16[192,2048]{1,0:T(8,128)(2,1)} %bitcast.11.back_ref, bf16[128,2048]{1,0:T(8,128)(2,1)S(1)} %copy-done.1, f32[128,2048]{1,0:T(8,128)S(1)} %get-tuple-element.37.refs_1_, ...), custom_call_target="tpu_custom_call" | custom-call | tf_op jit(solution)/shard_map/mix_second/pallas_call | solution.py:560
  (25 shorter events, 0.1 us)
Async XLA Ops:
  2.3 17.3 %collective-permute-start = (bf16[64,2048]{1,0:T(8,128)(2,1)}, bf16[64,2048]{1,0:T(8,128)(2,1)S(1)}, u32[]{:S(2)}, u32[]{:S(2)}) collective-permute-start(bf16[64,2048]{1,0:T(8,128)(2,1)} %get-tuple-element.23), channel_id=1, source_target_pairs={{0,8},{1,9},{2,10},{3,11},{4,12},{5,13},{6,14},{7,15},{8,0},{9,1},... | collective-permute-start | bytes 786440 | tf_op jit(solution)/shard_map/ppermute | solution.py:401
  6.4 13.2 %all-to-all-start = ((s32[16,1,128]{2,1,0:T(1,128)}), s32[16,1,128]{2,1,0:T(1,128)S(1)}, u32[]{:S(2)}, u32[]{:S(2)}) async-start(s32[16,1,128]{2,1,0:T(1,128)} %get-tuple-element.22), calls=%async_computation | async-start | bytes 16384 | tf_op jit(solution)/shard_map/all_to_all | solution.py:366
  19.6 3.1 %copy-start.2 = (bf16[64,2048]{1,0:T(8,128)(2,1)}, bf16[64,2048]{1,0:T(8,128)(2,1)S(1)}, u32[]{:S(2)}) copy-start(bf16[64,2048]{1,0:T(8,128)(2,1)S(1)} %collective-permute-done._.refs_0_) | copy-start | bytes 786436
  22.7 5.2 %copy-start.12 = (s32[128,16]{0,1:T(8,128)S(1)}, s32[128,16]{0,1:T(8,128)}, u32[]{:S(2)}) copy-start(s32[128,16]{0,1:T(8,128)} %param.11) | copy-start | bytes 24580
  22.7 5.2 %copy-start.7 = (s32[128]{0:T(128)S(1)}, s32[128]{0:T(128)}, u32[]{:S(2)}) copy-start(s32[128]{0:T(128)} %param.12) | copy-start | bytes 1540
  22.7 5.2 %copy-start.8 = (s32[128,4]{0,1:T(4,128)S(1)}, s32[128,4]{0,1:T(4,128)}, u32[]{:S(2)}) copy-start(s32[128,4]{0,1:T(4,128)} %param.13) | copy-start | bytes 6148
  22.7 5.2 %copy-start.9 = (f32[128,4]{0,1:T(4,128)S(1)}, f32[128,4]{0,1:T(4,128)}, u32[]{:S(2)}) copy-start(f32[128,4]{0,1:T(4,128)} %param.14) | copy-start | bytes 6148
  22.7 31.9 %copy-start.6 = (bf16[128,2048]{1,0:T(8,128)(2,1)S(1)}, bf16[128,2048]{1,0:T(8,128)(2,1)}, u32[]{:S(2)}) copy-start(bf16[128,2048]{1,0:T(8,128)(2,1)} %values_ref.1) | copy-start | bytes 1572868
  22.7 31.8 %all-to-all-start.1 = ((bf16[16,16,2048]{2,1,0:T(8,128)(2,1)}), bf16[16,16,2048]{2,1,0:T(8,128)(2,1)S(1)}, u32[]{:S(2)}, u32[]{:S(2)}) async-start(bf16[16,16,2048]{2,1,0:T(8,128)(2,1)} %bitcast.25), calls=%async_computation.1 | async-start | bytes 2097152 | tf_op jit(solution)/shard_map/all_to_all | solution.py:366
  28.8 29.0 %copy-start.4 = (f32[128,128]{1,0:T(8,128)}, f32[128,128]{1,0:T(8,128)S(1)}, u32[]{:S(2)}) copy-start(f32[128,128]{1,0:T(8,128)S(1)} %get-tuple-element.25.columns_ref) | copy-start | bytes 196612
  28.8 25.8 %collective-permute-start.1 = (s32[4,128]{1,0:T(4,128)S(1)}, s32[4,128]{1,0:T(4,128)S(1)}, u32[]{:S(2)}, u32[]{:S(2)}) collective-permute-start(s32[4,128]{1,0:T(4,128)S(1)} %get-tuple-element.28), channel_id=1, source_target_pairs={{0,8},{1,9},{2,10},{3,11},{4,12},{5,13},{6,14},{7,15},{8,0},{9,1},... | collective-permute-start | bytes 6152 | tf_op jit(solution)/shard_map/ppermute | solution.py:401
  31.7 22.9 %collective-permute-start.2 = (f32[4,128]{1,0:T(4,128)S(1)}, f32[4,128]{1,0:T(4,128)S(1)}, u32[]{:S(2)}, u32[]{:S(2)}) collective-permute-start(f32[4,128]{1,0:T(4,128)S(1)} %get-tuple-element.29), channel_id=1, source_target_pairs={{0,8},{1,9},{2,10},{3,11},{4,12},{5,13},{6,14},{7,15},{8,0},{9,1},... | collective-permute-start | bytes 6152 | tf_op jit(solution)/shard_map/ppermute | solution.py:401
  55.0 25.5 %collective-permute-start.3 = (bf16[128,2048]{1,0:T(8,128)(2,1)S(1)}, bf16[128,2048]{1,0:T(8,128)(2,1)S(1)}, u32[]{:S(2)}, u32[]{:S(2)}) collective-permute-start(bf16[128,2048]{1,0:T(8,128)(2,1)S(1)} %token_state.1.state_ref._), channel_id=1, source_target_pairs={{0,8},{1,9},{2,10},{3,11},{4,12},{5,13},{6,14},{7,15},{8,0},{9,1},... | collective-permute-start | bytes 1572872 | tf_op jit(solution)/shard_map/ppermute | solution.py:401
  56.5 24.0 %copy-start = (bf16[128,2048]{1,0:T(8,128)(2,1)S(1)}, bf16[128,2048]{1,0:T(8,128)(2,1)}, u32[]{:S(2)}) copy-start(bf16[128,2048]{1,0:T(8,128)(2,1)} %refs_0_.5) | copy-start | bytes 1572868
  57.7 26.6 %all-to-all-start.2 = ((bf16[8,24,2048]{2,1,0:T(8,128)(2,1)}), bf16[8,24,2048]{2,1,0:T(8,128)(2,1)}, u32[]{:S(2)}, u32[]{:S(2)}) async-start(bf16[8,24,2048]{2,1,0:T(8,128)(2,1)} %bitcast.27), calls=%async_computation.2 | async-start | bytes 1572864 | tf_op jit(solution)/shard_map/all_to_all | solution.py:366
  84.3 23.6 %all-to-all-start.4 = ((bf16[8,48,2048]{2,1,0:T(8,128)(2,1)}), bf16[8,48,2048]{2,1,0:T(8,128)(2,1)S(1)}, u32[]{:S(2)}, u32[]{:S(2)}) async-start(bf16[8,48,2048]{2,1,0:T(8,128)(2,1)} %bitcast.22), calls=%async_computation.4 | async-start | bytes 3145728 | tf_op jit(solution)/shard_map/all_to_all | solution.py:366
  107.9 1.1 copy-start.11
  109.1 29.2 %all-to-all-start.3 = ((bf16[8,48,2048]{2,1,0:T(8,128)(2,1)}), bf16[8,48,2048]{2,1,0:T(8,128)(2,1)S(1)}, u32[]{:S(2)}, u32[]{:S(2)}) async-start(bf16[8,48,2048]{2,1,0:T(8,128)(2,1)} %near_first.1.refs_0_), calls=%async_computation.3 | async-start | bytes 3145728 | tf_op jit(solution)/shard_map/all_to_all | solution.py:366
  112.7 25.5 %collective-permute-start.4 = (bf16[64,2048]{1,0:T(8,128)(2,1)S(1)}, bf16[64,2048]{1,0:T(8,128)(2,1)S(1)}, u32[]{:S(2)}, u32[]{:S(2)}) collective-permute-start(bf16[64,2048]{1,0:T(8,128)(2,1)S(1)} %get-tuple-element.35), channel_id=1, source_target_pairs={{0,8},{1,9},{2,10},{3,11},{4,12},{5,13},{6,14},{7,15},{8,0},{9,1},... | collective-permute-start | bytes 786440 | tf_op jit(solution)/shard_map/ppermute | solution.py:401
  138.3 1.2 copy-start.10
  139.5 24.1 %all-to-all-start.5 = ((bf16[8,48,2048]{2,1,0:T(8,128)(2,1)}), bf16[8,48,2048]{2,1,0:T(8,128)(2,1)S(1)}, u32[]{:S(2)}, u32[]{:S(2)}) async-start(bf16[8,48,2048]{2,1,0:T(8,128)(2,1)} %ordered.3), calls=%async_computation.5 | async-start | bytes 3145728 | tf_op jit(solution)/shard_map/all_to_all | solution.py:366
  143.5 20.1 %copy-start.3 = (bf16[64,2048]{1,0:T(8,128)(2,1)S(1)}, bf16[64,2048]{1,0:T(8,128)(2,1)}, u32[]{:S(2)}) copy-start(bf16[64,2048]{1,0:T(8,128)(2,1)} %copy-done.2) | copy-start | bytes 786436
  165.2 25.8 %collective-permute-start.5 = (bf16[128,2048]{1,0:T(8,128)(2,1)S(1)}, bf16[128,2048]{1,0:T(8,128)(2,1)S(1)}, u32[]{:S(2)}, u32[]{:S(2)}) collective-permute-start(bf16[128,2048]{1,0:T(8,128)(2,1)S(1)} %get-tuple-element.36.refs_1_), channel_id=1, source_target_pairs={{0,8},{1,9},{2,10},{3,11},{4,12},{5,13},{6,14},{7,15},{8,0},{9,1},... | collective-permute-start | bytes 1572872 | tf_op jit(solution)/shard_map/ppermute | solution.py:401
  167.0 27.7 %all-to-all-start.6 = ((bf16[8,24,2048]{2,1,0:T(8,128)(2,1)}), bf16[8,24,2048]{2,1,0:T(8,128)(2,1)}, u32[]{:S(2)}, u32[]{:S(2)}) async-start(bf16[8,24,2048]{2,1,0:T(8,128)(2,1)} %ordered.4), calls=%async_computation.6 | async-start | bytes 1572864 | tf_op jit(solution)/shard_map/all_to_all | solution.py:366
  171.2 23.4 %collective-permute-start.6 = (f32[8,128]{1,0:T(8,128)}, f32[8,128]{1,0:T(8,128)}, u32[]{:S(2)}, u32[]{:S(2)}) collective-permute-start(f32[8,128]{1,0:T(8,128)} %get-tuple-element.39), channel_id=1, source_target_pairs={{0,8},{1,9},{2,10},{3,11},{4,12},{5,13},{6,14},{7,15},{8,0},{9,1},... | collective-permute-start | bytes 12296 | tf_op jit(solution)/shard_map/ppermute | solution.py:401
  191.0 1.0 copy-start.1
  191.0 1.0 copy-start.5

commit v18 on v17

--- a/solution.py
+++ b/solution.py
@@ -289,7 +289,7 @@
             out_ref[2 * pair + odd] = jnp.concatenate(parts, axis=0).astype(BF16)
 
 
-def expert_call(name, first, count, rows_in, weights, front=(), after=()):
+def expert_call(name, first, count, rows_in, weights, front=(), after=(), grant=46):
     w_gate, w_up, w_down = weights
     _, features, width = w_gate.shape
     half = rows_in.shape[0]
@@ -314,7 +314,7 @@
             pltpu.SemaphoreType.DMA((held, 10)),
             pltpu.SemaphoreType.DMA,
         ],
-        compiler_params=pltpu.CompilerParams(vmem_limit_bytes=46 * 1024 * 1024),
+        compiler_params=pltpu.CompilerParams(vmem_limit_bytes=grant * 1024 * 1024),
         cost_estimate=pl.CostEstimate(
             flops=12 * count * rows * features * width,
             bytes_accessed=6 * count * features * width,
@@ -535,9 +535,9 @@
 
     weights = (w_gate, w_up, w_down)
     sent_both = expert_call(
-        "near_first", 0, 2, near_rows, weights, front=(later_sent,), after=(far_sent,)
-    )
-    far_out = expert_call("far_experts", 0, 4, far_rows, weights, after=(sent_both,))
+        "near_first", 0, 2, near_rows, weights, front=(later_sent,), after=(far_sent,), grant=63
+    )
+    far_out = expert_call("far_experts", 0, 4, far_rows, weights, after=(sent_both,), grant=63)
     both = swap(sent_both, halves)
     far_back = swap(ordered(in_hbm(far_out), in_hbm(both), other_grads[1]), halves)
     near_out = expert_call("near_second", 2, 2, both, weights)
@@ -566,11 +566,6 @@
             name=name,
         )(slot_of, columns, back.reshape(-1, features), *operands, *after)
 
-    far_mixed, far_grads = mixed_rows(
-        "mix_far", far_of, far_columns, far_back, other_grads, BF16, after=(in_hbm(near_out),)
-    )
-    near_back = swap(ordered(in_hbm(near_out), far_mixed), halves)
-    far_sums = ordered(mirrored(far_mixed), flops=400_000_000_000)
     sums, sum_grads = mixed_rows(
         "mix_first",
         near_of,
@@ -578,8 +573,17 @@
         in_hbm(both.reshape(slots, features)),
         (out_grad,),
         F32,
-        added=(far_sums,),
-    )
+    )
+    far_mixed, far_grads = mixed_rows(
+        "mix_far",
+        far_of,
+        far_columns,
+        far_back,
+        other_grads,
+        BF16,
+        after=(in_hbm(near_out), sum_grads),
+    )
+    near_back = swap(ordered(in_hbm(near_out), far_mixed), halves)
     mixed, grads = mixed_rows(
         "mix_second",
         near_of,
@@ -589,7 +593,7 @@
         BF16,
         start=slots,
         lines=TOP,
-        added=(sums,),
+        added=(sums, ordered(mirrored(far_mixed), flops=400_000_000_000)),
         added_grads=(sum_grads, mirrored(far_grads)),
     )
     return mixed, grads.T

time: 198 us -> 197 us (level)
  local copies, waits for them, and re-layouts: 3.41 us -> 1.03 us
    unnamed x26, local copies, waits for them, and re-layouts: 3.41 us -> 1.03 us
  transfers between devices with their start and end apart: 14 -> 14, of which waited for: 8 -> 10; matrix products, arithmetic and copies ran while one was open for 0% -> 0% of each run, Pallas kernels for 31% -> 32%
where the time goes in v18:
time: 197 us; the launch traced here: 196 us
  waiting for transfers between devices  80.6 us (41%)
  Pallas kernels  71.8 us (36%)
  starting transfers between devices  41.9 us (21%)
    ppermute x7, waiting for transfers between devices, mirrored(): return lax.ppermute(array, 'expert', pairs)  59.1 us
    pallas_call x3, Pallas kernels, expert_call(): pl.pallas_call(functools.partial(expert_kernel, first, count, bool(front)...  53.2 us
    all_to_all x7, starting transfers between devices, swap(): lax.all_to_all(array, 'expert', split_axis=0, concat_axis=0, tiled=True,...  29.9 us
    all_to_all x7, waiting for transfers between devices, swap(): lax.all_to_all(array, 'expert', split_axis=0, concat_axis=0, tiled=True,...  21.5 us
    ppermute x7, starting transfers between devices, mirrored(): return lax.ppermute(array, 'expert', pairs)  12 us
    pallas_call x3, Pallas kernels, mixed_rows(): pl.pallas_call(functools.partial(mix_kernel, len(grads), len(added), len(...  7.15 us
  transfers between devices with their start and end apart: 14, of which 10 were waited for; matrix products, arithmetic and copies ran while one was open for 0% of the time, Pallas kernels for 32%

profile of v18, /device:TPU:0, one launch (start us, length us, event | category | flops | bytes accessed | tf_op | source)
XLA Modules:
  0.0 196.4 jit_solution(17989363900015549818)
XLA Ops:
  0.6 1.7 repeat_rows.1
  2.3 4.0 %collective-permute-start = (bf16[64,2048]{1,0:T(8,128)(2,1)}, bf16[64,2048]{1,0:T(8,128)(2,1)S(1)}, u32[]{:S(2)}, u32[]{:S(2)}) collective-permute-start(bf16[64,2048]{1,0:T(8,128)(2,1)} %get-tuple-element.23), channel_id=1, source_target_pairs={{0,8},{1,9},{2,10},{3,11},{4,12},{5,13},{6,14},{7,15},{8,0},{9,1},... | collective-permute-start | bytes 786440 | tf_op jit(solution)/shard_map/ppermute | solution.py:401
  6.4 3.9 %all-to-all-start = ((s32[16,1,128]{2,1,0:T(1,128)}), s32[16,1,128]{2,1,0:T(1,128)S(1)}, u32[]{:S(2)}, u32[]{:S(2)}) async-start(s32[16,1,128]{2,1,0:T(1,128)} %get-tuple-element.22), calls=%async_computation | async-start | bytes 16384 | tf_op jit(solution)/shard_map/all_to_all | solution.py:366
  10.3 0.1 pad_add_fusion.me_ref
  10.4 9.2 %all-to-all-done.rows_ref = s32[16,1,128]{2,1,0:T(1,128)S(1)} async-done(((s32[16,1,128]{2,1,0:T(1,128)}), s32[16,1,128]{2,1,0:T(1,128)S(1)}, u32[]{:S(2)}, u32[]{:S(2)}) %all-to-all-start) | async-done | bytes 8224 | tf_op jit(solution)/shard_map/all_to_all | solution.py:366
  19.6 0.0 collective-permute-done._.refs_0_
  19.6 3.0 %fetch_rows.1._ = bf16[256,2048]{1,0:T(8,128)(2,1)} custom-call(s32[2]{0:T(128)S(1)} %pad_add_fusion.me_ref, s32[16,1,128]{2,1,0:T(1,128)S(1)} %all-to-all-done.rows_ref, bf16[256,2048]{1,0:T(8,128)(2,1)} %table_hbm.1, bf16[64,2048]{1,0:T(8,128)(2,1)S(1)} %collective-permute-done._.refs_0_), custom_call_target="tpu_custom_call" | custom-call | tf_op jit(solution)/shard_map/fetch_rows/pallas_call | solution.py:434
  22.7 0.0 copy-start.12
  22.7 0.0 copy-start.9
  22.7 0.0 copy-start.10
  22.7 0.0 copy-start.11
  22.7 0.0 copy-start.8
  22.7 5.1 %all-to-all-start.1 = ((bf16[16,16,2048]{2,1,0:T(8,128)(2,1)}), bf16[16,16,2048]{2,1,0:T(8,128)(2,1)S(1)}, u32[]{:S(2)}, u32[]{:S(2)}) async-start(bf16[16,16,2048]{2,1,0:T(8,128)(2,1)} %bitcast.24), calls=%async_computation.1 | async-start | bytes 2097152 | tf_op jit(solution)/shard_map/all_to_all | solution.py:366
  27.9 0.9 near_plan.1
  28.8 2.9 %collective-permute-start.1 = (s32[4,128]{1,0:T(4,128)S(1)}, s32[4,128]{1,0:T(4,128)S(1)}, u32[]{:S(2)}, u32[]{:S(2)}) collective-permute-start(s32[4,128]{1,0:T(4,128)S(1)} %get-tuple-element.28), channel_id=1, source_target_pairs={{0,8},{1,9},{2,10},{3,11},{4,12},{5,13},{6,14},{7,15},{8,0},{9,1},... | collective-permute-start | bytes 6152 | tf_op jit(solution)/shard_map/ppermute | solution.py:401
  31.7 0.1 collective-permute-start.2
  31.8 22.8 %collective-permute-done.1.ids_ref = s32[4,128]{1,0:T(4,128)S(1)} collective-permute-done((s32[4,128]{1,0:T(4,128)S(1)}, s32[4,128]{1,0:T(4,128)S(1)}, u32[]{:S(2)}, u32[]{:S(2)}) %collective-permute-start.1) | collective-permute-done | bytes 2080 | tf_op jit(solution)/shard_map/ppermute | solution.py:401
  54.5 0.0 collective-permute-done.2.weights_ref
  54.6 0.0 all-to-all-done.1
  54.6 0.4 token_state.1.state_ref._
  55.0 1.5 collective-permute-start.3
  56.5 1.2 first_slots.1
  57.7 4.2 %all-to-all-start.2 = ((bf16[8,24,2048]{2,1,0:T(8,128)(2,1)}), bf16[8,24,2048]{2,1,0:T(8,128)(2,1)}, u32[]{:S(2)}, u32[]{:S(2)}) async-start(bf16[8,24,2048]{2,1,0:T(8,128)(2,1)} %bitcast.26), calls=%async_computation.2 | async-start | bytes 1572864 | tf_op jit(solution)/shard_map/all_to_all | solution.py:366
  61.9 0.8 far_plan.1
  62.8 17.7 %collective-permute-done.3.state_ref = bf16[128,2048]{1,0:T(8,128)(2,1)S(1)} collective-permute-done((bf16[128,2048]{1,0:T(8,128)(2,1)S(1)}, bf16[128,2048]{1,0:T(8,128)(2,1)S(1)}, u32[]{:S(2)}, u32[]{:S(2)}) %collective-permute-start.3) | collective-permute-done | bytes 524320 | tf_op jit(solution)/shard_map/ppermute | solution.py:401
  80.5 2.2 %far_slots.1 = (bf16[384,2048]{1,0:T(8,128)(2,1)}, bf16[64,2048]{1,0:T(8,128)(2,1)}) custom-call(bf16[384,128]{1,0:T(8,128)(2,1)S(1)} %get-tuple-element.31.pick_ref, bf16[128,2048]{1,0:T(8,128)(2,1)S(1)} %collective-permute-done.3.state_ref, bf16[128,2048]{1,0:T(8,128)(2,1)S(1)} %copy-done), custom_call_target="tpu_custom_call" | custom-call | flops 399999991808 | bytes 3145728 | tf_op jit(solution)/shard_map/far_slots/pallas_call | solution.py:515
  82.6 1.7 all-to-all-done.2.rows_hbm
  84.3 4.3 %all-to-all-start.4 = ((bf16[8,48,2048]{2,1,0:T(8,128)(2,1)}), bf16[8,48,2048]{2,1,0:T(8,128)(2,1)}, u32[]{:S(2)}, u32[]{:S(2)}) async-start(bf16[8,48,2048]{2,1,0:T(8,128)(2,1)} %bitcast.21), calls=%async_computation.4 | async-start | bytes 3145728 | tf_op jit(solution)/shard_map/all_to_all | solution.py:366
  88.6 1.2 later_slots.1
  89.9 14.9 %near_first.1.refs_0_ = bf16[8,48,2048]{2,1,0:T(8,128)(2,1)} custom-call(bf16[8,24,2048]{2,1,0:T(8,128)(2,1)} %all-to-all-done.2.rows_hbm, bf16[8,24,2048]{2,1,0:T(8,128)(2,1)} %bitcast.25, bf16[8,48,2048]{2,1,0:T(8,128)(2,1)} %bitcast.23, bf16[4,2048,1408]{2,1,0:T(8,128)(2,1)} %refs_1_.3, bf16[4,2048,1408]{2,1,0:T(8,128)(2,1)} %refs_2_.5, ...), custom_call_target="tpu_custom_call" | custom-call | flops 6643777536 | bytes 34603008 | tf_op jit(solution)/shard_map/near_first/pallas_call | solution.py:301
  104.8 3.9 %all-to-all-done.4.rows_hbm = bf16[8,48,2048]{2,1,0:T(8,128)(2,1)} async-done(((bf16[8,48,2048]{2,1,0:T(8,128)(2,1)}), bf16[8,48,2048]{2,1,0:T(8,128)(2,1)}, u32[]{:S(2)}, u32[]{:S(2)}) %all-to-all-start.4) | async-done | bytes 1572896 | tf_op jit(solution)/shard_map/all_to_all | solution.py:366
  108.7 4.3 %all-to-all-start.3 = ((bf16[8,48,2048]{2,1,0:T(8,128)(2,1)}), bf16[8,48,2048]{2,1,0:T(8,128)(2,1)}, u32[]{:S(2)}, u32[]{:S(2)}) async-start(bf16[8,48,2048]{2,1,0:T(8,128)(2,1)} %near_first.1.refs_0_), calls=%async_computation.3 | async-start | bytes 3145728 | tf_op jit(solution)/shard_map/all_to_all | solution.py:366
  113.0 0.5 collective-permute-start.4
  113.5 24.4 %far_experts.1.refs_0_ = bf16[8,48,2048]{2,1,0:T(8,128)(2,1)} custom-call(bf16[8,48,2048]{2,1,0:T(8,128)(2,1)} %all-to-all-done.4.rows_hbm, bf16[8,48,2048]{2,1,0:T(8,128)(2,1)} %near_first.1.refs_0_, bf16[4,2048,1408]{2,1,0:T(8,128)(2,1)} %refs_1_.3, bf16[4,2048,1408]{2,1,0:T(8,128)(2,1)} %refs_2_.5, bf16[4,1408,2048]{2,1,0:T(8,128)(2,1)} %refs_3_.3), custom_call_target="tpu_custom_call" | custom-call | flops 13287555072 | bytes 69206016 | tf_op jit(solution)/shard_map/far_experts/pallas_call | solution.py:301
  137.9 0.8 all-to-all-done.3.rows_hbm.refs_1_
  138.7 3.9 %all-to-all-start.5 = ((bf16[8,48,2048]{2,1,0:T(8,128)(2,1)}), bf16[8,48,2048]{2,1,0:T(8,128)(2,1)S(1)}, u32[]{:S(2)}, u32[]{:S(2)}) async-start(bf16[8,48,2048]{2,1,0:T(8,128)(2,1)} %ordered.3), calls=%async_computation.5 | async-start | bytes 3145728 | tf_op jit(solution)/shard_map/all_to_all | solution.py:366
  142.6 2.6 %mix_first.1 = (f32[128,2048]{1,0:T(8,128)S(1)}, f32[8,128]{1,0:T(8,128)S(1)}) custom-call(s32[128,128]{1,0:T(8,128)S(1)} %get-tuple-element.24.slots_ref, f32[128,128]{1,0:T(8,128)S(1)} %copy-done.6, bf16[384,2048]{1,0:T(8,128)(2,1)} %bitcast.11.back_ref, bf16[128,2048]{1,0:T(8,128)(2,1)S(1)} %copy-done), custom_call_target="tpu_custom_call" | custom-call | tf_op jit(solution)/shard_map/mix_first/pallas_call | solution.py:560
  145.3 1.0 copy-done.1
  146.2 13.8 %near_second.1.refs_2_.refs_0_ = bf16[8,24,2048]{2,1,0:T(8,128)(2,1)} custom-call(bf16[8,48,2048]{2,1,0:T(8,128)(2,1)} %all-to-all-done.3.rows_hbm.refs_1_, bf16[4,2048,1408]{2,1,0:T(8,128)(2,1)} %refs_1_.3, bf16[4,2048,1408]{2,1,0:T(8,128)(2,1)} %refs_2_.5, bf16[4,1408,2048]{2,1,0:T(8,128)(2,1)} %refs_3_.3), custom_call_target="tpu_custom_call" | custom-call | flops 6643777536 | bytes 34603008 | tf_op jit(solution)/shard_map/near_second/pallas_call | solution.py:301
  160.1 2.3 %all-to-all-done.5 = bf16[8,48,2048]{2,1,0:T(8,128)(2,1)S(1)} async-done(((bf16[8,48,2048]{2,1,0:T(8,128)(2,1)}), bf16[8,48,2048]{2,1,0:T(8,128)(2,1)S(1)}, u32[]{:S(2)}, u32[]{:S(2)}) %all-to-all-start.5) | async-done | bytes 1572896 | tf_op jit(solution)/shard_map/all_to_all | solution.py:366
  162.4 1.7 mix_far.1
  164.1 2.3 %collective-permute-start.5 = (bf16[128,2048]{1,0:T(8,128)(2,1)S(1)}, bf16[128,2048]{1,0:T(8,128)(2,1)S(1)}, u32[]{:S(2)}, u32[]{:S(2)}) collective-permute-start(bf16[128,2048]{1,0:T(8,128)(2,1)S(1)} %get-tuple-element.37.refs_1_), channel_id=1, source_target_pairs={{0,8},{1,9},{2,10},{3,11},{4,12},{5,13},{6,14},{7,15},{8,0},{9,1},... | collective-permute-start | bytes 1572872 | tf_op jit(solution)/shard_map/ppermute | solution.py:401
  166.4 4.2 %all-to-all-start.6 = ((bf16[8,24,2048]{2,1,0:T(8,128)(2,1)}), bf16[8,24,2048]{2,1,0:T(8,128)(2,1)}, u32[]{:S(2)}, u32[]{:S(2)}) async-start(bf16[8,24,2048]{2,1,0:T(8,128)(2,1)} %ordered.4), calls=%async_computation.6 | async-start | bytes 1572864 | tf_op jit(solution)/shard_map/all_to_all | solution.py:366
  170.6 0.7 collective-permute-start.6
  171.3 18.5 %collective-permute-done.5.refs_0_ = bf16[128,2048]{1,0:T(8,128)(2,1)S(1)} collective-permute-done((bf16[128,2048]{1,0:T(8,128)(2,1)S(1)}, bf16[128,2048]{1,0:T(8,128)(2,1)S(1)}, u32[]{:S(2)}, u32[]{:S(2)}) %collective-permute-start.5) | collective-permute-done | bytes 524320 | tf_op jit(solution)/shard_map/ppermute | solution.py:401
  189.8 0.1 collective-permute-done.6.refs_4_
  190.0 3.5 %all-to-all-done.6 = bf16[8,24,2048]{2,1,0:T(8,128)(2,1)} async-done(((bf16[8,24,2048]{2,1,0:T(8,128)(2,1)}), bf16[8,24,2048]{2,1,0:T(8,128)(2,1)}, u32[]{:S(2)}, u32[]{:S(2)}) %all-to-all-start.6) | async-done | bytes 786464 | tf_op jit(solution)/shard_map/all_to_all | solution.py:366
  193.5 2.9 %mix_second.1 = (bf16[128,2048]{1,0:T(8,128)(2,1)}, f32[4,128]{1,0:T(4,128)}) custom-call(s32[128,128]{1,0:T(8,128)S(1)} %get-tuple-element.24.slots_ref, f32[128,128]{1,0:T(8,128)S(1)} %copy-done.7, bf16[192,2048]{1,0:T(8,128)(2,1)} %bitcast.12.back_ref, bf16[128,2048]{1,0:T(8,128)(2,1)S(1)} %copy-done, f32[128,2048]{1,0:T(8,128)S(1)} %copy-done.2, ...), custom_call_target="tpu_custom_call" | custom-call | tf_op jit(solution)/shard_map/mix_second/pallas_call | solution.py:560
  (25 shorter events, 0.1 us)
Async XLA Ops:
  2.3 17.3 %collective-permute-start = (bf16[64,2048]{1,0:T(8,128)(2,1)}, bf16[64,2048]{1,0:T(8,128)(2,1)S(1)}, u32[]{:S(2)}, u32[]{:S(2)}) collective-permute-start(bf16[64,2048]{1,0:T(8,128)(2,1)} %get-tuple-element.23), channel_id=1, source_target_pairs={{0,8},{1,9},{2,10},{3,11},{4,12},{5,13},{6,14},{7,15},{8,0},{9,1},... | collective-permute-start | bytes 786440 | tf_op jit(solution)/shard_map/ppermute | solution.py:401
  6.4 13.2 %all-to-all-start = ((s32[16,1,128]{2,1,0:T(1,128)}), s32[16,1,128]{2,1,0:T(1,128)S(1)}, u32[]{:S(2)}, u32[]{:S(2)}) async-start(s32[16,1,128]{2,1,0:T(1,128)} %get-tuple-element.22), calls=%async_computation | async-start | bytes 16384 | tf_op jit(solution)/shard_map/all_to_all | solution.py:366
  19.6 3.1 %copy-start.3 = (bf16[64,2048]{1,0:T(8,128)(2,1)}, bf16[64,2048]{1,0:T(8,128)(2,1)S(1)}, u32[]{:S(2)}) copy-start(bf16[64,2048]{1,0:T(8,128)(2,1)S(1)} %collective-permute-done._.refs_0_) | copy-start | bytes 786436
  22.7 5.2 %copy-start.12 = (s32[128,16]{0,1:T(8,128)S(1)}, s32[128,16]{0,1:T(8,128)}, u32[]{:S(2)}) copy-start(s32[128,16]{0,1:T(8,128)} %param.11) | copy-start | bytes 24580
  22.7 5.2 %copy-start.9 = (s32[128]{0:T(128)S(1)}, s32[128]{0:T(128)}, u32[]{:S(2)}) copy-start(s32[128]{0:T(128)} %param.12) | copy-start | bytes 1540
  22.7 5.2 %copy-start.10 = (s32[128,4]{0,1:T(4,128)S(1)}, s32[128,4]{0,1:T(4,128)}, u32[]{:S(2)}) copy-start(s32[128,4]{0,1:T(4,128)} %param.13) | copy-start | bytes 6148
  22.7 5.2 %copy-start.11 = (f32[128,4]{0,1:T(4,128)S(1)}, f32[128,4]{0,1:T(4,128)}, u32[]{:S(2)}) copy-start(f32[128,4]{0,1:T(4,128)} %param.14) | copy-start | bytes 6148
  22.7 31.9 %copy-start.8 = (bf16[128,2048]{1,0:T(8,128)(2,1)S(1)}, bf16[128,2048]{1,0:T(8,128)(2,1)}, u32[]{:S(2)}) copy-start(bf16[128,2048]{1,0:T(8,128)(2,1)} %values_ref.1) | copy-start | bytes 1572868
  22.7 31.8 %all-to-all-start.1 = ((bf16[16,16,2048]{2,1,0:T(8,128)(2,1)}), bf16[16,16,2048]{2,1,0:T(8,128)(2,1)S(1)}, u32[]{:S(2)}, u32[]{:S(2)}) async-start(bf16[16,16,2048]{2,1,0:T(8,128)(2,1)} %bitcast.24), calls=%async_computation.1 | async-start | bytes 2097152 | tf_op jit(solution)/shard_map/all_to_all | solution.py:366
  28.8 28.9 %copy-start.5 = (f32[128,128]{1,0:T(8,128)}, f32[128,128]{1,0:T(8,128)S(1)}, u32[]{:S(2)}) copy-start(f32[128,128]{1,0:T(8,128)S(1)} %get-tuple-element.25.columns_ref) | copy-start | bytes 196612
  28.8 25.8 %collective-permute-start.1 = (s32[4,128]{1,0:T(4,128)S(1)}, s32[4,128]{1,0:T(4,128)S(1)}, u32[]{:S(2)}, u32[]{:S(2)}) collective-permute-start(s32[4,128]{1,0:T(4,128)S(1)} %get-tuple-element.28), channel_id=1, source_target_pairs={{0,8},{1,9},{2,10},{3,11},{4,12},{5,13},{6,14},{7,15},{8,0},{9,1},... | collective-permute-start | bytes 6152 | tf_op jit(solution)/shard_map/ppermute | solution.py:401
  31.7 22.9 %collective-permute-start.2 = (f32[4,128]{1,0:T(4,128)S(1)}, f32[4,128]{1,0:T(4,128)S(1)}, u32[]{:S(2)}, u32[]{:S(2)}) collective-permute-start(f32[4,128]{1,0:T(4,128)S(1)} %get-tuple-element.29), channel_id=1, source_target_pairs={{0,8},{1,9},{2,10},{3,11},{4,12},{5,13},{6,14},{7,15},{8,0},{9,1},... | collective-permute-start | bytes 6152 | tf_op jit(solution)/shard_map/ppermute | solution.py:401
  55.0 25.5 %collective-permute-start.3 = (bf16[128,2048]{1,0:T(8,128)(2,1)S(1)}, bf16[128,2048]{1,0:T(8,128)(2,1)S(1)}, u32[]{:S(2)}, u32[]{:S(2)}) collective-permute-start(bf16[128,2048]{1,0:T(8,128)(2,1)S(1)} %token_state.1.state_ref._), channel_id=1, source_target_pairs={{0,8},{1,9},{2,10},{3,11},{4,12},{5,13},{6,14},{7,15},{8,0},{9,1},... | collective-permute-start | bytes 1572872 | tf_op jit(solution)/shard_map/ppermute | solution.py:401
  56.5 24.0 %copy-start = (bf16[128,2048]{1,0:T(8,128)(2,1)S(1)}, bf16[128,2048]{1,0:T(8,128)(2,1)}, u32[]{:S(2)}) copy-start(bf16[128,2048]{1,0:T(8,128)(2,1)} %refs_0_.5) | copy-start | bytes 1572868
  57.7 26.6 %all-to-all-start.2 = ((bf16[8,24,2048]{2,1,0:T(8,128)(2,1)}), bf16[8,24,2048]{2,1,0:T(8,128)(2,1)}, u32[]{:S(2)}, u32[]{:S(2)}) async-start(bf16[8,24,2048]{2,1,0:T(8,128)(2,1)} %bitcast.26), calls=%async_computation.2 | async-start | bytes 1572864 | tf_op jit(solution)/shard_map/all_to_all | solution.py:366
  84.3 24.4 %all-to-all-start.4 = ((bf16[8,48,2048]{2,1,0:T(8,128)(2,1)}), bf16[8,48,2048]{2,1,0:T(8,128)(2,1)}, u32[]{:S(2)}, u32[]{:S(2)}) async-start(bf16[8,48,2048]{2,1,0:T(8,128)(2,1)} %bitcast.21), calls=%async_computation.4 | async-start | bytes 3145728 | tf_op jit(solution)/shard_map/all_to_all | solution.py:366
  108.7 30.0 %all-to-all-start.3 = ((bf16[8,48,2048]{2,1,0:T(8,128)(2,1)}), bf16[8,48,2048]{2,1,0:T(8,128)(2,1)}, u32[]{:S(2)}, u32[]{:S(2)}) async-start(bf16[8,48,2048]{2,1,0:T(8,128)(2,1)} %near_first.1.refs_0_), calls=%async_computation.3 | async-start | bytes 3145728 | tf_op jit(solution)/shard_map/all_to_all | solution.py:366
  113.0 24.9 %collective-permute-start.4 = (bf16[64,2048]{1,0:T(8,128)(2,1)}, bf16[64,2048]{1,0:T(8,128)(2,1)S(1)}, u32[]{:S(2)}, u32[]{:S(2)}) collective-permute-start(bf16[64,2048]{1,0:T(8,128)(2,1)} %get-tuple-element.35), channel_id=1, source_target_pairs={{0,8},{1,9},{2,10},{3,11},{4,12},{5,13},{6,14},{7,15},{8,0},{9,1},... | collective-permute-start | bytes 786440 | tf_op jit(solution)/shard_map/ppermute | solution.py:401
  138.7 3.9 %copy-start.6 = (f32[128,128]{1,0:T(8,128)S(1)}, f32[128,128]{1,0:T(8,128)}, u32[]{:S(2)}) copy-start(f32[128,128]{1,0:T(8,128)} %copy-done.5) | copy-start | bytes 196612
  138.7 23.7 %all-to-all-start.5 = ((bf16[8,48,2048]{2,1,0:T(8,128)(2,1)}), bf16[8,48,2048]{2,1,0:T(8,128)(2,1)S(1)}, u32[]{:S(2)}, u32[]{:S(2)}) async-start(bf16[8,48,2048]{2,1,0:T(8,128)(2,1)} %ordered.3), calls=%async_computation.5 | async-start | bytes 3145728 | tf_op jit(solution)/shard_map/all_to_all | solution.py:366
  145.3 1.0 copy-start.1
  146.2 16.2 %copy-start.4 = (bf16[64,2048]{1,0:T(8,128)(2,1)S(1)}, bf16[64,2048]{1,0:T(8,128)(2,1)}, u32[]{:S(2)}) copy-start(bf16[64,2048]{1,0:T(8,128)(2,1)} %copy-done.3) | copy-start | bytes 786436
  164.1 25.7 %collective-permute-start.5 = (bf16[128,2048]{1,0:T(8,128)(2,1)S(1)}, bf16[128,2048]{1,0:T(8,128)(2,1)S(1)}, u32[]{:S(2)}, u32[]{:S(2)}) collective-permute-start(bf16[128,2048]{1,0:T(8,128)(2,1)S(1)} %get-tuple-element.37.refs_1_), channel_id=1, source_target_pairs={{0,8},{1,9},{2,10},{3,11},{4,12},{5,13},{6,14},{7,15},{8,0},{9,1},... | collective-permute-start | bytes 1572872 | tf_op jit(solution)/shard_map/ppermute | solution.py:401
  166.4 27.1 %all-to-all-start.6 = ((bf16[8,24,2048]{2,1,0:T(8,128)(2,1)}), bf16[8,24,2048]{2,1,0:T(8,128)(2,1)}, u32[]{:S(2)}, u32[]{:S(2)}) async-start(bf16[8,24,2048]{2,1,0:T(8,128)(2,1)} %ordered.4), calls=%async_computation.6 | async-start | bytes 1572864 | tf_op jit(solution)/shard_map/all_to_all | solution.py:366
  170.6 19.3 %collective-permute-start.6 = (f32[8,128]{1,0:T(8,128)}, f32[8,128]{1,0:T(8,128)}, u32[]{:S(2)}, u32[]{:S(2)}) collective-permute-start(f32[8,128]{1,0:T(8,128)} %get-tuple-element.39), channel_id=1, source_target_pairs={{0,8},{1,9},{2,10},{3,11},{4,12},{5,13},{6,14},{7,15},{8,0},{9,1},... | collective-permute-start | bytes 12296 | tf_op jit(solution)/shard_map/ppermute | solution.py:401
  189.8 3.7 %copy-start.2 = (f32[128,2048]{1,0:T(8,128)S(1)}, f32[128,2048]{1,0:T(8,128)}, u32[]{:S(2)}) copy-start(f32[128,2048]{1,0:T(8,128)} %copy-done.1) | copy-start | bytes 3145732
  189.8 3.7 %copy-start.7 = (f32[128,128]{1,0:T(8,128)S(1)}, f32[128,128]{1,0:T(8,128)}, u32[]{:S(2)}) copy-start(f32[128,128]{1,0:T(8,128)} %copy-done.5) | copy-start | bytes 196612

commit v19 on v18

--- a/solution.py
+++ b/solution.py
@@ -204,7 +204,7 @@
         after + 4 :
     ]
     held, features, width = wg_ref.shape
-    half = rows_ref.shape[0]
+    half = x_ref.shape[1] // CAP
     up_cuts = ((0, 512), (512, 512), (1024, width - 1024))
     down_cuts = tuple((at, 512) for at in range(0, features, 512))
 
@@ -232,14 +232,23 @@
         copy.start()
 
     low = iota((PAIR, features), 0) < CAP
+    lines = rows_ref.shape[0] // half
+
+    def pair_rows(ref, pair):
+        block = 2 * PAIR
+        return ref[pair * block : (pair + 1) * block, :].astype(F32)
+
     for chunk in range(count // 2):
-        here = slice(chunk * PAIR, (chunk + 1) * PAIR)
         for quad in range(half // 4):
             ones, twos = [], []
-            for pair in range(2):
-                source = 4 * quad + 2 * pair
-                even = rows_ref[source, here, :].astype(F32)
-                odd = rows_ref[source + 1, here, :].astype(F32)
+            for pair in (2 * quad, 2 * quad + 1):
+                if lines == PAIR:
+                    rows = pair_rows(rows_ref, pair)
+                    even, odd = rows[:PAIR], rows[PAIR:]
+                else:
+                    here = slice(chunk * PAIR, (chunk + 1) * PAIR)
+                    even = pair_rows(rows_ref, 2 * pair)[here]
+                    odd = pair_rows(rows_ref, 2 * pair + 1)[here]
                 ones.append(jnp.where(low, even, odd))
                 twos.append(jnp.where(low, odd, even))
             rows = slice(quad * 2 * PAIR, (quad + 1) * 2 * PAIR)
@@ -277,16 +286,22 @@
                 refill(n, 1)
             n += 1
 
+    block = 2 * PAIR
     for pair in range(half // 2):
         rows = slice(pair * PAIR, (pair + 1) * PAIR)
         values = [result_ref[j, rows, :] for j in range(count)]
+        results = []
         for odd in range(2):
             parts = [
                 jnp.where(low, values[j + odd], values[j + 1 - odd]) for j in range(0, count, 2)
             ]
             if join:
-                parts = [front_ref[2 * pair + odd].astype(F32)] + parts
-            out_ref[2 * pair + odd] = jnp.concatenate(parts, axis=0).astype(BF16)
+                parts = [pair_rows(front_ref, pair)[odd * PAIR : (odd + 1) * PAIR]] + parts
+            results += parts
+        for n in range(0, len(results), 2):
+            at = (pair * len(results) + n) * PAIR
+            two = jnp.concatenate(results[n : n + 2], axis=0)
+            out_ref[at : at + block, :] = two.astype(BF16)
 
 
 def expert_call(name, first, count, rows_in, weights, front=(), after=(), grant=46):
@@ -294,13 +309,15 @@
     _, features, width = w_gate.shape
     half = rows_in.shape[0]
     rows = half * CAP
+    lines = count * CAP + len(front) * PAIR
+    rows_in, *front = [array.reshape(-1, features) for array in (rows_in, *front)]
     held = 2
     anywhere = pl.BlockSpec(memory_space=pl.ANY)
     hbm = pl.BlockSpec(memory_space=pltpu.HBM)
     vmem = pl.BlockSpec(memory_space=VMEM)
     return pl.pallas_call(
         functools.partial(expert_kernel, first, count, bool(front), len(after)),
-        out_shape=pltpu.HBM((half, count * CAP + len(front) * PAIR, features), BF16),
+        out_shape=pltpu.HBM((half * lines, features), BF16),
         in_specs=[hbm] + [vmem] * len(front) + [anywhere] * len(after) + [hbm] * 3,
         out_specs=vmem,
         scratch_shapes=[
@@ -323,7 +340,7 @@
         name=name,
     )(
         *[in_hbm(array) for array in (rows_in, *front, *after, w_gate, w_up, w_down)],
-    )
+    ).reshape(half, lines, features)
 
 
 def mix_kernel(grads, added, added_grads, start, slots_ref, columns_ref, back_ref, *refs):

time: 197 us -> 197 us (level)
  no operation moved by 1% of the time
where the time goes in v19:
time: 197 us; the launch traced here: 196 us
  waiting for transfers between devices  80.6 us (41%)
  Pallas kernels  71.8 us (36%)
  starting transfers between devices  41.9 us (21%)
    ppermute x7, waiting for transfers between devices, mirrored(): return lax.ppermute(array, 'expert', pairs)  59.1 us
    pallas_call x3, Pallas kernels, expert_call(): pl.pallas_call(functools.partial(expert_kernel, first, count, bool(front)...  53.2 us
    all_to_all x7, starting transfers between devices, swap(): lax.all_to_all(array, 'expert', split_axis=0, concat_axis=0, tiled=True,...  29.9 us
    all_to_all x7, waiting for transfers between devices, swap(): lax.all_to_all(array, 'expert', split_axis=0, concat_axis=0, tiled=True,...  21.5 us
    ppermute x7, starting transfers between devices, mirrored(): return lax.ppermute(array, 'expert', pairs)  12 us
    pallas_call x3, Pallas kernels, mixed_rows(): pl.pallas_call(functools.partial(mix_kernel, len(grads), len(added), len(...  7.15 us
  transfers between devices with their start and end apart: 14, of which 10 were waited for; matrix products, arithmetic and copies ran while one was open for 0% of the time, Pallas kernels for 32%

profile of v19, /device:TPU:0, one launch (start us, length us, event | category | flops | bytes accessed | tf_op | source)
XLA Modules:
  0.0 196.4 jit_solution(12950725407970534747)
XLA Ops:
  0.6 1.7 repeat_rows.1
  2.3 4.0 %collective-permute-start = (bf16[64,2048]{1,0:T(8,128)(2,1)}, bf16[64,2048]{1,0:T(8,128)(2,1)S(1)}, u32[]{:S(2)}, u32[]{:S(2)}) collective-permute-start(bf16[64,2048]{1,0:T(8,128)(2,1)} %get-tuple-element.23), channel_id=1, source_target_pairs={{0,8},{1,9},{2,10},{3,11},{4,12},{5,13},{6,14},{7,15},{8,0},{9,1},... | collective-permute-start | bytes 786440 | tf_op jit(solution)/shard_map/ppermute | solution.py:418
  6.4 3.9 %all-to-all-start = ((s32[16,1,128]{2,1,0:T(1,128)}), s32[16,1,128]{2,1,0:T(1,128)S(1)}, u32[]{:S(2)}, u32[]{:S(2)}) async-start(s32[16,1,128]{2,1,0:T(1,128)} %get-tuple-element.22), calls=%async_computation | async-start | bytes 16384 | tf_op jit(solution)/shard_map/all_to_all | solution.py:383
  10.3 0.1 pad_add_fusion.me_ref
  10.4 9.2 %all-to-all-done.rows_ref = s32[16,1,128]{2,1,0:T(1,128)S(1)} async-done(((s32[16,1,128]{2,1,0:T(1,128)}), s32[16,1,128]{2,1,0:T(1,128)S(1)}, u32[]{:S(2)}, u32[]{:S(2)}) %all-to-all-start) | async-done | bytes 8224 | tf_op jit(solution)/shard_map/all_to_all | solution.py:383
  19.6 0.0 collective-permute-done._.refs_0_
  19.6 3.0 %fetch_rows.1._ = bf16[256,2048]{1,0:T(8,128)(2,1)} custom-call(s32[2]{0:T(128)S(1)} %pad_add_fusion.me_ref, s32[16,1,128]{2,1,0:T(1,128)S(1)} %all-to-all-done.rows_ref, bf16[256,2048]{1,0:T(8,128)(2,1)} %table_hbm.1, bf16[64,2048]{1,0:T(8,128)(2,1)S(1)} %collective-permute-done._.refs_0_), custom_call_target="tpu_custom_call" | custom-call | tf_op jit(solution)/shard_map/fetch_rows/pallas_call | solution.py:451
  22.7 0.0 copy-start.12
  22.7 0.0 copy-start.9
  22.7 0.0 copy-start.10
  22.7 0.0 copy-start.11
  22.7 0.0 copy-start.8
  22.7 5.1 %all-to-all-start.1 = ((bf16[16,16,2048]{2,1,0:T(8,128)(2,1)}), bf16[16,16,2048]{2,1,0:T(8,128)(2,1)S(1)}, u32[]{:S(2)}, u32[]{:S(2)}) async-start(bf16[16,16,2048]{2,1,0:T(8,128)(2,1)} %bitcast.33), calls=%async_computation.1 | async-start | bytes 2097152 | tf_op jit(solution)/shard_map/all_to_all | solution.py:383
  27.9 0.9 near_plan.1
  28.8 2.9 %collective-permute-start.1 = (s32[4,128]{1,0:T(4,128)S(1)}, s32[4,128]{1,0:T(4,128)S(1)}, u32[]{:S(2)}, u32[]{:S(2)}) collective-permute-start(s32[4,128]{1,0:T(4,128)S(1)} %get-tuple-element.28), channel_id=1, source_target_pairs={{0,8},{1,9},{2,10},{3,11},{4,12},{5,13},{6,14},{7,15},{8,0},{9,1},... | collective-permute-start | bytes 6152 | tf_op jit(solution)/shard_map/ppermute | solution.py:418
  31.7 0.1 collective-permute-start.2
  31.8 22.8 %collective-permute-done.1.ids_ref = s32[4,128]{1,0:T(4,128)S(1)} collective-permute-done((s32[4,128]{1,0:T(4,128)S(1)}, s32[4,128]{1,0:T(4,128)S(1)}, u32[]{:S(2)}, u32[]{:S(2)}) %collective-permute-start.1) | collective-permute-done | bytes 2080 | tf_op jit(solution)/shard_map/ppermute | solution.py:418
  54.5 0.0 collective-permute-done.2.weights_ref
  54.6 0.0 all-to-all-done.1
  54.6 0.4 token_state.1.state_ref._
  55.0 1.5 collective-permute-start.3
  56.5 1.2 first_slots.1
  57.7 4.2 %all-to-all-start.2 = ((bf16[8,24,2048]{2,1,0:T(8,128)(2,1)}), bf16[8,24,2048]{2,1,0:T(8,128)(2,1)}, u32[]{:S(2)}, u32[]{:S(2)}) async-start(bf16[8,24,2048]{2,1,0:T(8,128)(2,1)} %bitcast.34), calls=%async_computation.2 | async-start | bytes 1572864 | tf_op jit(solution)/shard_map/all_to_all | solution.py:383
  61.9 0.8 far_plan.1
  62.8 17.7 %collective-permute-done.3.state_ref = bf16[128,2048]{1,0:T(8,128)(2,1)S(1)} collective-permute-done((bf16[128,2048]{1,0:T(8,128)(2,1)S(1)}, bf16[128,2048]{1,0:T(8,128)(2,1)S(1)}, u32[]{:S(2)}, u32[]{:S(2)}) %collective-permute-start.3) | collective-permute-done | bytes 524320 | tf_op jit(solution)/shard_map/ppermute | solution.py:418
  80.5 2.2 %far_slots.1 = (bf16[384,2048]{1,0:T(8,128)(2,1)}, bf16[64,2048]{1,0:T(8,128)(2,1)}) custom-call(bf16[384,128]{1,0:T(8,128)(2,1)S(1)} %get-tuple-element.31.pick_ref, bf16[128,2048]{1,0:T(8,128)(2,1)S(1)} %collective-permute-done.3.state_ref, bf16[128,2048]{1,0:T(8,128)(2,1)S(1)} %copy-done), custom_call_target="tpu_custom_call" | custom-call | flops 399999991808 | bytes 3145728 | tf_op jit(solution)/shard_map/far_slots/pallas_call | solution.py:532
  82.6 1.7 all-to-all-done.2
  84.3 4.3 %all-to-all-start.4 = ((bf16[8,48,2048]{2,1,0:T(8,128)(2,1)}), bf16[8,48,2048]{2,1,0:T(8,128)(2,1)}, u32[]{:S(2)}, u32[]{:S(2)}) async-start(bf16[8,48,2048]{2,1,0:T(8,128)(2,1)} %bitcast.25), calls=%async_computation.4 | async-start | bytes 3145728 | tf_op jit(solution)/shard_map/all_to_all | solution.py:383
  88.6 1.2 later_slots.1.refs_0_
  89.9 14.9 %near_first.1 = bf16[384,2048]{1,0:T(8,128)(2,1)} custom-call(bf16[192,2048]{1,0:T(8,128)(2,1)} %bitcast.8.rows_hbm, bf16[192,2048]{1,0:T(8,128)(2,1)} %later_slots.1.refs_0_, bf16[8,48,2048]{2,1,0:T(8,128)(2,1)} %bitcast.27, bf16[4,2048,1408]{2,1,0:T(8,128)(2,1)} %refs_1_.3, bf16[4,2048,1408]{2,1,0:T(8,128)(2,1)} %refs_2_.5, bf16[4,1408,2048]{2,1,0:T(8,128)(2,1)} %refs_3_.3), custom_call_target="tpu_custom_call" | custom-call | flops 6643777536 | bytes 34603008 | tf_op jit(solution)/shard_map/near_first/pallas_call | solution.py:318
  104.8 3.9 %all-to-all-done.4 = bf16[8,48,2048]{2,1,0:T(8,128)(2,1)} async-done(((bf16[8,48,2048]{2,1,0:T(8,128)(2,1)}), bf16[8,48,2048]{2,1,0:T(8,128)(2,1)}, u32[]{:S(2)}, u32[]{:S(2)}) %all-to-all-start.4) | async-done | bytes 1572896 | tf_op jit(solution)/shard_map/all_to_all | solution.py:383
  108.7 4.3 %all-to-all-start.3 = ((bf16[8,48,2048]{2,1,0:T(8,128)(2,1)}), bf16[8,48,2048]{2,1,0:T(8,128)(2,1)}, u32[]{:S(2)}, u32[]{:S(2)}) async-start(bf16[8,48,2048]{2,1,0:T(8,128)(2,1)} %bitcast.29), calls=%async_computation.3 | async-start | bytes 3145728 | tf_op jit(solution)/shard_map/all_to_all | solution.py:383
  113.0 0.5 collective-permute-start.4
  113.5 24.4 %far_experts.1 = bf16[384,2048]{1,0:T(8,128)(2,1)} custom-call(bf16[384,2048]{1,0:T(8,128)(2,1)} %bitcast.13.rows_hbm, bf16[8,48,2048]{2,1,0:T(8,128)(2,1)} %bitcast.30, bf16[4,2048,1408]{2,1,0:T(8,128)(2,1)} %refs_1_.3, bf16[4,2048,1408]{2,1,0:T(8,128)(2,1)} %refs_2_.5, bf16[4,1408,2048]{2,1,0:T(8,128)(2,1)} %refs_3_.3), custom_call_target="tpu_custom_call" | custom-call | flops 13287555072 | bytes 69206016 | tf_op jit(solution)/shard_map/far_experts/pallas_call | solution.py:318
  137.9 0.8 all-to-all-done.3.refs_1_
  138.7 3.9 %all-to-all-start.5 = ((bf16[8,48,2048]{2,1,0:T(8,128)(2,1)}), bf16[8,48,2048]{2,1,0:T(8,128)(2,1)S(1)}, u32[]{:S(2)}, u32[]{:S(2)}) async-start(bf16[8,48,2048]{2,1,0:T(8,128)(2,1)} %ordered.3), calls=%async_computation.5 | async-start | bytes 3145728 | tf_op jit(solution)/shard_map/all_to_all | solution.py:383
  142.6 2.6 %mix_first.1 = (f32[128,2048]{1,0:T(8,128)S(1)}, f32[8,128]{1,0:T(8,128)S(1)}) custom-call(s32[128,128]{1,0:T(8,128)S(1)} %get-tuple-element.24.slots_ref, f32[128,128]{1,0:T(8,128)S(1)} %copy-done.6, bf16[384,2048]{1,0:T(8,128)(2,1)} %bitcast.11.rows_hbm.back_ref, bf16[128,2048]{1,0:T(8,128)(2,1)S(1)} %copy-done), custom_call_target="tpu_custom_call" | custom-call | tf_op jit(solution)/shard_map/mix_first/pallas_call | solution.py:577
  145.3 1.0 copy-done.1
  146.2 13.8 %near_second.1 = bf16[192,2048]{1,0:T(8,128)(2,1)} custom-call(bf16[384,2048]{1,0:T(8,128)(2,1)} %bitcast.11.rows_hbm.back_ref, bf16[4,2048,1408]{2,1,0:T(8,128)(2,1)} %refs_1_.3, bf16[4,2048,1408]{2,1,0:T(8,128)(2,1)} %refs_2_.5, bf16[4,1408,2048]{2,1,0:T(8,128)(2,1)} %refs_3_.3), custom_call_target="tpu_custom_call" | custom-call | flops 6643777536 | bytes 34603008 | tf_op jit(solution)/shard_map/near_second/pallas_call | solution.py:318
  160.1 2.3 %all-to-all-done.5 = bf16[8,48,2048]{2,1,0:T(8,128)(2,1)S(1)} async-done(((bf16[8,48,2048]{2,1,0:T(8,128)(2,1)}), bf16[8,48,2048]{2,1,0:T(8,128)(2,1)S(1)}, u32[]{:S(2)}, u32[]{:S(2)}) %all-to-all-start.5) | async-done | bytes 1572896 | tf_op jit(solution)/shard_map/all_to_all | solution.py:383
  162.4 1.7 mix_far.1
  164.1 2.3 %collective-permute-start.5 = (bf16[128,2048]{1,0:T(8,128)(2,1)S(1)}, bf16[128,2048]{1,0:T(8,128)(2,1)S(1)}, u32[]{:S(2)}, u32[]{:S(2)}) collective-permute-start(bf16[128,2048]{1,0:T(8,128)(2,1)S(1)} %get-tuple-element.37.refs_1_), channel_id=1, source_target_pairs={{0,8},{1,9},{2,10},{3,11},{4,12},{5,13},{6,14},{7,15},{8,0},{9,1},... | collective-permute-start | bytes 1572872 | tf_op jit(solution)/shard_map/ppermute | solution.py:418
  166.4 4.2 %all-to-all-start.6 = ((bf16[8,24,2048]{2,1,0:T(8,128)(2,1)}), bf16[8,24,2048]{2,1,0:T(8,128)(2,1)}, u32[]{:S(2)}, u32[]{:S(2)}) async-start(bf16[8,24,2048]{2,1,0:T(8,128)(2,1)} %ordered.4), calls=%async_computation.6 | async-start | bytes 1572864 | tf_op jit(solution)/shard_map/all_to_all | solution.py:383
  170.6 0.7 collective-permute-start.6
  171.3 18.5 %collective-permute-done.5.refs_0_ = bf16[128,2048]{1,0:T(8,128)(2,1)S(1)} collective-permute-done((bf16[128,2048]{1,0:T(8,128)(2,1)S(1)}, bf16[128,2048]{1,0:T(8,128)(2,1)S(1)}, u32[]{:S(2)}, u32[]{:S(2)}) %collective-permute-start.5) | collective-permute-done | bytes 524320 | tf_op jit(solution)/shard_map/ppermute | solution.py:418
  189.8 0.1 collective-permute-done.6.refs_4_
  190.0 3.5 %all-to-all-done.6 = bf16[8,24,2048]{2,1,0:T(8,128)(2,1)} async-done(((bf16[8,24,2048]{2,1,0:T(8,128)(2,1)}), bf16[8,24,2048]{2,1,0:T(8,128)(2,1)}, u32[]{:S(2)}, u32[]{:S(2)}) %all-to-all-start.6) | async-done | bytes 786464 | tf_op jit(solution)/shard_map/all_to_all | solution.py:383
  193.5 2.9 %mix_second.1 = (bf16[128,2048]{1,0:T(8,128)(2,1)}, f32[4,128]{1,0:T(4,128)}) custom-call(s32[128,128]{1,0:T(8,128)S(1)} %get-tuple-element.24.slots_ref, f32[128,128]{1,0:T(8,128)S(1)} %copy-done.7, bf16[192,2048]{1,0:T(8,128)(2,1)} %bitcast.16.back_ref, bf16[128,2048]{1,0:T(8,128)(2,1)S(1)} %copy-done, f32[128,2048]{1,0:T(8,128)S(1)} %copy-done.2, ...), custom_call_target="tpu_custom_call" | custom-call | tf_op jit(solution)/shard_map/mix_second/pallas_call | solution.py:577
  (25 shorter events, 0.1 us)
Async XLA Ops:
  2.3 17.3 %collective-permute-start = (bf16[64,2048]{1,0:T(8,128)(2,1)}, bf16[64,2048]{1,0:T(8,128)(2,1)S(1)}, u32[]{:S(2)}, u32[]{:S(2)}) collective-permute-start(bf16[64,2048]{1,0:T(8,128)(2,1)} %get-tuple-element.23), channel_id=1, source_target_pairs={{0,8},{1,9},{2,10},{3,11},{4,12},{5,13},{6,14},{7,15},{8,0},{9,1},... | collective-permute-start | bytes 786440 | tf_op jit(solution)/shard_map/ppermute | solution.py:418
  6.4 13.2 %all-to-all-start = ((s32[16,1,128]{2,1,0:T(1,128)}), s32[16,1,128]{2,1,0:T(1,128)S(1)}, u32[]{:S(2)}, u32[]{:S(2)}) async-start(s32[16,1,128]{2,1,0:T(1,128)} %get-tuple-element.22), calls=%async_computation | async-start | bytes 16384 | tf_op jit(solution)/shard_map/all_to_all | solution.py:383
  19.6 3.1 %copy-start.3 = (bf16[64,2048]{1,0:T(8,128)(2,1)}, bf16[64,2048]{1,0:T(8,128)(2,1)S(1)}, u32[]{:S(2)}) copy-start(bf16[64,2048]{1,0:T(8,128)(2,1)S(1)} %collective-permute-done._.refs_0_) | copy-start | bytes 786436
  22.7 5.2 %copy-start.12 = (s32[128,16]{0,1:T(8,128)S(1)}, s32[128,16]{0,1:T(8,128)}, u32[]{:S(2)}) copy-start(s32[128,16]{0,1:T(8,128)} %param.11) | copy-start | bytes 24580
  22.7 5.2 %copy-start.9 = (s32[128]{0:T(128)S(1)}, s32[128]{0:T(128)}, u32[]{:S(2)}) copy-start(s32[128]{0:T(128)} %param.12) | copy-start | bytes 1540
  22.7 5.2 %copy-start.10 = (s32[128,4]{0,1:T(4,128)S(1)}, s32[128,4]{0,1:T(4,128)}, u32[]{:S(2)}) copy-start(s32[128,4]{0,1:T(4,128)} %param.13) | copy-start | bytes 6148
  22.7 5.2 %copy-start.11 = (f32[128,4]{0,1:T(4,128)S(1)}, f32[128,4]{0,1:T(4,128)}, u32[]{:S(2)}) copy-start(f32[128,4]{0,1:T(4,128)} %param.14) | copy-start | bytes 6148
  22.7 31.9 %copy-start.8 = (bf16[128,2048]{1,0:T(8,128)(2,1)S(1)}, bf16[128,2048]{1,0:T(8,128)(2,1)}, u32[]{:S(2)}) copy-start(bf16[128,2048]{1,0:T(8,128)(2,1)} %values_ref.1) | copy-start | bytes 1572868
  22.7 31.8 %all-to-all-start.1 = ((bf16[16,16,2048]{2,1,0:T(8,128)(2,1)}), bf16[16,16,2048]{2,1,0:T(8,128)(2,1)S(1)}, u32[]{:S(2)}, u32[]{:S(2)}) async-start(bf16[16,16,2048]{2,1,0:T(8,128)(2,1)} %bitcast.33), calls=%async_computation.1 | async-start | bytes 2097152 | tf_op jit(solution)/shard_map/all_to_all | solution.py:383
  28.8 28.9 %copy-start.5 = (f32[128,128]{1,0:T(8,128)}, f32[128,128]{1,0:T(8,128)S(1)}, u32[]{:S(2)}) copy-start(f32[128,128]{1,0:T(8,128)S(1)} %get-tuple-element.25.columns_ref) | copy-start | bytes 196612
  28.8 25.8 %collective-permute-start.1 = (s32[4,128]{1,0:T(4,128)S(1)}, s32[4,128]{1,0:T(4,128)S(1)}, u32[]{:S(2)}, u32[]{:S(2)}) collective-permute-start(s32[4,128]{1,0:T(4,128)S(1)} %get-tuple-element.28), channel_id=1, source_target_pairs={{0,8},{1,9},{2,10},{3,11},{4,12},{5,13},{6,14},{7,15},{8,0},{9,1},... | collective-permute-start | bytes 6152 | tf_op jit(solution)/shard_map/ppermute | solution.py:418
  31.7 22.9 %collective-permute-start.2 = (f32[4,128]{1,0:T(4,128)S(1)}, f32[4,128]{1,0:T(4,128)S(1)}, u32[]{:S(2)}, u32[]{:S(2)}) collective-permute-start(f32[4,128]{1,0:T(4,128)S(1)} %get-tuple-element.29), channel_id=1, source_target_pairs={{0,8},{1,9},{2,10},{3,11},{4,12},{5,13},{6,14},{7,15},{8,0},{9,1},... | collective-permute-start | bytes 6152 | tf_op jit(solution)/shard_map/ppermute | solution.py:418
  55.0 25.5 %collective-permute-start.3 = (bf16[128,2048]{1,0:T(8,128)(2,1)S(1)}, bf16[128,2048]{1,0:T(8,128)(2,1)S(1)}, u32[]{:S(2)}, u32[]{:S(2)}) collective-permute-start(bf16[128,2048]{1,0:T(8,128)(2,1)S(1)} %token_state.1.state_ref._), channel_id=1, source_target_pairs={{0,8},{1,9},{2,10},{3,11},{4,12},{5,13},{6,14},{7,15},{8,0},{9,1},... | collective-permute-start | bytes 1572872 | tf_op jit(solution)/shard_map/ppermute | solution.py:418
  56.5 24.0 %copy-start = (bf16[128,2048]{1,0:T(8,128)(2,1)S(1)}, bf16[128,2048]{1,0:T(8,128)(2,1)}, u32[]{:S(2)}) copy-start(bf16[128,2048]{1,0:T(8,128)(2,1)} %refs_0_.5) | copy-start | bytes 1572868
  57.7 26.6 %all-to-all-start.2 = ((bf16[8,24,2048]{2,1,0:T(8,128)(2,1)}), bf16[8,24,2048]{2,1,0:T(8,128)(2,1)}, u32[]{:S(2)}, u32[]{:S(2)}) async-start(bf16[8,24,2048]{2,1,0:T(8,128)(2,1)} %bitcast.34), calls=%async_computation.2 | async-start | bytes 1572864 | tf_op jit(solution)/shard_map/all_to_all | solution.py:383
  84.3 24.4 %all-to-all-start.4 = ((bf16[8,48,2048]{2,1,0:T(8,128)(2,1)}), bf16[8,48,2048]{2,1,0:T(8,128)(2,1)}, u32[]{:S(2)}, u32[]{:S(2)}) async-start(bf16[8,48,2048]{2,1,0:T(8,128)(2,1)} %bitcast.25), calls=%async_computation.4 | async-start | bytes 3145728 | tf_op jit(solution)/shard_map/all_to_all | solution.py:383
  108.7 30.0 %all-to-all-start.3 = ((bf16[8,48,2048]{2,1,0:T(8,128)(2,1)}), bf16[8,48,2048]{2,1,0:T(8,128)(2,1)}, u32[]{:S(2)}, u32[]{:S(2)}) async-start(bf16[8,48,2048]{2,1,0:T(8,128)(2,1)} %bitcast.29), calls=%async_computation.3 | async-start | bytes 3145728 | tf_op jit(solution)/shard_map/all_to_all | solution.py:383
  113.0 24.9 %collective-permute-start.4 = (bf16[64,2048]{1,0:T(8,128)(2,1)}, bf16[64,2048]{1,0:T(8,128)(2,1)S(1)}, u32[]{:S(2)}, u32[]{:S(2)}) collective-permute-start(bf16[64,2048]{1,0:T(8,128)(2,1)} %get-tuple-element.35), channel_id=1, source_target_pairs={{0,8},{1,9},{2,10},{3,11},{4,12},{5,13},{6,14},{7,15},{8,0},{9,1},... | collective-permute-start | bytes 786440 | tf_op jit(solution)/shard_map/ppermute | solution.py:418
  138.7 3.9 %copy-start.6 = (f32[128,128]{1,0:T(8,128)S(1)}, f32[128,128]{1,0:T(8,128)}, u32[]{:S(2)}) copy-start(f32[128,128]{1,0:T(8,128)} %copy-done.5) | copy-start | bytes 196612
  138.7 23.7 %all-to-all-start.5 = ((bf16[8,48,2048]{2,1,0:T(8,128)(2,1)}), bf16[8,48,2048]{2,1,0:T(8,128)(2,1)S(1)}, u32[]{:S(2)}, u32[]{:S(2)}) async-start(bf16[8,48,2048]{2,1,0:T(8,128)(2,1)} %ordered.3), calls=%async_computation.5 | async-start | bytes 3145728 | tf_op jit(solution)/shard_map/all_to_all | solution.py:383
  145.3 1.0 copy-start.1
  146.2 16.2 %copy-start.4 = (bf16[64,2048]{1,0:T(8,128)(2,1)S(1)}, bf16[64,2048]{1,0:T(8,128)(2,1)}, u32[]{:S(2)}) copy-start(bf16[64,2048]{1,0:T(8,128)(2,1)} %copy-done.3) | copy-start | bytes 786436
  164.1 25.7 %collective-permute-start.5 = (bf16[128,2048]{1,0:T(8,128)(2,1)S(1)}, bf16[128,2048]{1,0:T(8,128)(2,1)S(1)}, u32[]{:S(2)}, u32[]{:S(2)}) collective-permute-start(bf16[128,2048]{1,0:T(8,128)(2,1)S(1)} %get-tuple-element.37.refs_1_), channel_id=1, source_target_pairs={{0,8},{1,9},{2,10},{3,11},{4,12},{5,13},{6,14},{7,15},{8,0},{9,1},... | collective-permute-start | bytes 1572872 | tf_op jit(solution)/shard_map/ppermute | solution.py:418
  166.4 27.1 %all-to-all-start.6 = ((bf16[8,24,2048]{2,1,0:T(8,128)(2,1)}), bf16[8,24,2048]{2,1,0:T(8,128)(2,1)}, u32[]{:S(2)}, u32[]{:S(2)}) async-start(bf16[8,24,2048]{2,1,0:T(8,128)(2,1)} %ordered.4), calls=%async_computation.6 | async-start | bytes 1572864 | tf_op jit(solution)/shard_map/all_to_all | solution.py:383
  170.6 19.3 %collective-permute-start.6 = (f32[8,128]{1,0:T(8,128)}, f32[8,128]{1,0:T(8,128)}, u32[]{:S(2)}, u32[]{:S(2)}) collective-permute-start(f32[8,128]{1,0:T(8,128)} %get-tuple-element.39), channel_id=1, source_target_pairs={{0,8},{1,9},{2,10},{3,11},{4,12},{5,13},{6,14},{7,15},{8,0},{9,1},... | collective-permute-start | bytes 12296 | tf_op jit(solution)/shard_map/ppermute | solution.py:418
  189.8 3.7 %copy-start.2 = (f32[128,2048]{1,0:T(8,128)S(1)}, f32[128,2048]{1,0:T(8,128)}, u32[]{:S(2)}) copy-start(f32[128,2048]{1,0:T(8,128)} %copy-done.1) | copy-start | bytes 3145732
  189.8 3.7 %copy-start.7 = (f32[128,128]{1,0:T(8,128)S(1)}, f32[128,128]{1,0:T(8,128)}, u32[]{:S(2)}) copy-start(f32[128,128]{1,0:T(8,128)} %copy-done.5) | copy-start | bytes 196612

commit v20 on v19

--- a/solution.py
+++ b/solution.py
@@ -191,7 +191,7 @@
             pltpu.make_async_copy(sent_ref.at[:, cols], out_hbm.at[:, cols], sem.at[n])
         )
         copies[-1].start()
-    lower_grad_ref[...] = grad_ref[tok_rows // 2 :, :]
+    lower_grad_ref[...] = grad_ref[tok_rows - lower_grad_ref.shape[0] :, :]
     for copy in copies:
         copy.wait()
 
@@ -429,7 +429,7 @@
             name="ordered",
         )(array, *earlier_arrays)
 
-    upper = tok_rows // 2
+    upper = 3 * tok_rows // 8
     all_rows, upper_grad = pl.pallas_call(
         repeat_kernel,
         out_shape=(

time: 197 us -> 195 us (0.990)
  waiting for transfers between devices: 80.6 us -> 78.1 us
    all_to_all x7, waiting for transfers between devices: 21.5 us -> 18.8 us  [swap(): lax.all_to_all(array, 'expert', split_axis=0, concat_axis=0, tiled=True,...]
  transfers between devices with their start and end apart: 14 -> 14, of which waited for: 10 -> 11; matrix products, arithmetic and copies ran while one was open for 0% -> 0% of each run, Pallas kernels for 32% -> 32%
where the time goes in v20:
time: 195 us; the launch traced here: 194 us
  waiting for transfers between devices  78.1 us (40%)
  Pallas kernels  71.8 us (37%)
  starting transfers between devices  41.9 us (21%)
    ppermute x7, waiting for transfers between devices, mirrored(): return lax.ppermute(array, 'expert', pairs)  59.3 us
    pallas_call x3, Pallas kernels, expert_call(): pl.pallas_call(functools.partial(expert_kernel, first, count, bool(front)...  53.2 us
    all_to_all x7, starting transfers between devices, swap(): lax.all_to_all(array, 'expert', split_axis=0, concat_axis=0, tiled=True,...  29.9 us
    all_to_all x7, waiting for transfers between devices, swap(): lax.all_to_all(array, 'expert', split_axis=0, concat_axis=0, tiled=True,...  18.8 us
    ppermute x7, starting transfers between devices, mirrored(): return lax.ppermute(array, 'expert', pairs)  12 us
    pallas_call x3, Pallas kernels, mixed_rows(): pl.pallas_call(functools.partial(mix_kernel, len(grads), len(added), len(...  7.15 us
  transfers between devices with their start and end apart: 14, of which 11 were waited for; matrix products, arithmetic and copies ran while one was open for 0% of the time, Pallas kernels for 32%

profile of v20, /device:TPU:0, one launch (start us, length us, event | category | flops | bytes accessed | tf_op | source)
XLA Modules:
  0.0 193.8 jit_solution(15471877296304098773)
XLA Ops:
  0.6 1.6 repeat_rows.1
  2.3 4.0 %collective-permute-start = (bf16[48,2048]{1,0:T(8,128)(2,1)}, bf16[48,2048]{1,0:T(8,128)(2,1)S(1)}, u32[]{:S(2)}, u32[]{:S(2)}) collective-permute-start(bf16[48,2048]{1,0:T(8,128)(2,1)} %get-tuple-element.23), channel_id=1, source_target_pairs={{0,8},{1,9},{2,10},{3,11},{4,12},{5,13},{6,14},{7,15},{8,0},{9,1},... | collective-permute-start | bytes 589832 | tf_op jit(solution)/shard_map/ppermute | solution.py:418
  6.3 3.9 %all-to-all-start = ((s32[16,1,128]{2,1,0:T(1,128)}), s32[16,1,128]{2,1,0:T(1,128)S(1)}, u32[]{:S(2)}, u32[]{:S(2)}) async-start(s32[16,1,128]{2,1,0:T(1,128)} %get-tuple-element.22), calls=%async_computation | async-start | bytes 16384 | tf_op jit(solution)/shard_map/all_to_all | solution.py:383
  10.2 0.1 pad_add_fusion.me_ref
  10.3 6.4 %all-to-all-done.rows_ref = s32[16,1,128]{2,1,0:T(1,128)S(1)} async-done(((s32[16,1,128]{2,1,0:T(1,128)}), s32[16,1,128]{2,1,0:T(1,128)S(1)}, u32[]{:S(2)}, u32[]{:S(2)}) %all-to-all-start) | async-done | bytes 8224 | tf_op jit(solution)/shard_map/all_to_all | solution.py:383
  16.7 0.0 collective-permute-done._.refs_0_
  16.8 3.0 %fetch_rows.1._ = bf16[256,2048]{1,0:T(8,128)(2,1)} custom-call(s32[2]{0:T(128)S(1)} %pad_add_fusion.me_ref, s32[16,1,128]{2,1,0:T(1,128)S(1)} %all-to-all-done.rows_ref, bf16[256,2048]{1,0:T(8,128)(2,1)} %table_hbm.1, bf16[48,2048]{1,0:T(8,128)(2,1)S(1)} %collective-permute-done._.refs_0_), custom_call_target="tpu_custom_call" | custom-call | tf_op jit(solution)/shard_map/fetch_rows/pallas_call | solution.py:451
  19.8 0.0 copy-start.14
  19.8 0.0 copy-start.11
  19.8 0.0 copy-start.12
  19.8 0.0 copy-start.13
  19.8 0.0 copy-start.8
  19.9 5.1 %all-to-all-start.1 = ((bf16[16,16,2048]{2,1,0:T(8,128)(2,1)}), bf16[16,16,2048]{2,1,0:T(8,128)(2,1)S(1)}, u32[]{:S(2)}, u32[]{:S(2)}) async-start(bf16[16,16,2048]{2,1,0:T(8,128)(2,1)} %bitcast.33), calls=%async_computation.1 | async-start | bytes 2097152 | tf_op jit(solution)/shard_map/all_to_all | solution.py:383
  25.0 0.9 near_plan.1
  25.9 2.9 %collective-permute-start.1 = (s32[4,128]{1,0:T(4,128)S(1)}, s32[4,128]{1,0:T(4,128)S(1)}, u32[]{:S(2)}, u32[]{:S(2)}) collective-permute-start(s32[4,128]{1,0:T(4,128)S(1)} %get-tuple-element.28), channel_id=1, source_target_pairs={{0,8},{1,9},{2,10},{3,11},{4,12},{5,13},{6,14},{7,15},{8,0},{9,1},... | collective-permute-start | bytes 6152 | tf_op jit(solution)/shard_map/ppermute | solution.py:418
  28.8 0.1 collective-permute-start.2
  28.9 22.8 %collective-permute-done.1.ids_ref = s32[4,128]{1,0:T(4,128)S(1)} collective-permute-done((s32[4,128]{1,0:T(4,128)S(1)}, s32[4,128]{1,0:T(4,128)S(1)}, u32[]{:S(2)}, u32[]{:S(2)}) %collective-permute-start.1) | collective-permute-done | bytes 2080 | tf_op jit(solution)/shard_map/ppermute | solution.py:418
  51.7 0.0 collective-permute-done.2.weights_ref
  51.7 0.4 token_state.1.state_ref._
  52.1 1.5 collective-permute-start.3
  53.6 1.2 first_slots.1
  54.8 4.2 %all-to-all-start.2 = ((bf16[8,24,2048]{2,1,0:T(8,128)(2,1)}), bf16[8,24,2048]{2,1,0:T(8,128)(2,1)}, u32[]{:S(2)}, u32[]{:S(2)}) async-start(bf16[8,24,2048]{2,1,0:T(8,128)(2,1)} %bitcast.34), calls=%async_computation.2 | async-start | bytes 1572864 | tf_op jit(solution)/shard_map/all_to_all | solution.py:383
  59.1 0.8 far_plan.1
  59.9 17.7 %collective-permute-done.3.state_ref = bf16[128,2048]{1,0:T(8,128)(2,1)S(1)} collective-permute-done((bf16[128,2048]{1,0:T(8,128)(2,1)S(1)}, bf16[128,2048]{1,0:T(8,128)(2,1)S(1)}, u32[]{:S(2)}, u32[]{:S(2)}) %collective-permute-start.3) | collective-permute-done | bytes 524320 | tf_op jit(solution)/shard_map/ppermute | solution.py:418
  77.6 2.2 %far_slots.1 = (bf16[384,2048]{1,0:T(8,128)(2,1)}, bf16[80,2048]{1,0:T(8,128)(2,1)}) custom-call(bf16[384,128]{1,0:T(8,128)(2,1)S(1)} %get-tuple-element.31.pick_ref, bf16[128,2048]{1,0:T(8,128)(2,1)S(1)} %collective-permute-done.3.state_ref, bf16[128,2048]{1,0:T(8,128)(2,1)S(1)} %copy-done), custom_call_target="tpu_custom_call" | custom-call | flops 399999991808 | bytes 3145728 | tf_op jit(solution)/shard_map/far_slots/pallas_call | solution.py:532
  79.8 1.7 all-to-all-done.2
  81.5 4.3 %all-to-all-start.4 = ((bf16[8,48,2048]{2,1,0:T(8,128)(2,1)}), bf16[8,48,2048]{2,1,0:T(8,128)(2,1)}, u32[]{:S(2)}, u32[]{:S(2)}) async-start(bf16[8,48,2048]{2,1,0:T(8,128)(2,1)} %bitcast.25), calls=%async_computation.4 | async-start | bytes 3145728 | tf_op jit(solution)/shard_map/all_to_all | solution.py:383
  85.8 1.2 later_slots.1.refs_0_
  87.0 14.9 %near_first.1 = bf16[384,2048]{1,0:T(8,128)(2,1)} custom-call(bf16[192,2048]{1,0:T(8,128)(2,1)} %bitcast.8.rows_hbm, bf16[192,2048]{1,0:T(8,128)(2,1)} %later_slots.1.refs_0_, bf16[8,48,2048]{2,1,0:T(8,128)(2,1)} %bitcast.27, bf16[4,2048,1408]{2,1,0:T(8,128)(2,1)} %refs_1_.3, bf16[4,2048,1408]{2,1,0:T(8,128)(2,1)} %refs_2_.5, bf16[4,1408,2048]{2,1,0:T(8,128)(2,1)} %refs_3_.3), custom_call_target="tpu_custom_call" | custom-call | flops 6643777536 | bytes 34603008 | tf_op jit(solution)/shard_map/near_first/pallas_call | solution.py:318
  102.0 3.9 %all-to-all-done.4 = bf16[8,48,2048]{2,1,0:T(8,128)(2,1)} async-done(((bf16[8,48,2048]{2,1,0:T(8,128)(2,1)}), bf16[8,48,2048]{2,1,0:T(8,128)(2,1)}, u32[]{:S(2)}, u32[]{:S(2)}) %all-to-all-start.4) | async-done | bytes 1572896 | tf_op jit(solution)/shard_map/all_to_all | solution.py:383
  105.9 4.3 %all-to-all-start.3 = ((bf16[8,48,2048]{2,1,0:T(8,128)(2,1)}), bf16[8,48,2048]{2,1,0:T(8,128)(2,1)}, u32[]{:S(2)}, u32[]{:S(2)}) async-start(bf16[8,48,2048]{2,1,0:T(8,128)(2,1)} %bitcast.29), calls=%async_computation.3 | async-start | bytes 3145728 | tf_op jit(solution)/shard_map/all_to_all | solution.py:383
  110.2 0.5 collective-permute-start.4
  110.6 24.4 %far_experts.1 = bf16[384,2048]{1,0:T(8,128)(2,1)} custom-call(bf16[384,2048]{1,0:T(8,128)(2,1)} %bitcast.13.rows_hbm, bf16[8,48,2048]{2,1,0:T(8,128)(2,1)} %bitcast.30, bf16[4,2048,1408]{2,1,0:T(8,128)(2,1)} %refs_1_.3, bf16[4,2048,1408]{2,1,0:T(8,128)(2,1)} %refs_2_.5, bf16[4,1408,2048]{2,1,0:T(8,128)(2,1)} %refs_3_.3), custom_call_target="tpu_custom_call" | custom-call | flops 13287555072 | bytes 69206016 | tf_op jit(solution)/shard_map/far_experts/pallas_call | solution.py:318
  135.1 0.1 collective-permute-done.4.refs_2_.refs_1_
  135.2 2.1 %all-to-all-done.3.refs_1_ = bf16[8,48,2048]{2,1,0:T(8,128)(2,1)} async-done(((bf16[8,48,2048]{2,1,0:T(8,128)(2,1)}), bf16[8,48,2048]{2,1,0:T(8,128)(2,1)}, u32[]{:S(2)}, u32[]{:S(2)}) %all-to-all-start.3) | async-done | bytes 1572896 | tf_op jit(solution)/shard_map/all_to_all | solution.py:383
  137.3 3.9 %all-to-all-start.5 = ((bf16[8,48,2048]{2,1,0:T(8,128)(2,1)}), bf16[8,48,2048]{2,1,0:T(8,128)(2,1)S(1)}, u32[]{:S(2)}, u32[]{:S(2)}) async-start(bf16[8,48,2048]{2,1,0:T(8,128)(2,1)} %ordered.3), calls=%async_computation.5 | async-start | bytes 3145728 | tf_op jit(solution)/shard_map/all_to_all | solution.py:383
  141.2 2.6 %mix_first.1 = (f32[128,2048]{1,0:T(8,128)S(1)}, f32[8,128]{1,0:T(8,128)S(1)}) custom-call(s32[128,128]{1,0:T(8,128)S(1)} %get-tuple-element.24.slots_ref, f32[128,128]{1,0:T(8,128)S(1)} %copy-done.6, bf16[384,2048]{1,0:T(8,128)(2,1)} %bitcast.11.rows_hbm.back_ref, bf16[128,2048]{1,0:T(8,128)(2,1)S(1)} %copy-done), custom_call_target="tpu_custom_call" | custom-call | tf_op jit(solution)/shard_map/mix_first/pallas_call | solution.py:577
  143.8 1.0 copy-done.1
  144.8 13.8 %near_second.1 = bf16[192,2048]{1,0:T(8,128)(2,1)} custom-call(bf16[384,2048]{1,0:T(8,128)(2,1)} %bitcast.11.rows_hbm.back_ref, bf16[4,2048,1408]{2,1,0:T(8,128)(2,1)} %refs_1_.3, bf16[4,2048,1408]{2,1,0:T(8,128)(2,1)} %refs_2_.5, bf16[4,1408,2048]{2,1,0:T(8,128)(2,1)} %refs_3_.3), custom_call_target="tpu_custom_call" | custom-call | flops 6643777536 | bytes 34603008 | tf_op jit(solution)/shard_map/near_second/pallas_call | solution.py:318
  158.6 2.3 %all-to-all-done.5 = bf16[8,48,2048]{2,1,0:T(8,128)(2,1)S(1)} async-done(((bf16[8,48,2048]{2,1,0:T(8,128)(2,1)}), bf16[8,48,2048]{2,1,0:T(8,128)(2,1)S(1)}, u32[]{:S(2)}, u32[]{:S(2)}) %all-to-all-start.5) | async-done | bytes 1572896 | tf_op jit(solution)/shard_map/all_to_all | solution.py:383
  161.0 1.7 mix_far.1
  162.7 1.2 collective-permute-start.5
  163.8 4.2 %all-to-all-start.6 = ((bf16[8,24,2048]{2,1,0:T(8,128)(2,1)}), bf16[8,24,2048]{2,1,0:T(8,128)(2,1)}, u32[]{:S(2)}, u32[]{:S(2)}) async-start(bf16[8,24,2048]{2,1,0:T(8,128)(2,1)} %ordered.4), calls=%async_computation.6 | async-start | bytes 1572864 | tf_op jit(solution)/shard_map/all_to_all | solution.py:383
  168.1 1.8 collective-permute-start.6
  169.9 18.5 %collective-permute-done.5.refs_0_ = bf16[128,2048]{1,0:T(8,128)(2,1)S(1)} collective-permute-done((bf16[128,2048]{1,0:T(8,128)(2,1)S(1)}, bf16[128,2048]{1,0:T(8,128)(2,1)S(1)}, u32[]{:S(2)}, u32[]{:S(2)}) %collective-permute-start.5) | collective-permute-done | bytes 524320 | tf_op jit(solution)/shard_map/ppermute | solution.py:418
  188.4 0.1 collective-permute-done.6.refs_4_
  188.6 2.4 %all-to-all-done.6 = bf16[8,24,2048]{2,1,0:T(8,128)(2,1)} async-done(((bf16[8,24,2048]{2,1,0:T(8,128)(2,1)}), bf16[8,24,2048]{2,1,0:T(8,128)(2,1)}, u32[]{:S(2)}, u32[]{:S(2)}) %all-to-all-start.6) | async-done | bytes 786464 | tf_op jit(solution)/shard_map/all_to_all | solution.py:383
  191.0 2.9 %mix_second.1 = (bf16[128,2048]{1,0:T(8,128)(2,1)}, f32[4,128]{1,0:T(4,128)}) custom-call(s32[128,128]{1,0:T(8,128)S(1)} %get-tuple-element.24.slots_ref, f32[128,128]{1,0:T(8,128)S(1)} %copy-done.7, bf16[192,2048]{1,0:T(8,128)(2,1)} %bitcast.16.back_ref, bf16[128,2048]{1,0:T(8,128)(2,1)S(1)} %copy-done, f32[128,2048]{1,0:T(8,128)S(1)} %copy-done.2, ...), custom_call_target="tpu_custom_call" | custom-call | tf_op jit(solution)/shard_map/mix_second/pallas_call | solution.py:577
  (29 shorter events, 0.1 us)
Async XLA Ops:
  2.3 14.5 %collective-permute-start = (bf16[48,2048]{1,0:T(8,128)(2,1)}, bf16[48,2048]{1,0:T(8,128)(2,1)S(1)}, u32[]{:S(2)}, u32[]{:S(2)}) collective-permute-start(bf16[48,2048]{1,0:T(8,128)(2,1)} %get-tuple-element.23), channel_id=1, source_target_pairs={{0,8},{1,9},{2,10},{3,11},{4,12},{5,13},{6,14},{7,15},{8,0},{9,1},... | collective-permute-start | bytes 589832 | tf_op jit(solution)/shard_map/ppermute | solution.py:418
  6.3 10.4 %all-to-all-start = ((s32[16,1,128]{2,1,0:T(1,128)}), s32[16,1,128]{2,1,0:T(1,128)S(1)}, u32[]{:S(2)}, u32[]{:S(2)}) async-start(s32[16,1,128]{2,1,0:T(1,128)} %get-tuple-element.22), calls=%async_computation | async-start | bytes 16384 | tf_op jit(solution)/shard_map/all_to_all | solution.py:383
  16.7 3.1 %copy-start.3 = (bf16[48,2048]{1,0:T(8,128)(2,1)}, bf16[48,2048]{1,0:T(8,128)(2,1)S(1)}, u32[]{:S(2)}) copy-start(bf16[48,2048]{1,0:T(8,128)(2,1)S(1)} %collective-permute-done._.refs_0_) | copy-start | bytes 589828
  19.8 5.2 %copy-start.14 = (s32[128,16]{0,1:T(8,128)S(1)}, s32[128,16]{0,1:T(8,128)}, u32[]{:S(2)}) copy-start(s32[128,16]{0,1:T(8,128)} %param.11) | copy-start | bytes 24580
  19.8 5.2 %copy-start.11 = (s32[128]{0:T(128)S(1)}, s32[128]{0:T(128)}, u32[]{:S(2)}) copy-start(s32[128]{0:T(128)} %param.12) | copy-start | bytes 1540
  19.8 5.2 %copy-start.12 = (s32[128,4]{0,1:T(4,128)S(1)}, s32[128,4]{0,1:T(4,128)}, u32[]{:S(2)}) copy-start(s32[128,4]{0,1:T(4,128)} %param.13) | copy-start | bytes 6148
  19.8 5.2 %copy-start.13 = (f32[128,4]{0,1:T(4,128)S(1)}, f32[128,4]{0,1:T(4,128)}, u32[]{:S(2)}) copy-start(f32[128,4]{0,1:T(4,128)} %param.14) | copy-start | bytes 6148
  19.8 31.9 %copy-start.8 = (bf16[128,2048]{1,0:T(8,128)(2,1)S(1)}, bf16[128,2048]{1,0:T(8,128)(2,1)}, u32[]{:S(2)}) copy-start(bf16[128,2048]{1,0:T(8,128)(2,1)} %values_ref.1) | copy-start | bytes 1572868
  19.9 31.8 %all-to-all-start.1 = ((bf16[16,16,2048]{2,1,0:T(8,128)(2,1)}), bf16[16,16,2048]{2,1,0:T(8,128)(2,1)S(1)}, u32[]{:S(2)}, u32[]{:S(2)}) async-start(bf16[16,16,2048]{2,1,0:T(8,128)(2,1)} %bitcast.33), calls=%async_computation.1 | async-start | bytes 2097152 | tf_op jit(solution)/shard_map/all_to_all | solution.py:383
  25.9 28.9 %copy-start.5 = (f32[128,128]{1,0:T(8,128)}, f32[128,128]{1,0:T(8,128)S(1)}, u32[]{:S(2)}) copy-start(f32[128,128]{1,0:T(8,128)S(1)} %get-tuple-element.25.columns_ref) | copy-start | bytes 196612
  25.9 25.8 %collective-permute-start.1 = (s32[4,128]{1,0:T(4,128)S(1)}, s32[4,128]{1,0:T(4,128)S(1)}, u32[]{:S(2)}, u32[]{:S(2)}) collective-permute-start(s32[4,128]{1,0:T(4,128)S(1)} %get-tuple-element.28), channel_id=1, source_target_pairs={{0,8},{1,9},{2,10},{3,11},{4,12},{5,13},{6,14},{7,15},{8,0},{9,1},... | collective-permute-start | bytes 6152 | tf_op jit(solution)/shard_map/ppermute | solution.py:418
  28.8 22.9 %collective-permute-start.2 = (f32[4,128]{1,0:T(4,128)S(1)}, f32[4,128]{1,0:T(4,128)S(1)}, u32[]{:S(2)}, u32[]{:S(2)}) collective-permute-start(f32[4,128]{1,0:T(4,128)S(1)} %get-tuple-element.29), channel_id=1, source_target_pairs={{0,8},{1,9},{2,10},{3,11},{4,12},{5,13},{6,14},{7,15},{8,0},{9,1},... | collective-permute-start | bytes 6152 | tf_op jit(solution)/shard_map/ppermute | solution.py:418
  52.1 25.5 %collective-permute-start.3 = (bf16[128,2048]{1,0:T(8,128)(2,1)S(1)}, bf16[128,2048]{1,0:T(8,128)(2,1)S(1)}, u32[]{:S(2)}, u32[]{:S(2)}) collective-permute-start(bf16[128,2048]{1,0:T(8,128)(2,1)S(1)} %token_state.1.state_ref._), channel_id=1, source_target_pairs={{0,8},{1,9},{2,10},{3,11},{4,12},{5,13},{6,14},{7,15},{8,0},{9,1},... | collective-permute-start | bytes 1572872 | tf_op jit(solution)/shard_map/ppermute | solution.py:418
  53.6 24.0 %copy-start = (bf16[128,2048]{1,0:T(8,128)(2,1)S(1)}, bf16[128,2048]{1,0:T(8,128)(2,1)}, u32[]{:S(2)}) copy-start(bf16[128,2048]{1,0:T(8,128)(2,1)} %refs_0_.5) | copy-start | bytes 1572868
  54.8 26.6 %all-to-all-start.2 = ((bf16[8,24,2048]{2,1,0:T(8,128)(2,1)}), bf16[8,24,2048]{2,1,0:T(8,128)(2,1)}, u32[]{:S(2)}, u32[]{:S(2)}) async-start(bf16[8,24,2048]{2,1,0:T(8,128)(2,1)} %bitcast.34), calls=%async_computation.2 | async-start | bytes 1572864 | tf_op jit(solution)/shard_map/all_to_all | solution.py:383
  59.9 19.9 %copy-start.9 = (f32[128,128]{1,0:T(8,128)}, f32[128,128]{1,0:T(8,128)S(1)}, u32[]{:S(2)}) copy-start(f32[128,128]{1,0:T(8,128)S(1)} %get-tuple-element.34.columns_ref) | copy-start | bytes 196612
  81.5 24.4 %all-to-all-start.4 = ((bf16[8,48,2048]{2,1,0:T(8,128)(2,1)}), bf16[8,48,2048]{2,1,0:T(8,128)(2,1)}, u32[]{:S(2)}, u32[]{:S(2)}) async-start(bf16[8,48,2048]{2,1,0:T(8,128)(2,1)} %bitcast.25), calls=%async_computation.4 | async-start | bytes 3145728 | tf_op jit(solution)/shard_map/all_to_all | solution.py:383
  105.9 31.4 %all-to-all-start.3 = ((bf16[8,48,2048]{2,1,0:T(8,128)(2,1)}), bf16[8,48,2048]{2,1,0:T(8,128)(2,1)}, u32[]{:S(2)}, u32[]{:S(2)}) async-start(bf16[8,48,2048]{2,1,0:T(8,128)(2,1)} %bitcast.29), calls=%async_computation.3 | async-start | bytes 3145728 | tf_op jit(solution)/shard_map/all_to_all | solution.py:383
  110.2 25.0 %collective-permute-start.4 = (bf16[80,2048]{1,0:T(8,128)(2,1)}, bf16[80,2048]{1,0:T(8,128)(2,1)S(1)}, u32[]{:S(2)}, u32[]{:S(2)}) collective-permute-start(bf16[80,2048]{1,0:T(8,128)(2,1)} %get-tuple-element.35), channel_id=1, source_target_pairs={{0,8},{1,9},{2,10},{3,11},{4,12},{5,13},{6,14},{7,15},{8,0},{9,1},... | collective-permute-start | bytes 983048 | tf_op jit(solution)/shard_map/ppermute | solution.py:418
  137.3 3.9 %copy-start.6 = (f32[128,128]{1,0:T(8,128)S(1)}, f32[128,128]{1,0:T(8,128)}, u32[]{:S(2)}) copy-start(f32[128,128]{1,0:T(8,128)} %copy-done.5) | copy-start | bytes 196612
  137.3 23.7 %all-to-all-start.5 = ((bf16[8,48,2048]{2,1,0:T(8,128)(2,1)}), bf16[8,48,2048]{2,1,0:T(8,128)(2,1)S(1)}, u32[]{:S(2)}, u32[]{:S(2)}) async-start(bf16[8,48,2048]{2,1,0:T(8,128)(2,1)} %ordered.3), calls=%async_computation.5 | async-start | bytes 3145728 | tf_op jit(solution)/shard_map/all_to_all | solution.py:383
  143.8 1.0 copy-start.1
  144.8 16.2 %copy-start.4 = (bf16[48,2048]{1,0:T(8,128)(2,1)S(1)}, bf16[48,2048]{1,0:T(8,128)(2,1)}, u32[]{:S(2)}) copy-start(bf16[48,2048]{1,0:T(8,128)(2,1)} %copy-done.3) | copy-start | bytes 589828
  144.8 16.2 %copy-start.10 = (f32[128,128]{1,0:T(8,128)S(1)}, f32[128,128]{1,0:T(8,128)}, u32[]{:S(2)}) copy-start(f32[128,128]{1,0:T(8,128)} %copy-done.9) | copy-start | bytes 196612
  162.7 25.7 %collective-permute-start.5 = (bf16[128,2048]{1,0:T(8,128)(2,1)S(1)}, bf16[128,2048]{1,0:T(8,128)(2,1)S(1)}, u32[]{:S(2)}, u32[]{:S(2)}) collective-permute-start(bf16[128,2048]{1,0:T(8,128)(2,1)S(1)} %get-tuple-element.37.refs_1_), channel_id=1, source_target_pairs={{0,8},{1,9},{2,10},{3,11},{4,12},{5,13},{6,14},{7,15},{8,0},{9,1},... | collective-permute-start | bytes 1572872 | tf_op jit(solution)/shard_map/ppermute | solution.py:418
  163.8 27.1 %all-to-all-start.6 = ((bf16[8,24,2048]{2,1,0:T(8,128)(2,1)}), bf16[8,24,2048]{2,1,0:T(8,128)(2,1)}, u32[]{:S(2)}, u32[]{:S(2)}) async-start(bf16[8,24,2048]{2,1,0:T(8,128)(2,1)} %ordered.4), calls=%async_computation.6 | async-start | bytes 1572864 | tf_op jit(solution)/shard_map/all_to_all | solution.py:383
  168.1 20.5 %collective-permute-start.6 = (f32[8,128]{1,0:T(8,128)}, f32[8,128]{1,0:T(8,128)}, u32[]{:S(2)}, u32[]{:S(2)}) collective-permute-start(f32[8,128]{1,0:T(8,128)} %get-tuple-element.39), channel_id=1, source_target_pairs={{0,8},{1,9},{2,10},{3,11},{4,12},{5,13},{6,14},{7,15},{8,0},{9,1},... | collective-permute-start | bytes 12296 | tf_op jit(solution)/shard_map/ppermute | solution.py:418
  188.4 2.5 %copy-start.2 = (f32[128,2048]{1,0:T(8,128)S(1)}, f32[128,2048]{1,0:T(8,128)}, u32[]{:S(2)}) copy-start(f32[128,2048]{1,0:T(8,128)} %copy-done.1) | copy-start | bytes 3145732
  188.4 2.5 %copy-start.7 = (f32[128,128]{1,0:T(8,128)S(1)}, f32[128,128]{1,0:T(8,128)}, u32[]{:S(2)}) copy-start(f32[128,128]{1,0:T(8,128)} %copy-done.5) | copy-start | bytes 196612
